TPU v7x, 32 devices: a whole 2x2x4 slice. The times are simulated.
32 devices in a mesh: space: 8 (over z, x), filt: 4 (over y, core).
Axes of the slice: x: 2, y: 2, z: 4, core: 2. Of those that a mesh axis runs over, the one named last changes fastest.
Arguments:
- inputs: bfloat16 [8, 32, 32, 256], P('space'), may hold values from -6 to 6
- out_grad: bfloat16 [8, 256, 1024], P('space', 'filt'), may hold values from -6 to 6
- pre_act: bfloat16 [8, 256, 1024], P('space', 'filt'), may hold values from -8 to 8
- weight: bfloat16 [27, 256, 256], P(None, 'filt'), may hold values from -0.078125 to 0.078125
Outputs:
- grad_input: bfloat16 [8, 32, 32, 256], P('space', 'filt')
- grad_weight: float32 [256, 27, 256], P('space', None, 'filt')
All inputs are finite; a program needn't handle non-finite values.
Results may differ from a plain program's by a relative error of at most 0.0049.
Values may be sent and summed in bfloat16 or wider, within the bound.
No kernel may reach another device: no remote copies, remote signals or barrier semaphores. Data moves between devices by JAX's collectives and lax.ppermute only.
A program may use at most 64 MiB of HBM per device.

v0:
```python
import jax
import jax.numpy as jnp
from jax import lax
from jax.sharding import PartitionSpec as P


def extended(block, sides, width):
    for axis, dim in sides:
        count = lax.axis_size(axis)
        forward = [(i, i + 1) for i in range(count - 1)]
        backward = [(target, source) for source, target in forward]
        low = lax.ppermute(
            lax.slice_in_dim(block, block.shape[dim] - width, None, axis=dim), axis, forward
        )
        high = lax.ppermute(lax.slice_in_dim(block, 0, width, axis=dim), axis, backward)
        block = jnp.concatenate([low, block, high], axis=dim)
    return block


def silu_grad(values):
    sig = jax.nn.sigmoid(values)
    return sig * (1.0 + values * (1.0 - sig))


def on_device(inputs, out_grad, pre_act, weight):
    slab_depth, grid_height, grid_width, in_chans = inputs.shape
    tap_count = weight.shape[0]
    filt_local = weight.shape[1]
    cell_count = slab_depth * grid_height * grid_width
    d_pre = (out_grad.astype(jnp.float32) * silu_grad(pre_act.astype(jnp.float32))).astype(
        jnp.bfloat16
    )
    rimmed = extended(d_pre, (("space", 0),), 1)
    rim_grid = rimmed.reshape(slab_depth + 2, filt_local, grid_height, grid_width)
    padded = jnp.pad(rim_grid, ((0, 0), (0, 0), (1, 1), (1, 1)))
    slices = []
    for offset_d in range(3):
        for offset_h in range(3):
            for offset_w in range(3):
                window = padded[
                    2 - offset_d : 2 - offset_d + slab_depth,
                    :,
                    2 - offset_h : 2 - offset_h + grid_height,
                    2 - offset_w : 2 - offset_w + grid_width,
                ]
                slices.append(jnp.moveaxis(window, 1, 0).reshape(filt_local, cell_count))
    stacked = jnp.concatenate(slices, axis=0)
    flat_kernel = weight.reshape(tap_count * filt_local, in_chans)
    partial_sum = lax.dot_general(
        stacked, flat_kernel, (((0,), (0,)), ((), ())), preferred_element_type=jnp.float32
    )
    in_rimmed = extended(inputs, (("space", 0),), 1)
    in_padded = jnp.pad(in_rimmed, ((0, 0), (1, 1), (1, 1), (0, 0)))
    grad_flat = jnp.moveaxis(d_pre, 1, 0).reshape(filt_local, cell_count)
    results = []
    for offset_d in range(3):
        for offset_h in range(3):
            for offset_w in range(3):
                shifted = in_padded[
                    offset_d : offset_d + slab_depth,
                    offset_h : offset_h + grid_height,
                    offset_w : offset_w + grid_width,
                ].reshape(cell_count, in_chans)
                results.append(
                    lax.dot_general(
                        shifted,
                        grad_flat,
                        (((0,), (1,)), ((), ())),
                        preferred_element_type=jnp.float32,
                    )
                )
    all_terms = jnp.stack(results, axis=1)
    grad_scale = float(cell_count * lax.axis_size("space")) ** (-0.5)
    grad_weight = lax.psum_scatter(all_terms, "space", scatter_dimension=0, tiled=True) * grad_scale
    partial_grid = partial_sum.reshape(slab_depth, grid_height, grid_width, in_chans)
    whole_sum = lax.psum(partial_grid, "filt")
    share_rows = grid_height // lax.axis_size("filt")
    grad_input = lax.dynamic_slice_in_dim(
        whole_sum, lax.axis_index("filt") * share_rows, share_rows, 1
    ).astype(jnp.bfloat16)
    return (grad_input, grad_weight)


def solution(mesh):
    placed = (
        P("space", None, None, None),
        P("space", "filt", None),
        P("space", "filt", None),
        P(None, "filt", None),
    )
    return jax.shard_map(
        on_device,
        mesh=mesh,
        in_specs=placed,
        out_specs=(P("space", "filt", None, None), P("space", None, "filt")),
        check_vma=False,
    )
```

profile of v0, /device:TPU:0, one launch (start us, length us, event | category | flops | bytes accessed | tf_op | source)
XLA Modules:
  0.0 191.8 jit_solution(17451770392506983613)
XLA Ops:
  7.2 1.2 fusion.39
  8.4 4.8 %collective-permute-start = (bf16[1,64,1024]{2,1,0:T(8,128)(2,1)S(1)}, bf16[1,64,1024]{2,1,0:T(8,128)(2,1)S(1)}, u32[]{:S(2)}, u32[]{:S(2)}) collective-permute-start(bf16[1,64,1024]{2,1,0:T(8,128)(2,1)S(1)} %fusion.39), channel_id=1, source_target_pairs={{0,4},{4,8},{8,12},{12,16},{16,20},{20,24},{24,28},{1,5},{5,9},{9,... | collective-permute-start | bytes 393224 | tf_op jit(solution)/shard_map/ppermute | solution.py:12
  13.2 1.3 collective-permute-start.1
  14.5 4.6 %collective-permute-start.2 = (bf16[1,32,32,256]{3,2,1,0:T(8,128)(2,1)}, bf16[1,32,32,256]{3,2,1,0:T(8,128)(2,1)S(1)}, u32[]{:S(2)}, u32[]{:S(2)}) collective-permute-start(bf16[1,32,32,256]{3,2,1,0:T(8,128)(2,1)} %param.4), channel_id=1, source_target_pairs={{0,4},{4,8},{8,12},{12,16},{16,20},{20,24},{24,28},{1,5},{5,9},{9,... | collective-permute-start | bytes 1572872 | tf_op jit(solution)/shard_map/ppermute | solution.py:12
  19.1 1.3 collective-permute-start.3
  22.2 2.6 %pad_slice_fusion = (bf16[1,64,32,32]{1,3,2,0:T(8,128)(2,1)S(1)}, bf16[1,64,32,32]{1,3,2,0:T(8,128)(2,1)}, bf16[1,64,32,32]{1,3,2,0:T(8,128)(2,1)}, bf16[1,64,32...) fusion(bf16[3,64,32,32]{1,3,2,0:T(8,128)(2,1)S(1)} %bitcast.263), kind=kLoop, calls=%fused_computation.13 | loop fusion | bytes 2883584 | tf_op jit(solution)/shard_map/slice | solution.py:40
  24.8 1.2 pad_slice_fusion.1
  26.0 1.8 copy.45
  27.8 1.1 copy.44
  29.6 1.7 copy.46
  31.3 1.7 copy.47
  33.0 1.7 copy.48
  34.8 1.7 copy.49
  36.5 1.7 copy.50
  38.2 1.7 copy.51
  39.9 1.7 copy.52
  41.7 1.7 copy.53
  43.5 1.6 constant_dynamic-update-slice_fusion.22
  45.1 1.6 constant_dynamic-update-slice_fusion.21
  46.7 1.6 constant_dynamic-update-slice_fusion.20
  48.2 1.6 bitcast_dynamic-update-slice_fusion.2
  49.8 1.6 constant_dynamic-update-slice_fusion.19
  51.4 1.6 constant_dynamic-update-slice_fusion.18
  52.9 1.6 constant_dynamic-update-slice_fusion.17
  54.5 1.6 constant_dynamic-update-slice_fusion.16
  56.1 1.6 constant_dynamic-update-slice_fusion.15
  57.6 1.6 constant_dynamic-update-slice_fusion.14
  59.2 1.1 select_maximum_fusion
  60.7 2.5 %fusion.67 = (bf16[1,32,32,256]{3,2,1,0:T(8,128)(2,1)S(1)}, bf16[1,32,32,256]{3,2,1,0:T(8,128)(2,1)S(1)}, bf16[1,32,32,256]{3,2,1,0:T(8,128)(2,1)S(1)}, bf16[1,3...) fusion(bf16[3,34,34,256]{3,2,1,0:T(8,128)(2,1)S(1)} %select_max, ...), kind=kLoop, calls=%fused_computation.157 | loop fusion | bytes 19922944 | tf_op jit(solution)/shard_map/slice | solution.py:59
  63.2 0.8 fusion.29
  64.1 0.8 fusion.28
  64.9 0.8 fusion.27
  65.8 0.8 fusion.26
  66.6 0.8 fusion.32
  67.5 0.8 fusion.25
  68.3 0.8 fusion.24
  69.1 0.8 fusion.23
  70.8 0.8 fusion.21
  71.7 0.8 fusion.20
  72.5 0.8 fusion.19
  73.3 0.8 fusion.18
  75.0 0.8 fusion.17
  75.8 0.8 fusion.16
  76.7 0.9 fusion.15
  77.5 0.8 fusion.14
  78.4 0.8 fusion.13
  79.2 0.8 fusion.12
  80.1 0.8 fusion.11
  80.9 0.8 fusion.10
  81.8 0.8 fusion.30
  82.6 0.8 fusion.9
  83.4 0.8 fusion.8
  84.3 0.8 fusion.7
  85.1 0.9 fusion.6
  86.0 5.5 %copy.69 = f32[256,27,64]{2,1,0:T(8,128)} copy(f32[256,27,64]{0,2,1:T(8,128)} %fusion.6) | data formatting | bytes 3538944 | tf_op jit(solution)/shard_map/stack | solution.py:72
  94.2 1.1 copy.63
  95.3 1.1 copy.64
  96.4 1.1 copy.65
  107.7 5.8 %copy.68 = bf16[1024,1728]{1,0:T(8,128)(2,1)} copy(bf16[1024,1728]{0,1:T(8,128)(2,1)} %bitcast.265) | data formatting | bytes 7077888 | tf_op jit(solution)/shard_map/dot_general | solution.py:49
  113.5 3.2 %convolution_bitcast_fusion = f32[1,32,32,256]{3,2,1,0:T(8,128)S(1)} fusion(bf16[32,32,1728]{2,1,0:T(8,128)(2,1)} %bitcast.266, bf16[1728,256,1]{1,0,2:T(8,128)(2,1)S(1)} %bitcast.262), kind=kOutput, calls=%fused_computation.12 | convolution fusion | flops 905969664 | bytes 5472256 | tf_op jit(solution)/shard_map/dot_general | solution.py:49
  116.7 26.1 %all-reduce.3 = bf16[1,32,32,256]{3,2,1,0:T(8,128)(2,1)S(1)} all-reduce(f32[1,32,32,256]{3,2,1,0:T(8,128)S(1)} %convolution_bitcast_fusion), channel_id=1, replica_groups=mesh['space'=8,'filt'=4] {'filt'}, use_global_device_ids=true, to_apply=%region_0.1 | all-reduce | flops 262144 | bytes 1572864 | tf_op jit(solution)/shard_map/psum | solution.py:76
  143.4 39.4 %reduce-scatter.2.cloned.1.call-done = f32[32,27,64]{2,1,0:T(8,128)} async-done(((f32[256,27,64]{2,1,0:T(8,128)}), f32[32,27,64]{2,1,0:T(8,128)}) %reduce-scatter.2.cloned.1.call-update) | async-done | bytes 221200 | tf_op jit(solution)/shard_map/reduce_scatter | solution.py:74
  182.8 1.1 broadcast_multiply_fusion
  183.9 1.0 copy.70
  (70 shorter events, 18.1 us)
Async XLA Ops:
  7.2 106.3 %copy-start = (bf16[27,64,256]{2,1,0:T(8,128)(2,1)S(1)}, bf16[27,64,256]{2,1,0:T(8,128)(2,1)}, u32[]{:S(2)}) copy-start(bf16[27,64,256]{2,1,0:T(8,128)(2,1)} %param.7) | copy-start | bytes 2654212
  7.2 175.6 %reduce-scatter.2.cloned.1.call-start = ((), (), s32[]{:S(2)}) async-start(), calls=%async_computation.1 | async-start | bytes 4718592 | tf_op jit(solution)/shard_map/reduce_scatter | solution.py:74
  8.4 12.1 %collective-permute-start = (bf16[1,64,1024]{2,1,0:T(8,128)(2,1)S(1)}, bf16[1,64,1024]{2,1,0:T(8,128)(2,1)S(1)}, u32[]{:S(2)}, u32[]{:S(2)}) collective-permute-start(bf16[1,64,1024]{2,1,0:T(8,128)(2,1)S(1)} %fusion.39), channel_id=1, source_target_pairs={{0,4},{4,8},{8,12},{12,16},{16,20},{20,24},{24,28},{1,5},{5,9},{9,... | collective-permute-start | bytes 393224 | tf_op jit(solution)/shard_map/ppermute | solution.py:12
  13.2 7.2 %collective-permute-start.1 = (bf16[1,64,1024]{2,1,0:T(8,128)(2,1)S(1)}, bf16[1,64,1024]{2,1,0:T(8,128)(2,1)S(1)}, u32[]{:S(2)}, u32[]{:S(2)}) collective-permute-start(bf16[1,64,1024]{2,1,0:T(8,128)(2,1)S(1)} %fusion.39), channel_id=1, source_target_pairs={{4,0},{8,4},{12,8},{16,12},{20,16},{24,20},{28,24},{5,1},{9,5},{13... | collective-permute-start | bytes 393224 | tf_op jit(solution)/shard_map/ppermute | solution.py:15
  14.5 44.7 %collective-permute-start.2 = (bf16[1,32,32,256]{3,2,1,0:T(8,128)(2,1)}, bf16[1,32,32,256]{3,2,1,0:T(8,128)(2,1)S(1)}, u32[]{:S(2)}, u32[]{:S(2)}) collective-permute-start(bf16[1,32,32,256]{3,2,1,0:T(8,128)(2,1)} %param.4), channel_id=1, source_target_pairs={{0,4},{4,8},{8,12},{12,16},{16,20},{20,24},{24,28},{1,5},{5,9},{9,... | collective-permute-start | bytes 1572872 | tf_op jit(solution)/shard_map/ppermute | solution.py:12
  19.1 40.1 %collective-permute-start.3 = (bf16[1,32,32,256]{3,2,1,0:T(8,128)(2,1)}, bf16[1,32,32,256]{3,2,1,0:T(8,128)(2,1)S(1)}, u32[]{:S(2)}, u32[]{:S(2)}) collective-permute-start(bf16[1,32,32,256]{3,2,1,0:T(8,128)(2,1)} %param.4), channel_id=1, source_target_pairs={{4,0},{8,4},{12,8},{16,12},{20,16},{24,20},{28,24},{5,1},{9,5},{13... | collective-permute-start | bytes 1572872 | tf_op jit(solution)/shard_map/ppermute | solution.py:15
  20.4 0.7 copy-start.12
  21.1 0.7 copy-start.14
  26.0 17.3 %copy-start.9 = (bf16[1,64,32,32]{1,3,2,0:T(8,128)(2,1)S(1)}, bf16[1,64,32,32]{1,3,2,0:T(8,128)(2,1)}, u32[]{:S(2)}) copy-start(bf16[1,64,32,32]{1,3,2,0:T(8,128)(2,1)} %get-tuple-element.46) | copy-start | bytes 393220
  26.0 33.2 %copy-start.1 = (bf16[1,32,32,256]{3,2,1,0:T(8,128)(2,1)S(1)}, bf16[1,32,32,256]{3,2,1,0:T(8,128)(2,1)}, u32[]{:S(2)}) copy-start(bf16[1,32,32,256]{3,2,1,0:T(8,128)(2,1)} %param.4) | copy-start | bytes 1572868
  91.4 0.9 copy-start.8
  91.4 1.7 copy-start.7
  91.5 1.9 copy-start.6
  91.5 2.0 %copy-start.5 = (bf16[1,64,32,32]{1,3,2,0:T(8,128)(2,1)S(1)}, bf16[1,64,32,32]{1,3,2,0:T(8,128)(2,1)}, u32[]{:S(2)}) copy-start(bf16[1,64,32,32]{1,3,2,0:T(8,128)(2,1)} %get-tuple-element.50) | copy-start | bytes 393220
  91.5 2.2 %copy-start.4 = (bf16[1,64,32,32]{1,3,2,0:T(8,128)(2,1)S(1)}, bf16[1,64,32,32]{1,3,2,0:T(8,128)(2,1)}, u32[]{:S(2)}) copy-start(bf16[1,64,32,32]{1,3,2,0:T(8,128)(2,1)} %get-tuple-element.51) | copy-start | bytes 393220
  91.5 2.3 %copy-start.3 = (bf16[1,64,32,32]{1,3,2,0:T(8,128)(2,1)S(1)}, bf16[1,64,32,32]{1,3,2,0:T(8,128)(2,1)}, u32[]{:S(2)}) copy-start(bf16[1,64,32,32]{1,3,2,0:T(8,128)(2,1)} %get-tuple-element.52) | copy-start | bytes 393220
  91.5 2.4 %copy-start.2 = (bf16[1,64,32,32]{1,3,2,0:T(8,128)(2,1)S(1)}, bf16[1,64,32,32]{1,3,2,0:T(8,128)(2,1)}, u32[]{:S(2)}) copy-start(bf16[1,64,32,32]{1,3,2,0:T(8,128)(2,1)} %get-tuple-element.53) | copy-start | bytes 393220
  93.2 4.3 %copy-start.10 = (bf16[1,64,32,32]{1,3,2,0:T(8,128)(2,1)S(1)}, bf16[1,64,32,32]{1,3,2,0:T(8,128)(2,1)}, u32[]{:S(2)}) copy-start(bf16[1,64,32,32]{1,3,2,0:T(8,128)(2,1)} %get-tuple-element.55) | copy-start | bytes 393220
  93.3 4.4 %copy-start.11 = (bf16[64,1024]{1,0:T(8,128)(2,1)S(1)}, bf16[64,1024]{1,0:T(8,128)(2,1)}, u32[]{:S(2)}) copy-start(bf16[64,1024]{1,0:T(8,128)(2,1)} %copy.55) | copy-start | bytes 393220
  94.2 10.2 %copy-start.13 = (bf16[1,64,1024]{2,1,0:T(8,128)(2,1)S(1)}, bf16[1,64,1024]{2,1,0:T(8,128)(2,1)}, u32[]{:S(2)}) copy-start(bf16[1,64,1024]{2,1,0:T(8,128)(2,1)} %copy-done.12) | copy-start | bytes 393220
Sparse Core Ops, SparseCore 0:
  91.6 91.1 reduce-scatter.1
where the time goes:
time: 193 us; the launch traced here: 192 us
  local copies, waits for them, and re-layouts  70.6 us (37%)
  waiting for transfers between devices  39.4 us (20%)
  blocking collectives  26.1 us (14%)
  matrix products  25.9 us (13%)
  between operations  14.4 us (7%)
  starting transfers between devices  12.1 us (6%)
  other arithmetic  3.34 us (2%)
    reduce_scatter x1, waiting for transfers between devices, on_device(): lax.psum_scatter(all_terms, 'space', scatter_dimension=0, tiled=True)  39.4 us
    unnamed x57, local copies, waits for them, and re-layouts  28.9 us
    psum x1, blocking collectives, on_device(): whole_sum = lax.psum(partial_grid, 'filt')  26.1 us
    dot_general x27, matrix products, on_device(): lax.dot_general(shifted, grad_flat, (((0,), (1,)), ((), ())), preferred_e...  22.7 us
    another operation x24, local copies, waits for them, and re-layouts, on_device(): slices.append(jnp.moveaxis(window, 1, 0).reshape(filt_local, cell_count))  21.9 us
    ppermute x2, starting transfers between devices, extended(): lax.ppermute(lax.slice_in_dim(block, block.shape[dim] - width, None, axis...  9.43 us
    dot_general x1, local copies, waits for them, and re-layouts, on_device(): lax.dot_general(stacked, flat_kernel, (((0,), (0,)), ((), ())), preferred...  5.8 us
    another operation x1, local copies, waits for them, and re-layouts, on_device(): all_terms = jnp.stack(results, axis=1)  5.47 us
  transfers between devices with their start and end apart: 5, of which 1 were waited for; matrix products, arithmetic and copies ran while one was open for 33% of the time, Pallas kernels for 0%

commit v1 on v0

v1 whole, which is shorter than its diff:
```python
import functools

import jax
import jax.numpy as jnp
from jax import lax
from jax.experimental import pallas as pl
from jax.experimental.pallas import tpu as pltpu
from jax.sharding import PartitionSpec as P

MIB = 1 << 20
PAIRED = ((0, 0), (2, 0), (0, 1), (2, 1), (0, 2), (2, 2), (1, 0), (1, 2))
VMEM = pl.BlockSpec(memory_space=pltpu.VMEM)
SMEM = pl.BlockSpec(memory_space=pltpu.SMEM)


def silu_grad(values):
    sig = jax.nn.sigmoid(values)
    return sig * (1.0 + values * (1.0 - sig))


def bits_of(count):
    return count.bit_length() - 1


def reversed_bits(value, width):
    return sum(((value >> bit) & 1) << (width - 1 - bit) for bit in range(width))


def call(kernel, outs, scratch=(), flops=0, bytes_accessed=0, limit=24):
    return functools.partial(
        pl.pallas_call,
        kernel,
        out_shape=outs,
        scratch_shapes=scratch,
        compiler_params=pltpu.CompilerParams(vmem_limit_bytes=limit * MIB),
        cost_estimate=pl.CostEstimate(flops=flops, bytes_accessed=bytes_accessed, transcendentals=0),
    )


def windows_kernel(width, blocks, place, own, near, far, inputs, paired, single, keep, send, tall, tall_own, flipped):
    filt, cells = own.shape
    chans = inputs.shape[1]
    rows = chans // blocks
    index = place[0]
    even = lax.rem(index, 2) == 0

    above = jnp.where(even, near[...], far[...])
    below = jnp.where(even, far[...], near[...])
    both = jnp.concatenate([above, below], axis=0).astype(jnp.float32)
    tall[pl.ds(8, cells), :] = both.T
    mine = own[...].astype(jnp.float32)
    tall_own[pl.ds(0, width), :] = jnp.zeros((width, 2 * filt), jnp.float32)
    tall_own[pl.ds(width + cells, width), :] = jnp.zeros((width, 2 * filt), jnp.float32)
    tall_own[pl.ds(width, cells), :] = jnp.concatenate([mine, mine], axis=0).T

    row = lax.broadcasted_iota(jnp.int32, (cells, 2 * filt), 0)
    column = row & (width - 1) if width & (width - 1) == 0 else lax.rem(row, width)
    lane = lax.broadcasted_iota(jnp.int32, (cells, 2 * filt), 1)
    left = lane < filt
    not_last = column != width - 1
    not_first = column != 0

    zero_rows = jnp.zeros((width, paired.shape[1]), jnp.bfloat16)
    paired[pl.ds(0, width), :] = zero_rows
    paired[pl.ds(width + cells, width), :] = zero_rows
    body = pl.ds(width, cells)
    lanes = 2 * filt
    paired[body, 0:lanes] = jnp.where(not_last, tall[pl.ds(9, cells), :], 0.0).astype(jnp.bfloat16)
    paired[body, lanes : 2 * lanes] = tall[pl.ds(8, cells), :].astype(jnp.bfloat16)
    paired[body, 2 * lanes : 3 * lanes] = jnp.where(not_first, tall[pl.ds(7, cells), :], 0.0).astype(jnp.bfloat16)
    after = jnp.where(not_last, tall_own[pl.ds(width + 1, cells), :], 0.0)
    before = jnp.where(not_first, tall_own[pl.ds(width - 1, cells), :], 0.0)
    paired[body, 3 * lanes : 4 * lanes] = jnp.where(left, after, before).astype(jnp.bfloat16)

    up, level, down = (tall_own[pl.ds((2 - b) * width, cells), :] for b in range(3))
    single[:, 0:lanes] = jnp.where(left, up, level).astype(jnp.bfloat16)
    single[:, lanes : lanes + filt] = down[:, 0:filt].astype(jnp.bfloat16)

    order = lax.broadcasted_iota(jnp.int32, (chans, chans), 0)
    count = bits_of(blocks)
    block = index ^ reversed_bits(order >> bits_of(rows), count)
    source = (block << bits_of(rows)) | (order & (rows - 1))
    picked = (lax.broadcasted_iota(jnp.int32, (chans, chans), 1) == source).astype(jnp.bfloat16)
    turned = lax.dot_general(picked, inputs[...], (((1,), (1,)), ((), ())), preferred_element_type=jnp.float32)
    flipped[...] = turned.astype(jnp.bfloat16)

    half = chans // 2
    wide = paired.shape[1]
    for b in range(4):
        window = paired[pl.ds((2 - b) * width, cells), :] if b < 3 else single[...]
        lo = b * wide
        hi = lo + window.shape[1]
        sent = jnp.dot(flipped[pl.ds(half, half), :], window, preferred_element_type=jnp.float32)
        send[:, lo:hi] = sent.astype(jnp.bfloat16)
        kept = jnp.dot(flipped[pl.ds(0, half), :], window, preferred_element_type=jnp.float32)
        keep[:, lo:hi] = kept


def spread_kernel(width, groups, place, paired, single, weight, keep, send, ordered, ordered_single):
    cells = single.shape[0]
    filt = weight.shape[1]
    part = cells // groups
    index = place[1]
    for b in range(3):
        for slot, (a, c) in enumerate(PAIRED):
            ordered[b, pl.ds(slot * filt, filt), :] = weight[9 * a + 3 * b + c]
        ordered_single[pl.ds(b * filt, filt), :] = weight[9 + 3 * b + 1]
    count = bits_of(groups)
    for target in reversed(range(groups)):
        block = 0
        for bit in range(count):
            differs = (target >> (count - 1 - bit)) & 1
            block = block + (((index >> bit) & 1) ^ differs) * (1 << bit)
        start = pl.multiple_of(block * part, part)
        total = jnp.dot(single[pl.ds(start, part), :], ordered_single[...], preferred_element_type=jnp.float32)
        for b in range(3):
            window = paired[pl.ds(pl.multiple_of(start + (2 - b) * width, width), part), :]
            total = total + jnp.dot(window, ordered[b], preferred_element_type=jnp.float32)
        if target < groups // 2:
            keep[pl.ds(target * part, part), :] = total
        else:
            send[pl.ds((target - groups // 2) * part, part), :] = total.astype(jnp.bfloat16)


def halve_kernel(kept, came, keep, send):
    half = keep.shape[0]
    keep[...] = kept[0:half, :] + came[0:half, :].astype(jnp.float32)
    send[...] = (kept[half:, :] + came[half:, :].astype(jnp.float32)).astype(jnp.bfloat16)


def last_input_kernel(kept, came, out):
    out[...] = (kept[...] + came[...].astype(jnp.float32)).astype(out.dtype)


def last_weight_kernel(scale, filt, kept, came, out):
    total = (kept[...] + came[...].astype(jnp.float32)) * scale
    wide = len(PAIRED) * filt
    for b in range(3):
        for slot, (a, c) in enumerate(PAIRED):
            lo = b * wide + slot * filt
            out[:, 9 * a + 3 * b + c, :] = total[:, lo : lo + filt]
        lo = 3 * wide + b * filt
        out[:, 9 + 3 * b + 1, :] = total[:, lo : lo + filt]


def swapped(value, axis, distance):
    count = lax.axis_size(axis)
    return lax.ppermute(value, axis, [(i, i ^ distance) for i in range(count)])


def halved(kept, sent, axis):
    count = lax.axis_size(axis)
    distance = 1
    while True:
        came = swapped(sent, axis, distance)
        distance *= 2
        if distance == count:
            return kept, came
        rows, lanes = kept.shape
        if rows // 2 % 16:
            total = kept + came.astype(jnp.float32)
            kept, sent = total[: rows // 2], total[rows // 2 :].astype(jnp.bfloat16)
            continue
        outs = (
            jax.ShapeDtypeStruct((rows // 2, lanes), jnp.float32),
            jax.ShapeDtypeStruct((rows // 2, lanes), jnp.bfloat16),
        )
        kept, sent = call(halve_kernel, outs, flops=rows * lanes, bytes_accessed=9 * rows * lanes)(
            in_specs=[VMEM] * 2, out_specs=[VMEM] * 2
        )(kept, came)


def on_device(inputs, out_grad, pre_act, weight):
    _, height, width, chans = inputs.shape
    taps, filt, _ = weight.shape
    cells = height * width
    blocks, groups = lax.axis_size("space"), lax.axis_size("filt")
    place = jnp.stack([lax.axis_index("space"), lax.axis_index("filt")]).astype(jnp.int32)

    own = (out_grad.astype(jnp.float32) * silu_grad(pre_act.astype(jnp.float32))).astype(jnp.bfloat16)[0]
    near = swapped(own, "space", 1)
    far_pairs = [(i, i + 1) for i in range(1, blocks - 1, 2)]
    far = lax.ppermute(own, "space", far_pairs + [(target, source) for source, target in far_pairs])

    flat = inputs.reshape(cells, chans)
    wide = len(PAIRED) * filt
    flops = 2 * cells * taps * filt * chans
    paired, single, kept, sent = call(
        functools.partial(windows_kernel, width, blocks),
        (
            jax.ShapeDtypeStruct((cells + 2 * width, wide), jnp.bfloat16),
            jax.ShapeDtypeStruct((cells, 3 * filt), jnp.bfloat16),
            jax.ShapeDtypeStruct((chans // 2, taps * filt), jnp.float32),
            jax.ShapeDtypeStruct((chans // 2, taps * filt), jnp.bfloat16),
        ),
        (
            pltpu.VMEM((cells + 16, 2 * filt), jnp.float32),
            pltpu.VMEM((cells + 2 * width, 2 * filt), jnp.float32),
            pltpu.VMEM((chans, cells), jnp.bfloat16),
        ),
        flops=flops,
        bytes_accessed=4 * MIB,
    )(in_specs=[SMEM] + [VMEM] * 4, out_specs=[VMEM] * 4)(place, own, near, far, flat)

    kept_in, sent_in = call(
        functools.partial(spread_kernel, width, groups),
        (
            jax.ShapeDtypeStruct((cells // 2, chans), jnp.float32),
            jax.ShapeDtypeStruct((cells // 2, chans), jnp.bfloat16),
        ),
        (
            pltpu.VMEM((3, wide, chans), jnp.bfloat16),
            pltpu.VMEM((3 * filt, chans), jnp.bfloat16),
        ),
        flops=flops,
        bytes_accessed=4 * MIB,
    )(in_specs=[SMEM] + [VMEM] * 3, out_specs=[VMEM] * 2)(place, paired, single, weight)

    kept, came = halved(kept, sent, "space")
    kept_in, came_in = halved(kept_in, sent_in, "filt")
    grad_scale = float(cells * blocks) ** (-0.5)
    grad_weight = call(
        functools.partial(last_weight_kernel, grad_scale, filt),
        jax.ShapeDtypeStruct((chans // blocks, taps, filt), jnp.float32),
    )(in_specs=[VMEM] * 2, out_specs=VMEM)(kept, came)
    grad_input = call(
        last_input_kernel, jax.ShapeDtypeStruct((cells // groups, chans), jnp.bfloat16)
    )(in_specs=[VMEM] * 2, out_specs=VMEM)(kept_in, came_in)
    return grad_input.reshape(1, height // groups, width, chans), grad_weight


def solution(mesh):
    placed = (
        P("space", None, None, None),
        P("space", "filt", None),
        P("space", "filt", None),
        P(None, "filt", None),
    )
    return jax.shard_map(
        on_device,
        mesh=mesh,
        in_specs=placed,
        out_specs=(P("space", "filt", None, None), P("space", None, "filt")),
        check_vma=False,
    )
```

time: 193 us -> 42.3 us (0.22)
  local copies, waits for them, and re-layouts: 70.6 us -> 2.07 us
  blocking collectives: 26.1 us -> 0 us
  matrix products: 25.9 us -> 0 us
  waiting for transfers between devices: 39.4 us -> 16.4 us
  between operations: 14.4 us -> 0.7 us
  Pallas kernels: 0 us -> 5.22 us
  starting transfers between devices: 12.1 us -> 16.6 us
  other arithmetic: 3.34 us -> 1.16 us
    reduce_scatter x1 -> x0, waiting for transfers between devices: 39.4 us -> none  [on_device(): lax.psum_scatter(all_terms, 'space', scatter_dimension=0, tiled=True)]
    another operation x25 -> x0, local copies, waits for them, and re-layouts: 27.4 us -> none  [the longest x24 21.9 us: on_device(): slices.append(jnp.moveaxis(window, 1, 0).reshape(filt_local, cell_count))]
    unnamed x57 -> x5, local copies, waits for them, and re-layouts: 28.9 us -> 2.07 us
    psum x1 -> x0, blocking collectives: 26.1 us -> none  [on_device(): whole_sum = lax.psum(partial_grid, 'filt')]
    dot_general x28 -> x0, matrix products: 25.9 us -> none  [the longest x27 22.7 us: on_device(): lax.dot_general(shifted, grad_flat, (((0,), (1,)), ((), ())), preferred_e...]
    ppermute x4 -> x7, waiting for transfers between devices: 0.01 us -> 16.4 us  [the longest x6 16.4 us: swapped(): return lax.ppermute(value, axis, [(i, i ^ distance) for i in range(count)])]
    slice x4 -> x0, local copies, waits for them, and re-layouts: 6.8 us -> none  [the longest x2 3.85 us: on_device(): padded[2 - offset_d:2 - offset_d + slab_depth, :, 2 - offset_h:2 - offset...]
    dot_general x1 -> x0, local copies, waits for them, and re-layouts: 5.8 us -> none  [on_device(): lax.dot_general(stacked, flat_kernel, (((0,), (0,)), ((), ())), preferred...]
  transfers between devices with their start and end apart: 5 -> 7, of which waited for: 1 -> 4; matrix products, arithmetic and copies ran while one was open for 33% -> 0% of each run, Pallas kernels for 0% -> 6%
where the time goes in v1:
time: 42.3 us; the launch traced here: 42.1 us
  starting transfers between devices  16.6 us (39%)
  waiting for transfers between devices  16.4 us (39%)
  Pallas kernels  5.22 us (12%)
  local copies, waits for them, and re-layouts  2.07 us (5%)
  other arithmetic  1.16 us (3%)
  between operations  0.7 us (2%)
    ppermute x6, waiting for transfers between devices, swapped(): return lax.ppermute(value, axis, [(i, i ^ distance) for i in range(count)])  16.4 us
    ppermute x6, starting transfers between devices, swapped(): return lax.ppermute(value, axis, [(i, i ^ distance) for i in range(count)])  15.9 us
    pallas_call x1, Pallas kernels, on_device(): call(functools.partial(windows_kernel, width, blocks), (jax.ShapeDtypeStr...  2.21 us
    unnamed x5, local copies, waits for them, and re-layouts  2.07 us
    pallas_call x1, Pallas kernels, on_device(): call(functools.partial(spread_kernel, width, groups), (jax.ShapeDtypeStru...  1.64 us
    squeeze x1, other arithmetic, on_device(): (out_grad.astype(jnp.float32) * silu_grad(pre_act.astype(jnp.float32))).a...  1.08 us
  transfers between devices with their start and end apart: 7, of which 4 were waited for; matrix products, arithmetic and copies ran while one was open for 0% of the time, Pallas kernels for 6%

profile of v1, /device:TPU:0, one launch (start us, length us, event | category | flops | bytes accessed | tf_op | source)
XLA Modules:
  0.0 42.1 jit_solution(14934525132680450627)
XLA Ops:
  0.6 1.1 %fusion.7.own = bf16[64,1024]{1,0:T(8,128)(2,1)S(1)} fusion(bf16[1,64,1024]{2,1,0:T(8,128)(2,1)} %param.6, bf16[1,64,1024]{2,1,0:T(8,128)(2,1)} %param.5), kind=kLoop, calls=%fused_computation.9 | loop fusion | flops 720896 | bytes 393216 | tf_op jit(solution)/shard_map/squeeze | solution.py:180
  1.7 3.0 %collective-permute-start = (bf16[64,1024]{1,0:T(8,128)(2,1)S(1)}, bf16[64,1024]{1,0:T(8,128)(2,1)S(1)}, u32[]{:S(2)}, u32[]{:S(2)}) collective-permute-start(bf16[64,1024]{1,0:T(8,128)(2,1)S(1)} %fusion.7.own), channel_id=1, source_target_pairs={{0,4},{4,0},{8,12},{12,8},{16,20},{20,16},{24,28},{28,24},{1,5},{5... | collective-permute-start | bytes 393224 | tf_op jit(solution)/shard_map/ppermute | solution.py:148
  4.7 0.7 %collective-permute-start.1 = (bf16[64,1024]{1,0:T(8,128)(2,1)S(1)}, bf16[64,1024]{1,0:T(8,128)(2,1)S(1)}, u32[]{:S(2)}, u32[]{:S(2)}) collective-permute-start(bf16[64,1024]{1,0:T(8,128)(2,1)S(1)} %fusion.7.own), channel_id=1, source_target_pairs={{4,8},{12,16},{20,24},{8,4},{16,12},{24,20},{5,9},{13,17},{21,25},... | collective-permute-start | bytes 393224 | tf_op jit(solution)/shard_map/ppermute | solution.py:183
  5.4 0.1 pad_add_fusion.place
  5.5 2.8 %collective-permute-done.near = bf16[64,1024]{1,0:T(8,128)(2,1)S(1)} collective-permute-done((bf16[64,1024]{1,0:T(8,128)(2,1)S(1)}, bf16[64,1024]{1,0:T(8,128)(2,1)S(1)}, u32[]{:S(2)}, u32[]{:S(2)}) %collective-permute-start) | collective-permute-done | bytes 131104 | tf_op jit(solution)/shard_map/ppermute | solution.py:148
  8.2 0.0 collective-permute-done.1.far
  8.2 0.0 copy-start.1
  8.2 1.0 %copy-done.1 = bf16[1,32,32,256]{3,2,1,0:T(8,128)(2,1)S(1)} copy-done((bf16[1,32,32,256]{3,2,1,0:T(8,128)(2,1)S(1)}, bf16[1,32,32,256]{3,2,1,0:T(8,128)(2,1)}, u32[]{:S(2)}) %copy-start.1) | copy-done | bytes 524312
  9.3 0.0 copy-start
  9.3 2.2 %shard_map.59 = (bf16[1088,512]{1,0:T(8,128)(2,1)S(1)}, bf16[1024,192]{1,0:T(8,128)(2,1)S(1)}, f32[128,1728]{1,0:T(8,128)S(1)}, bf16[128,1728]{1,0:T(8,128)(2,1)S(1)}) custom-call(s32[2]{0:T(128)S(1)} %pad_add_fusion.place, bf16[64,1024]{1,0:T(8,128)(2,1)S(1)} %fusion.7.own, bf16[64,1024]{1,0:T(8,128)(2,1)S(1)} %collective-permute-done.near, ...), custom_call_target="tpu_custom_call" | custom-call | flops 905969664 | bytes 4194304 | tf_op jit(solution)/shard_map/pallas_call | solution.py:188
  11.5 4.7 %collective-permute-start.4 = (bf16[128,1728]{1,0:T(8,128)(2,1)S(1)}, bf16[128,1728]{1,0:T(8,128)(2,1)S(1)}, u32[]{:S(2)}, u32[]{:S(2)}) collective-permute-start(bf16[128,1728]{1,0:T(8,128)(2,1)S(1)} %get-tuple-element.21), channel_id=1, source_target_pairs={{0,4},{4,0},{8,12},{12,8},{16,20},{20,16},{24,28},{28,24},{1,5},{5... | collective-permute-start | bytes 1327112 | tf_op jit(solution)/shard_map/ppermute | solution.py:148
  16.2 0.0 copy-done
  16.2 1.6 %shard_map.60 = (f32[512,256]{1,0:T(8,128)S(1)}, bf16[512,256]{1,0:T(8,128)(2,1)S(1)}) custom-call(s32[2]{0:T(128)S(1)} %pad_add_fusion.place, bf16[1088,512]{1,0:T(8,128)(2,1)S(1)} %get-tuple-element.14.paired, bf16[1024,192]{1,0:T(8,128)(2,1)S(1)} %get-tuple-element.15.single, bf16[27,64,256]{2,1,0:T(8,128)(2,1)S(1)} %copy-done), custom_call_target="tpu_custom_call" | custom-call | flops 905969664 | bytes 4194304 | tf_op jit(solution)/shard_map/pallas_call | solution.py:205
  17.8 0.1 collective-permute-start.2
  17.9 7.9 %collective-permute-done.4.came = bf16[128,1728]{1,0:T(8,128)(2,1)S(1)} collective-permute-done((bf16[128,1728]{1,0:T(8,128)(2,1)S(1)}, bf16[128,1728]{1,0:T(8,128)(2,1)S(1)}, u32[]{:S(2)}, u32[]{:S(2)}) %collective-permute-start.4) | collective-permute-done | bytes 442400 | tf_op jit(solution)/shard_map/ppermute | solution.py:148
  25.8 0.1 shard_map.63
  25.9 2.4 %collective-permute-start.5 = (bf16[64,1728]{1,0:T(8,128)(2,1)S(1)}, bf16[64,1728]{1,0:T(8,128)(2,1)S(1)}, u32[]{:S(2)}, u32[]{:S(2)}) collective-permute-start(bf16[64,1728]{1,0:T(8,128)(2,1)S(1)} %get-tuple-element.23), channel_id=1, source_target_pairs={{0,8},{4,12},{8,0},{12,4},{16,24},{20,28},{24,16},{28,20},{1,9},{5... | collective-permute-start | bytes 663560 | tf_op jit(solution)/shard_map/ppermute | solution.py:148
  28.3 0.0 collective-permute-done.2.came
  28.4 1.6 %collective-permute-start.3 = (bf16[256,256]{1,0:T(8,128)(2,1)S(1)}, bf16[256,256]{1,0:T(8,128)(2,1)S(1)}, u32[]{:S(2)}, u32[]{:S(2)}) collective-permute-start(bf16[256,256]{1,0:T(8,128)(2,1)S(1)} %get-tuple-element.19), channel_id=1, source_target_pairs={{0,2},{1,3},{2,0},{3,1},{4,6},{5,7},{6,4},{7,5},{8,10},{9,11},{10,... | collective-permute-start | bytes 393224 | tf_op jit(solution)/shard_map/ppermute | solution.py:148
  30.0 2.4 %collective-permute-done.5.came = bf16[64,1728]{1,0:T(8,128)(2,1)S(1)} collective-permute-done((bf16[64,1728]{1,0:T(8,128)(2,1)S(1)}, bf16[64,1728]{1,0:T(8,128)(2,1)S(1)}, u32[]{:S(2)}, u32[]{:S(2)}) %collective-permute-start.5) | collective-permute-done | bytes 221216 | tf_op jit(solution)/shard_map/ppermute | solution.py:148
  32.4 4.1 %collective-permute-start.6 = (bf16[32,1728]{1,0:T(8,128)(2,1)S(1)}, bf16[32,1728]{1,0:T(8,128)(2,1)S(1)}, u32[]{:S(2)}, u32[]{:S(2)}) collective-permute-start(bf16[32,1728]{1,0:T(8,128)(2,1)S(1)} %get-tuple-element.25), channel_id=1, source_target_pairs={{0,16},{4,20},{8,24},{12,28},{16,0},{20,4},{24,8},{28,12},{1,17},{... | collective-permute-start | bytes 331784 | tf_op jit(solution)/shard_map/ppermute | solution.py:148
  36.5 0.0 collective-permute-done.3.came
  36.5 0.7 %shard_map.62 = bf16[256,256]{1,0:T(8,128)(2,1)} custom-call(f32[256,256]{1,0:T(8,128)S(1)} %get-tuple-element.18.kept, bf16[256,256]{1,0:T(8,128)(2,1)S(1)} %collective-permute-done.3.came), custom_call_target="tpu_custom_call" | custom-call | tf_op jit(solution)/shard_map/pallas_call | solution.py:226
  37.2 3.3 %collective-permute-done.6.came = bf16[32,1728]{1,0:T(8,128)(2,1)S(1)} collective-permute-done((bf16[32,1728]{1,0:T(8,128)(2,1)S(1)}, bf16[32,1728]{1,0:T(8,128)(2,1)S(1)}, u32[]{:S(2)}, u32[]{:S(2)}) %collective-permute-start.6) | collective-permute-done | bytes 110624 | tf_op jit(solution)/shard_map/ppermute | solution.py:148
  40.5 0.5 %shard_map.65 = f32[32,27,64]{2,1,0:T(8,128)S(1)} custom-call(f32[32,1728]{1,0:T(8,128)S(1)} %get-tuple-element.24.kept, bf16[32,1728]{1,0:T(8,128)(2,1)S(1)} %collective-permute-done.6.came), custom_call_target="tpu_custom_call" | custom-call | tf_op jit(solution)/shard_map/pallas_call | solution.py:222
  41.0 1.0 %copy.6 = f32[32,27,64]{2,0,1:T(8,128)} copy(f32[32,27,64]{2,1,0:T(8,128)S(1)} %shard_map.65) | data formatting | bytes 442368
  (2 shorter events, 0.1 us)
Async XLA Ops:
  1.7 6.5 %collective-permute-start = (bf16[64,1024]{1,0:T(8,128)(2,1)S(1)}, bf16[64,1024]{1,0:T(8,128)(2,1)S(1)}, u32[]{:S(2)}, u32[]{:S(2)}) collective-permute-start(bf16[64,1024]{1,0:T(8,128)(2,1)S(1)} %fusion.7.own), channel_id=1, source_target_pairs={{0,4},{4,0},{8,12},{12,8},{16,20},{20,16},{24,28},{28,24},{1,5},{5... | collective-permute-start | bytes 393224 | tf_op jit(solution)/shard_map/ppermute | solution.py:148
  4.7 3.5 %collective-permute-start.1 = (bf16[64,1024]{1,0:T(8,128)(2,1)S(1)}, bf16[64,1024]{1,0:T(8,128)(2,1)S(1)}, u32[]{:S(2)}, u32[]{:S(2)}) collective-permute-start(bf16[64,1024]{1,0:T(8,128)(2,1)S(1)} %fusion.7.own), channel_id=1, source_target_pairs={{4,8},{12,16},{20,24},{8,4},{16,12},{24,20},{5,9},{13,17},{21,25},... | collective-permute-start | bytes 393224 | tf_op jit(solution)/shard_map/ppermute | solution.py:183
  8.2 1.0 %copy-start.1 = (bf16[1,32,32,256]{3,2,1,0:T(8,128)(2,1)S(1)}, bf16[1,32,32,256]{3,2,1,0:T(8,128)(2,1)}, u32[]{:S(2)}) copy-start(bf16[1,32,32,256]{3,2,1,0:T(8,128)(2,1)} %param.4) | copy-start | bytes 1572868
  9.3 6.9 %copy-start = (bf16[27,64,256]{2,1,0:T(8,128)(2,1)S(1)}, bf16[27,64,256]{2,1,0:T(8,128)(2,1)}, u32[]{:S(2)}) copy-start(bf16[27,64,256]{2,1,0:T(8,128)(2,1)} %weight.1) | copy-start | bytes 2654212
  11.5 14.4 %collective-permute-start.4 = (bf16[128,1728]{1,0:T(8,128)(2,1)S(1)}, bf16[128,1728]{1,0:T(8,128)(2,1)S(1)}, u32[]{:S(2)}, u32[]{:S(2)}) collective-permute-start(bf16[128,1728]{1,0:T(8,128)(2,1)S(1)} %get-tuple-element.21), channel_id=1, source_target_pairs={{0,4},{4,0},{8,12},{12,8},{16,20},{20,16},{24,28},{28,24},{1,5},{5... | collective-permute-start | bytes 1327112 | tf_op jit(solution)/shard_map/ppermute | solution.py:148
  17.8 10.5 %collective-permute-start.2 = (bf16[512,256]{1,0:T(8,128)(2,1)S(1)}, bf16[512,256]{1,0:T(8,128)(2,1)S(1)}, u32[]{:S(2)}, u32[]{:S(2)}) collective-permute-start(bf16[512,256]{1,0:T(8,128)(2,1)S(1)} %get-tuple-element.17), channel_id=1, source_target_pairs={{0,1},{1,0},{2,3},{3,2},{4,5},{5,4},{6,7},{7,6},{8,9},{9,8},{10,11... | collective-permute-start | bytes 786440 | tf_op jit(solution)/shard_map/ppermute | solution.py:148
  25.9 6.4 %collective-permute-start.5 = (bf16[64,1728]{1,0:T(8,128)(2,1)S(1)}, bf16[64,1728]{1,0:T(8,128)(2,1)S(1)}, u32[]{:S(2)}, u32[]{:S(2)}) collective-permute-start(bf16[64,1728]{1,0:T(8,128)(2,1)S(1)} %get-tuple-element.23), channel_id=1, source_target_pairs={{0,8},{4,12},{8,0},{12,4},{16,24},{20,28},{24,16},{28,20},{1,9},{5... | collective-permute-start | bytes 663560 | tf_op jit(solution)/shard_map/ppermute | solution.py:148
  28.4 8.1 %collective-permute-start.3 = (bf16[256,256]{1,0:T(8,128)(2,1)S(1)}, bf16[256,256]{1,0:T(8,128)(2,1)S(1)}, u32[]{:S(2)}, u32[]{:S(2)}) collective-permute-start(bf16[256,256]{1,0:T(8,128)(2,1)S(1)} %get-tuple-element.19), channel_id=1, source_target_pairs={{0,2},{1,3},{2,0},{3,1},{4,6},{5,7},{6,4},{7,5},{8,10},{9,11},{10,... | collective-permute-start | bytes 393224 | tf_op jit(solution)/shard_map/ppermute | solution.py:148
  32.4 8.1 %collective-permute-start.6 = (bf16[32,1728]{1,0:T(8,128)(2,1)S(1)}, bf16[32,1728]{1,0:T(8,128)(2,1)S(1)}, u32[]{:S(2)}, u32[]{:S(2)}) collective-permute-start(bf16[32,1728]{1,0:T(8,128)(2,1)S(1)} %get-tuple-element.25), channel_id=1, source_target_pairs={{0,16},{4,20},{8,24},{12,28},{16,0},{20,4},{24,8},{28,12},{1,17},{... | collective-permute-start | bytes 331784 | tf_op jit(solution)/shard_map/ppermute | solution.py:148

commit v2 on v1

v2 whole, which is shorter than its diff:
```python
import functools

import jax
import jax.numpy as jnp
from jax import lax
from jax.experimental import pallas as pl
from jax.experimental.pallas import tpu as pltpu
from jax.sharding import PartitionSpec as P

MIB = 1 << 20
VMEM = pl.BlockSpec(memory_space=pltpu.VMEM)
SMEM = pl.BlockSpec(memory_space=pltpu.SMEM)


def silu_grad(values):
    sig = jax.nn.sigmoid(values)
    return sig * (1.0 + values * (1.0 - sig))


def bits_of(count):
    return count.bit_length() - 1


def reversed_bits(value, width):
    return sum(((value >> bit) & 1) << (width - 1 - bit) for bit in range(width))


def call(kernel, outs, scratch=(), flops=0, bytes_accessed=0, limit=24):
    return functools.partial(
        pl.pallas_call,
        kernel,
        out_shape=outs,
        scratch_shapes=scratch,
        compiler_params=pltpu.CompilerParams(vmem_limit_bytes=limit * MIB),
        cost_estimate=pl.CostEstimate(flops=flops, bytes_accessed=bytes_accessed, transcendentals=0),
    )


def lay_windows(width, first, second, windows, tall):
    filt, cells = first.shape
    lanes = 2 * filt
    tall[pl.ds(8, cells), :] = jnp.concatenate([first, second], axis=0).astype(jnp.float32).T
    row = lax.broadcasted_iota(jnp.int32, (cells, lanes), 0)
    column = row & (width - 1) if width & (width - 1) == 0 else lax.rem(row, width)
    zero_rows = jnp.zeros((width, windows.shape[1]), jnp.bfloat16)
    windows[pl.ds(0, width), :] = zero_rows
    windows[pl.ds(width + cells, width), :] = zero_rows
    body = pl.ds(width, cells)
    windows[body, 0:lanes] = jnp.where(column != width - 1, tall[pl.ds(9, cells), :], 0.0).astype(jnp.bfloat16)
    windows[body, lanes : 2 * lanes] = tall[pl.ds(8, cells), :].astype(jnp.bfloat16)
    windows[body, 2 * lanes : 3 * lanes] = jnp.where(column != 0, tall[pl.ds(7, cells), :], 0.0).astype(jnp.bfloat16)


def turn_kernel(blocks, place, inputs, mine, sent):
    chans = inputs.shape[1]
    rows = chans // blocks
    half, part = mine.shape[0], sent.shape[0]
    count = bits_of(blocks)
    order = lax.broadcasted_iota(jnp.int32, (half + part, chans), 0)
    order = order + jnp.where(order >= half, (place[1] & 1) * part, 0)
    block = place[0] ^ reversed_bits(order >> bits_of(rows), count)
    source = (block << bits_of(rows)) | (order & (rows - 1))
    picked = (lax.broadcasted_iota(jnp.int32, (half + part, chans), 1) == source).astype(jnp.bfloat16)
    turned = lax.dot_general(picked, inputs[...], (((1,), (1,)), ((), ())), preferred_element_type=jnp.float32)
    turned = turned.astype(jnp.bfloat16)
    mine[...] = turned[0:half, :]
    sent[...] = turned[half:, :]


def near_kernel(width, place, own, near, mine, came, other, windows, turned, outer, middle, tall):
    filt, cells = own.shape
    half = mine.shape[0]
    lanes = 2 * filt
    even = place[0] & 1 == 0
    first_core = place[1] & 1 == 0
    lay_windows(
        width, jnp.where(even, own[...], near[...]), jnp.where(even, near[...], own[...]), windows, tall
    )
    theirs = jnp.concatenate(
        [jnp.where(first_core, came[...], other[...]), jnp.where(first_core, other[...], came[...])], axis=0
    )
    turned[0:half, :] = jnp.where(even, mine[...], theirs)
    turned[half:, :] = jnp.where(even, theirs, mine[...])
    left = lax.broadcasted_iota(jnp.int32, (half, lanes), 1) < filt
    for b in range(3):
        terms = jnp.dot(turned[...], windows[pl.ds((2 - b) * width, cells), :], preferred_element_type=jnp.float32)
        for c in range(3):
            tap = 3 * b + c
            lower = terms[0:half, c * lanes : (c + 1) * lanes]
            upper = terms[half:, c * lanes : (c + 1) * lanes]
            outer[:, tap * lanes : (tap + 1) * lanes] = jnp.where(left, upper, lower)
            lo = tap // 2 * lanes
            if tap % 2 == 0:
                before = lower + pltpu.roll(upper, filt, 1)
                if tap == 8:
                    middle[:, lo : lo + filt] = before[:, 0:filt]
            else:
                middle[:, lo : lo + lanes] = jnp.where(left, before, pltpu.roll(lower, filt, 1) + upper)


def far_kernel(width, place, two_off, one_off, turned, outer, middle, windows, keep, send, tall):
    filt, cells = two_off.shape
    half = turned.shape[0] // 2
    lanes = 2 * filt
    even = place[0] & 1 == 0
    lay_windows(
        width,
        jnp.where(even, one_off[...], two_off[...]),
        jnp.where(even, two_off[...], one_off[...]),
        windows,
        tall,
    )
    left = lax.broadcasted_iota(jnp.int32, (half, lanes), 1) < filt
    kept = half // 2
    for b in range(3):
        terms = jnp.dot(turned[...], windows[pl.ds((2 - b) * width, cells), :], preferred_element_type=jnp.float32)
        for c in range(3):
            lo = (3 * b + c) * lanes
            lower = terms[0:half, c * lanes : (c + 1) * lanes]
            upper = terms[half:, c * lanes : (c + 1) * lanes]
            total = outer[:, lo : lo + lanes] + jnp.where(left, lower, upper)
            keep[:, lo : lo + lanes] = total[0:kept, :]
            send[:, lo : lo + lanes] = total[kept:, :].astype(jnp.bfloat16)
    keep[:, 9 * lanes :] = middle[0:kept, :]
    send[:, 9 * lanes :] = middle[kept:, :].astype(jnp.bfloat16)


def spread_kernel(width, groups, place, pair, ends, weight, keep, send, ordered):
    cells = pair.shape[0] - 2 * width
    filt = weight.shape[1]
    part = cells // groups
    index = place[1]
    odd = place[0] & 1
    even = odd == 0
    for b in range(3):
        for c in range(3):
            tap = 3 * b + c
            zero = jnp.zeros_like(weight[0])
            rows = (
                weight[9 * (1 + odd) + tap],
                weight[9 * odd + tap],
                jnp.where(even, weight[18 + tap], zero),
                jnp.where(even, zero, weight[tap]),
            )
            for slot, value in zip((2 * c, 2 * c + 1, 2 * c + 6, 2 * c + 7), rows):
                ordered[b, pl.ds(slot * filt, filt), :] = value
    count = bits_of(groups)
    for target in reversed(range(groups)):
        block = 0
        for bit in range(count):
            differs = (target >> (count - 1 - bit)) & 1
            block = block + (((index >> bit) & 1) ^ differs) * (1 << bit)
        total = 0.0
        for b in range(3):
            rows = pl.ds(pl.multiple_of(block * part + (2 - b) * width, width), part)
            window = jnp.concatenate([pair[rows, :], ends[rows, :]], axis=1)
            total = total + jnp.dot(window, ordered[b], preferred_element_type=jnp.float32)
        if target < groups // 2:
            keep[pl.ds(target * part, part), :] = total
        else:
            send[pl.ds((target - groups // 2) * part, part), :] = total.astype(jnp.bfloat16)


def halve_kernel(kept, came, keep, send):
    half = keep.shape[0]
    keep[...] = kept[0:half, :] + came[0:half, :].astype(jnp.float32)
    send[...] = (kept[half:, :] + came[half:, :].astype(jnp.float32)).astype(jnp.bfloat16)


def last_input_kernel(kept, came, out):
    out[...] = (kept[...] + came[...].astype(jnp.float32)).astype(out.dtype)


def last_weight_kernel(scale, filt, kept, came, out):
    total = (kept[...] + came[...].astype(jnp.float32)) * scale
    for tap in range(9):
        for slot, place in ((2 * tap, 18 + tap), (2 * tap + 1, tap), (18 + tap, 9 + tap)):
            out[place] = total[:, slot * filt : (slot + 1) * filt]


def swapped(value, axis, distance):
    count = lax.axis_size(axis)
    return lax.ppermute(value, axis, [(i, i ^ distance) for i in range(count)])


def halved(kept, came):
    rows, lanes = kept.shape
    if rows // 2 % 16:
        total = kept + came.astype(jnp.float32)
        return total[: rows // 2], total[rows // 2 :].astype(jnp.bfloat16)
    outs = (
        jax.ShapeDtypeStruct((rows // 2, lanes), jnp.float32),
        jax.ShapeDtypeStruct((rows // 2, lanes), jnp.bfloat16),
    )
    return call(halve_kernel, outs, flops=rows * lanes, bytes_accessed=9 * rows * lanes)(
        in_specs=[VMEM] * 2, out_specs=[VMEM] * 2
    )(kept, came)


def after(value, other):
    return lax.optimization_barrier((value, other))[0]


def on_device(inputs, out_grad, pre_act, weight):
    _, height, width, chans = inputs.shape
    taps, filt, _ = weight.shape
    cells = height * width
    blocks, groups = lax.axis_size("space"), lax.axis_size("filt")
    half, quarter = chans // 2, chans // 4
    place = jnp.stack([lax.axis_index("space"), lax.axis_index("filt")]).astype(jnp.int32)
    bf16, f32 = jnp.bfloat16, jnp.float32
    shape = jax.ShapeDtypeStruct
    flops = 2 * cells * taps * filt * chans
    lanes = 6 * filt
    windows_shape = shape((cells + 2 * width, lanes), bf16)
    tall = pltpu.VMEM((cells + 16, 2 * filt), f32)

    own = (out_grad.astype(f32) * silu_grad(pre_act.astype(f32))).astype(bf16)[0]
    near = swapped(own, "space", 1)
    two_pairs = [(i, i - 2) for i in range(2, blocks, 2)] + [(i, i + 2) for i in range(1, blocks - 2, 2)]
    two_off = lax.ppermute(own, "space", two_pairs)
    mine, sent = call(
        functools.partial(turn_kernel, blocks),
        (shape((half, cells), bf16), shape((quarter, cells), bf16)),
        bytes_accessed=MIB,
    )(in_specs=[SMEM, VMEM], out_specs=[VMEM] * 2)(place, after(inputs.reshape(cells, chans), own))
    came = swapped(sent, "space", 1)
    one_off = swapped(two_off, "space", 1)
    other = swapped(came, "filt", 1)

    pair, turned, outer, middle = call(
        functools.partial(near_kernel, width),
        (
            windows_shape,
            shape((chans, cells), bf16),
            shape((half, 18 * filt), f32),
            shape((half, 9 * filt), f32),
        ),
        (tall,),
        flops=flops,
        bytes_accessed=4 * MIB,
    )(in_specs=[SMEM] + [VMEM] * 5, out_specs=[VMEM] * 4)(place, own, near, mine, came, other)

    ends, kept, sent = call(
        functools.partial(far_kernel, width),
        (windows_shape, shape((quarter, taps * filt), f32), shape((quarter, taps * filt), bf16)),
        (tall,),
        flops=flops,
        bytes_accessed=4 * MIB,
    )(in_specs=[SMEM] + [VMEM] * 5, out_specs=[VMEM] * 3)(place, two_off, one_off, turned, outer, middle)
    came = swapped(sent, "space", 2)

    kept_in, sent_in = call(
        functools.partial(spread_kernel, width, groups),
        (shape((cells // 2, chans), f32), shape((cells // 2, chans), bf16)),
        (pltpu.VMEM((3, 2 * lanes, chans), bf16),),
        flops=flops,
        bytes_accessed=4 * MIB,
    )(in_specs=[SMEM] + [VMEM] * 3, out_specs=[VMEM] * 2)(place, pair, ends, weight)
    came_in = swapped(sent_in, "filt", 1)

    distance, distance_in = 4, 2
    while distance < blocks or distance_in < groups:
        if distance < blocks:
            kept, sent = halved(kept, came)
            came = swapped(sent, "space", distance)
            distance *= 2
        if distance_in < groups:
            kept_in, sent_in = halved(kept_in, after(came_in, sent))
            came_in = swapped(sent_in, "filt", distance_in)
            distance_in *= 2

    grad_scale = float(cells * blocks) ** (-0.5)
    grad_weight = call(
        functools.partial(last_weight_kernel, grad_scale, filt), shape((taps, chans // blocks, filt), f32)
    )(in_specs=[VMEM] * 2, out_specs=VMEM)(kept, came)
    grad_input = call(last_input_kernel, shape((cells // groups, chans), bf16))(
        in_specs=[VMEM] * 2, out_specs=VMEM
    )(kept_in, came_in)
    return grad_input.reshape(1, height // groups, width, chans), jnp.transpose(grad_weight, (1, 0, 2))


def solution(mesh):
    placed = (
        P("space", None, None, None),
        P("space", "filt", None),
        P("space", "filt", None),
        P(None, "filt", None),
    )
    return jax.shard_map(
        on_device,
        mesh=mesh,
        in_specs=placed,
        out_specs=(P("space", "filt", None, None), P("space", None, "filt")),
        check_vma=False,
    )
```

time: 42.3 us -> 41.6 us (0.983)
  starting transfers between devices: 16.6 us -> 13 us
  Pallas kernels: 5.22 us -> 7.99 us
  waiting for transfers between devices: 16.4 us -> 17.5 us
  local copies, waits for them, and re-layouts: 2.07 us -> 1.05 us
    ppermute x6 -> x8, starting transfers between devices: 15.9 us -> 11.7 us  [swapped(): return lax.ppermute(value, axis, [(i, i ^ distance) for i in range(count)])]
    pallas_call x4 -> x6, Pallas kernels: 5.05 us -> 7.89 us  [the longest x1 1.93 us: on_device(): call(functools.partial(spread_kernel, width, groups), (shape((cells // 2,...]
    ppermute x1, waiting for transfers between devices: 0.01 us -> 2.76 us  [on_device(): two_off = lax.ppermute(own, 'space', two_pairs)]
    ppermute x6 -> x8, waiting for transfers between devices: 16.4 us -> 14.7 us  [swapped(): return lax.ppermute(value, axis, [(i, i ^ distance) for i in range(count)])]
    unnamed x5 -> x4, local copies, waits for them, and re-layouts: 2.07 us -> 1.05 us
    ppermute x1, starting transfers between devices: 0.66 us -> 1.28 us  [on_device(): two_off = lax.ppermute(own, 'space', two_pairs)]
  transfers between devices with their start and end apart: 7 -> 9, of which waited for: 4 -> 5; matrix products, arithmetic and copies ran while one was open for 0% -> 0% of each run, Pallas kernels for 6% -> 7%
where the time goes in v2:
time: 41.6 us; the launch traced here: 41.4 us
  waiting for transfers between devices  17.5 us (42%)
  starting transfers between devices  13 us (31%)
  Pallas kernels  7.99 us (19%)
  other arithmetic  1.16 us (3%)
  local copies, waits for them, and re-layouts  1.05 us (3%)
  between operations  0.71 us (2%)
    ppermute x8, waiting for transfers between devices, swapped(): return lax.ppermute(value, axis, [(i, i ^ distance) for i in range(count)])  14.7 us
    ppermute x8, starting transfers between devices, swapped(): return lax.ppermute(value, axis, [(i, i ^ distance) for i in range(count)])  11.7 us
    ppermute x1, waiting for transfers between devices, on_device(): two_off = lax.ppermute(own, 'space', two_pairs)  2.76 us
    pallas_call x1, Pallas kernels, on_device(): call(functools.partial(spread_kernel, width, groups), (shape((cells // 2,...  1.93 us
    pallas_call x1, Pallas kernels, on_device(): call(functools.partial(near_kernel, width), (windows_shape, shape((chans,...  1.81 us
    pallas_call x1, Pallas kernels, on_device(): call(functools.partial(far_kernel, width), (windows_shape, shape((quarter...  1.72 us
    ppermute x1, starting transfers between devices, on_device(): two_off = lax.ppermute(own, 'space', two_pairs)  1.28 us
    squeeze x1, other arithmetic, on_device(): (out_grad.astype(f32) * silu_grad(pre_act.astype(f32))).astype(bf16)[0]  1.08 us
  transfers between devices with their start and end apart: 9, of which 5 were waited for; matrix products, arithmetic and copies ran while one was open for 0% of the time, Pallas kernels for 7%

profile of v2, /device:TPU:0, one launch (start us, length us, event | category | flops | bytes accessed | tf_op | source)
XLA Modules:
  0.0 41.4 jit_solution(14418648752858417555)
XLA Ops:
  0.6 1.1 %fusion.7.own = bf16[64,1024]{1,0:T(8,128)(2,1)S(1)} fusion(bf16[1,64,1024]{2,1,0:T(8,128)(2,1)} %param.6, bf16[1,64,1024]{2,1,0:T(8,128)(2,1)} %param.5), kind=kLoop, calls=%fused_computation.9 | loop fusion | flops 720896 | bytes 393216 | tf_op jit(solution)/shard_map/squeeze | solution.py:218
  1.7 0.1 pad_add_fusion.place
  1.8 0.0 copy-start
  1.8 1.0 %copy-done = bf16[1,32,32,256]{3,2,1,0:T(8,128)(2,1)S(1)} copy-done((bf16[1,32,32,256]{3,2,1,0:T(8,128)(2,1)S(1)}, bf16[1,32,32,256]{3,2,1,0:T(8,128)(2,1)}, u32[]{:S(2)}) %copy-start) | copy-done | bytes 524312
  2.8 0.9 %shard_map.59 = (bf16[128,1024]{1,0:T(8,128)(2,1)S(1)}, bf16[64,1024]{1,0:T(8,128)(2,1)S(1)}) custom-call(s32[2]{0:T(128)S(1)} %pad_add_fusion.place, bf16[1024,256]{1,0:T(8,128)(2,1)S(1)} %bitcast.7), custom_call_target="tpu_custom_call" | custom-call | bytes 1048576 | tf_op jit(solution)/shard_map/pallas_call | solution.py:222
  3.7 3.0 %collective-permute-start.1 = (bf16[64,1024]{1,0:T(8,128)(2,1)S(1)}, bf16[64,1024]{1,0:T(8,128)(2,1)S(1)}, u32[]{:S(2)}, u32[]{:S(2)}) collective-permute-start(bf16[64,1024]{1,0:T(8,128)(2,1)S(1)} %get-tuple-element.21), channel_id=1, source_target_pairs={{0,4},{4,0},{8,12},{12,8},{16,20},{20,16},{24,28},{28,24},{1,5},{5... | collective-permute-start | bytes 393224 | tf_op jit(solution)/shard_map/ppermute | solution.py:183
  6.7 1.3 %collective-permute-start.3 = (bf16[64,1024]{1,0:T(8,128)(2,1)S(1)}, bf16[64,1024]{1,0:T(8,128)(2,1)S(1)}, u32[]{:S(2)}, u32[]{:S(2)}) collective-permute-start(bf16[64,1024]{1,0:T(8,128)(2,1)S(1)} %fusion.7.own), channel_id=1, source_target_pairs={{8,0},{16,8},{24,16},{4,12},{12,20},{20,28},{9,1},{17,9},{25,17},{... | collective-permute-start | bytes 393224 | tf_op jit(solution)/shard_map/ppermute | solution.py:221
  8.0 2.8 %collective-permute-start = (bf16[64,1024]{1,0:T(8,128)(2,1)S(1)}, bf16[64,1024]{1,0:T(8,128)(2,1)S(1)}, u32[]{:S(2)}, u32[]{:S(2)}) collective-permute-start(bf16[64,1024]{1,0:T(8,128)(2,1)S(1)} %fusion.7.own), channel_id=1, source_target_pairs={{0,4},{4,0},{8,12},{12,8},{16,20},{20,16},{24,28},{28,24},{1,5},{5... | collective-permute-start | bytes 393224 | tf_op jit(solution)/shard_map/ppermute | solution.py:183
  10.8 0.0 collective-permute-done.1.came
  10.8 0.0 collective-permute-start.2
  10.8 2.8 %collective-permute-done.3.two_off = bf16[64,1024]{1,0:T(8,128)(2,1)S(1)} collective-permute-done((bf16[64,1024]{1,0:T(8,128)(2,1)S(1)}, bf16[64,1024]{1,0:T(8,128)(2,1)S(1)}, u32[]{:S(2)}, u32[]{:S(2)}) %collective-permute-start.3) | collective-permute-done | bytes 131104 | tf_op jit(solution)/shard_map/ppermute | solution.py:221
  13.6 0.0 collective-permute-start.4
  13.6 0.5 %collective-permute-done.near = bf16[64,1024]{1,0:T(8,128)(2,1)S(1)} collective-permute-done((bf16[64,1024]{1,0:T(8,128)(2,1)S(1)}, bf16[64,1024]{1,0:T(8,128)(2,1)S(1)}, u32[]{:S(2)}, u32[]{:S(2)}) %collective-permute-start) | collective-permute-done | bytes 131104 | tf_op jit(solution)/shard_map/ppermute | solution.py:183
  14.0 0.0 collective-permute-done.2.other
  14.0 1.8 %shard_map.60 = (bf16[1088,384]{1,0:T(8,128)(2,1)S(1)}, bf16[256,1024]{1,0:T(8,128)(2,1)S(1)}, f32[128,1152]{1,0:T(8,128)S(1)}, f32[128,576]{1,0:T(8,128)S(1)}) custom-call(s32[2]{0:T(128)S(1)} %pad_add_fusion.place, bf16[64,1024]{1,0:T(8,128)(2,1)S(1)} %fusion.7.own, bf16[64,1024]{1,0:T(8,128)(2,1)S(1)} %collective-permute-done.near, ...), custom_call_target="tpu_custom_call" | custom-call | flops 905969664 | bytes 4194304 | tf_op jit(solution)/shard_map/pallas_call | solution.py:231
  15.9 2.7 %collective-permute-done.4.one_off = bf16[64,1024]{1,0:T(8,128)(2,1)S(1)} collective-permute-done((bf16[64,1024]{1,0:T(8,128)(2,1)S(1)}, bf16[64,1024]{1,0:T(8,128)(2,1)S(1)}, u32[]{:S(2)}, u32[]{:S(2)}) %collective-permute-start.4) | collective-permute-done | bytes 131104 | tf_op jit(solution)/shard_map/ppermute | solution.py:183
  18.5 0.0 copy-start.1
  18.5 1.7 %shard_map.61 = (bf16[1088,384]{1,0:T(8,128)(2,1)S(1)}, f32[64,1728]{1,0:T(8,128)S(1)}, bf16[64,1728]{1,0:T(8,128)(2,1)S(1)}) custom-call(s32[2]{0:T(128)S(1)} %pad_add_fusion.place, bf16[64,1024]{1,0:T(8,128)(2,1)S(1)} %collective-permute-done.3.two_off, bf16[64,1024]{1,0:T(8,128)(2,1)S(1)} %collective-permute-done.4.one_off, ...), custom_call_target="tpu_custom_call" | custom-call | flops 905969664 | bytes 4194304 | tf_op jit(solution)/shard_map/pallas_call | solution.py:244
  20.3 0.0 copy-done.1
  20.3 1.9 %shard_map.62 = (f32[512,256]{1,0:T(8,128)S(1)}, bf16[512,256]{1,0:T(8,128)(2,1)S(1)}) custom-call(s32[2]{0:T(128)S(1)} %pad_add_fusion.place, bf16[1088,384]{1,0:T(8,128)(2,1)S(1)} %get-tuple-element.22.pair, bf16[1088,384]{1,0:T(8,128)(2,1)S(1)} %get-tuple-element.26.ends, bf16[27,64,256]{2,1,0:T(8,128)(2,1)S(1)} %copy-done.1), custom_call_target="tpu_custom_call" | custom-call | flops 905969664 | bytes 4194304 | tf_op jit(solution)/shard_map/pallas_call | solution.py:253
  22.2 0.1 collective-permute-start.5
  22.3 1.6 %collective-permute-start.6 = (bf16[64,1728]{1,0:T(8,128)(2,1)S(1)}, bf16[64,1728]{1,0:T(8,128)(2,1)S(1)}, u32[]{:S(2)}, u32[]{:S(2)}) collective-permute-start(bf16[64,1728]{1,0:T(8,128)(2,1)S(1)} %get-tuple-element.30), channel_id=1, source_target_pairs={{0,8},{4,12},{8,0},{12,4},{16,24},{20,28},{24,16},{28,20},{1,9},{5... | collective-permute-start | bytes 663560 | tf_op jit(solution)/shard_map/ppermute | solution.py:183
  23.9 6.4 %collective-permute-done.6.came = bf16[64,1728]{1,0:T(8,128)(2,1)S(1)} collective-permute-done((bf16[64,1728]{1,0:T(8,128)(2,1)S(1)}, bf16[64,1728]{1,0:T(8,128)(2,1)S(1)}, u32[]{:S(2)}, u32[]{:S(2)}) %collective-permute-start.6) | collective-permute-done | bytes 221216 | tf_op jit(solution)/shard_map/ppermute | solution.py:183
  30.3 0.1 shard_map.63
  30.4 0.0 collective-permute-done.5.came
  30.4 1.6 %collective-permute-start.7 = (bf16[256,256]{1,0:T(8,128)(2,1)S(1)}, bf16[256,256]{1,0:T(8,128)(2,1)S(1)}, u32[]{:S(2)}, u32[]{:S(2)}) collective-permute-start(bf16[256,256]{1,0:T(8,128)(2,1)S(1)} %get-tuple-element.34), channel_id=1, source_target_pairs={{0,2},{1,3},{2,0},{3,1},{4,6},{5,7},{6,4},{7,5},{8,10},{9,11},{10,... | collective-permute-start | bytes 393224 | tf_op jit(solution)/shard_map/ppermute | solution.py:183
  32.0 2.6 %collective-permute-start.8 = (bf16[32,1728]{1,0:T(8,128)(2,1)S(1)}, bf16[32,1728]{1,0:T(8,128)(2,1)S(1)}, u32[]{:S(2)}, u32[]{:S(2)}) collective-permute-start(bf16[32,1728]{1,0:T(8,128)(2,1)S(1)} %get-tuple-element.31), channel_id=1, source_target_pairs={{0,16},{4,20},{8,24},{12,28},{16,0},{20,4},{24,8},{28,12},{1,17},{... | collective-permute-start | bytes 331784 | tf_op jit(solution)/shard_map/ppermute | solution.py:183
  34.6 5.2 %collective-permute-done.8.came = bf16[32,1728]{1,0:T(8,128)(2,1)S(1)} collective-permute-done((bf16[32,1728]{1,0:T(8,128)(2,1)S(1)}, bf16[32,1728]{1,0:T(8,128)(2,1)S(1)}, u32[]{:S(2)}, u32[]{:S(2)}) %collective-permute-start.8) | collective-permute-done | bytes 110624 | tf_op jit(solution)/shard_map/ppermute | solution.py:183
  39.8 0.9 %shard_map.66 = f32[27,32,64]{2,1,0:T(8,128)} custom-call(f32[32,1728]{1,0:T(8,128)S(1)} %get-tuple-element.35.kept, bf16[32,1728]{1,0:T(8,128)(2,1)S(1)} %collective-permute-done.8.came), custom_call_target="tpu_custom_call" | custom-call | tf_op jit(solution)/shard_map/pallas_call | solution.py:274
  40.7 0.0 collective-permute-done.7.came
  40.7 0.7 %shard_map.65 = bf16[256,256]{1,0:T(8,128)(2,1)} custom-call(f32[256,256]{1,0:T(8,128)S(1)} %get-tuple-element.33.kept, bf16[256,256]{1,0:T(8,128)(2,1)S(1)} %collective-permute-done.7.came), custom_call_target="tpu_custom_call" | custom-call | tf_op jit(solution)/shard_map/pallas_call | solution.py:277
  (1 shorter events, 0.0 us)
Async XLA Ops:
  1.8 1.0 %copy-start = (bf16[1,32,32,256]{3,2,1,0:T(8,128)(2,1)S(1)}, bf16[1,32,32,256]{3,2,1,0:T(8,128)(2,1)}, u32[]{:S(2)}) copy-start(bf16[1,32,32,256]{3,2,1,0:T(8,128)(2,1)} %param.4) | copy-start | bytes 1572868
  3.7 7.1 %collective-permute-start.1 = (bf16[64,1024]{1,0:T(8,128)(2,1)S(1)}, bf16[64,1024]{1,0:T(8,128)(2,1)S(1)}, u32[]{:S(2)}, u32[]{:S(2)}) collective-permute-start(bf16[64,1024]{1,0:T(8,128)(2,1)S(1)} %get-tuple-element.21), channel_id=1, source_target_pairs={{0,4},{4,0},{8,12},{12,8},{16,20},{20,16},{24,28},{28,24},{1,5},{5... | collective-permute-start | bytes 393224 | tf_op jit(solution)/shard_map/ppermute | solution.py:183
  6.7 6.8 %collective-permute-start.3 = (bf16[64,1024]{1,0:T(8,128)(2,1)S(1)}, bf16[64,1024]{1,0:T(8,128)(2,1)S(1)}, u32[]{:S(2)}, u32[]{:S(2)}) collective-permute-start(bf16[64,1024]{1,0:T(8,128)(2,1)S(1)} %fusion.7.own), channel_id=1, source_target_pairs={{8,0},{16,8},{24,16},{4,12},{12,20},{20,28},{9,1},{17,9},{25,17},{... | collective-permute-start | bytes 393224 | tf_op jit(solution)/shard_map/ppermute | solution.py:221
  8.0 6.0 %collective-permute-start = (bf16[64,1024]{1,0:T(8,128)(2,1)S(1)}, bf16[64,1024]{1,0:T(8,128)(2,1)S(1)}, u32[]{:S(2)}, u32[]{:S(2)}) collective-permute-start(bf16[64,1024]{1,0:T(8,128)(2,1)S(1)} %fusion.7.own), channel_id=1, source_target_pairs={{0,4},{4,0},{8,12},{12,8},{16,20},{20,16},{24,28},{28,24},{1,5},{5... | collective-permute-start | bytes 393224 | tf_op jit(solution)/shard_map/ppermute | solution.py:183
  10.8 3.2 %collective-permute-start.2 = (bf16[64,1024]{1,0:T(8,128)(2,1)S(1)}, bf16[64,1024]{1,0:T(8,128)(2,1)S(1)}, u32[]{:S(2)}, u32[]{:S(2)}) collective-permute-start(bf16[64,1024]{1,0:T(8,128)(2,1)S(1)} %collective-permute-done.1.came), channel_id=1, source_target_pairs={{0,1},{1,0},{2,3},{3,2},{4,5},{5,4},{6,7},{7,6},{8,9},{9,8},{10,11... | collective-permute-start | bytes 393224 | tf_op jit(solution)/shard_map/ppermute | solution.py:183
  13.6 5.0 %collective-permute-start.4 = (bf16[64,1024]{1,0:T(8,128)(2,1)S(1)}, bf16[64,1024]{1,0:T(8,128)(2,1)S(1)}, u32[]{:S(2)}, u32[]{:S(2)}) collective-permute-start(bf16[64,1024]{1,0:T(8,128)(2,1)S(1)} %collective-permute-done.3.two_off), channel_id=1, source_target_pairs={{0,4},{4,0},{8,12},{12,8},{16,20},{20,16},{24,28},{28,24},{1,5},{5... | collective-permute-start | bytes 393224 | tf_op jit(solution)/shard_map/ppermute | solution.py:183
  18.5 1.7 %copy-start.1 = (bf16[27,64,256]{2,1,0:T(8,128)(2,1)S(1)}, bf16[27,64,256]{2,1,0:T(8,128)(2,1)}, u32[]{:S(2)}) copy-start(bf16[27,64,256]{2,1,0:T(8,128)(2,1)} %weight.1) | copy-start | bytes 2654212
  22.2 8.2 %collective-permute-start.5 = (bf16[512,256]{1,0:T(8,128)(2,1)S(1)}, bf16[512,256]{1,0:T(8,128)(2,1)S(1)}, u32[]{:S(2)}, u32[]{:S(2)}) collective-permute-start(bf16[512,256]{1,0:T(8,128)(2,1)S(1)} %get-tuple-element.28), channel_id=1, source_target_pairs={{0,1},{1,0},{2,3},{3,2},{4,5},{5,4},{6,7},{7,6},{8,9},{9,8},{10,11... | collective-permute-start | bytes 786440 | tf_op jit(solution)/shard_map/ppermute | solution.py:183
  22.3 8.0 %collective-permute-start.6 = (bf16[64,1728]{1,0:T(8,128)(2,1)S(1)}, bf16[64,1728]{1,0:T(8,128)(2,1)S(1)}, u32[]{:S(2)}, u32[]{:S(2)}) collective-permute-start(bf16[64,1728]{1,0:T(8,128)(2,1)S(1)} %get-tuple-element.30), channel_id=1, source_target_pairs={{0,8},{4,12},{8,0},{12,4},{16,24},{20,28},{24,16},{28,20},{1,9},{5... | collective-permute-start | bytes 663560 | tf_op jit(solution)/shard_map/ppermute | solution.py:183
  30.4 10.3 %collective-permute-start.7 = (bf16[256,256]{1,0:T(8,128)(2,1)S(1)}, bf16[256,256]{1,0:T(8,128)(2,1)S(1)}, u32[]{:S(2)}, u32[]{:S(2)}) collective-permute-start(bf16[256,256]{1,0:T(8,128)(2,1)S(1)} %get-tuple-element.34), channel_id=1, source_target_pairs={{0,2},{1,3},{2,0},{3,1},{4,6},{5,7},{6,4},{7,5},{8,10},{9,11},{10,... | collective-permute-start | bytes 393224 | tf_op jit(solution)/shard_map/ppermute | solution.py:183
  32.0 7.8 %collective-permute-start.8 = (bf16[32,1728]{1,0:T(8,128)(2,1)S(1)}, bf16[32,1728]{1,0:T(8,128)(2,1)S(1)}, u32[]{:S(2)}, u32[]{:S(2)}) collective-permute-start(bf16[32,1728]{1,0:T(8,128)(2,1)S(1)} %get-tuple-element.31), channel_id=1, source_target_pairs={{0,16},{4,20},{8,24},{12,28},{16,0},{20,4},{24,8},{28,12},{1,17},{... | collective-permute-start | bytes 331784 | tf_op jit(solution)/shard_map/ppermute | solution.py:183

commit v3 on v2

v3 whole, which is shorter than its diff:
```python
import functools

import jax
import jax.numpy as jnp
from jax import lax
from jax.experimental import pallas as pl
from jax.experimental.pallas import tpu as pltpu
from jax.sharding import PartitionSpec as P

MIB = 1 << 20
VMEM = pl.BlockSpec(memory_space=pltpu.VMEM)
SMEM = pl.BlockSpec(memory_space=pltpu.SMEM)


def silu_grad(values):
    sig = jax.nn.sigmoid(values)
    return sig * (1.0 + values * (1.0 - sig))


def bits_of(count):
    return count.bit_length() - 1


def reversed_bits(value, width):
    return sum(((value >> bit) & 1) << (width - 1 - bit) for bit in range(width))


def call(kernel, outs, scratch=(), flops=0, bytes_accessed=0, limit=24):
    return functools.partial(
        pl.pallas_call,
        kernel,
        out_shape=outs,
        scratch_shapes=scratch,
        compiler_params=pltpu.CompilerParams(vmem_limit_bytes=limit * MIB),
        cost_estimate=pl.CostEstimate(flops=flops, bytes_accessed=bytes_accessed, transcendentals=0),
    )


def lay_windows(width, first, second, windows, tall):
    filt, cells = first.shape
    lanes = 2 * filt
    tall[pl.ds(8, cells), :] = jnp.concatenate([first, second], axis=0).astype(jnp.float32).T
    row = lax.broadcasted_iota(jnp.int32, (cells, lanes), 0)
    column = row & (width - 1) if width & (width - 1) == 0 else lax.rem(row, width)
    zero_rows = jnp.zeros((width, windows.shape[1]), jnp.bfloat16)
    windows[pl.ds(0, width), :] = zero_rows
    windows[pl.ds(width + cells, width), :] = zero_rows
    body = pl.ds(width, cells)
    windows[body, 0:lanes] = jnp.where(column != width - 1, tall[pl.ds(9, cells), :], 0.0).astype(jnp.bfloat16)
    windows[body, lanes : 2 * lanes] = tall[pl.ds(8, cells), :].astype(jnp.bfloat16)
    windows[body, 2 * lanes : 3 * lanes] = jnp.where(column != 0, tall[pl.ds(7, cells), :], 0.0).astype(jnp.bfloat16)


def turn_kernel(blocks, place, inputs, mine, sent):
    chans = inputs.shape[1]
    rows = chans // blocks
    half, part = mine.shape[0], sent.shape[0]
    count = bits_of(blocks)
    order = lax.broadcasted_iota(jnp.int32, (half + part, chans), 0)
    order = order + jnp.where(order >= half, (place[1] & 1) * part, 0)
    block = place[0] ^ reversed_bits(order >> bits_of(rows), count)
    source = (block << bits_of(rows)) | (order & (rows - 1))
    picked = (lax.broadcasted_iota(jnp.int32, (half + part, chans), 1) == source).astype(jnp.bfloat16)
    turned = lax.dot_general(picked, inputs[...], (((1,), (1,)), ((), ())), preferred_element_type=jnp.float32)
    turned = turned.astype(jnp.bfloat16)
    mine[...] = turned[0:half, :]
    sent[...] = turned[half:, :]


def order_kernel(place, weight, ordered):
    filt = weight.shape[1]
    odd = place[0] & 1
    zero = jnp.zeros(weight.shape[1:], jnp.bfloat16)
    for tap in range(9):
        b, c = divmod(tap, 3)
        rows = (weight[9 + tap], weight[18 * odd + tap], weight[18 - 18 * odd + tap], zero)
        for slot, value in zip((2 * c, 2 * c + 1, 2 * c + 6, 2 * c + 7), rows):
            ordered[b, pl.ds(slot * filt, filt), :] = value


def spread_kernel(width, groups, place, own, near, one_off, ordered, pair, ones, keep, send, tall):
    filt, cells = own.shape
    part = cells // groups
    index = place[1]
    lay_windows(width, own[...], near[...], pair, tall)
    lay_windows(width, one_off[...], one_off[...], ones, tall)
    count = bits_of(groups)
    for target in reversed(range(groups)):
        block = 0
        for bit in range(count):
            differs = (target >> (count - 1 - bit)) & 1
            block = block + (((index >> bit) & 1) ^ differs) * (1 << bit)
        total = 0.0
        for b in range(3):
            rows = pl.ds(pl.multiple_of(block * part + (2 - b) * width, width), part)
            window = jnp.concatenate([pair[rows, :], ones[rows, :]], axis=1)
            total = total + jnp.dot(window, ordered[b], preferred_element_type=jnp.float32)
        if target < groups // 2:
            keep[pl.ds(target * part, part), :] = total
        else:
            send[pl.ds((target - groups // 2) * part, part), :] = total.astype(jnp.bfloat16)


def mine_kernel(width, place, mine, pair, ones, two_off, twos, first, second, tall):
    filt, cells = two_off.shape
    lanes = 2 * filt
    wide = pair.shape[1]
    lay_windows(width, two_off[...], two_off[...], twos, tall)
    for b in range(3):
        rows = pl.ds((2 - b) * width, cells)
        first[:, b * wide : (b + 1) * wide] = jnp.dot(mine[...], pair[rows, :], preferred_element_type=jnp.float32)
        second[:, b * wide : (b + 1) * wide] = jnp.dot(mine[...], ones[rows, :], preferred_element_type=jnp.float32)


def theirs_kernel(width, filt, place, came, other, pair, twos, first, second, keep, *sends):
    half = first.shape[0]
    lanes = 2 * filt
    wide = pair.shape[1]
    cells = came.shape[1]
    first_core = place[1] & 1 == 0
    theirs = jnp.concatenate(
        [jnp.where(first_core, came[...], other[...]), jnp.where(first_core, other[...], came[...])], axis=0
    )
    left = lax.broadcasted_iota(jnp.int32, (half, lanes), 1) < filt
    part = half // (len(sends) + 1)

    def store(lo, hi, value):
        keep[:, lo:hi] = value[0:part, :]
        for number, send in enumerate(sends, 1):
            send[:, lo:hi] = value[number * part : (number + 1) * part, :].astype(jnp.bfloat16)

    for b in range(3):
        rows = pl.ds((2 - b) * width, cells)
        near_terms = jnp.dot(theirs, pair[rows, :], preferred_element_type=jnp.float32)
        far_terms = jnp.dot(theirs, twos[rows, :], preferred_element_type=jnp.float32)
        for c in range(3):
            tap = 3 * b + c
            cut = slice(c * lanes, (c + 1) * lanes)
            lo = b * wide + c * lanes
            crossed = jnp.where(left, pltpu.roll(near_terms[:, cut], filt, 1), far_terms[:, cut])
            store(lo, lo + lanes, first[:, lo : lo + lanes] + crossed)
            outer = second[:, lo : lo + lanes] + near_terms[:, cut]
            lo = 3 * wide + tap // 2 * lanes
            if tap == 8:
                store(lo, lo + filt, outer[:, 0:filt])
            elif tap % 2 == 0:
                before = outer
            else:
                store(lo, lo + lanes, jnp.where(left, before, pltpu.roll(outer, filt, 1)))


def halve_kernel(kept, came, keep, send):
    half = keep.shape[0]
    keep[...] = kept[0:half, :] + came[0:half, :].astype(jnp.float32)
    send[...] = (kept[half:, :] + came[half:, :].astype(jnp.float32)).astype(jnp.bfloat16)


def last_input_kernel(kept, came, out):
    out[...] = (kept[...] + came[...].astype(jnp.float32)).astype(out.dtype)


def last_weight_kernel(scale, filt, place, kept, *rest):
    *came, out = rest
    odd = place[0] & 1
    total = kept[...]
    for piece in came:
        total = total + piece[...].astype(jnp.float32)
    total = total * scale
    for tap in range(9):
        slots = ((2 * tap, 9 + tap), (2 * tap + 1, 18 * odd + tap), (18 + tap, 18 - 18 * odd + tap))
        for slot, target in slots:
            out[target] = total[:, slot * filt : (slot + 1) * filt]


def swapped(value, axis, distance):
    count = lax.axis_size(axis)
    return lax.ppermute(value, axis, [(i, i ^ distance) for i in range(count)])


def halved(kept, came):
    rows, lanes = kept.shape
    if rows // 2 % 16:
        total = kept + came.astype(jnp.float32)
        return total[: rows // 2], total[rows // 2 :].astype(jnp.bfloat16)
    outs = (
        jax.ShapeDtypeStruct((rows // 2, lanes), jnp.float32),
        jax.ShapeDtypeStruct((rows // 2, lanes), jnp.bfloat16),
    )
    return call(halve_kernel, outs, flops=rows * lanes, bytes_accessed=9 * rows * lanes)(
        in_specs=[VMEM] * 2, out_specs=[VMEM] * 2
    )(kept, came)


def after(value, other):
    return lax.optimization_barrier((value, other))[0]


def on_device(inputs, out_grad, pre_act, weight):
    _, height, width, chans = inputs.shape
    taps, filt, _ = weight.shape
    cells = height * width
    blocks, groups = lax.axis_size("space"), lax.axis_size("filt")
    half, quarter = chans // 2, chans // 4
    place = jnp.stack([lax.axis_index("space"), lax.axis_index("filt")]).astype(jnp.int32)
    bf16, f32 = jnp.bfloat16, jnp.float32
    shape = jax.ShapeDtypeStruct
    flops = 2 * cells * taps * filt * chans
    lanes = 6 * filt
    windows_shape = shape((cells + 2 * width, lanes), bf16)
    tall = pltpu.VMEM((cells + 16, 2 * filt), f32)

    own = (out_grad.astype(f32) * silu_grad(pre_act.astype(f32))).astype(bf16)[0]
    one_pairs = [(i, i + 1) for i in range(1, blocks - 1, 2)]
    one_off = lax.ppermute(own, "space", one_pairs + [(target, source) for source, target in one_pairs])
    near = swapped(own, "space", 1)
    mine, sent = call(
        functools.partial(turn_kernel, blocks),
        (shape((half, cells), bf16), shape((quarter, cells), bf16)),
        bytes_accessed=MIB,
    )(in_specs=[SMEM, VMEM], out_specs=[VMEM] * 2)(after(place, own), inputs.reshape(cells, chans))
    came = swapped(sent, "space", 1)
    two_pairs = [(i, i - 2) for i in range(2, blocks, 2)] + [(i, i + 2) for i in range(1, blocks - 2, 2)]
    two_off = lax.ppermute(own, "space", two_pairs)

    ordered = call(order_kernel, shape((3, 2 * lanes, chans), bf16), bytes_accessed=MIB)(
        in_specs=[SMEM, VMEM], out_specs=VMEM
    )(after(place, mine), weight)
    pair, ones, kept_in, sent_in = call(
        functools.partial(spread_kernel, width, groups),
        (windows_shape, windows_shape, shape((cells // 2, chans), f32), shape((cells // 2, chans), bf16)),
        (tall,),
        flops=flops,
        bytes_accessed=4 * MIB,
    )(in_specs=[SMEM] + [VMEM] * 4, out_specs=[VMEM] * 4)(place, own, near, one_off, ordered)
    other = swapped(after(came, sent_in), "filt", 1)
    came_in = swapped(sent_in, "filt", 1)

    twos, first, second = call(
        functools.partial(mine_kernel, width),
        (windows_shape, shape((half, 3 * lanes), f32), shape((half, 3 * lanes), f32)),
        (tall,),
        flops=flops,
        bytes_accessed=4 * MIB,
    )(in_specs=[SMEM] + [VMEM] * 4, out_specs=[VMEM] * 3)(place, mine, pair, ones, two_off)

    radix = min(4, blocks // 2)
    piece = half // radix
    kept, *sends = call(
        functools.partial(theirs_kernel, width, filt),
        (shape((piece, taps * filt), f32),) + (shape((piece, taps * filt), bf16),) * (radix - 1),
        flops=flops,
        bytes_accessed=4 * MIB,
    )(in_specs=[SMEM] + [VMEM] * 6, out_specs=[VMEM] * radix)(place, came, other, pair, twos, first, second)

    came_in = after(came_in, kept)
    distance = 2
    while True:
        spans = {2: (1,), 4: (2, 1, 3)}[radix]
        arrived = [swapped(sends[n - 1], "space", spans[n - 1] * distance) for n in range(1, radix)]
        distance *= radix
        if distance >= blocks:
            break
        total = kept
        for part in arrived:
            total = total + part.astype(f32)
        radix = min(4, blocks // distance)
        piece //= radix
        kept, *sends = (total[n * piece : (n + 1) * piece] for n in range(radix))
        sends = [value.astype(bf16) for value in sends]

    distance_in = 2
    while distance_in < groups:
        kept_in, sent_in = halved(kept_in, came_in)
        came_in = swapped(sent_in, "filt", distance_in)
        distance_in *= 2
    grad_input = call(last_input_kernel, shape((cells // groups, chans), bf16))(
        in_specs=[VMEM] * 2, out_specs=VMEM
    )(kept_in, came_in)
    grad_scale = float(cells * blocks) ** (-0.5)
    grad_weight = call(
        functools.partial(last_weight_kernel, grad_scale, filt), shape((taps, chans // blocks, filt), f32)
    )(in_specs=[SMEM] + [VMEM] * (len(arrived) + 1), out_specs=VMEM)(after(place, grad_input), kept, *arrived)
    return grad_input.reshape(1, height // groups, width, chans), jnp.transpose(grad_weight, (1, 0, 2))


def solution(mesh):
    placed = (
        P("space", None, None, None),
        P("space", "filt", None),
        P("space", "filt", None),
        P(None, "filt", None),
    )
    return jax.shard_map(
        on_device,
        mesh=mesh,
        in_specs=placed,
        out_specs=(P("space", "filt", None, None), P("space", None, "filt")),
        check_vma=False,
    )
```

time: 41.6 us -> 37.2 us (0.89)
  waiting for transfers between devices: 17.5 us -> 6.75 us
  starting transfers between devices: 13 us -> 18 us
  Pallas kernels: 7.99 us -> 9.13 us
    ppermute x8, waiting for transfers between devices: 14.7 us -> 6.74 us  [swapped(): return lax.ppermute(value, axis, [(i, i ^ distance) for i in range(count)])]
    ppermute x8, starting transfers between devices: 11.7 us -> 16.1 us  [swapped(): return lax.ppermute(value, axis, [(i, i ^ distance) for i in range(count)])]
    ppermute x1, waiting for transfers between devices: 2.76 us -> 0.01 us  [on_device(): two_off = lax.ppermute(own, 'space', two_pairs)]
    ppermute x0 -> x1, starting transfers between devices: none -> 0.66 us  [on_device(): lax.ppermute(own, 'space', one_pairs + [(target, source) for source, targ...]
    pallas_call x3 -> x4, Pallas kernels: 5.45 us -> 6.1 us  [the longest x1 2.31 us: on_device(): call(functools.partial(spread_kernel, width, groups), (windows_shape, win...]
    pallas_call x1, Pallas kernels: 0.89 us -> 1.44 us  [on_device(): call(functools.partial(last_weight_kernel, grad_scale, filt), shape((taps...]
  transfers between devices with their start and end apart: 9 -> 10, of which waited for: 5 -> 1; matrix products, arithmetic and copies ran while one was open for 0% -> 0% of each run, Pallas kernels for 7% -> 21%
where the time goes in v3:
time: 37.2 us; the launch traced here: 36.9 us
  starting transfers between devices  18 us (48%)
  Pallas kernels  9.13 us (25%)
  waiting for transfers between devices  6.75 us (18%)
  other arithmetic  1.24 us (3%)
  local copies, waits for them, and re-layouts  1.05 us (3%)
  between operations  0.76 us (2%)
    ppermute x8, starting transfers between devices, swapped(): return lax.ppermute(value, axis, [(i, i ^ distance) for i in range(count)])  16.1 us
    ppermute x8, waiting for transfers between devices, swapped(): return lax.ppermute(value, axis, [(i, i ^ distance) for i in range(count)])  6.74 us
    pallas_call x1, Pallas kernels, on_device(): call(functools.partial(spread_kernel, width, groups), (windows_shape, win...  2.31 us
    pallas_call x1, Pallas kernels, on_device(): call(functools.partial(mine_kernel, width), (windows_shape, shape((half,...  1.6 us
    pallas_call x1, Pallas kernels, on_device(): call(functools.partial(theirs_kernel, width, filt), (shape((piece, taps *...  1.58 us
    pallas_call x1, Pallas kernels, on_device(): call(functools.partial(last_weight_kernel, grad_scale, filt), shape((taps...  1.44 us
    ppermute x1, starting transfers between devices, on_device(): two_off = lax.ppermute(own, 'space', two_pairs)  1.29 us
    squeeze x1, other arithmetic, on_device(): (out_grad.astype(f32) * silu_grad(pre_act.astype(f32))).astype(bf16)[0]  1.16 us
  transfers between devices with their start and end apart: 10, of which 1 were waited for; matrix products, arithmetic and copies ran while one was open for 0% of the time, Pallas kernels for 21%

profile of v3, /device:TPU:0, one launch (start us, length us, event | category | flops | bytes accessed | tf_op | source)
XLA Modules:
  0.0 36.9 jit_solution(15874131781203299132)
XLA Ops:
  0.6 0.0 copy-start
  0.6 1.2 %fusion.7.own = bf16[64,1024]{1,0:T(8,128)(2,1)S(1)} fusion(bf16[1,64,1024]{2,1,0:T(8,128)(2,1)} %param.6, bf16[1,64,1024]{2,1,0:T(8,128)(2,1)} %param.5), kind=kLoop, calls=%fused_computation.9 | loop fusion | flops 720896 | bytes 393216 | tf_op jit(solution)/shard_map/squeeze | solution.py:212
  1.8 3.0 %collective-permute-start = (bf16[64,1024]{1,0:T(8,128)(2,1)S(1)}, bf16[64,1024]{1,0:T(8,128)(2,1)S(1)}, u32[]{:S(2)}, u32[]{:S(2)}) collective-permute-start(bf16[64,1024]{1,0:T(8,128)(2,1)S(1)} %fusion.7.own), channel_id=1, source_target_pairs={{0,4},{4,0},{8,12},{12,8},{16,20},{20,16},{24,28},{28,24},{1,5},{5... | collective-permute-start | bytes 393224 | tf_op jit(solution)/shard_map/ppermute | solution.py:177
  4.8 0.7 %collective-permute-start.1 = (bf16[64,1024]{1,0:T(8,128)(2,1)S(1)}, bf16[64,1024]{1,0:T(8,128)(2,1)S(1)}, u32[]{:S(2)}, u32[]{:S(2)}) collective-permute-start(bf16[64,1024]{1,0:T(8,128)(2,1)S(1)} %fusion.7.own), channel_id=1, source_target_pairs={{4,8},{12,16},{20,24},{8,4},{16,12},{24,20},{5,9},{13,17},{21,25},... | collective-permute-start | bytes 393224 | tf_op jit(solution)/shard_map/ppermute | solution.py:214
  5.5 1.3 %collective-permute-start.5 = (bf16[64,1024]{1,0:T(8,128)(2,1)S(1)}, bf16[64,1024]{1,0:T(8,128)(2,1)S(1)}, u32[]{:S(2)}, u32[]{:S(2)}) collective-permute-start(bf16[64,1024]{1,0:T(8,128)(2,1)S(1)} %fusion.7.own), channel_id=1, source_target_pairs={{8,0},{16,8},{24,16},{4,12},{12,20},{20,28},{9,1},{17,9},{25,17},{... | collective-permute-start | bytes 393224 | tf_op jit(solution)/shard_map/ppermute | solution.py:223
  6.8 0.1 pad_add_fusion.place
  6.9 0.0 copy-start.1
  6.9 1.0 %copy-done.1 = bf16[1,32,32,256]{3,2,1,0:T(8,128)(2,1)S(1)} copy-done((bf16[1,32,32,256]{3,2,1,0:T(8,128)(2,1)S(1)}, bf16[1,32,32,256]{3,2,1,0:T(8,128)(2,1)}, u32[]{:S(2)}) %copy-start.1) | copy-done | bytes 524312
  7.9 0.9 %shard_map.59 = (bf16[128,1024]{1,0:T(8,128)(2,1)S(1)}, bf16[64,1024]{1,0:T(8,128)(2,1)S(1)}) custom-call(s32[2]{0:T(128)S(1)} %pad_add_fusion.place, bf16[1024,256]{1,0:T(8,128)(2,1)S(1)} %bitcast.7), custom_call_target="tpu_custom_call" | custom-call | bytes 1048576 | tf_op jit(solution)/shard_map/pallas_call | solution.py:216
  8.8 6.5 %collective-permute-start.3 = (bf16[64,1024]{1,0:T(8,128)(2,1)S(1)}, bf16[64,1024]{1,0:T(8,128)(2,1)S(1)}, u32[]{:S(2)}, u32[]{:S(2)}) collective-permute-start(bf16[64,1024]{1,0:T(8,128)(2,1)S(1)} %get-tuple-element.27), channel_id=1, source_target_pairs={{0,4},{4,0},{8,12},{12,8},{16,20},{20,16},{24,28},{28,24},{1,5},{5... | collective-permute-start | bytes 393224 | tf_op jit(solution)/shard_map/ppermute | solution.py:177
  15.3 0.0 copy-done
  15.3 0.6 %shard_map.60.ordered = bf16[3,768,256]{2,1,0:T(8,128)(2,1)S(1)} custom-call(s32[2]{0:T(128)S(1)} %pad_add_fusion.place, bf16[27,64,256]{2,1,0:T(8,128)(2,1)S(1)} %copy-done), custom_call_target="tpu_custom_call" | custom-call | bytes 1048576 | tf_op jit(solution)/shard_map/pallas_call | solution.py:225
  15.9 0.0 collective-permute-done.near
  15.9 0.0 collective-permute-done.1.one_off
  16.0 2.3 %shard_map.61 = (bf16[1088,384]{1,0:T(8,128)(2,1)S(1)}, bf16[1088,384]{1,0:T(8,128)(2,1)S(1)}, f32[512,256]{1,0:T(8,128)S(1)}, bf16[512,256]{1,0:T(8,128)(2,1)S(1)}) custom-call(s32[2]{0:T(128)S(1)} %pad_add_fusion.place, bf16[64,1024]{1,0:T(8,128)(2,1)S(1)} %fusion.7.own, bf16[64,1024]{1,0:T(8,128)(2,1)S(1)} %collective-permute-done.near, ...), custom_call_target="tpu_custom_call" | custom-call | flops 905969664 | bytes 4194304 | tf_op jit(solution)/shard_map/pallas_call | solution.py:228
  18.3 0.1 collective-permute-start.2
  18.4 0.0 collective-permute-done.3.came
  18.4 0.5 %collective-permute-start.4 = (bf16[64,1024]{1,0:T(8,128)(2,1)S(1)}, bf16[64,1024]{1,0:T(8,128)(2,1)S(1)}, u32[]{:S(2)}, u32[]{:S(2)}) collective-permute-start(bf16[64,1024]{1,0:T(8,128)(2,1)S(1)} %collective-permute-done.3.came), channel_id=1, source_target_pairs={{0,1},{1,0},{2,3},{3,2},{4,5},{5,4},{6,7},{7,6},{8,9},{9,8},{10,11... | collective-permute-start | bytes 393224 | tf_op jit(solution)/shard_map/ppermute | solution.py:177
  18.9 0.0 collective-permute-done.5.two_off
  18.9 1.6 %shard_map.62 = (bf16[1088,384]{1,0:T(8,128)(2,1)S(1)}, f32[128,1152]{1,0:T(8,128)S(1)}, f32[128,1152]{1,0:T(8,128)S(1)}) custom-call(s32[2]{0:T(128)S(1)} %pad_add_fusion.place, bf16[128,1024]{1,0:T(8,128)(2,1)S(1)} %get-tuple-element.23.mine, bf16[1088,384]{1,0:T(8,128)(2,1)S(1)} %get-tuple-element.29.pair, bf16[1088,384]{1,0:T(8,128)(2,1)S(1)} %get-tuple-element.30.ones, ...), custom_call_target="tpu_custom_call" | custom-call | flops 905969664 | bytes 4194304 | tf_op jit(solution)/shard_map/pallas_call | solution.py:238
  20.5 0.0 collective-permute-done.4.other
  20.5 1.6 %shard_map.63 = (f32[32,1728]{1,0:T(8,128)S(1)}, bf16[32,1728]{1,0:T(8,128)(2,1)S(1)}, bf16[32,1728]{1,0:T(8,128)(2,1)S(1)}, bf16[32,1728]{1,0:T(8,128)(2,1)S(1)}) custom-call(s32[2]{0:T(128)S(1)} %pad_add_fusion.place, bf16[64,1024]{1,0:T(8,128)(2,1)S(1)} %collective-permute-done.3.came, bf16[64,1024]{1,0:T(8,128)(2,1)S(1)} %collective-permute-done.4.other, ...), custom_call_target="tpu_custom_call" | custom-call | flops 905969664 | bytes 4194304 | tf_op jit(solution)/shard_map/pallas_call | solution.py:248
  22.1 0.0 collective-permute-done.2.came
  22.1 1.6 %collective-permute-start.6 = (bf16[256,256]{1,0:T(8,128)(2,1)S(1)}, bf16[256,256]{1,0:T(8,128)(2,1)S(1)}, u32[]{:S(2)}, u32[]{:S(2)}) collective-permute-start(bf16[256,256]{1,0:T(8,128)(2,1)S(1)} %get-tuple-element.37), channel_id=1, source_target_pairs={{0,2},{1,3},{2,0},{3,1},{4,6},{5,7},{6,4},{7,5},{8,10},{9,11},{10,... | collective-permute-start | bytes 393224 | tf_op jit(solution)/shard_map/ppermute | solution.py:177
  23.7 1.0 %collective-permute-start.7 = (bf16[32,1728]{1,0:T(8,128)(2,1)S(1)}, bf16[32,1728]{1,0:T(8,128)(2,1)S(1)}, u32[]{:S(2)}, u32[]{:S(2)}) collective-permute-start(bf16[32,1728]{1,0:T(8,128)(2,1)S(1)} %get-tuple-element.39), channel_id=1, source_target_pairs={{0,16},{4,20},{8,24},{12,28},{16,0},{20,4},{24,8},{28,12},{1,17},{... | collective-permute-start | bytes 331784 | tf_op jit(solution)/shard_map/ppermute | solution.py:177
  24.7 0.8 %collective-permute-start.8 = (bf16[32,1728]{1,0:T(8,128)(2,1)S(1)}, bf16[32,1728]{1,0:T(8,128)(2,1)S(1)}, u32[]{:S(2)}, u32[]{:S(2)}) collective-permute-start(bf16[32,1728]{1,0:T(8,128)(2,1)S(1)} %get-tuple-element.40), channel_id=1, source_target_pairs={{0,8},{4,12},{8,0},{12,4},{16,24},{20,28},{24,16},{28,20},{1,9},{5... | collective-permute-start | bytes 331784 | tf_op jit(solution)/shard_map/ppermute | solution.py:177
  25.6 2.5 %collective-permute-start.9 = (bf16[32,1728]{1,0:T(8,128)(2,1)S(1)}, bf16[32,1728]{1,0:T(8,128)(2,1)S(1)}, u32[]{:S(2)}, u32[]{:S(2)}) collective-permute-start(bf16[32,1728]{1,0:T(8,128)(2,1)S(1)} %get-tuple-element.41), channel_id=1, source_target_pairs={{0,24},{4,28},{8,16},{12,20},{16,8},{20,12},{24,0},{28,4},{1,25},{... | collective-permute-start | bytes 331784 | tf_op jit(solution)/shard_map/ppermute | solution.py:177
  28.1 0.0 collective-permute-done.6.came
  28.1 0.7 %shard_map.65 = bf16[256,256]{1,0:T(8,128)(2,1)} custom-call(f32[256,256]{1,0:T(8,128)S(1)} %get-tuple-element.36.kept, bf16[256,256]{1,0:T(8,128)(2,1)S(1)} %collective-permute-done.6.came), custom_call_target="tpu_custom_call" | custom-call | tf_op jit(solution)/shard_map/pallas_call | solution.py:276
  28.8 6.7 %collective-permute-done.7.rest_0_ = bf16[32,1728]{1,0:T(8,128)(2,1)S(1)} collective-permute-done((bf16[32,1728]{1,0:T(8,128)(2,1)S(1)}, bf16[32,1728]{1,0:T(8,128)(2,1)S(1)}, u32[]{:S(2)}, u32[]{:S(2)}) %collective-permute-start.7) | collective-permute-done | bytes 110624 | tf_op jit(solution)/shard_map/ppermute | solution.py:177
  35.5 0.0 collective-permute-done.8.rest_1_
  35.5 0.0 collective-permute-done.9.rest_2_
  35.5 1.4 %shard_map.66 = f32[27,32,64]{2,1,0:T(8,128)} custom-call(s32[2]{0:T(128)S(1)} %pad_add_fusion.place, f32[32,1728]{1,0:T(8,128)S(1)} %get-tuple-element.34.kept, bf16[32,1728]{1,0:T(8,128)(2,1)S(1)} %collective-permute-done.7.rest_0_, bf16[32,1728]{1,0:T(8,128)(2,1)S(1)} %collective-permute-done.8.rest_1_, bf16[32,1728]{1,0:T(8,128)(2,1)S(1)} %collective-permute-done.9.rest_2_), custom_call_target="tpu_custom_call" | custom-call | tf_op jit(solution)/shard_map/pallas_call | solution.py:280
  (1 shorter events, 0.0 us)
Async XLA Ops:
  0.6 14.7 %copy-start = (bf16[27,64,256]{2,1,0:T(8,128)(2,1)S(1)}, bf16[27,64,256]{2,1,0:T(8,128)(2,1)}, u32[]{:S(2)}) copy-start(bf16[27,64,256]{2,1,0:T(8,128)(2,1)} %weight.1) | copy-start | bytes 2654212
  1.8 14.1 %collective-permute-start = (bf16[64,1024]{1,0:T(8,128)(2,1)S(1)}, bf16[64,1024]{1,0:T(8,128)(2,1)S(1)}, u32[]{:S(2)}, u32[]{:S(2)}) collective-permute-start(bf16[64,1024]{1,0:T(8,128)(2,1)S(1)} %fusion.7.own), channel_id=1, source_target_pairs={{0,4},{4,0},{8,12},{12,8},{16,20},{20,16},{24,28},{28,24},{1,5},{5... | collective-permute-start | bytes 393224 | tf_op jit(solution)/shard_map/ppermute | solution.py:177
  4.8 11.1 %collective-permute-start.1 = (bf16[64,1024]{1,0:T(8,128)(2,1)S(1)}, bf16[64,1024]{1,0:T(8,128)(2,1)S(1)}, u32[]{:S(2)}, u32[]{:S(2)}) collective-permute-start(bf16[64,1024]{1,0:T(8,128)(2,1)S(1)} %fusion.7.own), channel_id=1, source_target_pairs={{4,8},{12,16},{20,24},{8,4},{16,12},{24,20},{5,9},{13,17},{21,25},... | collective-permute-start | bytes 393224 | tf_op jit(solution)/shard_map/ppermute | solution.py:214
  5.5 13.4 %collective-permute-start.5 = (bf16[64,1024]{1,0:T(8,128)(2,1)S(1)}, bf16[64,1024]{1,0:T(8,128)(2,1)S(1)}, u32[]{:S(2)}, u32[]{:S(2)}) collective-permute-start(bf16[64,1024]{1,0:T(8,128)(2,1)S(1)} %fusion.7.own), channel_id=1, source_target_pairs={{8,0},{16,8},{24,16},{4,12},{12,20},{20,28},{9,1},{17,9},{25,17},{... | collective-permute-start | bytes 393224 | tf_op jit(solution)/shard_map/ppermute | solution.py:223
  6.9 1.0 %copy-start.1 = (bf16[1,32,32,256]{3,2,1,0:T(8,128)(2,1)S(1)}, bf16[1,32,32,256]{3,2,1,0:T(8,128)(2,1)}, u32[]{:S(2)}) copy-start(bf16[1,32,32,256]{3,2,1,0:T(8,128)(2,1)} %param.4) | copy-start | bytes 1572868
  8.8 9.6 %collective-permute-start.3 = (bf16[64,1024]{1,0:T(8,128)(2,1)S(1)}, bf16[64,1024]{1,0:T(8,128)(2,1)S(1)}, u32[]{:S(2)}, u32[]{:S(2)}) collective-permute-start(bf16[64,1024]{1,0:T(8,128)(2,1)S(1)} %get-tuple-element.27), channel_id=1, source_target_pairs={{0,4},{4,0},{8,12},{12,8},{16,20},{20,16},{24,28},{28,24},{1,5},{5... | collective-permute-start | bytes 393224 | tf_op jit(solution)/shard_map/ppermute | solution.py:177
  18.3 3.8 %collective-permute-start.2 = (bf16[512,256]{1,0:T(8,128)(2,1)S(1)}, bf16[512,256]{1,0:T(8,128)(2,1)S(1)}, u32[]{:S(2)}, u32[]{:S(2)}) collective-permute-start(bf16[512,256]{1,0:T(8,128)(2,1)S(1)} %get-tuple-element.26), channel_id=1, source_target_pairs={{0,1},{1,0},{2,3},{3,2},{4,5},{5,4},{6,7},{7,6},{8,9},{9,8},{10,11... | collective-permute-start | bytes 786440 | tf_op jit(solution)/shard_map/ppermute | solution.py:177
  18.4 2.1 %collective-permute-start.4 = (bf16[64,1024]{1,0:T(8,128)(2,1)S(1)}, bf16[64,1024]{1,0:T(8,128)(2,1)S(1)}, u32[]{:S(2)}, u32[]{:S(2)}) collective-permute-start(bf16[64,1024]{1,0:T(8,128)(2,1)S(1)} %collective-permute-done.3.came), channel_id=1, source_target_pairs={{0,1},{1,0},{2,3},{3,2},{4,5},{5,4},{6,7},{7,6},{8,9},{9,8},{10,11... | collective-permute-start | bytes 393224 | tf_op jit(solution)/shard_map/ppermute | solution.py:177
  22.1 6.0 %collective-permute-start.6 = (bf16[256,256]{1,0:T(8,128)(2,1)S(1)}, bf16[256,256]{1,0:T(8,128)(2,1)S(1)}, u32[]{:S(2)}, u32[]{:S(2)}) collective-permute-start(bf16[256,256]{1,0:T(8,128)(2,1)S(1)} %get-tuple-element.37), channel_id=1, source_target_pairs={{0,2},{1,3},{2,0},{3,1},{4,6},{5,7},{6,4},{7,5},{8,10},{9,11},{10,... | collective-permute-start | bytes 393224 | tf_op jit(solution)/shard_map/ppermute | solution.py:177
  23.7 11.8 %collective-permute-start.7 = (bf16[32,1728]{1,0:T(8,128)(2,1)S(1)}, bf16[32,1728]{1,0:T(8,128)(2,1)S(1)}, u32[]{:S(2)}, u32[]{:S(2)}) collective-permute-start(bf16[32,1728]{1,0:T(8,128)(2,1)S(1)} %get-tuple-element.39), channel_id=1, source_target_pairs={{0,16},{4,20},{8,24},{12,28},{16,0},{20,4},{24,8},{28,12},{1,17},{... | collective-permute-start | bytes 331784 | tf_op jit(solution)/shard_map/ppermute | solution.py:177
  24.7 10.8 %collective-permute-start.8 = (bf16[32,1728]{1,0:T(8,128)(2,1)S(1)}, bf16[32,1728]{1,0:T(8,128)(2,1)S(1)}, u32[]{:S(2)}, u32[]{:S(2)}) collective-permute-start(bf16[32,1728]{1,0:T(8,128)(2,1)S(1)} %get-tuple-element.40), channel_id=1, source_target_pairs={{0,8},{4,12},{8,0},{12,4},{16,24},{20,28},{24,16},{28,20},{1,9},{5... | collective-permute-start | bytes 331784 | tf_op jit(solution)/shard_map/ppermute | solution.py:177
  25.6 10.0 %collective-permute-start.9 = (bf16[32,1728]{1,0:T(8,128)(2,1)S(1)}, bf16[32,1728]{1,0:T(8,128)(2,1)S(1)}, u32[]{:S(2)}, u32[]{:S(2)}) collective-permute-start(bf16[32,1728]{1,0:T(8,128)(2,1)S(1)} %get-tuple-element.41), channel_id=1, source_target_pairs={{0,24},{4,28},{8,16},{12,20},{16,8},{20,12},{24,0},{28,4},{1,25},{... | collective-permute-start | bytes 331784 | tf_op jit(solution)/shard_map/ppermute | solution.py:177

commit v4 on v3

v4 whole, which is shorter than its diff:
```python
import functools

import jax
import jax.numpy as jnp
from jax import lax
from jax.experimental import pallas as pl
from jax.experimental.pallas import tpu as pltpu
from jax.sharding import PartitionSpec as P

MIB = 1 << 20
FIRST = 60
VMEM = pl.BlockSpec(memory_space=pltpu.VMEM)


def silu_grad(values):
    sig = jax.nn.sigmoid(values)
    return sig * (1.0 + values * (1.0 - sig))


def bits_of(count):
    return count.bit_length() - 1


def reversed_bits(value, width):
    return sum(((value >> bit) & 1) << (width - 1 - bit) for bit in range(width))


def call(kernel, outs, scratch=(), flops=0, bytes_accessed=0, limit=24):
    return functools.partial(
        pl.pallas_call,
        kernel,
        out_shape=outs,
        scratch_shapes=scratch,
        compiler_params=pltpu.CompilerParams(vmem_limit_bytes=limit * MIB),
        cost_estimate=pl.CostEstimate(flops=flops, bytes_accessed=bytes_accessed, transcendentals=0),
    )


def lay_windows(width, first, second, windows, tall):
    filt, cells = first.shape
    lanes = 2 * filt
    tall[pl.ds(8, cells), :] = jnp.concatenate([first, second], axis=0).astype(jnp.float32).T
    row = lax.broadcasted_iota(jnp.int32, (cells, lanes), 0)
    column = row & (width - 1) if width & (width - 1) == 0 else lax.rem(row, width)
    zero_rows = jnp.zeros((width, windows.shape[1]), jnp.bfloat16)
    windows[pl.ds(0, width), :] = zero_rows
    windows[pl.ds(width + cells, width), :] = zero_rows
    body = pl.ds(width, cells)
    windows[body, 0:lanes] = jnp.where(column != width - 1, tall[pl.ds(9, cells), :], 0.0).astype(jnp.bfloat16)
    windows[body, lanes : 2 * lanes] = tall[pl.ds(8, cells), :].astype(jnp.bfloat16)
    windows[body, 2 * lanes : 3 * lanes] = jnp.where(column != 0, tall[pl.ds(7, cells), :], 0.0).astype(jnp.bfloat16)


def first_kernel(blocks, out_grad, pre_act, inputs, mine, sent, grads, acts, cells_in, loaded):
    cells, chans = inputs.shape
    rows = chans // blocks
    filt = out_grad.shape[0]
    half, part = mine.shape[0], sent.shape[0] - filt
    step = cells // 4
    copies = [pltpu.make_async_copy(out_grad, grads, loaded.at[0]), pltpu.make_async_copy(pre_act, acts, loaded.at[1])]
    for number in range(4):
        rung = pl.ds(number * step, step)
        copies.append(pltpu.make_async_copy(inputs.at[rung, :], cells_in.at[rung, :], loaded.at[2 + number]))
    for copy in copies:
        copy.start()
    count = bits_of(blocks)
    order = lax.broadcasted_iota(jnp.int32, (half + part, chans), 0)
    order = order + jnp.where(order >= half, (lax.axis_index("filt") & 1) * part, 0)
    block = lax.axis_index("space") ^ reversed_bits(order >> bits_of(rows), count)
    source = (block << bits_of(rows)) | (order & (rows - 1))
    picked = (lax.broadcasted_iota(jnp.int32, (half + part, chans), 1) == source).astype(jnp.bfloat16)
    copies[0].wait()
    copies[1].wait()
    d_pre = grads[...].astype(jnp.float32) * silu_grad(acts[...].astype(jnp.float32))
    sent[0:filt, :] = d_pre.astype(sent.dtype)
    for number in range(4):
        copies[2 + number].wait()
        rung = pl.ds(number * step, step)
        turned = lax.dot_general(
            picked, cells_in[rung, :], (((1,), (1,)), ((), ())), preferred_element_type=jnp.float32
        ).astype(jnp.bfloat16)
        mine[:, rung] = turned[0:half, :]
        sent[filt:, rung] = turned[half:, :]


def order_kernel(weight, ordered):
    filt = weight.shape[1]
    odd = lax.axis_index("space") & 1
    zero = jnp.zeros(weight.shape[1:], jnp.bfloat16)
    for tap in range(9):
        b, c = divmod(tap, 3)
        rows = (weight[9 + tap], weight[18 * odd + tap], weight[18 - 18 * odd + tap], zero)
        for slot, value in zip((2 * c, 2 * c + 1, 2 * c + 6, 2 * c + 7), rows):
            ordered[b, pl.ds(slot * filt, filt), :] = value


def near_kernel(width, sent, came, mine, two_off, ordered, pair, twos, first, spread, tall):
    filt, cells = two_off.shape
    wide = pair.shape[1]
    lay_windows(width, two_off[...], two_off[...], twos, tall)
    lay_windows(width, sent[0:filt, :], came[0:filt, :], pair, tall)
    total = 0.0
    for b in range(3):
        rows = pl.ds((2 - b) * width, cells)
        first[:, b * wide : (b + 1) * wide] = jnp.dot(mine[...], pair[rows, :], preferred_element_type=jnp.float32)
        total = total + jnp.dot(pair[rows, :], ordered[b, 0:wide, :], preferred_element_type=jnp.float32)
    spread[...] = total


def one_kernel(width, one_off, mine, ones, second, tall):
    cells = mine.shape[1]
    wide = ones.shape[1]
    lay_windows(width, one_off[...], one_off[...], ones, tall)
    for b in range(3):
        rows = pl.ds((2 - b) * width, cells)
        second[:, b * wide : (b + 1) * wide] = jnp.dot(mine[...], ones[rows, :], preferred_element_type=jnp.float32)


def theirs_kernel(width, came, other, pair, twos, first, second, keep, *sends):
    half = first.shape[0]
    cells = came.shape[1]
    wide = pair.shape[1]
    lanes = wide // 3
    filt = lanes // 2
    first_core = lax.axis_index("filt") & 1 == 0
    here = came[filt:, :]
    theirs = jnp.concatenate(
        [jnp.where(first_core, here, other[...]), jnp.where(first_core, other[...], here)], axis=0
    )
    left = lax.broadcasted_iota(jnp.int32, (half, lanes), 1) < filt
    part = half // (len(sends) + 1)

    def store(lo, hi, value):
        keep[:, lo:hi] = value[0:part, :]
        for number, send in enumerate(sends, 1):
            send[:, lo:hi] = value[number * part : (number + 1) * part, :].astype(jnp.bfloat16)

    for b in range(3):
        rows = pl.ds((2 - b) * width, cells)
        near_terms = jnp.dot(theirs, pair[rows, :], preferred_element_type=jnp.float32)
        far_terms = jnp.dot(theirs, twos[rows, :], preferred_element_type=jnp.float32)
        for c in range(3):
            tap = 3 * b + c
            cut = slice(c * lanes, (c + 1) * lanes)
            lo = b * wide + c * lanes
            crossed = jnp.where(left, pltpu.roll(near_terms[:, cut], filt, 1), far_terms[:, cut])
            store(lo, lo + lanes, first[:, lo : lo + lanes] + crossed)
            outer = second[:, lo : lo + lanes] + near_terms[:, cut]
            lo = 3 * wide + tap // 2 * lanes
            if tap == 8:
                store(lo, lo + filt, outer[:, 0:filt])
            elif tap % 2 == 0:
                before = outer
            else:
                store(lo, lo + lanes, jnp.where(left, before, pltpu.roll(outer, filt, 1)))


def spread_kernel(width, ones, ordered, spread, send):
    cells = spread.shape[0]
    wide = ones.shape[1]
    total = spread[...]
    for b in range(3):
        window = ones[pl.ds((2 - b) * width, cells), :]
        total = total + jnp.dot(window, ordered[b, wide:, :], preferred_element_type=jnp.float32)
    send[...] = total.astype(jnp.bfloat16).reshape(send.shape)


def last_input_kernel(came, out):
    total = came[0].astype(jnp.float32)
    for number in range(1, came.shape[0]):
        total = total + came[number].astype(jnp.float32)
    out[...] = total.astype(out.dtype)


def last_weight_kernel(scale, filt, kept, *rest):
    *came, out = rest
    odd = lax.axis_index("space") & 1
    total = kept[...]
    for piece in came:
        total = total + piece[...].astype(jnp.float32)
    total = total * scale
    for tap in range(9):
        slots = ((2 * tap, 9 + tap), (2 * tap + 1, 18 * odd + tap), (18 + tap, 18 - 18 * odd + tap))
        for slot, target in slots:
            out[target] = total[:, slot * filt : (slot + 1) * filt]


def swapped(value, axis, distance):
    count = lax.axis_size(axis)
    return lax.ppermute(value, axis, [(i, i ^ distance) for i in range(count)])


def after(value, other):
    return lax.optimization_barrier((value, other))[0]


def on_device(inputs, out_grad, pre_act, weight):
    _, height, width, chans = inputs.shape
    taps, filt, _ = weight.shape
    cells = height * width
    blocks, groups = lax.axis_size("space"), lax.axis_size("filt")
    half, quarter = chans // 2, chans // 4
    bf16, f32 = jnp.bfloat16, jnp.float32
    shape = jax.ShapeDtypeStruct
    flops = 2 * cells * taps * filt * chans
    lanes = 6 * filt
    windows_shape = shape((cells + 2 * width, lanes), bf16)
    tall = pltpu.VMEM((cells + 16, 2 * filt), f32)

    mine, sent = call(
        functools.partial(first_kernel, blocks),
        (shape((half, cells), bf16), shape((filt + quarter, cells), bf16)),
        (
            pltpu.VMEM((filt, cells), bf16),
            pltpu.VMEM((filt, cells), bf16),
            pltpu.VMEM((cells, chans), bf16),
            pltpu.SemaphoreType.DMA((6,)),
        ),
        bytes_accessed=MIB,
        limit=FIRST,
    )(in_specs=[pl.BlockSpec(memory_space=pl.ANY)] * 3, out_specs=[VMEM] * 2)(
        out_grad[0], pre_act[0], inputs.reshape(cells, chans)
    )
    came = swapped(sent, "space", 1)
    own = sent[0:filt]
    two_pairs = [(i, i - 2) for i in range(2, blocks, 2)] + [(i, i + 2) for i in range(1, blocks - 2, 2)]
    two_off = lax.ppermute(own, "space", two_pairs)
    one_pairs = [(i, i + 1) for i in range(1, blocks - 1, 2)]
    one_off = lax.ppermute(own, "space", one_pairs + [(target, source) for source, target in one_pairs])
    other = swapped(came[filt:], "filt", 1)

    ordered = call(order_kernel, shape((3, 2 * lanes, chans), bf16), bytes_accessed=MIB)(
        in_specs=[VMEM], out_specs=VMEM
    )(after(weight, mine))
    pair, twos, first, spread = call(
        functools.partial(near_kernel, width),
        (windows_shape, windows_shape, shape((half, 3 * lanes), f32), shape((cells, chans), f32)),
        (tall,),
        flops=flops,
        bytes_accessed=4 * MIB,
    )(in_specs=[VMEM] * 5, out_specs=[VMEM] * 4)(sent, came, mine, two_off, ordered)
    ones, second = call(
        functools.partial(one_kernel, width),
        (windows_shape, shape((half, 3 * lanes), f32)),
        (tall,),
        flops=flops // 2,
        bytes_accessed=2 * MIB,
    )(in_specs=[VMEM] * 2, out_specs=[VMEM] * 2)(one_off, after(mine, first))
    radix = min(4, blocks // 2)
    piece = half // radix
    kept, *sends = call(
        functools.partial(theirs_kernel, width),
        (shape((piece, taps * filt), f32),) + (shape((piece, taps * filt), bf16),) * (radix - 1),
        flops=flops,
        bytes_accessed=4 * MIB,
    )(in_specs=[VMEM] * 6, out_specs=[VMEM] * radix)(came, other, pair, twos, first, second)
    sent_in = call(
        functools.partial(spread_kernel, width),
        shape((groups, cells // groups, chans), bf16),
        flops=flops // 3,
        bytes_accessed=4 * MIB,
    )(in_specs=[VMEM] * 3, out_specs=VMEM)(ones, ordered, spread)
    came_in = lax.all_to_all(sent_in, "filt", 0, 0, tiled=True)

    distance = 2
    while True:
        spans = {2: (1,), 4: (2, 1, 3)}[radix]
        arrived = [swapped(sends[n - 1], "space", spans[n - 1] * distance) for n in range(1, radix)]
        distance *= radix
        if distance >= blocks:
            break
        total = kept
        for part in arrived:
            total = total + part.astype(f32)
        radix = min(4, blocks // distance)
        piece //= radix
        kept, *sends = (total[n * piece : (n + 1) * piece] for n in range(radix))
        sends = [value.astype(bf16) for value in sends]

    grad_scale = float(cells * blocks) ** (-0.5)
    grad_weight = call(
        functools.partial(last_weight_kernel, grad_scale, filt), shape((taps, chans // blocks, filt), f32)
    )(in_specs=[VMEM] * (len(arrived) + 1), out_specs=VMEM)(kept, *arrived)
    grad_input = call(last_input_kernel, shape((cells // groups, chans), bf16))(in_specs=[VMEM], out_specs=VMEM)(came_in)
    return grad_input.reshape(1, height // groups, width, chans), jnp.transpose(grad_weight, (1, 0, 2))


def solution(mesh):
    placed = (
        P("space", None, None, None),
        P("space", "filt", None),
        P("space", "filt", None),
        P(None, "filt", None),
    )
    return jax.shard_map(
        on_device,
        mesh=mesh,
        in_specs=placed,
        out_specs=(P("space", "filt", None, None), P("space", None, "filt")),
        check_vma=False,
    )
```

time: 37.2 us -> 42.6 us (1.15)
  waiting for transfers between devices: 6.75 us -> 14 us
  starting transfers between devices: 18 us -> 14.7 us
  local copies, waits for them, and re-layouts: 1.05 us -> 2.85 us
  other arithmetic: 1.24 us -> 0 us
  Pallas kernels: 9.13 us -> 9.76 us
    ppermute x8 -> x5, starting transfers between devices: 16.1 us -> 9.31 us  [swapped(): return lax.ppermute(value, axis, [(i, i ^ distance) for i in range(count)])]
    ppermute x1, waiting for transfers between devices: 0.01 us -> 4.79 us  [on_device(): two_off = lax.ppermute(own, 'space', two_pairs)]
    all_to_all x0 -> x1, starting transfers between devices: none -> 3.47 us  [on_device(): came_in = lax.all_to_all(sent_in, 'filt', 0, 0, tiled=True)]
    ppermute x8 -> x5, waiting for transfers between devices: 6.74 us -> 9.19 us  [swapped(): return lax.ppermute(value, axis, [(i, i ^ distance) for i in range(count)])]
    pallas_call x5, Pallas kernels: 6.4 us -> 8.07 us  [the longest x1 2.88 us: on_device(): call(functools.partial(first_kernel, blocks), (shape((half, cells), bf16)...]
    squeeze x1 -> x0, other arithmetic: 1.16 us -> none  [on_device(): (out_grad.astype(f32) * silu_grad(pre_act.astype(f32))).astype(bf16)[0]]
    slice x0 -> x2, local copies, waits for them, and re-layouts: none -> 0.96 us  [the longest x1 0.95 us: on_device(): own = sent[0:filt]]
    unnamed x4 -> x10, local copies, waits for them, and re-layouts: 1.05 us -> 1.9 us
  transfers between devices with their start and end apart: 10 -> 8, of which waited for: 1 -> 4; matrix products, arithmetic and copies ran while one was open for 0% -> 2% of each run, Pallas kernels for 21% -> 9%
where the time goes in v4:
time: 42.6 us; the launch traced here: 42.1 us
  starting transfers between devices  14.7 us (35%)
  waiting for transfers between devices  14 us (33%)
  Pallas kernels  9.76 us (23%)
  local copies, waits for them, and re-layouts  2.85 us (7%)
  between operations  0.76 us (2%)
    ppermute x5, starting transfers between devices, swapped(): return lax.ppermute(value, axis, [(i, i ^ distance) for i in range(count)])  9.31 us
    ppermute x5, waiting for transfers between devices, swapped(): return lax.ppermute(value, axis, [(i, i ^ distance) for i in range(count)])  9.19 us
    ppermute x1, waiting for transfers between devices, on_device(): two_off = lax.ppermute(own, 'space', two_pairs)  4.79 us
    all_to_all x1, starting transfers between devices, on_device(): came_in = lax.all_to_all(sent_in, 'filt', 0, 0, tiled=True)  3.47 us
    pallas_call x1, Pallas kernels, on_device(): call(functools.partial(first_kernel, blocks), (shape((half, cells), bf16)...  2.88 us
    unnamed x10, local copies, waits for them, and re-layouts  1.9 us
    pallas_call x1, Pallas kernels, on_device(): call(functools.partial(spread_kernel, width), shape((groups, cells // gro...  1.76 us
    pallas_call x1, Pallas kernels, on_device(): call(functools.partial(near_kernel, width), (windows_shape, windows_shape...  1.71 us
  transfers between devices with their start and end apart: 8, of which 4 were waited for; matrix products, arithmetic and copies ran while one was open for 2% of the time, Pallas kernels for 9%

profile of v4, /device:TPU:0, one launch (start us, length us, event | category | flops | bytes accessed | tf_op | source)
XLA Modules:
  0.0 42.1 jit_solution(10993608122761052847)
XLA Ops:
  0.6 0.0 copy-start
  0.6 2.9 %shard_map.59 = (bf16[128,1024]{1,0:T(8,128)(2,1)}, bf16[128,1024]{1,0:T(8,128)(2,1)}) custom-call(bf16[64,1024]{1,0:T(8,128)(2,1)} %bitcast.8, bf16[64,1024]{1,0:T(8,128)(2,1)} %bitcast.9, bf16[1024,256]{1,0:T(8,128)(2,1)} %bitcast.5), custom_call_target="tpu_custom_call" | custom-call | bytes 1048576 | tf_op jit(solution)/shard_map/pallas_call | solution.py:210
  3.5 0.0 copy-start.1
  3.5 0.0 copy-start.2
  3.5 3.0 %collective-permute-start.1 = (bf16[128,1024]{1,0:T(8,128)(2,1)}, bf16[128,1024]{1,0:T(8,128)(2,1)S(1)}, u32[]{:S(2)}, u32[]{:S(2)}) collective-permute-start(bf16[128,1024]{1,0:T(8,128)(2,1)} %get-tuple-element.16.sent), channel_id=1, source_target_pairs={{0,4},{4,0},{8,12},{12,8},{16,20},{20,16},{24,28},{28,24},{1,5},{5... | collective-permute-start | bytes 786440 | tf_op jit(solution)/shard_map/ppermute | solution.py:190
  6.6 0.9 %slice.6 = bf16[64,1024]{1,0:T(8,128)(2,1)S(1)} slice(bf16[128,1024]{1,0:T(8,128)(2,1)} %get-tuple-element.16.sent), slice={[0:64], [0:1024]} | slice | bytes 262144 | tf_op jit(solution)/shard_map/slice | solution.py:225
  7.5 1.3 %collective-permute-start.2 = (bf16[64,1024]{1,0:T(8,128)(2,1)S(1)}, bf16[64,1024]{1,0:T(8,128)(2,1)S(1)}, u32[]{:S(2)}, u32[]{:S(2)}) collective-permute-start(bf16[64,1024]{1,0:T(8,128)(2,1)S(1)} %slice.6), channel_id=1, source_target_pairs={{8,0},{16,8},{24,16},{4,12},{12,20},{20,28},{9,1},{17,9},{25,17},{... | collective-permute-start | bytes 393224 | tf_op jit(solution)/shard_map/ppermute | solution.py:227
  8.8 0.7 %collective-permute-start = (bf16[64,1024]{1,0:T(8,128)(2,1)S(1)}, bf16[64,1024]{1,0:T(8,128)(2,1)S(1)}, u32[]{:S(2)}, u32[]{:S(2)}) collective-permute-start(bf16[64,1024]{1,0:T(8,128)(2,1)S(1)} %slice.6), channel_id=1, source_target_pairs={{4,8},{12,16},{20,24},{8,4},{16,12},{24,20},{5,9},{13,17},{21,25},... | collective-permute-start | bytes 393224 | tf_op jit(solution)/shard_map/ppermute | solution.py:229
  9.5 0.0 copy-done
  9.5 0.1 shard_map.60.ordered
  9.6 4.8 %collective-permute-done.2.two_off = bf16[64,1024]{1,0:T(8,128)(2,1)S(1)} collective-permute-done((bf16[64,1024]{1,0:T(8,128)(2,1)S(1)}, bf16[64,1024]{1,0:T(8,128)(2,1)S(1)}, u32[]{:S(2)}, u32[]{:S(2)}) %collective-permute-start.2) | collective-permute-done | bytes 131104 | tf_op jit(solution)/shard_map/ppermute | solution.py:227
  14.4 0.0 collective-permute-done.1.came
  14.4 0.0 copy-done.1
  14.4 0.0 copy-done.2
  14.4 1.7 %shard_map.61 = (bf16[1088,384]{1,0:T(8,128)(2,1)S(1)}, bf16[1088,384]{1,0:T(8,128)(2,1)S(1)}, f32[128,1152]{1,0:T(8,128)S(1)}, f32[1024,256]{1,0:T(8,128)S(1)}) custom-call(bf16[128,1024]{1,0:T(8,128)(2,1)S(1)} %copy-done.1, bf16[128,1024]{1,0:T(8,128)(2,1)S(1)} %collective-permute-done.1.came, bf16[128,1024]{1,0:T(8,128)(2,1)S(1)} %copy-done.2, ...), custom_call_target="tpu_custom_call" | custom-call | flops 905969664 | bytes 4194304 | tf_op jit(solution)/shard_map/pallas_call | solution.py:235
  16.1 0.0 collective-permute-done.one_off
  16.1 0.7 %shard_map.62 = (bf16[1088,384]{1,0:T(8,128)(2,1)S(1)}, f32[128,1152]{1,0:T(8,128)S(1)}) custom-call(bf16[64,1024]{1,0:T(8,128)(2,1)S(1)} %collective-permute-done.one_off, bf16[128,1024]{1,0:T(8,128)(2,1)S(1)} %copy-done.2), custom_call_target="tpu_custom_call" | custom-call | flops 452984832 | bytes 2097152 | tf_op jit(solution)/shard_map/pallas_call | solution.py:242
  16.9 0.0 copy-start.3
  16.9 0.8 %copy-done.3 = f32[128,1152]{1,0:T(8,128)} copy-done((f32[128,1152]{1,0:T(8,128)}, f32[128,1152]{1,0:T(8,128)S(1)}, u32[]{:S(2)}) %copy-start.3) | copy-done | bytes 589848
  17.7 1.8 %shard_map.63 = bf16[4,256,256]{2,1,0:T(8,128)(2,1)} custom-call(bf16[1088,384]{1,0:T(8,128)(2,1)S(1)} %get-tuple-element.21.ones, bf16[3,768,256]{2,1,0:T(8,128)(2,1)S(1)} %shard_map.60.ordered, f32[1024,256]{1,0:T(8,128)S(1)} %get-tuple-element.22.spread), custom_call_target="tpu_custom_call" | custom-call | flops 301989888 | bytes 4194304 | tf_op jit(solution)/shard_map/pallas_call | solution.py:257
  19.4 3.5 %all-to-all-start = ((bf16[4,256,256]{2,1,0:T(8,128)(2,1)}), bf16[4,256,256]{2,1,0:T(8,128)(2,1)S(1)}, u32[]{:S(2)}, u32[]{:S(2)}) async-start(bf16[4,256,256]{2,1,0:T(8,128)(2,1)} %shard_map.63), calls=%async_computation | async-start | bytes 1048576 | tf_op jit(solution)/shard_map/all_to_all | solution.py:263
  22.9 0.5 %collective-permute-start.3 = (bf16[64,1024]{1,0:T(8,128)(2,1)S(1)}, bf16[64,1024]{1,0:T(8,128)(2,1)S(1)}, u32[]{:S(2)}, u32[]{:S(2)}) collective-permute-start(bf16[64,1024]{1,0:T(8,128)(2,1)S(1)} %slice.8), channel_id=1, source_target_pairs={{0,1},{1,0},{2,3},{3,2},{4,5},{5,4},{6,7},{7,6},{8,9},{9,8},{10,11... | collective-permute-start | bytes 393224 | tf_op jit(solution)/shard_map/ppermute | solution.py:190
  23.5 1.0 %collective-permute-done.3.other = bf16[64,1024]{1,0:T(8,128)(2,1)S(1)} collective-permute-done((bf16[64,1024]{1,0:T(8,128)(2,1)S(1)}, bf16[64,1024]{1,0:T(8,128)(2,1)S(1)}, u32[]{:S(2)}, u32[]{:S(2)}) %collective-permute-start.3) | collective-permute-done | bytes 131104 | tf_op jit(solution)/shard_map/ppermute | solution.py:190
  24.4 0.0 copy-start.4
  24.5 1.1 %copy-done.4 = f32[128,1152]{1,0:T(8,128)S(1)} copy-done((f32[128,1152]{1,0:T(8,128)S(1)}, f32[128,1152]{1,0:T(8,128)}, u32[]{:S(2)}) %copy-start.4) | copy-done | bytes 589848
  25.5 1.0 %shard_map.65 = (f32[32,1728]{1,0:T(8,128)S(1)}, bf16[32,1728]{1,0:T(8,128)(2,1)S(1)}, bf16[32,1728]{1,0:T(8,128)(2,1)S(1)}, bf16[32,1728]{1,0:T(8,128)(2,1)S(1)}) custom-call(bf16[128,1024]{1,0:T(8,128)(2,1)S(1)} %collective-permute-done.1.came, bf16[64,1024]{1,0:T(8,128)(2,1)S(1)} %collective-permute-done.3.other, ...), custom_call_target="tpu_custom_call" | custom-call | flops 905969664 | bytes 4194304 | tf_op jit(solution)/shard_map/pallas_call | solution.py:251
  26.5 4.2 %collective-permute-start.4 = (bf16[32,1728]{1,0:T(8,128)(2,1)S(1)}, bf16[32,1728]{1,0:T(8,128)(2,1)S(1)}, u32[]{:S(2)}, u32[]{:S(2)}) collective-permute-start(bf16[32,1728]{1,0:T(8,128)(2,1)S(1)} %get-tuple-element.27), channel_id=1, source_target_pairs={{0,16},{4,20},{8,24},{12,28},{16,0},{20,4},{24,8},{28,12},{1,17},{... | collective-permute-start | bytes 331784 | tf_op jit(solution)/shard_map/ppermute | solution.py:190
  30.7 1.6 %collective-permute-start.5 = (bf16[32,1728]{1,0:T(8,128)(2,1)S(1)}, bf16[32,1728]{1,0:T(8,128)(2,1)S(1)}, u32[]{:S(2)}, u32[]{:S(2)}) collective-permute-start(bf16[32,1728]{1,0:T(8,128)(2,1)S(1)} %get-tuple-element.28), channel_id=1, source_target_pairs={{0,8},{4,12},{8,0},{12,4},{16,24},{20,28},{24,16},{28,20},{1,9},{5... | collective-permute-start | bytes 331784 | tf_op jit(solution)/shard_map/ppermute | solution.py:190
  32.3 0.0 collective-permute-start.6
  32.3 4.9 %collective-permute-done.4.rest_0_ = bf16[32,1728]{1,0:T(8,128)(2,1)S(1)} collective-permute-done((bf16[32,1728]{1,0:T(8,128)(2,1)S(1)}, bf16[32,1728]{1,0:T(8,128)(2,1)S(1)}, u32[]{:S(2)}, u32[]{:S(2)}) %collective-permute-start.4) | collective-permute-done | bytes 110624 | tf_op jit(solution)/shard_map/ppermute | solution.py:190
  37.1 0.0 collective-permute-done.5.rest_1_
  37.1 3.3 %collective-permute-done.6.rest_2_ = bf16[32,1728]{1,0:T(8,128)(2,1)S(1)} collective-permute-done((bf16[32,1728]{1,0:T(8,128)(2,1)S(1)}, bf16[32,1728]{1,0:T(8,128)(2,1)S(1)}, u32[]{:S(2)}, u32[]{:S(2)}) %collective-permute-start.6) | collective-permute-done | bytes 110624 | tf_op jit(solution)/shard_map/ppermute | solution.py:190
  40.5 0.9 %shard_map.66 = f32[27,32,64]{2,1,0:T(8,128)} custom-call(f32[32,1728]{1,0:T(8,128)S(1)} %get-tuple-element.26.kept, bf16[32,1728]{1,0:T(8,128)(2,1)S(1)} %collective-permute-done.4.rest_0_, bf16[32,1728]{1,0:T(8,128)(2,1)S(1)} %collective-permute-done.5.rest_1_, bf16[32,1728]{1,0:T(8,128)(2,1)S(1)} %collective-permute-done.6.rest_2_), custom_call_target="tpu_custom_call" | custom-call | tf_op jit(solution)/shard_map/pallas_call | solution.py:281
  41.4 0.0 all-to-all-done.came
  41.4 0.7 %shard_map.64 = bf16[256,256]{1,0:T(8,128)(2,1)} custom-call(bf16[4,256,256]{2,1,0:T(8,128)(2,1)S(1)} %all-to-all-done.came), custom_call_target="tpu_custom_call" | custom-call | tf_op jit(solution)/shard_map/pallas_call | solution.py:284
  (1 shorter events, 0.0 us)
Async XLA Ops:
  0.6 8.9 %copy-start = (bf16[27,64,256]{2,1,0:T(8,128)(2,1)S(1)}, bf16[27,64,256]{2,1,0:T(8,128)(2,1)}, u32[]{:S(2)}) copy-start(bf16[27,64,256]{2,1,0:T(8,128)(2,1)} %weight) | copy-start | bytes 2654212
  3.5 10.8 %copy-start.1 = (bf16[128,1024]{1,0:T(8,128)(2,1)S(1)}, bf16[128,1024]{1,0:T(8,128)(2,1)}, u32[]{:S(2)}) copy-start(bf16[128,1024]{1,0:T(8,128)(2,1)} %get-tuple-element.16.sent) | copy-start | bytes 786436
  3.5 10.8 %copy-start.2 = (bf16[128,1024]{1,0:T(8,128)(2,1)S(1)}, bf16[128,1024]{1,0:T(8,128)(2,1)}, u32[]{:S(2)}) copy-start(bf16[128,1024]{1,0:T(8,128)(2,1)} %get-tuple-element.20.mine) | copy-start | bytes 786436
  3.5 10.8 %collective-permute-start.1 = (bf16[128,1024]{1,0:T(8,128)(2,1)}, bf16[128,1024]{1,0:T(8,128)(2,1)S(1)}, u32[]{:S(2)}, u32[]{:S(2)}) collective-permute-start(bf16[128,1024]{1,0:T(8,128)(2,1)} %get-tuple-element.16.sent), channel_id=1, source_target_pairs={{0,4},{4,0},{8,12},{12,8},{16,20},{20,16},{24,28},{28,24},{1,5},{5... | collective-permute-start | bytes 786440 | tf_op jit(solution)/shard_map/ppermute | solution.py:190
  7.5 6.9 %collective-permute-start.2 = (bf16[64,1024]{1,0:T(8,128)(2,1)S(1)}, bf16[64,1024]{1,0:T(8,128)(2,1)S(1)}, u32[]{:S(2)}, u32[]{:S(2)}) collective-permute-start(bf16[64,1024]{1,0:T(8,128)(2,1)S(1)} %slice.6), channel_id=1, source_target_pairs={{8,0},{16,8},{24,16},{4,12},{12,20},{20,28},{9,1},{17,9},{25,17},{... | collective-permute-start | bytes 393224 | tf_op jit(solution)/shard_map/ppermute | solution.py:227
  8.8 7.3 %collective-permute-start = (bf16[64,1024]{1,0:T(8,128)(2,1)S(1)}, bf16[64,1024]{1,0:T(8,128)(2,1)S(1)}, u32[]{:S(2)}, u32[]{:S(2)}) collective-permute-start(bf16[64,1024]{1,0:T(8,128)(2,1)S(1)} %slice.6), channel_id=1, source_target_pairs={{4,8},{12,16},{20,24},{8,4},{16,12},{24,20},{5,9},{13,17},{21,25},... | collective-permute-start | bytes 393224 | tf_op jit(solution)/shard_map/ppermute | solution.py:229
  16.9 0.8 %copy-start.3 = (f32[128,1152]{1,0:T(8,128)}, f32[128,1152]{1,0:T(8,128)S(1)}, u32[]{:S(2)}) copy-start(f32[128,1152]{1,0:T(8,128)S(1)} %get-tuple-element.25.second) | copy-start | bytes 1769476
  19.4 21.9 %all-to-all-start = ((bf16[4,256,256]{2,1,0:T(8,128)(2,1)}), bf16[4,256,256]{2,1,0:T(8,128)(2,1)S(1)}, u32[]{:S(2)}, u32[]{:S(2)}) async-start(bf16[4,256,256]{2,1,0:T(8,128)(2,1)} %shard_map.63), calls=%async_computation | async-start | bytes 1048576 | tf_op jit(solution)/shard_map/all_to_all | solution.py:263
  22.9 1.5 %collective-permute-start.3 = (bf16[64,1024]{1,0:T(8,128)(2,1)S(1)}, bf16[64,1024]{1,0:T(8,128)(2,1)S(1)}, u32[]{:S(2)}, u32[]{:S(2)}) collective-permute-start(bf16[64,1024]{1,0:T(8,128)(2,1)S(1)} %slice.8), channel_id=1, source_target_pairs={{0,1},{1,0},{2,3},{3,2},{4,5},{5,4},{6,7},{7,6},{8,9},{9,8},{10,11... | collective-permute-start | bytes 393224 | tf_op jit(solution)/shard_map/ppermute | solution.py:190
  24.4 1.1 %copy-start.4 = (f32[128,1152]{1,0:T(8,128)S(1)}, f32[128,1152]{1,0:T(8,128)}, u32[]{:S(2)}) copy-start(f32[128,1152]{1,0:T(8,128)} %copy-done.3) | copy-start | bytes 1769476
  26.5 10.6 %collective-permute-start.4 = (bf16[32,1728]{1,0:T(8,128)(2,1)S(1)}, bf16[32,1728]{1,0:T(8,128)(2,1)S(1)}, u32[]{:S(2)}, u32[]{:S(2)}) collective-permute-start(bf16[32,1728]{1,0:T(8,128)(2,1)S(1)} %get-tuple-element.27), channel_id=1, source_target_pairs={{0,16},{4,20},{8,24},{12,28},{16,0},{20,4},{24,8},{28,12},{1,17},{... | collective-permute-start | bytes 331784 | tf_op jit(solution)/shard_map/ppermute | solution.py:190
  30.7 6.4 %collective-permute-start.5 = (bf16[32,1728]{1,0:T(8,128)(2,1)S(1)}, bf16[32,1728]{1,0:T(8,128)(2,1)S(1)}, u32[]{:S(2)}, u32[]{:S(2)}) collective-permute-start(bf16[32,1728]{1,0:T(8,128)(2,1)S(1)} %get-tuple-element.28), channel_id=1, source_target_pairs={{0,8},{4,12},{8,0},{12,4},{16,24},{20,28},{24,16},{28,20},{1,9},{5... | collective-permute-start | bytes 331784 | tf_op jit(solution)/shard_map/ppermute | solution.py:190
  32.3 8.2 %collective-permute-start.6 = (bf16[32,1728]{1,0:T(8,128)(2,1)S(1)}, bf16[32,1728]{1,0:T(8,128)(2,1)S(1)}, u32[]{:S(2)}, u32[]{:S(2)}) collective-permute-start(bf16[32,1728]{1,0:T(8,128)(2,1)S(1)} %get-tuple-element.29), channel_id=1, source_target_pairs={{0,24},{4,28},{8,16},{12,20},{16,8},{20,12},{24,0},{28,4},{1,25},{... | collective-permute-start | bytes 331784 | tf_op jit(solution)/shard_map/ppermute | solution.py:190

commit v5 on v3

v5 whole, which is shorter than its diff:
```python
import functools

import jax
import jax.numpy as jnp
from jax import lax
from jax.experimental import pallas as pl
from jax.experimental.pallas import tpu as pltpu
from jax.sharding import PartitionSpec as P

MIB = 1 << 20
VMEM = pl.BlockSpec(memory_space=pltpu.VMEM)


def silu_grad(values):
    sig = jax.nn.sigmoid(values)
    return sig * (1.0 + values * (1.0 - sig))


def bits_of(count):
    return count.bit_length() - 1


def reversed_bits(value, width):
    return sum(((value >> bit) & 1) << (width - 1 - bit) for bit in range(width))


def call(kernel, outs, scratch=(), flops=0, bytes_accessed=0, limit=24):
    return functools.partial(
        pl.pallas_call,
        kernel,
        out_shape=outs,
        scratch_shapes=scratch,
        compiler_params=pltpu.CompilerParams(vmem_limit_bytes=limit * MIB),
        cost_estimate=pl.CostEstimate(flops=flops, bytes_accessed=bytes_accessed, transcendentals=0),
    )


def lay_windows(width, first, second, windows, tall):
    filt, cells = first.shape
    lanes = 2 * filt
    tall[pl.ds(8, cells), :] = jnp.concatenate([first, second], axis=0).astype(jnp.float32).T
    row = lax.broadcasted_iota(jnp.int32, (cells, lanes), 0)
    column = row & (width - 1) if width & (width - 1) == 0 else lax.rem(row, width)
    zero_rows = jnp.zeros((width, windows.shape[1]), jnp.bfloat16)
    windows[pl.ds(0, width), :] = zero_rows
    windows[pl.ds(width + cells, width), :] = zero_rows
    body = pl.ds(width, cells)
    windows[body, 0:lanes] = jnp.where(column != width - 1, tall[pl.ds(9, cells), :], 0.0).astype(jnp.bfloat16)
    windows[body, lanes : 2 * lanes] = tall[pl.ds(8, cells), :].astype(jnp.bfloat16)
    windows[body, 2 * lanes : 3 * lanes] = jnp.where(column != 0, tall[pl.ds(7, cells), :], 0.0).astype(jnp.bfloat16)


def turn_kernel(blocks, inputs, mine, part):
    chans = inputs.shape[1]
    rows = chans // blocks
    half, quarter = mine.shape[0], part.shape[0]
    order = lax.broadcasted_iota(jnp.int32, (half + quarter, chans), 0)
    other_half = order >= half
    row = order + jnp.where(other_half, (lax.axis_index("filt") & 1) * quarter - half, 0)
    side = (lax.axis_index("space") & 1) ^ other_half.astype(jnp.int32)
    source = (2 * (row >> bits_of(rows)) + side) * rows + (row & (rows - 1))
    picked = (lax.broadcasted_iota(jnp.int32, (half + quarter, chans), 1) == source).astype(jnp.bfloat16)
    turned = lax.dot_general(picked, inputs[...], (((1,), (1,)), ((), ())), preferred_element_type=jnp.float32)
    turned = turned.astype(jnp.bfloat16)
    mine[...] = turned[0:half, :]
    part[...] = turned[half:, :]


def order_kernel(weight, ordered):
    filt = weight.shape[1]
    odd = lax.axis_index("space") & 1
    zero = jnp.zeros(weight.shape[1:], jnp.bfloat16)
    for tap in range(9):
        b, c = divmod(tap, 3)
        rows = (weight[9 + tap], weight[18 * odd + tap], weight[18 - 18 * odd + tap], zero)
        for slot, value in zip((2 * c, 2 * c + 1, 2 * c + 6, 2 * c + 7), rows):
            ordered[b, pl.ds(slot * filt, filt), :] = value


def near_kernel(width, own, came, mine, ordered, pair, first, spread, tall):
    filt, cells = own.shape
    wide = pair.shape[1]
    lay_windows(width, own[...], came[0:filt, :], pair, tall)
    total = 0.0
    for b in range(3):
        rows = pl.ds((2 - b) * width, cells)
        first[:, b * wide : (b + 1) * wide] = jnp.dot(mine[...], pair[rows, :], preferred_element_type=jnp.float32)
        total = total + jnp.dot(pair[rows, :], ordered[b, 0:wide, :], preferred_element_type=jnp.float32)
    spread[...] = total


def outer_kernel(width, two_off, mine, ones, twos, second, tall):
    cells = mine.shape[1]
    wide = ones.shape[1]
    lay_windows(width, two_off[...], two_off[...], twos, tall)
    for b in range(3):
        rows = pl.ds((2 - b) * width, cells)
        second[:, b * wide : (b + 1) * wide] = jnp.dot(mine[...], ones[rows, :], preferred_element_type=jnp.float32)


def theirs_kernel(width, came, other, pair, twos, first, second, send):
    half = first.shape[0]
    cells = came.shape[1]
    wide = pair.shape[1]
    lanes = wide // 3
    filt = lanes // 2
    first_core = lax.axis_index("filt") & 1 == 0
    here = came[filt:, :]
    theirs = jnp.concatenate(
        [jnp.where(first_core, here, other[...]), jnp.where(first_core, other[...], here)], axis=0
    )
    left = lax.broadcasted_iota(jnp.int32, (half, lanes), 1) < filt

    def store(lo, hi, value):
        send[:, lo:hi] = value.astype(jnp.bfloat16)

    for b in range(3):
        rows = pl.ds((2 - b) * width, cells)
        near_terms = jnp.dot(theirs, pair[rows, :], preferred_element_type=jnp.float32)
        far_terms = jnp.dot(theirs, twos[rows, :], preferred_element_type=jnp.float32)
        for c in range(3):
            tap = 3 * b + c
            cut = slice(c * lanes, (c + 1) * lanes)
            lo = b * wide + c * lanes
            crossed = jnp.where(left, pltpu.roll(near_terms[:, cut], filt, 1), far_terms[:, cut])
            store(lo, lo + lanes, first[:, lo : lo + lanes] + crossed)
            outer = second[:, lo : lo + lanes] + near_terms[:, cut]
            lo = 3 * wide + tap // 2 * lanes
            if tap == 8:
                store(lo, lo + filt, outer[:, 0:filt])
            elif tap % 2 == 0:
                before = outer
            else:
                store(lo, lo + lanes, jnp.where(left, before, pltpu.roll(outer, filt, 1)))


def spread_kernel(width, groups, one_off, ordered, spread, ones, keep, send, tall):
    cells = spread.shape[0]
    wide = ones.shape[1]
    lay_windows(width, one_off[...], one_off[...], ones, tall)
    part = cells // groups
    index = lax.axis_index("filt")
    count = bits_of(groups)
    for target in reversed(range(groups)):
        block = 0
        for bit in range(count):
            differs = (target >> (count - 1 - bit)) & 1
            block = block + (((index >> bit) & 1) ^ differs) * (1 << bit)
        start = pl.multiple_of(block * part, part)
        total = spread[pl.ds(start, part), :]
        for b in range(3):
            rows = pl.ds(pl.multiple_of(start + (2 - b) * width, width), part)
            total = total + jnp.dot(ones[rows, :], ordered[b, wide:, :], preferred_element_type=jnp.float32)
        if target < groups // 2:
            keep[pl.ds(target * part, part), :] = total
        else:
            send[pl.ds((target - groups // 2) * part, part), :] = total.astype(jnp.bfloat16)


def halve_kernel(kept, came, keep, send):
    half = keep.shape[0]
    keep[...] = kept[0:half, :] + came[0:half, :].astype(jnp.float32)
    send[...] = (kept[half:, :] + came[half:, :].astype(jnp.float32)).astype(jnp.bfloat16)


def last_input_kernel(kept, came, out):
    out[...] = (kept[...] + came[...].astype(jnp.float32)).astype(out.dtype)


def last_weight_kernel(scale, filt, came, out):
    odd = lax.axis_index("space") & 1
    total = came[0].astype(jnp.float32)
    for number in range(1, came.shape[0]):
        total = total + came[number].astype(jnp.float32)
    total = total * scale
    for tap in range(9):
        slots = ((2 * tap, 9 + tap), (2 * tap + 1, 18 * odd + tap), (18 + tap, 18 - 18 * odd + tap))
        for slot, target in slots:
            out[target] = total[:, slot * filt : (slot + 1) * filt]


def swapped(value, axis, distance):
    count = lax.axis_size(axis)
    return lax.ppermute(value, axis, [(i, i ^ distance) for i in range(count)])


def halved(kept, came):
    rows, lanes = kept.shape
    if rows // 2 % 16:
        total = kept + came.astype(jnp.float32)
        return total[: rows // 2], total[rows // 2 :].astype(jnp.bfloat16)
    outs = (
        jax.ShapeDtypeStruct((rows // 2, lanes), jnp.float32),
        jax.ShapeDtypeStruct((rows // 2, lanes), jnp.bfloat16),
    )
    return call(halve_kernel, outs, flops=rows * lanes, bytes_accessed=9 * rows * lanes)(
        in_specs=[VMEM] * 2, out_specs=[VMEM] * 2
    )(kept, came)


def after(value, other):
    return lax.optimization_barrier((value, other))[0]


def on_device(inputs, out_grad, pre_act, weight):
    _, height, width, chans = inputs.shape
    taps, filt, _ = weight.shape
    cells = height * width
    blocks, groups = lax.axis_size("space"), lax.axis_size("filt")
    half, quarter = chans // 2, chans // 4
    bf16, f32 = jnp.bfloat16, jnp.float32
    shape = jax.ShapeDtypeStruct
    flops = 2 * cells * taps * filt * chans
    lanes = 6 * filt
    windows_shape = shape((cells + 2 * width, lanes), bf16)
    tall = pltpu.VMEM((cells + 16, 2 * filt), f32)

    mine, part = call(
        functools.partial(turn_kernel, blocks),
        (shape((half, cells), bf16), shape((quarter, cells), bf16)),
        bytes_accessed=MIB,
    )(in_specs=[VMEM], out_specs=[VMEM] * 2)(inputs.reshape(cells, chans))
    own = (out_grad[0].astype(f32) * silu_grad(pre_act[0].astype(f32))).astype(bf16)
    sent = jnp.concatenate([own, part], axis=0)
    came = swapped(sent, "space", 1)
    two_pairs = [(i, i - 2) for i in range(2, blocks, 2)] + [(i, i + 2) for i in range(1, blocks - 2, 2)]
    two_off = lax.ppermute(own, "space", two_pairs)
    one_pairs = [(i, i + 1) for i in range(1, blocks - 1, 2)]
    one_off = lax.ppermute(own, "space", one_pairs + [(target, source) for source, target in one_pairs])
    other = swapped(came[filt:], "filt", 1)

    ordered = call(order_kernel, shape((3, 2 * lanes, chans), bf16), bytes_accessed=MIB)(
        in_specs=[VMEM], out_specs=VMEM
    )(after(weight, mine))
    pair, first, spread = call(
        functools.partial(near_kernel, width),
        (windows_shape, shape((half, 3 * lanes), f32), shape((cells, chans), f32)),
        (tall,),
        flops=flops,
        bytes_accessed=4 * MIB,
    )(in_specs=[VMEM] * 4, out_specs=[VMEM] * 3)(own, came, mine, ordered)
    ones, kept_in, sent_in = call(
        functools.partial(spread_kernel, width, groups),
        (windows_shape, shape((cells // 2, chans), f32), shape((cells // 2, chans), bf16)),
        (tall,),
        flops=flops // 3,
        bytes_accessed=4 * MIB,
    )(in_specs=[VMEM] * 3, out_specs=[VMEM] * 3)(one_off, ordered, spread)
    came_in = swapped(sent_in, "filt", 1)
    twos, second = call(
        functools.partial(outer_kernel, width),
        (windows_shape, shape((half, 3 * lanes), f32)),
        (tall,),
        flops=4 * flops,
        bytes_accessed=2 * MIB,
    )(in_specs=[VMEM] * 3, out_specs=[VMEM] * 2)(two_off, mine, ones)
    terms = call(
        functools.partial(theirs_kernel, width),
        shape((half, taps * filt), bf16),
        flops=4 * flops,
        bytes_accessed=4 * MIB,
    )(in_specs=[VMEM] * 6, out_specs=VMEM)(came, other, pair, twos, first, second)
    members = [list(range(side, blocks, 2)) for side in range(2)]
    pieces = lax.all_to_all(
        terms.reshape(blocks // 2, chans // blocks, taps * filt), "space", 0, 0, axis_index_groups=members, tiled=True
    )
    came_in = after(came_in, terms)
    distance_in = 2
    while distance_in < groups:
        kept_in, sent_in = halved(kept_in, came_in)
        came_in = swapped(sent_in, "filt", distance_in)
        distance_in *= 2
    grad_input = call(last_input_kernel, shape((cells // groups, chans), bf16))(
        in_specs=[VMEM] * 2, out_specs=VMEM
    )(kept_in, came_in)
    grad_scale = float(cells * blocks) ** (-0.5)
    grad_weight = call(
        functools.partial(last_weight_kernel, grad_scale, filt), shape((taps, chans // blocks, filt), f32)
    )(in_specs=[VMEM], out_specs=VMEM)(after(pieces, grad_input))
    return grad_input.reshape(1, height // groups, width, chans), jnp.transpose(grad_weight, (1, 0, 2))


def solution(mesh):
    placed = (
        P("space", None, None, None),
        P("space", "filt", None),
        P("space", "filt", None),
        P(None, "filt", None),
    )
    return jax.shard_map(
        on_device,
        mesh=mesh,
        in_specs=placed,
        out_specs=(P("space", "filt", None, None), P("space", None, "filt")),
        check_vma=False,
    )
```

time: 37.2 us -> 40.6 us (1.091)
  waiting for transfers between devices: 6.75 us -> 17.5 us
  starting transfers between devices: 18 us -> 12.7 us
  Pallas kernels: 9.13 us -> 7.2 us
    ppermute x8 -> x4, starting transfers between devices: 16.1 us -> 4.88 us  [swapped(): return lax.ppermute(value, axis, [(i, i ^ distance) for i in range(count)])]
    all_to_all x0 -> x1, starting transfers between devices: none -> 5.86 us  [on_device(): lax.all_to_all(terms.reshape(blocks // 2, chans // blocks, taps * filt),...]
    all_to_all x0 -> x1, waiting for transfers between devices: none -> 5.8 us  [on_device(): lax.all_to_all(terms.reshape(blocks // 2, chans // blocks, taps * filt),...]
    ppermute x8 -> x4, waiting for transfers between devices: 6.74 us -> 11.7 us  [swapped(): return lax.ppermute(value, axis, [(i, i ^ distance) for i in range(count)])]
    squeeze x1 -> x0, other arithmetic: 1.16 us -> none  [on_device(): (out_grad.astype(f32) * silu_grad(pre_act.astype(f32))).astype(bf16)[0]]
    convert_element_type x0 -> x1, other arithmetic: none -> 1.08 us  [on_device(): (out_grad[0].astype(f32) * silu_grad(pre_act[0].astype(f32))).astype(bf16)]
    pallas_call x1, Pallas kernels: 1.44 us -> 0.89 us  [on_device(): call(functools.partial(last_weight_kernel, grad_scale, filt), shape((taps...]
    pallas_call x1, Pallas kernels: 0.62 us -> 0.08 us  [on_device(): call(order_kernel, shape((3, 2 * lanes, chans), bf16), bytes_accessed=MIB)]
  transfers between devices with their start and end apart: 10 -> 7, of which waited for: 1 -> 4; matrix products, arithmetic and copies ran while one was open for 0% -> 0% of each run, Pallas kernels for 21% -> 10%
where the time goes in v5:
time: 40.6 us; the launch traced here: 40.4 us
  waiting for transfers between devices  17.5 us (43%)
  starting transfers between devices  12.7 us (31%)
  Pallas kernels  7.2 us (18%)
  local copies, waits for them, and re-layouts  1.13 us (3%)
  other arithmetic  1.1 us (3%)
  between operations  0.76 us (2%)
    ppermute x4, waiting for transfers between devices, swapped(): return lax.ppermute(value, axis, [(i, i ^ distance) for i in range(count)])  11.7 us
    all_to_all x1, starting transfers between devices, on_device(): lax.all_to_all(terms.reshape(blocks // 2, chans // blocks, taps * filt),...  5.86 us
    all_to_all x1, waiting for transfers between devices, on_device(): lax.all_to_all(terms.reshape(blocks // 2, chans // blocks, taps * filt),...  5.8 us
    ppermute x4, starting transfers between devices, swapped(): return lax.ppermute(value, axis, [(i, i ^ distance) for i in range(count)])  4.88 us
    pallas_call x1, Pallas kernels, on_device(): call(functools.partial(theirs_kernel, width), shape((half, taps * filt),...  1.76 us
    pallas_call x1, Pallas kernels, on_device(): call(functools.partial(near_kernel, width), (windows_shape, shape((half,...  1.56 us
    ppermute x1, starting transfers between devices, on_device(): two_off = lax.ppermute(own, 'space', two_pairs)  1.29 us
    pallas_call x1, Pallas kernels, on_device(): call(functools.partial(spread_kernel, width, groups), (windows_shape, sha...  1.23 us
  transfers between devices with their start and end apart: 7, of which 4 were waited for; matrix products, arithmetic and copies ran while one was open for 0% of the time, Pallas kernels for 10%

profile of v5, /device:TPU:0, one launch (start us, length us, event | category | flops | bytes accessed | tf_op | source)
XLA Modules:
  0.0 40.4 jit_solution(3769258650275193265)
XLA Ops:
  0.6 0.0 copy-start
  0.6 0.0 copy-start.1
  0.6 1.1 %copy-done.1 = bf16[1,32,32,256]{3,2,1,0:T(8,128)(2,1)S(1)} copy-done((bf16[1,32,32,256]{3,2,1,0:T(8,128)(2,1)S(1)}, bf16[1,32,32,256]{3,2,1,0:T(8,128)(2,1)}, u32[]{:S(2)}) %copy-start.1) | copy-done | bytes 524312
  1.8 0.3 shard_map.59
  2.1 1.1 %fusion.6.own = bf16[64,1024]{1,0:T(8,128)(2,1)S(1)} fusion(bf16[1,64,1024]{2,1,0:T(8,128)(2,1)} %param.5, bf16[1,64,1024]{2,1,0:T(8,128)(2,1)} %param.6), kind=kLoop, calls=%fused_computation.8 | loop fusion | flops 720896 | bytes 393216 | tf_op jit(solution)/shard_map/convert_element_type | solution.py:223
  3.2 3.0 %collective-permute-start.1 = (bf16[128,1024]{1,0:T(8,128)(2,1)S(1)}, bf16[128,1024]{1,0:T(8,128)(2,1)S(1)}, u32[]{:S(2)}, u32[]{:S(2)}) collective-permute-start(bf16[128,1024]{1,0:T(8,128)(2,1)S(1)} %pad_maximum_fusion), channel_id=1, source_target_pairs={{0,4},{4,0},{8,12},{12,8},{16,20},{20,16},{24,28},{28,24},{1,5},{5... | collective-permute-start | bytes 786440 | tf_op jit(solution)/shard_map/ppermute | solution.py:184
  6.2 0.7 %collective-permute-start = (bf16[64,1024]{1,0:T(8,128)(2,1)S(1)}, bf16[64,1024]{1,0:T(8,128)(2,1)S(1)}, u32[]{:S(2)}, u32[]{:S(2)}) collective-permute-start(bf16[64,1024]{1,0:T(8,128)(2,1)S(1)} %fusion.6.own), channel_id=1, source_target_pairs={{4,8},{12,16},{20,24},{8,4},{16,12},{24,20},{5,9},{13,17},{21,25},... | collective-permute-start | bytes 393224 | tf_op jit(solution)/shard_map/ppermute | solution.py:229
  6.9 1.3 %collective-permute-start.4 = (bf16[64,1024]{1,0:T(8,128)(2,1)S(1)}, bf16[64,1024]{1,0:T(8,128)(2,1)S(1)}, u32[]{:S(2)}, u32[]{:S(2)}) collective-permute-start(bf16[64,1024]{1,0:T(8,128)(2,1)S(1)} %fusion.6.own), channel_id=1, source_target_pairs={{8,0},{16,8},{24,16},{4,12},{12,20},{20,28},{9,1},{17,9},{25,17},{... | collective-permute-start | bytes 393224 | tf_op jit(solution)/shard_map/ppermute | solution.py:227
  8.2 0.0 copy-done
  8.2 0.1 shard_map.60.ordered
  8.3 6.3 %collective-permute-done.1.came = bf16[128,1024]{1,0:T(8,128)(2,1)S(1)} collective-permute-done((bf16[128,1024]{1,0:T(8,128)(2,1)S(1)}, bf16[128,1024]{1,0:T(8,128)(2,1)S(1)}, u32[]{:S(2)}, u32[]{:S(2)}) %collective-permute-start.1) | collective-permute-done | bytes 262176 | tf_op jit(solution)/shard_map/ppermute | solution.py:184
  14.6 0.1 collective-permute-start.3
  14.7 1.6 %shard_map.61 = (bf16[1088,384]{1,0:T(8,128)(2,1)S(1)}, f32[128,1152]{1,0:T(8,128)S(1)}, f32[1024,256]{1,0:T(8,128)S(1)}) custom-call(bf16[64,1024]{1,0:T(8,128)(2,1)S(1)} %fusion.6.own, bf16[128,1024]{1,0:T(8,128)(2,1)S(1)} %collective-permute-done.1.came, bf16[128,1024]{1,0:T(8,128)(2,1)S(1)} %get-tuple-element.17.mine, ...), custom_call_target="tpu_custom_call" | custom-call | flops 905969664 | bytes 4194304 | tf_op jit(solution)/shard_map/pallas_call | solution.py:235
  16.2 0.0 collective-permute-done.one_off
  16.3 1.2 %shard_map.62 = (bf16[1088,384]{1,0:T(8,128)(2,1)S(1)}, f32[512,256]{1,0:T(8,128)S(1)}, bf16[512,256]{1,0:T(8,128)(2,1)S(1)}) custom-call(bf16[64,1024]{1,0:T(8,128)(2,1)S(1)} %collective-permute-done.one_off, bf16[3,768,256]{2,1,0:T(8,128)(2,1)S(1)} %shard_map.60.ordered, f32[1024,256]{1,0:T(8,128)S(1)} %get-tuple-element.20.spread), custom_call_target="tpu_custom_call" | custom-call | flops 301989888 | bytes 4194304 | tf_op jit(solution)/shard_map/pallas_call | solution.py:242
  17.5 0.0 collective-permute-done.4.two_off
  17.5 0.6 %shard_map.63 = (bf16[1088,384]{1,0:T(8,128)(2,1)S(1)}, f32[128,1152]{1,0:T(8,128)S(1)}) custom-call(bf16[64,1024]{1,0:T(8,128)(2,1)S(1)} %collective-permute-done.4.two_off, bf16[128,1024]{1,0:T(8,128)(2,1)S(1)} %get-tuple-element.17.mine, bf16[1088,384]{1,0:T(8,128)(2,1)S(1)} %get-tuple-element.24.ones), custom_call_target="tpu_custom_call" | custom-call | flops 3623878656 | bytes 2097152 | tf_op jit(solution)/shard_map/pallas_call | solution.py:250
  18.1 0.0 collective-permute-done.3.other
  18.1 1.8 %shard_map.64 = bf16[128,1728]{1,0:T(8,128)(2,1)} custom-call(bf16[128,1024]{1,0:T(8,128)(2,1)S(1)} %collective-permute-done.1.came, bf16[64,1024]{1,0:T(8,128)(2,1)S(1)} %collective-permute-done.3.other, bf16[1088,384]{1,0:T(8,128)(2,1)S(1)} %get-tuple-element.23.pair, bf16[1088,384]{1,0:T(8,128)(2,1)S(1)} %get-tuple-element.25.twos, ...), custom_call_target="tpu_custom_call" | custom-call | flops 3623878656 | bytes 4194304 | tf_op jit(solution)/shard_map/pallas_call | solution.py:257
  19.9 5.9 %all-to-all-start = ((bf16[4,32,1728]{2,1,0:T(8,128)(2,1)}), bf16[4,32,1728]{2,1,0:T(8,128)(2,1)S(1)}, u32[]{:S(2)}, u32[]{:S(2)}) async-start(bf16[4,32,1728]{2,1,0:T(8,128)(2,1)} %bitcast.5), calls=%async_computation | async-start | bytes 917504 | tf_op jit(solution)/shard_map/all_to_all | solution.py:264
  25.8 0.2 collective-permute-start.2
  26.0 1.3 %collective-permute-done.2.came = bf16[512,256]{1,0:T(8,128)(2,1)S(1)} collective-permute-done((bf16[512,256]{1,0:T(8,128)(2,1)S(1)}, bf16[512,256]{1,0:T(8,128)(2,1)S(1)}, u32[]{:S(2)}, u32[]{:S(2)}) %collective-permute-start.2) | collective-permute-done | bytes 262176 | tf_op jit(solution)/shard_map/ppermute | solution.py:184
  27.3 1.6 %collective-permute-start.5 = (bf16[256,256]{1,0:T(8,128)(2,1)S(1)}, bf16[256,256]{1,0:T(8,128)(2,1)S(1)}, u32[]{:S(2)}, u32[]{:S(2)}) collective-permute-start(bf16[256,256]{1,0:T(8,128)(2,1)S(1)} %get-tuple-element.30), channel_id=1, source_target_pairs={{0,2},{1,3},{2,0},{3,1},{4,6},{5,7},{6,4},{7,5},{8,10},{9,11},{10,... | collective-permute-start | bytes 393224 | tf_op jit(solution)/shard_map/ppermute | solution.py:184
  28.9 4.1 %collective-permute-done.5.came = bf16[256,256]{1,0:T(8,128)(2,1)S(1)} collective-permute-done((bf16[256,256]{1,0:T(8,128)(2,1)S(1)}, bf16[256,256]{1,0:T(8,128)(2,1)S(1)}, u32[]{:S(2)}, u32[]{:S(2)}) %collective-permute-start.5) | collective-permute-done | bytes 131104 | tf_op jit(solution)/shard_map/ppermute | solution.py:184
  33.0 0.7 %shard_map.66 = bf16[256,256]{1,0:T(8,128)(2,1)} custom-call(f32[256,256]{1,0:T(8,128)S(1)} %get-tuple-element.29.kept, bf16[256,256]{1,0:T(8,128)(2,1)S(1)} %collective-permute-done.5.came), custom_call_target="tpu_custom_call" | custom-call | tf_op jit(solution)/shard_map/pallas_call | solution.py:273
  33.7 5.8 %all-to-all-done.came = bf16[4,32,1728]{2,1,0:T(8,128)(2,1)S(1)} async-done(((bf16[4,32,1728]{2,1,0:T(8,128)(2,1)}), bf16[4,32,1728]{2,1,0:T(8,128)(2,1)S(1)}, u32[]{:S(2)}, u32[]{:S(2)}) %all-to-all-start) | async-done | bytes 442400 | tf_op jit(solution)/shard_map/all_to_all | solution.py:264
  39.5 0.9 %shard_map.67 = f32[27,32,64]{2,1,0:T(8,128)} custom-call(bf16[4,32,1728]{2,1,0:T(8,128)(2,1)S(1)} %all-to-all-done.came), custom_call_target="tpu_custom_call" | custom-call | tf_op jit(solution)/shard_map/pallas_call | solution.py:277
  (3 shorter events, 0.1 us)
Async XLA Ops:
  0.6 7.5 %copy-start = (bf16[27,64,256]{2,1,0:T(8,128)(2,1)S(1)}, bf16[27,64,256]{2,1,0:T(8,128)(2,1)}, u32[]{:S(2)}) copy-start(bf16[27,64,256]{2,1,0:T(8,128)(2,1)} %weight) | copy-start | bytes 2654212
  0.6 1.1 %copy-start.1 = (bf16[1,32,32,256]{3,2,1,0:T(8,128)(2,1)S(1)}, bf16[1,32,32,256]{3,2,1,0:T(8,128)(2,1)}, u32[]{:S(2)}) copy-start(bf16[1,32,32,256]{3,2,1,0:T(8,128)(2,1)} %param.4) | copy-start | bytes 1572868
  3.2 11.4 %collective-permute-start.1 = (bf16[128,1024]{1,0:T(8,128)(2,1)S(1)}, bf16[128,1024]{1,0:T(8,128)(2,1)S(1)}, u32[]{:S(2)}, u32[]{:S(2)}) collective-permute-start(bf16[128,1024]{1,0:T(8,128)(2,1)S(1)} %pad_maximum_fusion), channel_id=1, source_target_pairs={{0,4},{4,0},{8,12},{12,8},{16,20},{20,16},{24,28},{28,24},{1,5},{5... | collective-permute-start | bytes 786440 | tf_op jit(solution)/shard_map/ppermute | solution.py:184
  6.2 10.0 %collective-permute-start = (bf16[64,1024]{1,0:T(8,128)(2,1)S(1)}, bf16[64,1024]{1,0:T(8,128)(2,1)S(1)}, u32[]{:S(2)}, u32[]{:S(2)}) collective-permute-start(bf16[64,1024]{1,0:T(8,128)(2,1)S(1)} %fusion.6.own), channel_id=1, source_target_pairs={{4,8},{12,16},{20,24},{8,4},{16,12},{24,20},{5,9},{13,17},{21,25},... | collective-permute-start | bytes 393224 | tf_op jit(solution)/shard_map/ppermute | solution.py:229
  6.9 10.6 %collective-permute-start.4 = (bf16[64,1024]{1,0:T(8,128)(2,1)S(1)}, bf16[64,1024]{1,0:T(8,128)(2,1)S(1)}, u32[]{:S(2)}, u32[]{:S(2)}) collective-permute-start(bf16[64,1024]{1,0:T(8,128)(2,1)S(1)} %fusion.6.own), channel_id=1, source_target_pairs={{8,0},{16,8},{24,16},{4,12},{12,20},{20,28},{9,1},{17,9},{25,17},{... | collective-permute-start | bytes 393224 | tf_op jit(solution)/shard_map/ppermute | solution.py:227
  14.6 3.5 %collective-permute-start.3 = (bf16[64,1024]{1,0:T(8,128)(2,1)S(1)}, bf16[64,1024]{1,0:T(8,128)(2,1)S(1)}, u32[]{:S(2)}, u32[]{:S(2)}) collective-permute-start(bf16[64,1024]{1,0:T(8,128)(2,1)S(1)} %slice.4), channel_id=1, source_target_pairs={{0,1},{1,0},{2,3},{3,2},{4,5},{5,4},{6,7},{7,6},{8,9},{9,8},{10,11... | collective-permute-start | bytes 393224 | tf_op jit(solution)/shard_map/ppermute | solution.py:184
  19.9 19.6 %all-to-all-start = ((bf16[4,32,1728]{2,1,0:T(8,128)(2,1)}), bf16[4,32,1728]{2,1,0:T(8,128)(2,1)S(1)}, u32[]{:S(2)}, u32[]{:S(2)}) async-start(bf16[4,32,1728]{2,1,0:T(8,128)(2,1)} %bitcast.5), calls=%async_computation | async-start | bytes 917504 | tf_op jit(solution)/shard_map/all_to_all | solution.py:264
  25.8 1.5 %collective-permute-start.2 = (bf16[512,256]{1,0:T(8,128)(2,1)S(1)}, bf16[512,256]{1,0:T(8,128)(2,1)S(1)}, u32[]{:S(2)}, u32[]{:S(2)}) collective-permute-start(bf16[512,256]{1,0:T(8,128)(2,1)S(1)} %get-tuple-element.22), channel_id=1, source_target_pairs={{0,1},{1,0},{2,3},{3,2},{4,5},{5,4},{6,7},{7,6},{8,9},{9,8},{10,11... | collective-permute-start | bytes 786440 | tf_op jit(solution)/shard_map/ppermute | solution.py:184
  27.3 5.7 %collective-permute-start.5 = (bf16[256,256]{1,0:T(8,128)(2,1)S(1)}, bf16[256,256]{1,0:T(8,128)(2,1)S(1)}, u32[]{:S(2)}, u32[]{:S(2)}) collective-permute-start(bf16[256,256]{1,0:T(8,128)(2,1)S(1)} %get-tuple-element.30), channel_id=1, source_target_pairs={{0,2},{1,3},{2,0},{3,1},{4,6},{5,7},{6,4},{7,5},{8,10},{9,11},{10,... | collective-permute-start | bytes 393224 | tf_op jit(solution)/shard_map/ppermute | solution.py:184

commit v6 on v3

v6 whole, which is shorter than its diff:
```python
import functools

import jax
import jax.numpy as jnp
from jax import lax
from jax.experimental import pallas as pl
from jax.experimental.pallas import tpu as pltpu
from jax.sharding import PartitionSpec as P

MIB = 1 << 20
EARLY, SPREAD, LATE, FINAL, ORDER = 3, 3, 3, 3, 3
VMEM = pl.BlockSpec(memory_space=pltpu.VMEM)


def silu_grad(values):
    sig = jax.nn.sigmoid(values)
    return sig * (1.0 + values * (1.0 - sig))


def bits_of(count):
    return count.bit_length() - 1


def reversed_bits(value, width):
    return sum(((value >> bit) & 1) << (width - 1 - bit) for bit in range(width))


def call(kernel, outs, scratch=(), flops=0, bytes_accessed=0, limit=24):
    return functools.partial(
        pl.pallas_call,
        kernel,
        out_shape=outs,
        scratch_shapes=scratch,
        compiler_params=pltpu.CompilerParams(vmem_limit_bytes=limit * MIB),
        cost_estimate=pl.CostEstimate(flops=flops, bytes_accessed=bytes_accessed, transcendentals=0),
    )


def lay_windows(width, first, second, windows, tall):
    filt, cells = first.shape
    lanes = 2 * filt
    tall[pl.ds(8, cells), :] = jnp.concatenate([first, second], axis=0).astype(jnp.float32).T
    row = lax.broadcasted_iota(jnp.int32, (cells, lanes), 0)
    column = row & (width - 1) if width & (width - 1) == 0 else lax.rem(row, width)
    zero_rows = jnp.zeros((width, windows.shape[1]), jnp.bfloat16)
    windows[pl.ds(0, width), :] = zero_rows
    windows[pl.ds(width + cells, width), :] = zero_rows
    body = pl.ds(width, cells)
    windows[body, 0:lanes] = jnp.where(column != width - 1, tall[pl.ds(9, cells), :], 0.0).astype(jnp.bfloat16)
    windows[body, lanes : 2 * lanes] = tall[pl.ds(8, cells), :].astype(jnp.bfloat16)
    windows[body, 2 * lanes : 3 * lanes] = jnp.where(column != 0, tall[pl.ds(7, cells), :], 0.0).astype(jnp.bfloat16)


def turn_kernel(blocks, inputs, mine, part):
    chans = inputs.shape[1]
    rows = chans // blocks
    half, quarter = mine.shape[0], part.shape[0]
    count = bits_of(blocks)
    order = lax.broadcasted_iota(jnp.int32, (half + quarter, chans), 0)
    order = order + jnp.where(order >= half, (lax.axis_index("filt") & 1) * quarter, 0)
    block = lax.axis_index("space") ^ reversed_bits(order >> bits_of(rows), count)
    source = (block << bits_of(rows)) | (order & (rows - 1))
    picked = (lax.broadcasted_iota(jnp.int32, (half + quarter, chans), 1) == source).astype(jnp.bfloat16)
    turned = lax.dot_general(picked, inputs[...], (((1,), (1,)), ((), ())), preferred_element_type=jnp.float32)
    turned = turned.astype(jnp.bfloat16)
    mine[...] = turned[0:half, :]
    part[...] = turned[half:, :]


def order_kernel(weight, early, late):
    filt = weight.shape[1]
    odd = lax.axis_index("space") & 1
    for tap in range(9):
        b, c = divmod(tap, 3)
        low, high = pl.ds(2 * c * filt, filt), pl.ds((2 * c + 1) * filt, filt)
        early[b, low, :] = jnp.zeros(weight.shape[1:], jnp.bfloat16)
        early[b, high, :] = weight[9 + tap]
        late[b, low, :] = weight[18 * odd + tap]
        late[b, high, :] = weight[18 - 18 * odd + tap]


def early_kernel(width, own, two_off, mine, came, other, weight, turned, terms, spread, windows, tall):
    cells = own.shape[1]
    half = mine.shape[0]
    wide = windows.shape[1]
    first_core = lax.axis_index("filt") & 1 == 0
    turned[0:half, :] = mine[...]
    turned[half : half + half // 2, :] = jnp.where(first_core, came[...], other[...])
    turned[half + half // 2 :, :] = jnp.where(first_core, other[...], came[...])
    lay_windows(width, two_off[...], own[...], windows, tall)
    total = 0.0
    for b in range(3):
        window = windows[pl.ds((2 - b) * width, cells), :]
        terms[:, b * wide : (b + 1) * wide] = jnp.dot(turned[...], window, preferred_element_type=jnp.float32)
        total = total + jnp.dot(window, weight[b], preferred_element_type=jnp.float32)
    spread[...] = total


def spread_kernel(width, groups, near, one_off, weight, spread, windows, keep, send, tall):
    cells = spread.shape[0]
    lay_windows(width, near[...], one_off[...], windows, tall)
    part = cells // groups
    index = lax.axis_index("filt")
    count = bits_of(groups)
    for target in reversed(range(groups)):
        block = 0
        for bit in range(count):
            differs = (target >> (count - 1 - bit)) & 1
            block = block + (((index >> bit) & 1) ^ differs) * (1 << bit)
        start = pl.multiple_of(block * part, part)
        total = spread[pl.ds(start, part), :]
        for b in range(3):
            rows = pl.ds(pl.multiple_of(start + (2 - b) * width, width), part)
            total = total + jnp.dot(windows[rows, :], weight[b], preferred_element_type=jnp.float32)
        if target < groups // 2:
            keep[pl.ds(target * part, part), :] = total
        else:
            send[pl.ds((target - groups // 2) * part, part), :] = total.astype(jnp.bfloat16)


def late_kernel(width, turned, windows, early, keep, *sends):
    half = turned.shape[0] // 2
    cells = turned.shape[1]
    wide = windows.shape[1]
    lanes = wide // 3
    filt = lanes // 2
    left = lax.broadcasted_iota(jnp.int32, (half, lanes), 1) < filt
    part = half // (len(sends) + 1)

    def store(lo, hi, value):
        keep[:, lo:hi] = value[0:part, :]
        for number, send in enumerate(sends, 1):
            send[:, lo:hi] = value[number * part : (number + 1) * part, :].astype(jnp.bfloat16)

    for b in range(3):
        window = windows[pl.ds((2 - b) * width, cells), :]
        terms = jnp.dot(turned[...], window, preferred_element_type=jnp.float32)
        for c in range(3):
            tap = 3 * b + c
            cut = slice(c * lanes, (c + 1) * lanes)
            lo = b * wide + c * lanes
            store(lo, lo + lanes, terms[0:half, cut] + early[half:, lo : lo + lanes])
            near_side, own_side = terms[half:, cut], early[0:half, lo : lo + lanes]
            lo = 3 * wide + tap // 2 * lanes
            if tap == 8:
                middle = near_side + pltpu.roll(own_side, filt, 1)
                store(lo, lo + filt, middle[:, 0:filt])
            elif tap % 2 == 0:
                before = near_side + pltpu.roll(own_side, filt, 1)
            else:
                store(lo, lo + lanes, jnp.where(left, before, pltpu.roll(near_side, filt, 1) + own_side))


def halve_kernel(kept, came, keep, send):
    half = keep.shape[0]
    keep[...] = kept[0:half, :] + came[0:half, :].astype(jnp.float32)
    send[...] = (kept[half:, :] + came[half:, :].astype(jnp.float32)).astype(jnp.bfloat16)


def last_input_kernel(kept, came, out):
    out[...] = (kept[...] + came[...].astype(jnp.float32)).astype(out.dtype)


def last_weight_kernel(scale, filt, kept, *rest):
    *came, out = rest
    odd = lax.axis_index("space") & 1
    total = kept[...]
    for piece in came:
        total = total + piece[...].astype(jnp.float32)
    total = total * scale
    for tap in range(9):
        slots = ((18 + tap, 9 + tap), (2 * tap, 18 * odd + tap), (2 * tap + 1, 18 - 18 * odd + tap))
        for slot, target in slots:
            out[target] = total[:, slot * filt : (slot + 1) * filt]


def swapped(value, axis, distance):
    count = lax.axis_size(axis)
    return lax.ppermute(value, axis, [(i, i ^ distance) for i in range(count)])


def halved(kept, came):
    rows, lanes = kept.shape
    if rows // 2 % 16:
        total = kept + came.astype(jnp.float32)
        return total[: rows // 2], total[rows // 2 :].astype(jnp.bfloat16)
    outs = (
        jax.ShapeDtypeStruct((rows // 2, lanes), jnp.float32),
        jax.ShapeDtypeStruct((rows // 2, lanes), jnp.bfloat16),
    )
    return call(halve_kernel, outs, flops=rows * lanes, bytes_accessed=9 * rows * lanes)(
        in_specs=[VMEM] * 2, out_specs=[VMEM] * 2
    )(kept, came)


def after(value, other):
    return lax.optimization_barrier((value, other))[0]


def on_device(inputs, out_grad, pre_act, weight):
    _, height, width, chans = inputs.shape
    taps, filt, _ = weight.shape
    cells = height * width
    blocks, groups = lax.axis_size("space"), lax.axis_size("filt")
    half, quarter = chans // 2, chans // 4
    bf16, f32 = jnp.bfloat16, jnp.float32
    shape = jax.ShapeDtypeStruct
    flops = 2 * cells * taps * filt * chans
    lanes = 6 * filt
    windows_shape = shape((cells + 2 * width, lanes), bf16)
    tall = pltpu.VMEM((cells + 16, 2 * filt), f32)

    own = (out_grad[0].astype(f32) * silu_grad(pre_act[0].astype(f32))).astype(bf16)
    mine, part = call(
        functools.partial(turn_kernel, blocks),
        (shape((half, cells), bf16), shape((quarter, cells), bf16)),
        bytes_accessed=MIB,
    )(in_specs=[VMEM], out_specs=[VMEM] * 2)(inputs.reshape(cells, chans))
    came = swapped(part, "space", 1)
    near = swapped(own, "space", 1)
    two_pairs = [(i, i - 2) for i in range(2, blocks, 2)] + [(i, i + 2) for i in range(1, blocks - 2, 2)]
    two_off = lax.ppermute(own, "space", two_pairs)
    one_pairs = [(i, i + 1) for i in range(1, blocks - 1, 2)]
    one_off = lax.ppermute(own, "space", one_pairs + [(target, source) for source, target in one_pairs])
    other = swapped(came, "filt", 1)

    weight_shape = shape((3, lanes, chans), bf16)
    early_weight, late_weight = call(order_kernel, (weight_shape, weight_shape), flops=ORDER * flops, bytes_accessed=MIB)(
        in_specs=[VMEM], out_specs=[VMEM] * 2
    )(after(weight, mine))
    turned, early, spread = call(
        functools.partial(early_kernel, width),
        (shape((chans, cells), bf16), shape((chans, 3 * lanes), f32), shape((cells, chans), f32)),
        (pltpu.VMEM(windows_shape.shape, bf16), tall),
        flops=EARLY * flops,
        bytes_accessed=4 * MIB,
    )(in_specs=[VMEM] * 6, out_specs=[VMEM] * 3)(own, two_off, mine, came, other, early_weight)
    windows, kept_in, sent_in = call(
        functools.partial(spread_kernel, width, groups),
        (windows_shape, shape((cells // 2, chans), f32), shape((cells // 2, chans), bf16)),
        (tall,),
        flops=SPREAD * flops,
        bytes_accessed=4 * MIB,
    )(in_specs=[VMEM] * 4, out_specs=[VMEM] * 3)(near, one_off, late_weight, spread)
    came_in = swapped(sent_in, "filt", 1)
    radix = min(4, blocks // 2)
    piece = half // radix
    kept, *sends = call(
        functools.partial(late_kernel, width),
        (shape((piece, taps * filt), f32),) + (shape((piece, taps * filt), bf16),) * (radix - 1),
        flops=LATE * flops,
        bytes_accessed=4 * MIB,
    )(in_specs=[VMEM] * 3, out_specs=[VMEM] * radix)(turned, windows, early)
    came_in = after(came_in, kept)

    distance = 2
    while True:
        spans = {2: (1,), 4: (2, 1, 3)}[radix]
        arrived = [swapped(sends[n - 1], "space", spans[n - 1] * distance) for n in range(1, radix)]
        distance *= radix
        if distance >= blocks:
            break
        total = kept
        for value in arrived:
            total = total + value.astype(f32)
        radix = min(4, blocks // distance)
        piece //= radix
        kept, *sends = (total[n * piece : (n + 1) * piece] for n in range(radix))
        sends = [value.astype(bf16) for value in sends]

    distance_in = 2
    while distance_in < groups:
        kept_in, sent_in = halved(kept_in, came_in)
        came_in = swapped(sent_in, "filt", distance_in)
        distance_in *= 2
    grad_scale = float(cells * blocks) ** (-0.5)
    grad_weight = call(
        functools.partial(last_weight_kernel, grad_scale, filt),
        shape((taps, chans // blocks, filt), f32),
        flops=FINAL * flops,
    )(in_specs=[VMEM] * (len(arrived) + 1), out_specs=VMEM)(kept, *arrived)
    grad_input = call(last_input_kernel, shape((cells // groups, chans), bf16))(
        in_specs=[VMEM] * 2, out_specs=VMEM
    )(after(kept_in, grad_weight), came_in)
    return grad_input.reshape(1, height // groups, width, chans), jnp.transpose(grad_weight, (1, 0, 2))


def solution(mesh):
    placed = (
        P("space", None, None, None),
        P("space", "filt", None),
        P("space", "filt", None),
        P(None, "filt", None),
    )
    return jax.shard_map(
        on_device,
        mesh=mesh,
        in_specs=placed,
        out_specs=(P("space", "filt", None, None), P("space", None, "filt")),
        check_vma=False,
    )
```

time: 37.2 us -> 35.6 us (0.957)
  Pallas kernels: 9.13 us -> 6.24 us
  waiting for transfers between devices: 6.75 us -> 7.91 us
  local copies, waits for them, and re-layouts: 1.05 us -> 2.2 us
  starting transfers between devices: 18 us -> 17.1 us
    pallas_call x4, Pallas kernels: 6.1 us -> 4.3 us  [the longest x1 1.96 us: on_device(): call(functools.partial(early_kernel, width), (shape((chans, cells), bf16)...]
    ppermute x8, waiting for transfers between devices: 6.74 us -> 7.91 us  [swapped(): return lax.ppermute(value, axis, [(i, i ^ distance) for i in range(count)])]
    squeeze x1 -> x0, other arithmetic: 1.16 us -> none  [on_device(): (out_grad.astype(f32) * silu_grad(pre_act.astype(f32))).astype(bf16)[0]]
    unnamed x4, local copies, waits for them, and re-layouts: 1.05 us -> 2.2 us
    convert_element_type x0 -> x1, other arithmetic: none -> 1.08 us  [on_device(): (out_grad[0].astype(f32) * silu_grad(pre_act[0].astype(f32))).astype(bf16)]
    ppermute x8, starting transfers between devices: 16.1 us -> 15.1 us  [swapped(): return lax.ppermute(value, axis, [(i, i ^ distance) for i in range(count)])]
    pallas_call x1, Pallas kernels: 1.44 us -> 0.89 us  [on_device(): call(functools.partial(last_weight_kernel, grad_scale, filt), shape((taps...]
    pallas_call x1, Pallas kernels: 0.87 us -> 0.33 us  [on_device(): call(functools.partial(turn_kernel, blocks), (shape((half, cells), bf16),...]
  transfers between devices with their start and end apart: 10 -> 10, of which waited for: 1 -> 5; matrix products, arithmetic and copies ran while one was open for 0% -> 3% of each run, Pallas kernels for 21% -> 11%
where the time goes in v6:
time: 35.6 us; the launch traced here: 35.3 us
  starting transfers between devices  17.1 us (48%)
  waiting for transfers between devices  7.91 us (22%)
  Pallas kernels  6.24 us (18%)
  local copies, waits for them, and re-layouts  2.2 us (6%)
  other arithmetic  1.08 us (3%)
  between operations  0.73 us (2%)
    ppermute x8, starting transfers between devices, swapped(): return lax.ppermute(value, axis, [(i, i ^ distance) for i in range(count)])  15.1 us
    ppermute x8, waiting for transfers between devices, swapped(): return lax.ppermute(value, axis, [(i, i ^ distance) for i in range(count)])  7.91 us
    unnamed x4, local copies, waits for them, and re-layouts  2.2 us
    pallas_call x1, Pallas kernels, on_device(): call(functools.partial(early_kernel, width), (shape((chans, cells), bf16)...  1.96 us
    ppermute x1, starting transfers between devices, on_device(): two_off = lax.ppermute(own, 'space', two_pairs)  1.29 us
    pallas_call x1, Pallas kernels, on_device(): call(functools.partial(spread_kernel, width, groups), (windows_shape, sha...  1.22 us
    convert_element_type x1, other arithmetic, on_device(): (out_grad[0].astype(f32) * silu_grad(pre_act[0].astype(f32))).astype(bf16)  1.08 us
    pallas_call x1, Pallas kernels, on_device(): call(functools.partial(late_kernel, width), (shape((piece, taps * filt),...  1.03 us
  transfers between devices with their start and end apart: 10, of which 5 were waited for; matrix products, arithmetic and copies ran while one was open for 3% of the time, Pallas kernels for 11%

profile of v6, /device:TPU:0, one launch (start us, length us, event | category | flops | bytes accessed | tf_op | source)
XLA Modules:
  0.0 35.3 jit_solution(7850798055084771230)
XLA Ops:
  0.6 0.0 copy-start
  0.6 1.0 %copy-done = bf16[1,32,32,256]{3,2,1,0:T(8,128)(2,1)S(1)} copy-done((bf16[1,32,32,256]{3,2,1,0:T(8,128)(2,1)S(1)}, bf16[1,32,32,256]{3,2,1,0:T(8,128)(2,1)}, u32[]{:S(2)}) %copy-start) | copy-done | bytes 524312
  1.7 0.3 shard_map.59
  2.0 3.0 %collective-permute-start.3 = (bf16[64,1024]{1,0:T(8,128)(2,1)S(1)}, bf16[64,1024]{1,0:T(8,128)(2,1)S(1)}, u32[]{:S(2)}, u32[]{:S(2)}) collective-permute-start(bf16[64,1024]{1,0:T(8,128)(2,1)S(1)} %get-tuple-element.24), channel_id=1, source_target_pairs={{0,4},{4,0},{8,12},{12,8},{16,20},{20,16},{24,28},{28,24},{1,5},{5... | collective-permute-start | bytes 393224 | tf_op jit(solution)/shard_map/ppermute | solution.py:179
  5.0 1.1 %fusion.6.own = bf16[64,1024]{1,0:T(8,128)(2,1)S(1)} fusion(bf16[1,64,1024]{2,1,0:T(8,128)(2,1)} %param.5, bf16[1,64,1024]{2,1,0:T(8,128)(2,1)} %param.6), kind=kLoop, calls=%fused_computation.8 | loop fusion | flops 720896 | bytes 393216 | tf_op jit(solution)/shard_map/convert_element_type | solution.py:213
  6.1 1.3 %collective-permute-start.2 = (bf16[64,1024]{1,0:T(8,128)(2,1)S(1)}, bf16[64,1024]{1,0:T(8,128)(2,1)S(1)}, u32[]{:S(2)}, u32[]{:S(2)}) collective-permute-start(bf16[64,1024]{1,0:T(8,128)(2,1)S(1)} %fusion.6.own), channel_id=1, source_target_pairs={{8,0},{16,8},{24,16},{4,12},{12,20},{20,28},{9,1},{17,9},{25,17},{... | collective-permute-start | bytes 393224 | tf_op jit(solution)/shard_map/ppermute | solution.py:222
  7.4 0.7 %collective-permute-start.1 = (bf16[64,1024]{1,0:T(8,128)(2,1)S(1)}, bf16[64,1024]{1,0:T(8,128)(2,1)S(1)}, u32[]{:S(2)}, u32[]{:S(2)}) collective-permute-start(bf16[64,1024]{1,0:T(8,128)(2,1)S(1)} %fusion.6.own), channel_id=1, source_target_pairs={{4,8},{12,16},{20,24},{8,4},{16,12},{24,20},{5,9},{13,17},{21,25},... | collective-permute-start | bytes 393224 | tf_op jit(solution)/shard_map/ppermute | solution.py:224
  8.1 5.4 %collective-permute-start = (bf16[64,1024]{1,0:T(8,128)(2,1)S(1)}, bf16[64,1024]{1,0:T(8,128)(2,1)S(1)}, u32[]{:S(2)}, u32[]{:S(2)}) collective-permute-start(bf16[64,1024]{1,0:T(8,128)(2,1)S(1)} %fusion.6.own), channel_id=1, source_target_pairs={{0,4},{4,0},{8,12},{12,8},{16,20},{20,16},{24,28},{28,24},{1,5},{5... | collective-permute-start | bytes 393224 | tf_op jit(solution)/shard_map/ppermute | solution.py:179
  13.5 0.0 collective-permute-done.3.came
  13.5 0.0 collective-permute-start.4
  13.5 0.0 copy-start.1
  13.5 1.2 %copy-done.1 = bf16[27,64,256]{2,1,0:T(8,128)(2,1)S(1)} copy-done((bf16[27,64,256]{2,1,0:T(8,128)(2,1)S(1)}, bf16[27,64,256]{2,1,0:T(8,128)(2,1)}, u32[]{:S(2)}) %copy-start.1) | copy-done | bytes 884760
  14.7 0.1 shard_map.60
  14.7 0.0 collective-permute-done.2.two_off
  14.7 0.1 collective-permute-done.4.other
  14.8 2.0 %shard_map.61 = (bf16[256,1024]{1,0:T(8,128)(2,1)S(1)}, f32[256,1152]{1,0:T(8,128)S(1)}, f32[1024,256]{1,0:T(8,128)S(1)}) custom-call(bf16[64,1024]{1,0:T(8,128)(2,1)S(1)} %fusion.6.own, bf16[64,1024]{1,0:T(8,128)(2,1)S(1)} %collective-permute-done.2.two_off, bf16[128,1024]{1,0:T(8,128)(2,1)S(1)} %get-tuple-element.21.mine, ...), custom_call_target="tpu_custom_call" | custom-call | flops 2717908992 | bytes 4194304 | tf_op jit(solution)/shard_map/pallas_call | solution.py:231
  16.8 0.0 collective-permute-done.1.one_off
  16.8 1.1 %collective-permute-done.near = bf16[64,1024]{1,0:T(8,128)(2,1)S(1)} collective-permute-done((bf16[64,1024]{1,0:T(8,128)(2,1)S(1)}, bf16[64,1024]{1,0:T(8,128)(2,1)S(1)}, u32[]{:S(2)}, u32[]{:S(2)}) %collective-permute-start) | collective-permute-done | bytes 131104 | tf_op jit(solution)/shard_map/ppermute | solution.py:179
  17.9 1.2 %shard_map.62 = (bf16[1088,384]{1,0:T(8,128)(2,1)S(1)}, f32[512,256]{1,0:T(8,128)S(1)}, bf16[512,256]{1,0:T(8,128)(2,1)S(1)}) custom-call(bf16[64,1024]{1,0:T(8,128)(2,1)S(1)} %collective-permute-done.near, bf16[64,1024]{1,0:T(8,128)(2,1)S(1)} %collective-permute-done.1.one_off, bf16[3,384,256]{2,1,0:T(8,128)(2,1)S(1)} %get-tuple-element.23.weight, ...), custom_call_target="tpu_custom_call" | custom-call | flops 2717908992 | bytes 4194304 | tf_op jit(solution)/shard_map/pallas_call | solution.py:238
  19.2 0.1 collective-permute-start.5
  19.2 1.0 %shard_map.63 = (f32[32,1728]{1,0:T(8,128)S(1)}, bf16[32,1728]{1,0:T(8,128)(2,1)S(1)}, bf16[32,1728]{1,0:T(8,128)(2,1)S(1)}, bf16[32,1728]{1,0:T(8,128)(2,1)S(1)}) custom-call(bf16[256,1024]{1,0:T(8,128)(2,1)S(1)} %get-tuple-element.29.turned, bf16[1088,384]{1,0:T(8,128)(2,1)S(1)} %get-tuple-element.30.windows, f32[256,1152]{1,0:T(8,128)S(1)} %get-tuple-element.31.early), custom_call_target="tpu_custom_call" | custom-call | flops 2717908992 | bytes 4194304 | tf_op jit(solution)/shard_map/pallas_call | solution.py:248
  20.3 3.5 %collective-permute-start.6 = (bf16[32,1728]{1,0:T(8,128)(2,1)S(1)}, bf16[32,1728]{1,0:T(8,128)(2,1)S(1)}, u32[]{:S(2)}, u32[]{:S(2)}) collective-permute-start(bf16[32,1728]{1,0:T(8,128)(2,1)S(1)} %get-tuple-element.35), channel_id=1, source_target_pairs={{0,16},{4,20},{8,24},{12,28},{16,0},{20,4},{24,8},{28,12},{1,17},{... | collective-permute-start | bytes 331784 | tf_op jit(solution)/shard_map/ppermute | solution.py:179
  23.7 1.6 %collective-permute-start.7 = (bf16[32,1728]{1,0:T(8,128)(2,1)S(1)}, bf16[32,1728]{1,0:T(8,128)(2,1)S(1)}, u32[]{:S(2)}, u32[]{:S(2)}) collective-permute-start(bf16[32,1728]{1,0:T(8,128)(2,1)S(1)} %get-tuple-element.36), channel_id=1, source_target_pairs={{0,8},{4,12},{8,0},{12,4},{16,24},{20,28},{24,16},{28,20},{1,9},{5... | collective-permute-start | bytes 331784 | tf_op jit(solution)/shard_map/ppermute | solution.py:179
  25.3 0.0 collective-permute-start.8
  25.3 0.0 collective-permute-done.5.came
  25.4 1.6 %collective-permute-start.9 = (bf16[256,256]{1,0:T(8,128)(2,1)S(1)}, bf16[256,256]{1,0:T(8,128)(2,1)S(1)}, u32[]{:S(2)}, u32[]{:S(2)}) collective-permute-start(bf16[256,256]{1,0:T(8,128)(2,1)S(1)} %get-tuple-element.39), channel_id=1, source_target_pairs={{0,2},{1,3},{2,0},{3,1},{4,6},{5,7},{6,4},{7,5},{8,10},{9,11},{10,... | collective-permute-start | bytes 393224 | tf_op jit(solution)/shard_map/ppermute | solution.py:179
  27.0 3.2 %collective-permute-done.6.rest_0_ = bf16[32,1728]{1,0:T(8,128)(2,1)S(1)} collective-permute-done((bf16[32,1728]{1,0:T(8,128)(2,1)S(1)}, bf16[32,1728]{1,0:T(8,128)(2,1)S(1)}, u32[]{:S(2)}, u32[]{:S(2)}) %collective-permute-start.6) | collective-permute-done | bytes 110624 | tf_op jit(solution)/shard_map/ppermute | solution.py:179
  30.2 0.1 collective-permute-done.7.rest_1_
  30.3 3.4 %collective-permute-done.8.rest_2_ = bf16[32,1728]{1,0:T(8,128)(2,1)S(1)} collective-permute-done((bf16[32,1728]{1,0:T(8,128)(2,1)S(1)}, bf16[32,1728]{1,0:T(8,128)(2,1)S(1)}, u32[]{:S(2)}, u32[]{:S(2)}) %collective-permute-start.8) | collective-permute-done | bytes 110624 | tf_op jit(solution)/shard_map/ppermute | solution.py:179
  33.7 0.9 %shard_map.65 = f32[27,32,64]{2,1,0:T(8,128)} custom-call(f32[32,1728]{1,0:T(8,128)S(1)} %get-tuple-element.32.kept, bf16[32,1728]{1,0:T(8,128)(2,1)S(1)} %collective-permute-done.6.rest_0_, bf16[32,1728]{1,0:T(8,128)(2,1)S(1)} %collective-permute-done.7.rest_1_, bf16[32,1728]{1,0:T(8,128)(2,1)S(1)} %collective-permute-done.8.rest_2_), custom_call_target="tpu_custom_call" | custom-call | flops 2717908992 | tf_op jit(solution)/shard_map/pallas_call | solution.py:277
  34.6 0.0 collective-permute-done.9.came
  34.6 0.7 %shard_map.66 = bf16[256,256]{1,0:T(8,128)(2,1)} custom-call(f32[256,256]{1,0:T(8,128)S(1)} %get-tuple-element.38.kept, bf16[256,256]{1,0:T(8,128)(2,1)S(1)} %collective-permute-done.9.came), custom_call_target="tpu_custom_call" | custom-call | tf_op jit(solution)/shard_map/pallas_call | solution.py:282
  (1 shorter events, 0.0 us)
Async XLA Ops:
  0.6 1.0 %copy-start = (bf16[1,32,32,256]{3,2,1,0:T(8,128)(2,1)S(1)}, bf16[1,32,32,256]{3,2,1,0:T(8,128)(2,1)}, u32[]{:S(2)}) copy-start(bf16[1,32,32,256]{3,2,1,0:T(8,128)(2,1)} %param.4) | copy-start | bytes 1572868
  2.0 11.5 %collective-permute-start.3 = (bf16[64,1024]{1,0:T(8,128)(2,1)S(1)}, bf16[64,1024]{1,0:T(8,128)(2,1)S(1)}, u32[]{:S(2)}, u32[]{:S(2)}) collective-permute-start(bf16[64,1024]{1,0:T(8,128)(2,1)S(1)} %get-tuple-element.24), channel_id=1, source_target_pairs={{0,4},{4,0},{8,12},{12,8},{16,20},{20,16},{24,28},{28,24},{1,5},{5... | collective-permute-start | bytes 393224 | tf_op jit(solution)/shard_map/ppermute | solution.py:179
  6.1 8.6 %collective-permute-start.2 = (bf16[64,1024]{1,0:T(8,128)(2,1)S(1)}, bf16[64,1024]{1,0:T(8,128)(2,1)S(1)}, u32[]{:S(2)}, u32[]{:S(2)}) collective-permute-start(bf16[64,1024]{1,0:T(8,128)(2,1)S(1)} %fusion.6.own), channel_id=1, source_target_pairs={{8,0},{16,8},{24,16},{4,12},{12,20},{20,28},{9,1},{17,9},{25,17},{... | collective-permute-start | bytes 393224 | tf_op jit(solution)/shard_map/ppermute | solution.py:222
  7.4 9.4 %collective-permute-start.1 = (bf16[64,1024]{1,0:T(8,128)(2,1)S(1)}, bf16[64,1024]{1,0:T(8,128)(2,1)S(1)}, u32[]{:S(2)}, u32[]{:S(2)}) collective-permute-start(bf16[64,1024]{1,0:T(8,128)(2,1)S(1)} %fusion.6.own), channel_id=1, source_target_pairs={{4,8},{12,16},{20,24},{8,4},{16,12},{24,20},{5,9},{13,17},{21,25},... | collective-permute-start | bytes 393224 | tf_op jit(solution)/shard_map/ppermute | solution.py:224
  8.1 9.9 %collective-permute-start = (bf16[64,1024]{1,0:T(8,128)(2,1)S(1)}, bf16[64,1024]{1,0:T(8,128)(2,1)S(1)}, u32[]{:S(2)}, u32[]{:S(2)}) collective-permute-start(bf16[64,1024]{1,0:T(8,128)(2,1)S(1)} %fusion.6.own), channel_id=1, source_target_pairs={{0,4},{4,0},{8,12},{12,8},{16,20},{20,16},{24,28},{28,24},{1,5},{5... | collective-permute-start | bytes 393224 | tf_op jit(solution)/shard_map/ppermute | solution.py:179
  13.5 1.3 %collective-permute-start.4 = (bf16[64,1024]{1,0:T(8,128)(2,1)S(1)}, bf16[64,1024]{1,0:T(8,128)(2,1)S(1)}, u32[]{:S(2)}, u32[]{:S(2)}) collective-permute-start(bf16[64,1024]{1,0:T(8,128)(2,1)S(1)} %collective-permute-done.3.came), channel_id=1, source_target_pairs={{0,1},{1,0},{2,3},{3,2},{4,5},{5,4},{6,7},{7,6},{8,9},{9,8},{10,11... | collective-permute-start | bytes 393224 | tf_op jit(solution)/shard_map/ppermute | solution.py:179
  13.5 1.2 %copy-start.1 = (bf16[27,64,256]{2,1,0:T(8,128)(2,1)S(1)}, bf16[27,64,256]{2,1,0:T(8,128)(2,1)}, u32[]{:S(2)}) copy-start(bf16[27,64,256]{2,1,0:T(8,128)(2,1)} %weight) | copy-start | bytes 2654212
  19.2 6.2 %collective-permute-start.5 = (bf16[512,256]{1,0:T(8,128)(2,1)S(1)}, bf16[512,256]{1,0:T(8,128)(2,1)S(1)}, u32[]{:S(2)}, u32[]{:S(2)}) collective-permute-start(bf16[512,256]{1,0:T(8,128)(2,1)S(1)} %get-tuple-element.28), channel_id=1, source_target_pairs={{0,1},{1,0},{2,3},{3,2},{4,5},{5,4},{6,7},{7,6},{8,9},{9,8},{10,11... | collective-permute-start | bytes 786440 | tf_op jit(solution)/shard_map/ppermute | solution.py:179
  20.3 9.9 %collective-permute-start.6 = (bf16[32,1728]{1,0:T(8,128)(2,1)S(1)}, bf16[32,1728]{1,0:T(8,128)(2,1)S(1)}, u32[]{:S(2)}, u32[]{:S(2)}) collective-permute-start(bf16[32,1728]{1,0:T(8,128)(2,1)S(1)} %get-tuple-element.35), channel_id=1, source_target_pairs={{0,16},{4,20},{8,24},{12,28},{16,0},{20,4},{24,8},{28,12},{1,17},{... | collective-permute-start | bytes 331784 | tf_op jit(solution)/shard_map/ppermute | solution.py:179
  23.7 6.6 %collective-permute-start.7 = (bf16[32,1728]{1,0:T(8,128)(2,1)S(1)}, bf16[32,1728]{1,0:T(8,128)(2,1)S(1)}, u32[]{:S(2)}, u32[]{:S(2)}) collective-permute-start(bf16[32,1728]{1,0:T(8,128)(2,1)S(1)} %get-tuple-element.36), channel_id=1, source_target_pairs={{0,8},{4,12},{8,0},{12,4},{16,24},{20,28},{24,16},{28,20},{1,9},{5... | collective-permute-start | bytes 331784 | tf_op jit(solution)/shard_map/ppermute | solution.py:179
  25.3 8.3 %collective-permute-start.8 = (bf16[32,1728]{1,0:T(8,128)(2,1)S(1)}, bf16[32,1728]{1,0:T(8,128)(2,1)S(1)}, u32[]{:S(2)}, u32[]{:S(2)}) collective-permute-start(bf16[32,1728]{1,0:T(8,128)(2,1)S(1)} %get-tuple-element.37), channel_id=1, source_target_pairs={{0,24},{4,28},{8,16},{12,20},{16,8},{20,12},{24,0},{28,4},{1,25},{... | collective-permute-start | bytes 331784 | tf_op jit(solution)/shard_map/ppermute | solution.py:179
  25.4 9.2 %collective-permute-start.9 = (bf16[256,256]{1,0:T(8,128)(2,1)S(1)}, bf16[256,256]{1,0:T(8,128)(2,1)S(1)}, u32[]{:S(2)}, u32[]{:S(2)}) collective-permute-start(bf16[256,256]{1,0:T(8,128)(2,1)S(1)} %get-tuple-element.39), channel_id=1, source_target_pairs={{0,2},{1,3},{2,0},{3,1},{4,6},{5,7},{6,4},{7,5},{8,10},{9,11},{10,... | collective-permute-start | bytes 393224 | tf_op jit(solution)/shard_map/ppermute | solution.py:179

commit v7 on v6

--- a/solution.py
+++ b/solution.py
@@ -8,7 +8,7 @@
 from jax.sharding import PartitionSpec as P
 
 MIB = 1 << 20
-EARLY, SPREAD, LATE, FINAL, ORDER = 3, 3, 3, 3, 3
+TURN, EARLY, TWO, SPREAD, LATE, FINAL, ORDER = 3, 3, 3, 3, 3, 3, 3
 VMEM = pl.BlockSpec(memory_space=pltpu.VMEM)
 
 
@@ -67,19 +67,23 @@
     part[...] = turned[half:, :]
 
 
+def grads_kernel(out_grad, pre_act, _, own):
+    own[...] = (out_grad[...].astype(jnp.float32) * silu_grad(pre_act[...].astype(jnp.float32))).astype(own.dtype)
+
+
 def order_kernel(weight, early, late):
     filt = weight.shape[1]
     odd = lax.axis_index("space") & 1
     for tap in range(9):
         b, c = divmod(tap, 3)
         low, high = pl.ds(2 * c * filt, filt), pl.ds((2 * c + 1) * filt, filt)
-        early[b, low, :] = jnp.zeros(weight.shape[1:], jnp.bfloat16)
-        early[b, high, :] = weight[9 + tap]
+        early[b, low, :] = weight[9 + tap]
+        early[b, high, :] = jnp.zeros(weight.shape[1:], jnp.bfloat16)
         late[b, low, :] = weight[18 * odd + tap]
         late[b, high, :] = weight[18 - 18 * odd + tap]
 
 
-def early_kernel(width, own, two_off, mine, came, other, weight, turned, terms, spread, windows, tall):
+def early_kernel(width, own, mine, came, other, weight, turned, terms, spread, windows, tall):
     cells = own.shape[1]
     half = mine.shape[0]
     wide = windows.shape[1]
@@ -87,7 +91,7 @@
     turned[0:half, :] = mine[...]
     turned[half : half + half // 2, :] = jnp.where(first_core, came[...], other[...])
     turned[half + half // 2 :, :] = jnp.where(first_core, other[...], came[...])
-    lay_windows(width, two_off[...], own[...], windows, tall)
+    lay_windows(width, own[...], own[...], windows, tall)
     total = 0.0
     for b in range(3):
         window = windows[pl.ds((2 - b) * width, cells), :]
@@ -118,7 +122,19 @@
             send[pl.ds((target - groups // 2) * part, part), :] = total.astype(jnp.bfloat16)
 
 
-def late_kernel(width, turned, windows, early, keep, *sends):
+def two_kernel(width, turned, two_off, terms, windows, tall):
+    half = turned.shape[0] // 2
+    cells = turned.shape[1]
+    wide = windows.shape[1]
+    lay_windows(width, two_off[...], two_off[...], windows, tall)
+    for b in range(3):
+        window = windows[pl.ds((2 - b) * width, cells), :]
+        terms[:, b * wide : (b + 1) * wide] = jnp.dot(
+            turned[pl.ds(half, half), :], window, preferred_element_type=jnp.float32
+        )
+
+
+def late_kernel(width, turned, windows, two, early, keep, *sends):
     half = turned.shape[0] // 2
     cells = turned.shape[1]
     wide = windows.shape[1]
@@ -139,16 +155,16 @@
             tap = 3 * b + c
             cut = slice(c * lanes, (c + 1) * lanes)
             lo = b * wide + c * lanes
-            store(lo, lo + lanes, terms[0:half, cut] + early[half:, lo : lo + lanes])
-            near_side, own_side = terms[half:, cut], early[0:half, lo : lo + lanes]
+            crossed = jnp.where(left, two[:, lo : lo + lanes], early[half:, lo : lo + lanes])
+            store(lo, lo + lanes, terms[0:half, cut] + crossed)
+            middle = terms[half:, cut] + early[0:half, lo : lo + lanes]
             lo = 3 * wide + tap // 2 * lanes
             if tap == 8:
-                middle = near_side + pltpu.roll(own_side, filt, 1)
                 store(lo, lo + filt, middle[:, 0:filt])
             elif tap % 2 == 0:
-                before = near_side + pltpu.roll(own_side, filt, 1)
+                before = middle
             else:
-                store(lo, lo + lanes, jnp.where(left, before, pltpu.roll(near_side, filt, 1) + own_side))
+                store(lo, lo + lanes, jnp.where(left, before, pltpu.roll(middle, filt, 1)))
 
 
 def halve_kernel(kept, came, keep, send):
@@ -157,17 +173,18 @@
     send[...] = (kept[half:, :] + came[half:, :].astype(jnp.float32)).astype(jnp.bfloat16)
 
 
-def last_input_kernel(kept, came, out):
-    out[...] = (kept[...] + came[...].astype(jnp.float32)).astype(out.dtype)
-
-
-def last_weight_kernel(scale, filt, kept, *rest):
+def sum_kernel(scale, kept, *rest):
     *came, out = rest
-    odd = lax.axis_index("space") & 1
     total = kept[...]
     for piece in came:
         total = total + piece[...].astype(jnp.float32)
-    total = total * scale
+    out[...] = total * scale
+
+
+def last_kernel(filt, summed, kept, came, out, grad_input):
+    grad_input[...] = (kept[...] + came[...].astype(jnp.float32)).astype(grad_input.dtype)
+    odd = lax.axis_index("space") & 1
+    total = summed[...]
     for tap in range(9):
         slots = ((18 + tap, 9 + tap), (2 * tap, 18 * odd + tap), (2 * tap + 1, 18 - 18 * odd + tap))
         for slot, target in slots:
@@ -210,13 +227,15 @@
     windows_shape = shape((cells + 2 * width, lanes), bf16)
     tall = pltpu.VMEM((cells + 16, 2 * filt), f32)
 
-    own = (out_grad[0].astype(f32) * silu_grad(pre_act[0].astype(f32))).astype(bf16)
     mine, part = call(
         functools.partial(turn_kernel, blocks),
         (shape((half, cells), bf16), shape((quarter, cells), bf16)),
-        bytes_accessed=MIB,
+        flops=TURN * flops,
     )(in_specs=[VMEM], out_specs=[VMEM] * 2)(inputs.reshape(cells, chans))
-    came = swapped(part, "space", 1)
+    own = call(grads_kernel, shape((filt, cells), bf16))(in_specs=[VMEM] * 3, out_specs=VMEM)(
+        out_grad[0], pre_act[0], part
+    )
+    came = swapped(after(part, own), "space", 1)
     near = swapped(own, "space", 1)
     two_pairs = [(i, i - 2) for i in range(2, blocks, 2)] + [(i, i + 2) for i in range(1, blocks - 2, 2)]
     two_off = lax.ppermute(own, "space", two_pairs)
@@ -234,14 +253,20 @@
         (pltpu.VMEM(windows_shape.shape, bf16), tall),
         flops=EARLY * flops,
         bytes_accessed=4 * MIB,
-    )(in_specs=[VMEM] * 6, out_specs=[VMEM] * 3)(own, two_off, mine, came, other, early_weight)
+    )(in_specs=[VMEM] * 5, out_specs=[VMEM] * 3)(own, mine, came, other, early_weight)
+    two = call(
+        functools.partial(two_kernel, width),
+        shape((half, 3 * lanes), f32),
+        (pltpu.VMEM(windows_shape.shape, bf16), tall),
+        flops=TWO * flops,
+    )(in_specs=[VMEM] * 2, out_specs=VMEM)(turned, two_off)
     windows, kept_in, sent_in = call(
         functools.partial(spread_kernel, width, groups),
         (windows_shape, shape((cells // 2, chans), f32), shape((cells // 2, chans), bf16)),
         (tall,),
         flops=SPREAD * flops,
         bytes_accessed=4 * MIB,
-    )(in_specs=[VMEM] * 4, out_specs=[VMEM] * 3)(near, one_off, late_weight, spread)
+    )(in_specs=[VMEM] * 4, out_specs=[VMEM] * 3)(near, one_off, late_weight, after(spread, two))
     came_in = swapped(sent_in, "filt", 1)
     radix = min(4, blocks // 2)
     piece = half // radix
@@ -250,7 +275,7 @@
         (shape((piece, taps * filt), f32),) + (shape((piece, taps * filt), bf16),) * (radix - 1),
         flops=LATE * flops,
         bytes_accessed=4 * MIB,
-    )(in_specs=[VMEM] * 3, out_specs=[VMEM] * radix)(turned, windows, early)
+    )(in_specs=[VMEM] * 4, out_specs=[VMEM] * radix)(turned, windows, two, early)
     came_in = after(came_in, kept)
 
     distance = 2
@@ -274,14 +299,13 @@
         came_in = swapped(sent_in, "filt", distance_in)
         distance_in *= 2
     grad_scale = float(cells * blocks) ** (-0.5)
-    grad_weight = call(
-        functools.partial(last_weight_kernel, grad_scale, filt),
-        shape((taps, chans // blocks, filt), f32),
-        flops=FINAL * flops,
+    summed = call(
+        functools.partial(sum_kernel, grad_scale), shape((chans // blocks, taps * filt), f32), flops=FINAL * flops
     )(in_specs=[VMEM] * (len(arrived) + 1), out_specs=VMEM)(kept, *arrived)
-    grad_input = call(last_input_kernel, shape((cells // groups, chans), bf16))(
-        in_specs=[VMEM] * 2, out_specs=VMEM
-    )(after(kept_in, grad_weight), came_in)
+    grad_weight, grad_input = call(
+        functools.partial(last_kernel, filt),
+        (shape((taps, chans // blocks, filt), f32), shape((cells // groups, chans), bf16)),
+    )(in_specs=[VMEM] * 3, out_specs=[VMEM] * 2)(summed, kept_in, came_in)
     return grad_input.reshape(1, height // groups, width, chans), jnp.transpose(grad_weight, (1, 0, 2))
 
 

time: 35.6 us -> 34.6 us (0.972)
  other arithmetic: 1.08 us -> 0 us
  local copies, waits for them, and re-layouts: 2.2 us -> 1.67 us
  waiting for transfers between devices: 7.91 us -> 8.33 us
    convert_element_type x1 -> x0, other arithmetic: 1.08 us -> none  [on_device(): (out_grad[0].astype(f32) * silu_grad(pre_act[0].astype(f32))).astype(bf16)]
    unnamed x4 -> x8, local copies, waits for them, and re-layouts: 2.2 us -> 1.67 us
    ppermute x8, waiting for transfers between devices: 7.91 us -> 8.32 us  [swapped(): return lax.ppermute(value, axis, [(i, i ^ distance) for i in range(count)])]
    pallas_call x2 -> x4, Pallas kernels: 1.57 us -> 1.79 us  [the longest x1 0.9 us: on_device(): call(functools.partial(last_kernel, filt), (shape((taps, chans // blocks,...]
  transfers between devices with their start and end apart: 10 -> 10, of which waited for: 5 -> 5; matrix products, arithmetic and copies ran while one was open for 3% -> 0% of each run, Pallas kernels for 11% -> 11%
where the time goes in v7:
time: 34.6 us; the launch traced here: 34.3 us
  starting transfers between devices  17.1 us (49%)
  waiting for transfers between devices  8.33 us (24%)
  Pallas kernels  6.46 us (19%)
  local copies, waits for them, and re-layouts  1.67 us (5%)
  between operations  0.75 us (2%)
    ppermute x8, starting transfers between devices, swapped(): return lax.ppermute(value, axis, [(i, i ^ distance) for i in range(count)])  15.1 us
    ppermute x8, waiting for transfers between devices, swapped(): return lax.ppermute(value, axis, [(i, i ^ distance) for i in range(count)])  8.32 us
    pallas_call x1, Pallas kernels, on_device(): call(functools.partial(early_kernel, width), (shape((chans, cells), bf16)...  1.96 us
    unnamed x8, local copies, waits for them, and re-layouts  1.67 us
    ppermute x1, starting transfers between devices, on_device(): two_off = lax.ppermute(own, 'space', two_pairs)  1.28 us
    pallas_call x1, Pallas kernels, on_device(): call(functools.partial(spread_kernel, width, groups), (windows_shape, sha...  1.22 us
    pallas_call x1, Pallas kernels, on_device(): call(functools.partial(late_kernel, width), (shape((piece, taps * filt),...  1.04 us
    pallas_call x1, Pallas kernels, on_device(): call(functools.partial(last_kernel, filt), (shape((taps, chans // blocks,...  0.9 us
  transfers between devices with their start and end apart: 10, of which 5 were waited for; matrix products, arithmetic and copies ran while one was open for 0% of the time, Pallas kernels for 11%

profile of v7, /device:TPU:0, one launch (start us, length us, event | category | flops | bytes accessed | tf_op | source)
XLA Modules:
  0.0 34.3 jit_solution(15866757886160575097)
XLA Ops:
  0.6 0.0 copy-start.3
  0.6 1.0 %copy-done.3 = bf16[1,32,32,256]{3,2,1,0:T(8,128)(2,1)S(1)} copy-done((bf16[1,32,32,256]{3,2,1,0:T(8,128)(2,1)S(1)}, bf16[1,32,32,256]{3,2,1,0:T(8,128)(2,1)}, u32[]{:S(2)}) %copy-start.3) | copy-done | bytes 524312
  1.7 0.0 copy-start
  1.7 0.0 copy-start.1
  1.7 0.0 copy-start.2
  1.7 0.3 shard_map.59
  2.0 0.6 %copy-done = bf16[1,64,1024]{2,1,0:T(8,128)(2,1)S(1)} copy-done((bf16[1,64,1024]{2,1,0:T(8,128)(2,1)S(1)}, bf16[1,64,1024]{2,1,0:T(8,128)(2,1)}, u32[]{:S(2)}) %copy-start) | copy-done | bytes 131096
  2.6 0.1 copy-done.1
  2.6 0.1 shard_map.60.own
  2.7 3.0 %collective-permute-start = (bf16[64,1024]{1,0:T(8,128)(2,1)S(1)}, bf16[64,1024]{1,0:T(8,128)(2,1)S(1)}, u32[]{:S(2)}, u32[]{:S(2)}) collective-permute-start(bf16[64,1024]{1,0:T(8,128)(2,1)S(1)} %get-tuple-element.26._), channel_id=1, source_target_pairs={{0,4},{4,0},{8,12},{12,8},{16,20},{20,16},{24,28},{28,24},{1,5},{5... | collective-permute-start | bytes 393224 | tf_op jit(solution)/shard_map/ppermute | solution.py:196
  5.7 1.3 %collective-permute-start.4 = (bf16[64,1024]{1,0:T(8,128)(2,1)S(1)}, bf16[64,1024]{1,0:T(8,128)(2,1)S(1)}, u32[]{:S(2)}, u32[]{:S(2)}) collective-permute-start(bf16[64,1024]{1,0:T(8,128)(2,1)S(1)} %shard_map.60.own), channel_id=1, source_target_pairs={{8,0},{16,8},{24,16},{4,12},{12,20},{20,28},{9,1},{17,9},{25,17},{... | collective-permute-start | bytes 393224 | tf_op jit(solution)/shard_map/ppermute | solution.py:241
  7.0 0.7 %collective-permute-start.3 = (bf16[64,1024]{1,0:T(8,128)(2,1)S(1)}, bf16[64,1024]{1,0:T(8,128)(2,1)S(1)}, u32[]{:S(2)}, u32[]{:S(2)}) collective-permute-start(bf16[64,1024]{1,0:T(8,128)(2,1)S(1)} %shard_map.60.own), channel_id=1, source_target_pairs={{4,8},{12,16},{20,24},{8,4},{16,12},{24,20},{5,9},{13,17},{21,25},... | collective-permute-start | bytes 393224 | tf_op jit(solution)/shard_map/ppermute | solution.py:243
  7.7 5.4 %collective-permute-start.2 = (bf16[64,1024]{1,0:T(8,128)(2,1)S(1)}, bf16[64,1024]{1,0:T(8,128)(2,1)S(1)}, u32[]{:S(2)}, u32[]{:S(2)}) collective-permute-start(bf16[64,1024]{1,0:T(8,128)(2,1)S(1)} %shard_map.60.own), channel_id=1, source_target_pairs={{0,4},{4,0},{8,12},{12,8},{16,20},{20,16},{24,28},{28,24},{1,5},{5... | collective-permute-start | bytes 393224 | tf_op jit(solution)/shard_map/ppermute | solution.py:196
  13.1 0.0 collective-permute-done.came
  13.1 0.0 collective-permute-start.1
  13.1 0.0 copy-done.2
  13.1 0.1 shard_map.61
  13.2 1.3 %collective-permute-done.1.other = bf16[64,1024]{1,0:T(8,128)(2,1)S(1)} collective-permute-done((bf16[64,1024]{1,0:T(8,128)(2,1)S(1)}, bf16[64,1024]{1,0:T(8,128)(2,1)S(1)}, u32[]{:S(2)}, u32[]{:S(2)}) %collective-permute-start.1) | collective-permute-done | bytes 131104 | tf_op jit(solution)/shard_map/ppermute | solution.py:196
  14.5 2.0 %shard_map.62 = (bf16[256,1024]{1,0:T(8,128)(2,1)S(1)}, f32[256,1152]{1,0:T(8,128)S(1)}, f32[1024,256]{1,0:T(8,128)S(1)}) custom-call(bf16[64,1024]{1,0:T(8,128)(2,1)S(1)} %shard_map.60.own, bf16[128,1024]{1,0:T(8,128)(2,1)S(1)} %get-tuple-element.25.mine, bf16[64,1024]{1,0:T(8,128)(2,1)S(1)} %collective-permute-done.came, ...), custom_call_target="tpu_custom_call" | custom-call | flops 2717908992 | bytes 4194304 | tf_op jit(solution)/shard_map/pallas_call | solution.py:250
  16.4 0.0 collective-permute-done.4.two_off
  16.4 0.7 %shard_map.63.two = f32[128,1152]{1,0:T(8,128)S(1)} custom-call(bf16[256,1024]{1,0:T(8,128)(2,1)S(1)} %get-tuple-element.29.turned, bf16[64,1024]{1,0:T(8,128)(2,1)S(1)} %collective-permute-done.4.two_off), custom_call_target="tpu_custom_call" | custom-call | flops 2717908992 | tf_op jit(solution)/shard_map/pallas_call | solution.py:257
  17.2 0.0 collective-permute-done.3.one_off
  17.2 0.4 %collective-permute-done.2.near = bf16[64,1024]{1,0:T(8,128)(2,1)S(1)} collective-permute-done((bf16[64,1024]{1,0:T(8,128)(2,1)S(1)}, bf16[64,1024]{1,0:T(8,128)(2,1)S(1)}, u32[]{:S(2)}, u32[]{:S(2)}) %collective-permute-start.2) | collective-permute-done | bytes 131104 | tf_op jit(solution)/shard_map/ppermute | solution.py:196
  17.6 1.2 %shard_map.64 = (bf16[1088,384]{1,0:T(8,128)(2,1)S(1)}, f32[512,256]{1,0:T(8,128)S(1)}, bf16[512,256]{1,0:T(8,128)(2,1)S(1)}) custom-call(bf16[64,1024]{1,0:T(8,128)(2,1)S(1)} %collective-permute-done.2.near, bf16[64,1024]{1,0:T(8,128)(2,1)S(1)} %collective-permute-done.3.one_off, bf16[3,384,256]{2,1,0:T(8,128)(2,1)S(1)} %get-tuple-element.30.weight, ...), custom_call_target="tpu_custom_call" | custom-call | flops 2717908992 | bytes 4194304 | tf_op jit(solution)/shard_map/pallas_call | solution.py:263
  18.8 0.1 collective-permute-start.8
  18.9 1.0 %shard_map.65 = (f32[32,1728]{1,0:T(8,128)S(1)}, bf16[32,1728]{1,0:T(8,128)(2,1)S(1)}, bf16[32,1728]{1,0:T(8,128)(2,1)S(1)}, bf16[32,1728]{1,0:T(8,128)(2,1)S(1)}) custom-call(bf16[256,1024]{1,0:T(8,128)(2,1)S(1)} %get-tuple-element.29.turned, bf16[1088,384]{1,0:T(8,128)(2,1)S(1)} %get-tuple-element.33.windows, f32[128,1152]{1,0:T(8,128)S(1)} %shard_map.63.two, ...), custom_call_target="tpu_custom_call" | custom-call | flops 2717908992 | bytes 4194304 | tf_op jit(solution)/shard_map/pallas_call | solution.py:273
  19.9 3.5 %collective-permute-start.5 = (bf16[32,1728]{1,0:T(8,128)(2,1)S(1)}, bf16[32,1728]{1,0:T(8,128)(2,1)S(1)}, u32[]{:S(2)}, u32[]{:S(2)}) collective-permute-start(bf16[32,1728]{1,0:T(8,128)(2,1)S(1)} %get-tuple-element.36), channel_id=1, source_target_pairs={{0,16},{4,20},{8,24},{12,28},{16,0},{20,4},{24,8},{28,12},{1,17},{... | collective-permute-start | bytes 331784 | tf_op jit(solution)/shard_map/ppermute | solution.py:196
  23.4 1.6 %collective-permute-start.6 = (bf16[32,1728]{1,0:T(8,128)(2,1)S(1)}, bf16[32,1728]{1,0:T(8,128)(2,1)S(1)}, u32[]{:S(2)}, u32[]{:S(2)}) collective-permute-start(bf16[32,1728]{1,0:T(8,128)(2,1)S(1)} %get-tuple-element.37), channel_id=1, source_target_pairs={{0,8},{4,12},{8,0},{12,4},{16,24},{20,28},{24,16},{28,20},{1,9},{5... | collective-permute-start | bytes 331784 | tf_op jit(solution)/shard_map/ppermute | solution.py:196
  25.0 0.0 collective-permute-start.7
  25.0 0.0 collective-permute-done.8.came
  25.0 1.6 %collective-permute-start.9 = (bf16[256,256]{1,0:T(8,128)(2,1)S(1)}, bf16[256,256]{1,0:T(8,128)(2,1)S(1)}, u32[]{:S(2)}, u32[]{:S(2)}) collective-permute-start(bf16[256,256]{1,0:T(8,128)(2,1)S(1)} %get-tuple-element.43), channel_id=1, source_target_pairs={{0,2},{1,3},{2,0},{3,1},{4,6},{5,7},{6,4},{7,5},{8,10},{9,11},{10,... | collective-permute-start | bytes 393224 | tf_op jit(solution)/shard_map/ppermute | solution.py:196
  26.6 3.2 %collective-permute-done.5.rest_0_ = bf16[32,1728]{1,0:T(8,128)(2,1)S(1)} collective-permute-done((bf16[32,1728]{1,0:T(8,128)(2,1)S(1)}, bf16[32,1728]{1,0:T(8,128)(2,1)S(1)}, u32[]{:S(2)}, u32[]{:S(2)}) %collective-permute-start.5) | collective-permute-done | bytes 110624 | tf_op jit(solution)/shard_map/ppermute | solution.py:196
  29.8 0.1 collective-permute-done.6.rest_1_
  29.9 3.4 %collective-permute-done.7.rest_2_ = bf16[32,1728]{1,0:T(8,128)(2,1)S(1)} collective-permute-done((bf16[32,1728]{1,0:T(8,128)(2,1)S(1)}, bf16[32,1728]{1,0:T(8,128)(2,1)S(1)}, u32[]{:S(2)}, u32[]{:S(2)}) %collective-permute-start.7) | collective-permute-done | bytes 110624 | tf_op jit(solution)/shard_map/ppermute | solution.py:196
  33.3 0.1 shard_map.66.summed
  33.4 0.0 collective-permute-done.9.came
  33.4 0.9 %shard_map.68 = (f32[27,32,64]{2,1,0:T(8,128)}, bf16[256,256]{1,0:T(8,128)(2,1)}) custom-call(f32[32,1728]{1,0:T(8,128)S(1)} %shard_map.66.summed, f32[256,256]{1,0:T(8,128)S(1)} %get-tuple-element.42.kept, bf16[256,256]{1,0:T(8,128)(2,1)S(1)} %collective-permute-done.9.came), custom_call_target="tpu_custom_call" | custom-call | tf_op jit(solution)/shard_map/pallas_call | solution.py:305
  (1 shorter events, 0.0 us)
Async XLA Ops:
  0.6 1.0 %copy-start.3 = (bf16[1,32,32,256]{3,2,1,0:T(8,128)(2,1)S(1)}, bf16[1,32,32,256]{3,2,1,0:T(8,128)(2,1)}, u32[]{:S(2)}) copy-start(bf16[1,32,32,256]{3,2,1,0:T(8,128)(2,1)} %param.4) | copy-start | bytes 1572868
  1.7 0.9 %copy-start = (bf16[1,64,1024]{2,1,0:T(8,128)(2,1)S(1)}, bf16[1,64,1024]{2,1,0:T(8,128)(2,1)}, u32[]{:S(2)}) copy-start(bf16[1,64,1024]{2,1,0:T(8,128)(2,1)} %param.5) | copy-start | bytes 393220
  1.7 1.0 %copy-start.1 = (bf16[1,64,1024]{2,1,0:T(8,128)(2,1)S(1)}, bf16[1,64,1024]{2,1,0:T(8,128)(2,1)}, u32[]{:S(2)}) copy-start(bf16[1,64,1024]{2,1,0:T(8,128)(2,1)} %param.6) | copy-start | bytes 393220
  1.7 11.4 %copy-start.2 = (bf16[27,64,256]{2,1,0:T(8,128)(2,1)S(1)}, bf16[27,64,256]{2,1,0:T(8,128)(2,1)}, u32[]{:S(2)}) copy-start(bf16[27,64,256]{2,1,0:T(8,128)(2,1)} %weight) | copy-start | bytes 2654212
  2.7 10.4 %collective-permute-start = (bf16[64,1024]{1,0:T(8,128)(2,1)S(1)}, bf16[64,1024]{1,0:T(8,128)(2,1)S(1)}, u32[]{:S(2)}, u32[]{:S(2)}) collective-permute-start(bf16[64,1024]{1,0:T(8,128)(2,1)S(1)} %get-tuple-element.26._), channel_id=1, source_target_pairs={{0,4},{4,0},{8,12},{12,8},{16,20},{20,16},{24,28},{28,24},{1,5},{5... | collective-permute-start | bytes 393224 | tf_op jit(solution)/shard_map/ppermute | solution.py:196
  5.7 10.7 %collective-permute-start.4 = (bf16[64,1024]{1,0:T(8,128)(2,1)S(1)}, bf16[64,1024]{1,0:T(8,128)(2,1)S(1)}, u32[]{:S(2)}, u32[]{:S(2)}) collective-permute-start(bf16[64,1024]{1,0:T(8,128)(2,1)S(1)} %shard_map.60.own), channel_id=1, source_target_pairs={{8,0},{16,8},{24,16},{4,12},{12,20},{20,28},{9,1},{17,9},{25,17},{... | collective-permute-start | bytes 393224 | tf_op jit(solution)/shard_map/ppermute | solution.py:241
  7.0 10.2 %collective-permute-start.3 = (bf16[64,1024]{1,0:T(8,128)(2,1)S(1)}, bf16[64,1024]{1,0:T(8,128)(2,1)S(1)}, u32[]{:S(2)}, u32[]{:S(2)}) collective-permute-start(bf16[64,1024]{1,0:T(8,128)(2,1)S(1)} %shard_map.60.own), channel_id=1, source_target_pairs={{4,8},{12,16},{20,24},{8,4},{16,12},{24,20},{5,9},{13,17},{21,25},... | collective-permute-start | bytes 393224 | tf_op jit(solution)/shard_map/ppermute | solution.py:243
  7.7 9.9 %collective-permute-start.2 = (bf16[64,1024]{1,0:T(8,128)(2,1)S(1)}, bf16[64,1024]{1,0:T(8,128)(2,1)S(1)}, u32[]{:S(2)}, u32[]{:S(2)}) collective-permute-start(bf16[64,1024]{1,0:T(8,128)(2,1)S(1)} %shard_map.60.own), channel_id=1, source_target_pairs={{0,4},{4,0},{8,12},{12,8},{16,20},{20,16},{24,28},{28,24},{1,5},{5... | collective-permute-start | bytes 393224 | tf_op jit(solution)/shard_map/ppermute | solution.py:196
  13.1 1.3 %collective-permute-start.1 = (bf16[64,1024]{1,0:T(8,128)(2,1)S(1)}, bf16[64,1024]{1,0:T(8,128)(2,1)S(1)}, u32[]{:S(2)}, u32[]{:S(2)}) collective-permute-start(bf16[64,1024]{1,0:T(8,128)(2,1)S(1)} %collective-permute-done.came), channel_id=1, source_target_pairs={{0,1},{1,0},{2,3},{3,2},{4,5},{5,4},{6,7},{7,6},{8,9},{9,8},{10,11... | collective-permute-start | bytes 393224 | tf_op jit(solution)/shard_map/ppermute | solution.py:196
  18.8 6.2 %collective-permute-start.8 = (bf16[512,256]{1,0:T(8,128)(2,1)S(1)}, bf16[512,256]{1,0:T(8,128)(2,1)S(1)}, u32[]{:S(2)}, u32[]{:S(2)}) collective-permute-start(bf16[512,256]{1,0:T(8,128)(2,1)S(1)} %get-tuple-element.40), channel_id=1, source_target_pairs={{0,1},{1,0},{2,3},{3,2},{4,5},{5,4},{6,7},{7,6},{8,9},{9,8},{10,11... | collective-permute-start | bytes 786440 | tf_op jit(solution)/shard_map/ppermute | solution.py:196
  19.9 9.9 %collective-permute-start.5 = (bf16[32,1728]{1,0:T(8,128)(2,1)S(1)}, bf16[32,1728]{1,0:T(8,128)(2,1)S(1)}, u32[]{:S(2)}, u32[]{:S(2)}) collective-permute-start(bf16[32,1728]{1,0:T(8,128)(2,1)S(1)} %get-tuple-element.36), channel_id=1, source_target_pairs={{0,16},{4,20},{8,24},{12,28},{16,0},{20,4},{24,8},{28,12},{1,17},{... | collective-permute-start | bytes 331784 | tf_op jit(solution)/shard_map/ppermute | solution.py:196
  23.4 6.6 %collective-permute-start.6 = (bf16[32,1728]{1,0:T(8,128)(2,1)S(1)}, bf16[32,1728]{1,0:T(8,128)(2,1)S(1)}, u32[]{:S(2)}, u32[]{:S(2)}) collective-permute-start(bf16[32,1728]{1,0:T(8,128)(2,1)S(1)} %get-tuple-element.37), channel_id=1, source_target_pairs={{0,8},{4,12},{8,0},{12,4},{16,24},{20,28},{24,16},{28,20},{1,9},{5... | collective-permute-start | bytes 331784 | tf_op jit(solution)/shard_map/ppermute | solution.py:196
  25.0 8.4 %collective-permute-start.7 = (bf16[32,1728]{1,0:T(8,128)(2,1)S(1)}, bf16[32,1728]{1,0:T(8,128)(2,1)S(1)}, u32[]{:S(2)}, u32[]{:S(2)}) collective-permute-start(bf16[32,1728]{1,0:T(8,128)(2,1)S(1)} %get-tuple-element.38), channel_id=1, source_target_pairs={{0,24},{4,28},{8,16},{12,20},{16,8},{20,12},{24,0},{28,4},{1,25},{... | collective-permute-start | bytes 331784 | tf_op jit(solution)/shard_map/ppermute | solution.py:196
  25.0 8.4 %collective-permute-start.9 = (bf16[256,256]{1,0:T(8,128)(2,1)S(1)}, bf16[256,256]{1,0:T(8,128)(2,1)S(1)}, u32[]{:S(2)}, u32[]{:S(2)}) collective-permute-start(bf16[256,256]{1,0:T(8,128)(2,1)S(1)} %get-tuple-element.43), channel_id=1, source_target_pairs={{0,2},{1,3},{2,0},{3,1},{4,6},{5,7},{6,4},{7,5},{8,10},{9,11},{10,... | collective-permute-start | bytes 393224 | tf_op jit(solution)/shard_map/ppermute | solution.py:196

commit v8 on v7

--- a/solution.py
+++ b/solution.py
@@ -237,16 +237,16 @@
     )
     came = swapped(after(part, own), "space", 1)
     near = swapped(own, "space", 1)
+    weight_shape = shape((3, lanes, chans), bf16)
+    early_weight, late_weight = call(order_kernel, (weight_shape, weight_shape), flops=int(ORDER * flops), bytes_accessed=MIB)(
+        in_specs=[VMEM], out_specs=[VMEM] * 2
+    )(after(weight, mine))
     two_pairs = [(i, i - 2) for i in range(2, blocks, 2)] + [(i, i + 2) for i in range(1, blocks - 2, 2)]
-    two_off = lax.ppermute(own, "space", two_pairs)
+    two_off = lax.ppermute(after(own, early_weight), "space", two_pairs)
     one_pairs = [(i, i + 1) for i in range(1, blocks - 1, 2)]
     one_off = lax.ppermute(own, "space", one_pairs + [(target, source) for source, target in one_pairs])
     other = swapped(came, "filt", 1)
 
-    weight_shape = shape((3, lanes, chans), bf16)
-    early_weight, late_weight = call(order_kernel, (weight_shape, weight_shape), flops=ORDER * flops, bytes_accessed=MIB)(
-        in_specs=[VMEM], out_specs=[VMEM] * 2
-    )(after(weight, mine))
     turned, early, spread = call(
         functools.partial(early_kernel, width),
         (shape((chans, cells), bf16), shape((chans, 3 * lanes), f32), shape((cells, chans), f32)),
@@ -266,7 +266,7 @@
         (tall,),
         flops=SPREAD * flops,
         bytes_accessed=4 * MIB,
-    )(in_specs=[VMEM] * 4, out_specs=[VMEM] * 3)(near, one_off, late_weight, after(spread, two))
+    )(in_specs=[VMEM] * 4, out_specs=[VMEM] * 3)(near, one_off, late_weight, spread)
     came_in = swapped(sent_in, "filt", 1)
     radix = min(4, blocks // 2)
     piece = half // radix

time: 34.6 us -> 33.4 us (0.965)
  starting transfers between devices: 17.1 us -> 15.8 us
    ppermute x1, waiting for transfers between devices: 0.01 us -> 2.69 us  [on_device(): two_off = lax.ppermute(after(own, early_weight), 'space', two_pairs)]
    ppermute x8, waiting for transfers between devices: 8.32 us -> 5.78 us  [swapped(): return lax.ppermute(value, axis, [(i, i ^ distance) for i in range(count)])]
    ppermute x8, starting transfers between devices: 15.1 us -> 13.9 us  [swapped(): return lax.ppermute(value, axis, [(i, i ^ distance) for i in range(count)])]
  transfers between devices with their start and end apart: 10 -> 10, of which waited for: 5 -> 3; matrix products, arithmetic and copies ran while one was open for 0% -> 0% of each run, Pallas kernels for 11% -> 15%
where the time goes in v8:
time: 33.4 us; the launch traced here: 33.2 us
  starting transfers between devices  15.8 us (47%)
  waiting for transfers between devices  8.48 us (25%)
  Pallas kernels  6.46 us (19%)
  local copies, waits for them, and re-layouts  1.67 us (5%)
  between operations  0.75 us (2%)
    ppermute x8, starting transfers between devices, swapped(): return lax.ppermute(value, axis, [(i, i ^ distance) for i in range(count)])  13.9 us
    ppermute x8, waiting for transfers between devices, swapped(): return lax.ppermute(value, axis, [(i, i ^ distance) for i in range(count)])  5.78 us
    ppermute x1, waiting for transfers between devices, on_device(): two_off = lax.ppermute(after(own, early_weight), 'space', two_pairs)  2.69 us
    pallas_call x1, Pallas kernels, on_device(): call(functools.partial(early_kernel, width), (shape((chans, cells), bf16)...  1.97 us
    unnamed x8, local copies, waits for them, and re-layouts  1.67 us
    ppermute x1, starting transfers between devices, on_device(): two_off = lax.ppermute(after(own, early_weight), 'space', two_pairs)  1.29 us
    pallas_call x1, Pallas kernels, on_device(): call(functools.partial(spread_kernel, width, groups), (windows_shape, sha...  1.22 us
    pallas_call x1, Pallas kernels, on_device(): call(functools.partial(late_kernel, width), (shape((piece, taps * filt),...  1.04 us
  transfers between devices with their start and end apart: 10, of which 3 were waited for; matrix products, arithmetic and copies ran while one was open for 0% of the time, Pallas kernels for 15%

profile of v8, /device:TPU:0, one launch (start us, length us, event | category | flops | bytes accessed | tf_op | source)
XLA Modules:
  0.0 33.2 jit_solution(17705214439180735598)
XLA Ops:
  0.6 0.0 copy-start.3
  0.6 1.0 %copy-done.3 = bf16[1,32,32,256]{3,2,1,0:T(8,128)(2,1)S(1)} copy-done((bf16[1,32,32,256]{3,2,1,0:T(8,128)(2,1)S(1)}, bf16[1,32,32,256]{3,2,1,0:T(8,128)(2,1)}, u32[]{:S(2)}) %copy-start.3) | copy-done | bytes 524312
  1.7 0.0 copy-start
  1.7 0.0 copy-start.1
  1.7 0.0 copy-start.2
  1.7 0.3 shard_map.59
  2.0 0.6 %copy-done = bf16[1,64,1024]{2,1,0:T(8,128)(2,1)S(1)} copy-done((bf16[1,64,1024]{2,1,0:T(8,128)(2,1)S(1)}, bf16[1,64,1024]{2,1,0:T(8,128)(2,1)}, u32[]{:S(2)}) %copy-start) | copy-done | bytes 131096
  2.6 0.1 copy-done.1
  2.6 0.1 shard_map.60.own
  2.7 3.0 %collective-permute-start = (bf16[64,1024]{1,0:T(8,128)(2,1)S(1)}, bf16[64,1024]{1,0:T(8,128)(2,1)S(1)}, u32[]{:S(2)}, u32[]{:S(2)}) collective-permute-start(bf16[64,1024]{1,0:T(8,128)(2,1)S(1)} %get-tuple-element.26._), channel_id=1, source_target_pairs={{0,4},{4,0},{8,12},{12,8},{16,20},{20,16},{24,28},{28,24},{1,5},{5... | collective-permute-start | bytes 393224 | tf_op jit(solution)/shard_map/ppermute | solution.py:196
  5.7 0.7 %collective-permute-start.3 = (bf16[64,1024]{1,0:T(8,128)(2,1)S(1)}, bf16[64,1024]{1,0:T(8,128)(2,1)S(1)}, u32[]{:S(2)}, u32[]{:S(2)}) collective-permute-start(bf16[64,1024]{1,0:T(8,128)(2,1)S(1)} %shard_map.60.own), channel_id=1, source_target_pairs={{4,8},{12,16},{20,24},{8,4},{16,12},{24,20},{5,9},{13,17},{21,25},... | collective-permute-start | bytes 393224 | tf_op jit(solution)/shard_map/ppermute | solution.py:247
  6.4 4.3 %collective-permute-start.2 = (bf16[64,1024]{1,0:T(8,128)(2,1)S(1)}, bf16[64,1024]{1,0:T(8,128)(2,1)S(1)}, u32[]{:S(2)}, u32[]{:S(2)}) collective-permute-start(bf16[64,1024]{1,0:T(8,128)(2,1)S(1)} %shard_map.60.own), channel_id=1, source_target_pairs={{0,4},{4,0},{8,12},{12,8},{16,20},{20,16},{24,28},{28,24},{1,5},{5... | collective-permute-start | bytes 393224 | tf_op jit(solution)/shard_map/ppermute | solution.py:196
  10.7 0.0 collective-permute-done.came
  10.8 0.0 collective-permute-start.1
  10.8 0.0 copy-done.2
  10.8 0.1 shard_map.61
  10.8 1.3 %collective-permute-start.4 = (bf16[64,1024]{1,0:T(8,128)(2,1)S(1)}, bf16[64,1024]{1,0:T(8,128)(2,1)S(1)}, u32[]{:S(2)}, u32[]{:S(2)}) collective-permute-start(bf16[64,1024]{1,0:T(8,128)(2,1)S(1)} %shard_map.60.own), channel_id=1, source_target_pairs={{8,0},{16,8},{24,16},{4,12},{12,20},{20,28},{9,1},{17,9},{25,17},{... | collective-permute-start | bytes 393224 | tf_op jit(solution)/shard_map/ppermute | solution.py:245
  12.1 0.0 collective-permute-done.1.other
  12.2 2.0 %shard_map.62 = (bf16[256,1024]{1,0:T(8,128)(2,1)S(1)}, f32[256,1152]{1,0:T(8,128)S(1)}, f32[1024,256]{1,0:T(8,128)S(1)}) custom-call(bf16[64,1024]{1,0:T(8,128)(2,1)S(1)} %shard_map.60.own, bf16[128,1024]{1,0:T(8,128)(2,1)S(1)} %get-tuple-element.25.mine, bf16[64,1024]{1,0:T(8,128)(2,1)S(1)} %collective-permute-done.came, ...), custom_call_target="tpu_custom_call" | custom-call | flops 2717908992 | bytes 4194304 | tf_op jit(solution)/shard_map/pallas_call | solution.py:250
  14.1 0.0 collective-permute-done.3.one_off
  14.1 0.1 collective-permute-done.2.near
  14.2 1.2 %shard_map.63 = (bf16[1088,384]{1,0:T(8,128)(2,1)S(1)}, f32[512,256]{1,0:T(8,128)S(1)}, bf16[512,256]{1,0:T(8,128)(2,1)S(1)}) custom-call(bf16[64,1024]{1,0:T(8,128)(2,1)S(1)} %collective-permute-done.2.near, bf16[64,1024]{1,0:T(8,128)(2,1)S(1)} %collective-permute-done.3.one_off, bf16[3,384,256]{2,1,0:T(8,128)(2,1)S(1)} %get-tuple-element.30.weight, ...), custom_call_target="tpu_custom_call" | custom-call | flops 2717908992 | bytes 4194304 | tf_op jit(solution)/shard_map/pallas_call | solution.py:263
  15.4 0.5 %collective-permute-start.8 = (bf16[512,256]{1,0:T(8,128)(2,1)S(1)}, bf16[512,256]{1,0:T(8,128)(2,1)S(1)}, u32[]{:S(2)}, u32[]{:S(2)}) collective-permute-start(bf16[512,256]{1,0:T(8,128)(2,1)S(1)} %get-tuple-element.40), channel_id=1, source_target_pairs={{0,1},{1,0},{2,3},{3,2},{4,5},{5,4},{6,7},{7,6},{8,9},{9,8},{10,11... | collective-permute-start | bytes 786440 | tf_op jit(solution)/shard_map/ppermute | solution.py:196
  16.0 2.7 %collective-permute-done.4.two_off = bf16[64,1024]{1,0:T(8,128)(2,1)S(1)} collective-permute-done((bf16[64,1024]{1,0:T(8,128)(2,1)S(1)}, bf16[64,1024]{1,0:T(8,128)(2,1)S(1)}, u32[]{:S(2)}, u32[]{:S(2)}) %collective-permute-start.4) | collective-permute-done | bytes 131104 | tf_op jit(solution)/shard_map/ppermute | solution.py:245
  18.6 0.7 %shard_map.64.two = f32[128,1152]{1,0:T(8,128)S(1)} custom-call(bf16[256,1024]{1,0:T(8,128)(2,1)S(1)} %get-tuple-element.29.turned, bf16[64,1024]{1,0:T(8,128)(2,1)S(1)} %collective-permute-done.4.two_off), custom_call_target="tpu_custom_call" | custom-call | flops 2717908992 | tf_op jit(solution)/shard_map/pallas_call | solution.py:257
  19.4 1.0 %shard_map.65 = (f32[32,1728]{1,0:T(8,128)S(1)}, bf16[32,1728]{1,0:T(8,128)(2,1)S(1)}, bf16[32,1728]{1,0:T(8,128)(2,1)S(1)}, bf16[32,1728]{1,0:T(8,128)(2,1)S(1)}) custom-call(bf16[256,1024]{1,0:T(8,128)(2,1)S(1)} %get-tuple-element.29.turned, bf16[1088,384]{1,0:T(8,128)(2,1)S(1)} %get-tuple-element.32.windows, f32[128,1152]{1,0:T(8,128)S(1)} %shard_map.64.two, ...), custom_call_target="tpu_custom_call" | custom-call | flops 2717908992 | bytes 4194304 | tf_op jit(solution)/shard_map/pallas_call | solution.py:273
  20.4 2.7 %collective-permute-start.5 = (bf16[32,1728]{1,0:T(8,128)(2,1)S(1)}, bf16[32,1728]{1,0:T(8,128)(2,1)S(1)}, u32[]{:S(2)}, u32[]{:S(2)}) collective-permute-start(bf16[32,1728]{1,0:T(8,128)(2,1)S(1)} %get-tuple-element.36), channel_id=1, source_target_pairs={{0,16},{4,20},{8,24},{12,28},{16,0},{20,4},{24,8},{28,12},{1,17},{... | collective-permute-start | bytes 331784 | tf_op jit(solution)/shard_map/ppermute | solution.py:196
  23.1 0.0 collective-permute-start.6
  23.1 1.8 %collective-permute-start.7 = (bf16[32,1728]{1,0:T(8,128)(2,1)S(1)}, bf16[32,1728]{1,0:T(8,128)(2,1)S(1)}, u32[]{:S(2)}, u32[]{:S(2)}) collective-permute-start(bf16[32,1728]{1,0:T(8,128)(2,1)S(1)} %get-tuple-element.38), channel_id=1, source_target_pairs={{0,24},{4,28},{8,16},{12,20},{16,8},{20,12},{24,0},{28,4},{1,25},{... | collective-permute-start | bytes 331784 | tf_op jit(solution)/shard_map/ppermute | solution.py:196
  24.9 0.0 collective-permute-done.8.came
  24.9 1.6 %collective-permute-start.9 = (bf16[256,256]{1,0:T(8,128)(2,1)S(1)}, bf16[256,256]{1,0:T(8,128)(2,1)S(1)}, u32[]{:S(2)}, u32[]{:S(2)}) collective-permute-start(bf16[256,256]{1,0:T(8,128)(2,1)S(1)} %get-tuple-element.43), channel_id=1, source_target_pairs={{0,2},{1,3},{2,0},{3,1},{4,6},{5,7},{6,4},{7,5},{8,10},{9,11},{10,... | collective-permute-start | bytes 393224 | tf_op jit(solution)/shard_map/ppermute | solution.py:196
  26.5 5.7 %collective-permute-done.5.rest_0_ = bf16[32,1728]{1,0:T(8,128)(2,1)S(1)} collective-permute-done((bf16[32,1728]{1,0:T(8,128)(2,1)S(1)}, bf16[32,1728]{1,0:T(8,128)(2,1)S(1)}, u32[]{:S(2)}, u32[]{:S(2)}) %collective-permute-start.5) | collective-permute-done | bytes 110624 | tf_op jit(solution)/shard_map/ppermute | solution.py:196
  32.2 0.0 collective-permute-done.6.rest_1_
  32.2 0.0 collective-permute-done.7.rest_2_
  32.2 0.1 shard_map.66.summed
  32.3 0.0 collective-permute-done.9.came
  32.3 0.9 %shard_map.68 = (f32[27,32,64]{2,1,0:T(8,128)}, bf16[256,256]{1,0:T(8,128)(2,1)}) custom-call(f32[32,1728]{1,0:T(8,128)S(1)} %shard_map.66.summed, f32[256,256]{1,0:T(8,128)S(1)} %get-tuple-element.42.kept, bf16[256,256]{1,0:T(8,128)(2,1)S(1)} %collective-permute-done.9.came), custom_call_target="tpu_custom_call" | custom-call | tf_op jit(solution)/shard_map/pallas_call | solution.py:305
  (1 shorter events, 0.0 us)
Async XLA Ops:
  0.6 1.0 %copy-start.3 = (bf16[1,32,32,256]{3,2,1,0:T(8,128)(2,1)S(1)}, bf16[1,32,32,256]{3,2,1,0:T(8,128)(2,1)}, u32[]{:S(2)}) copy-start(bf16[1,32,32,256]{3,2,1,0:T(8,128)(2,1)} %param.4) | copy-start | bytes 1572868
  1.7 0.9 %copy-start = (bf16[1,64,1024]{2,1,0:T(8,128)(2,1)S(1)}, bf16[1,64,1024]{2,1,0:T(8,128)(2,1)}, u32[]{:S(2)}) copy-start(bf16[1,64,1024]{2,1,0:T(8,128)(2,1)} %param.5) | copy-start | bytes 393220
  1.7 1.0 %copy-start.1 = (bf16[1,64,1024]{2,1,0:T(8,128)(2,1)S(1)}, bf16[1,64,1024]{2,1,0:T(8,128)(2,1)}, u32[]{:S(2)}) copy-start(bf16[1,64,1024]{2,1,0:T(8,128)(2,1)} %param.6) | copy-start | bytes 393220
  1.7 9.1 %copy-start.2 = (bf16[27,64,256]{2,1,0:T(8,128)(2,1)S(1)}, bf16[27,64,256]{2,1,0:T(8,128)(2,1)}, u32[]{:S(2)}) copy-start(bf16[27,64,256]{2,1,0:T(8,128)(2,1)} %weight) | copy-start | bytes 2654212
  2.7 8.0 %collective-permute-start = (bf16[64,1024]{1,0:T(8,128)(2,1)S(1)}, bf16[64,1024]{1,0:T(8,128)(2,1)S(1)}, u32[]{:S(2)}, u32[]{:S(2)}) collective-permute-start(bf16[64,1024]{1,0:T(8,128)(2,1)S(1)} %get-tuple-element.26._), channel_id=1, source_target_pairs={{0,4},{4,0},{8,12},{12,8},{16,20},{20,16},{24,28},{28,24},{1,5},{5... | collective-permute-start | bytes 393224 | tf_op jit(solution)/shard_map/ppermute | solution.py:196
  5.7 8.4 %collective-permute-start.3 = (bf16[64,1024]{1,0:T(8,128)(2,1)S(1)}, bf16[64,1024]{1,0:T(8,128)(2,1)S(1)}, u32[]{:S(2)}, u32[]{:S(2)}) collective-permute-start(bf16[64,1024]{1,0:T(8,128)(2,1)S(1)} %shard_map.60.own), channel_id=1, source_target_pairs={{4,8},{12,16},{20,24},{8,4},{16,12},{24,20},{5,9},{13,17},{21,25},... | collective-permute-start | bytes 393224 | tf_op jit(solution)/shard_map/ppermute | solution.py:247
  6.4 7.8 %collective-permute-start.2 = (bf16[64,1024]{1,0:T(8,128)(2,1)S(1)}, bf16[64,1024]{1,0:T(8,128)(2,1)S(1)}, u32[]{:S(2)}, u32[]{:S(2)}) collective-permute-start(bf16[64,1024]{1,0:T(8,128)(2,1)S(1)} %shard_map.60.own), channel_id=1, source_target_pairs={{0,4},{4,0},{8,12},{12,8},{16,20},{20,16},{24,28},{28,24},{1,5},{5... | collective-permute-start | bytes 393224 | tf_op jit(solution)/shard_map/ppermute | solution.py:196
  10.8 1.4 %collective-permute-start.1 = (bf16[64,1024]{1,0:T(8,128)(2,1)S(1)}, bf16[64,1024]{1,0:T(8,128)(2,1)S(1)}, u32[]{:S(2)}, u32[]{:S(2)}) collective-permute-start(bf16[64,1024]{1,0:T(8,128)(2,1)S(1)} %collective-permute-done.came), channel_id=1, source_target_pairs={{0,1},{1,0},{2,3},{3,2},{4,5},{5,4},{6,7},{7,6},{8,9},{9,8},{10,11... | collective-permute-start | bytes 393224 | tf_op jit(solution)/shard_map/ppermute | solution.py:196
  10.8 7.8 %collective-permute-start.4 = (bf16[64,1024]{1,0:T(8,128)(2,1)S(1)}, bf16[64,1024]{1,0:T(8,128)(2,1)S(1)}, u32[]{:S(2)}, u32[]{:S(2)}) collective-permute-start(bf16[64,1024]{1,0:T(8,128)(2,1)S(1)} %shard_map.60.own), channel_id=1, source_target_pairs={{8,0},{16,8},{24,16},{4,12},{12,20},{20,28},{9,1},{17,9},{25,17},{... | collective-permute-start | bytes 393224 | tf_op jit(solution)/shard_map/ppermute | solution.py:245
  15.4 9.4 %collective-permute-start.8 = (bf16[512,256]{1,0:T(8,128)(2,1)S(1)}, bf16[512,256]{1,0:T(8,128)(2,1)S(1)}, u32[]{:S(2)}, u32[]{:S(2)}) collective-permute-start(bf16[512,256]{1,0:T(8,128)(2,1)S(1)} %get-tuple-element.40), channel_id=1, source_target_pairs={{0,1},{1,0},{2,3},{3,2},{4,5},{5,4},{6,7},{7,6},{8,9},{9,8},{10,11... | collective-permute-start | bytes 786440 | tf_op jit(solution)/shard_map/ppermute | solution.py:196
  20.4 11.8 %collective-permute-start.5 = (bf16[32,1728]{1,0:T(8,128)(2,1)S(1)}, bf16[32,1728]{1,0:T(8,128)(2,1)S(1)}, u32[]{:S(2)}, u32[]{:S(2)}) collective-permute-start(bf16[32,1728]{1,0:T(8,128)(2,1)S(1)} %get-tuple-element.36), channel_id=1, source_target_pairs={{0,16},{4,20},{8,24},{12,28},{16,0},{20,4},{24,8},{28,12},{1,17},{... | collective-permute-start | bytes 331784 | tf_op jit(solution)/shard_map/ppermute | solution.py:196
  23.1 9.1 %collective-permute-start.6 = (bf16[32,1728]{1,0:T(8,128)(2,1)S(1)}, bf16[32,1728]{1,0:T(8,128)(2,1)S(1)}, u32[]{:S(2)}, u32[]{:S(2)}) collective-permute-start(bf16[32,1728]{1,0:T(8,128)(2,1)S(1)} %get-tuple-element.37), channel_id=1, source_target_pairs={{0,8},{4,12},{8,0},{12,4},{16,24},{20,28},{24,16},{28,20},{1,9},{5... | collective-permute-start | bytes 331784 | tf_op jit(solution)/shard_map/ppermute | solution.py:196
  23.1 9.1 %collective-permute-start.7 = (bf16[32,1728]{1,0:T(8,128)(2,1)S(1)}, bf16[32,1728]{1,0:T(8,128)(2,1)S(1)}, u32[]{:S(2)}, u32[]{:S(2)}) collective-permute-start(bf16[32,1728]{1,0:T(8,128)(2,1)S(1)} %get-tuple-element.38), channel_id=1, source_target_pairs={{0,24},{4,28},{8,16},{12,20},{16,8},{20,12},{24,0},{28,4},{1,25},{... | collective-permute-start | bytes 331784 | tf_op jit(solution)/shard_map/ppermute | solution.py:196
  24.9 7.4 %collective-permute-start.9 = (bf16[256,256]{1,0:T(8,128)(2,1)S(1)}, bf16[256,256]{1,0:T(8,128)(2,1)S(1)}, u32[]{:S(2)}, u32[]{:S(2)}) collective-permute-start(bf16[256,256]{1,0:T(8,128)(2,1)S(1)} %get-tuple-element.43), channel_id=1, source_target_pairs={{0,2},{1,3},{2,0},{3,1},{4,6},{5,7},{6,4},{7,5},{8,10},{9,11},{10,... | collective-permute-start | bytes 393224 | tf_op jit(solution)/shard_map/ppermute | solution.py:196

commit v9 on v7

--- a/solution.py
+++ b/solution.py
@@ -8,7 +8,7 @@
 from jax.sharding import PartitionSpec as P
 
 MIB = 1 << 20
-TURN, EARLY, TWO, SPREAD, LATE, FINAL, ORDER = 3, 3, 3, 3, 3, 3, 3
+PICK, TURN, EARLY, TWO, SPREAD, LATE, FINAL, ORDER = 3, 1, 3, 3, 3, 3, 3, 3
 VMEM = pl.BlockSpec(memory_space=pltpu.VMEM)
 
 
@@ -51,23 +51,27 @@
     windows[body, 2 * lanes : 3 * lanes] = jnp.where(column != 0, tall[pl.ds(7, cells), :], 0.0).astype(jnp.bfloat16)
 
 
-def turn_kernel(blocks, inputs, mine, part):
-    chans = inputs.shape[1]
+def pick_kernel(blocks, picked):
+    size, chans = picked.shape
     rows = chans // blocks
-    half, quarter = mine.shape[0], part.shape[0]
+    half = chans // 2
     count = bits_of(blocks)
-    order = lax.broadcasted_iota(jnp.int32, (half + quarter, chans), 0)
-    order = order + jnp.where(order >= half, (lax.axis_index("filt") & 1) * quarter, 0)
+    order = lax.broadcasted_iota(jnp.int32, (size, chans), 0)
+    order = order + jnp.where(order >= half, (lax.axis_index("filt") & 1) * (size - half), 0)
     block = lax.axis_index("space") ^ reversed_bits(order >> bits_of(rows), count)
     source = (block << bits_of(rows)) | (order & (rows - 1))
-    picked = (lax.broadcasted_iota(jnp.int32, (half + quarter, chans), 1) == source).astype(jnp.bfloat16)
-    turned = lax.dot_general(picked, inputs[...], (((1,), (1,)), ((), ())), preferred_element_type=jnp.float32)
+    picked[...] = (lax.broadcasted_iota(jnp.int32, (size, chans), 1) == source).astype(jnp.bfloat16)
+
+
+def turn_kernel(picked, inputs, _, mine, part):
+    half = mine.shape[0]
+    turned = lax.dot_general(picked[...], inputs[...], (((1,), (1,)), ((), ())), preferred_element_type=jnp.float32)
     turned = turned.astype(jnp.bfloat16)
     mine[...] = turned[0:half, :]
     part[...] = turned[half:, :]
 
 
-def grads_kernel(out_grad, pre_act, _, own):
+def grads_kernel(out_grad, pre_act, own):
     own[...] = (out_grad[...].astype(jnp.float32) * silu_grad(pre_act[...].astype(jnp.float32))).astype(own.dtype)
 
 
@@ -181,14 +185,21 @@
     out[...] = total * scale
 
 
-def last_kernel(filt, summed, kept, came, out, grad_input):
-    grad_input[...] = (kept[...] + came[...].astype(jnp.float32)).astype(grad_input.dtype)
+def last_kernel(filt, summed, kept, came, out, grad_input, taps, rows, done):
     odd = lax.axis_index("space") & 1
+    rows[...] = (kept[...] + came[...].astype(jnp.float32)).astype(rows.dtype)
+    copies = [pltpu.make_async_copy(rows, grad_input, done.at[3])]
+    copies[0].start()
     total = summed[...]
-    for tap in range(9):
-        slots = ((18 + tap, 9 + tap), (2 * tap, 18 * odd + tap), (2 * tap + 1, 18 - 18 * odd + tap))
-        for slot, target in slots:
-            out[target] = total[:, slot * filt : (slot + 1) * filt]
+    for group, (first, step, target) in enumerate(((18, 1, 1), (0, 2, 2 * odd), (1, 2, 2 - 2 * odd))):
+        for tap in range(9):
+            slot = first + step * tap
+            taps[group, tap] = total[:, slot * filt : (slot + 1) * filt]
+        copy = pltpu.make_async_copy(taps.at[group], out.at[pl.ds(target * 9, 9)], done.at[group])
+        copy.start()
+        copies.append(copy)
+    for copy in copies:
+        copy.wait()
 
 
 def swapped(value, axis, distance):
@@ -227,20 +238,22 @@
     windows_shape = shape((cells + 2 * width, lanes), bf16)
     tall = pltpu.VMEM((cells + 16, 2 * filt), f32)
 
+    picked = call(
+        functools.partial(pick_kernel, blocks), shape((half + quarter, chans), bf16), flops=PICK * flops
+    )(in_specs=[], out_specs=VMEM)()
+    own = call(grads_kernel, shape((filt, cells), bf16))(in_specs=[VMEM] * 2, out_specs=VMEM)(out_grad[0], pre_act[0])
     mine, part = call(
-        functools.partial(turn_kernel, blocks),
+        turn_kernel,
         (shape((half, cells), bf16), shape((quarter, cells), bf16)),
         flops=TURN * flops,
-    )(in_specs=[VMEM], out_specs=[VMEM] * 2)(inputs.reshape(cells, chans))
-    own = call(grads_kernel, shape((filt, cells), bf16))(in_specs=[VMEM] * 3, out_specs=VMEM)(
-        out_grad[0], pre_act[0], part
-    )
-    came = swapped(after(part, own), "space", 1)
-    near = swapped(own, "space", 1)
-    two_pairs = [(i, i - 2) for i in range(2, blocks, 2)] + [(i, i + 2) for i in range(1, blocks - 2, 2)]
-    two_off = lax.ppermute(own, "space", two_pairs)
+    )(in_specs=[VMEM] * 3, out_specs=[VMEM] * 2)(picked, inputs.reshape(cells, chans), own)
+    came = swapped(part, "space", 1)
     one_pairs = [(i, i + 1) for i in range(1, blocks - 1, 2)]
     one_off = lax.ppermute(own, "space", one_pairs + [(target, source) for source, target in one_pairs])
+    later = after(own, mine)
+    near = swapped(later, "space", 1)
+    two_pairs = [(i, i - 2) for i in range(2, blocks, 2)] + [(i, i + 2) for i in range(1, blocks - 2, 2)]
+    two_off = lax.ppermute(later, "space", two_pairs)
     other = swapped(came, "filt", 1)
 
     weight_shape = shape((3, lanes, chans), bf16)
@@ -302,10 +315,17 @@
     summed = call(
         functools.partial(sum_kernel, grad_scale), shape((chans // blocks, taps * filt), f32), flops=FINAL * flops
     )(in_specs=[VMEM] * (len(arrived) + 1), out_specs=VMEM)(kept, *arrived)
+    any_space = pl.BlockSpec(memory_space=pl.ANY)
+    rows_shape = (cells // groups, chans)
     grad_weight, grad_input = call(
         functools.partial(last_kernel, filt),
-        (shape((taps, chans // blocks, filt), f32), shape((cells // groups, chans), bf16)),
-    )(in_specs=[VMEM] * 3, out_specs=[VMEM] * 2)(summed, kept_in, came_in)
+        (shape((taps, chans // blocks, filt), f32), shape(rows_shape, bf16)),
+        (
+            pltpu.VMEM((3, 9, chans // blocks, filt), f32),
+            pltpu.VMEM(rows_shape, bf16),
+            pltpu.SemaphoreType.DMA((4,)),
+        ),
+    )(in_specs=[VMEM] * 3, out_specs=[any_space] * 2)(summed, kept_in, came_in)
     return grad_input.reshape(1, height // groups, width, chans), jnp.transpose(grad_weight, (1, 0, 2))
 
 

time: 34.6 us -> 33.8 us (0.977)
  waiting for transfers between devices: 8.33 us -> 7.6 us
  starting transfers between devices: 17.1 us -> 17.8 us
  local copies, waits for them, and re-layouts: 1.67 us -> 0.99 us
    ppermute x8, waiting for transfers between devices: 8.32 us -> 7.6 us  [swapped(): return lax.ppermute(value, axis, [(i, i ^ distance) for i in range(count)])]
    ppermute x8, starting transfers between devices: 15.1 us -> 15.8 us  [swapped(): return lax.ppermute(value, axis, [(i, i ^ distance) for i in range(count)])]
    unnamed x8, local copies, waits for them, and re-layouts: 1.67 us -> 0.99 us
  transfers between devices with their start and end apart: 10 -> 10, of which waited for: 5 -> 3; matrix products, arithmetic and copies ran while one was open for 0% -> 0% of each run, Pallas kernels for 11% -> 12%
where the time goes in v9:
time: 33.8 us; the launch traced here: 33.7 us
  starting transfers between devices  17.8 us (53%)
  waiting for transfers between devices  7.6 us (22%)
  Pallas kernels  6.53 us (19%)
  local copies, waits for them, and re-layouts  0.99 us (3%)
  between operations  0.77 us (2%)
    ppermute x8, starting transfers between devices, swapped(): return lax.ppermute(value, axis, [(i, i ^ distance) for i in range(count)])  15.8 us
    ppermute x8, waiting for transfers between devices, swapped(): return lax.ppermute(value, axis, [(i, i ^ distance) for i in range(count)])  7.6 us
    pallas_call x1, Pallas kernels, on_device(): call(functools.partial(early_kernel, width), (shape((chans, cells), bf16)...  1.96 us
    ppermute x1, starting transfers between devices, on_device(): two_off = lax.ppermute(later, 'space', two_pairs)  1.29 us
    pallas_call x1, Pallas kernels, on_device(): call(functools.partial(spread_kernel, width, groups), (windows_shape, sha...  1.23 us
    pallas_call x1, Pallas kernels, on_device(): call(functools.partial(late_kernel, width), (shape((piece, taps * filt),...  1.03 us
    unnamed x8, local copies, waits for them, and re-layouts  0.99 us
    pallas_call x1, Pallas kernels, on_device(): call(functools.partial(last_kernel, filt), (shape((taps, chans // blocks,...  0.9 us
  transfers between devices with their start and end apart: 10, of which 3 were waited for; matrix products, arithmetic and copies ran while one was open for 0% of the time, Pallas kernels for 12%

profile of v9, /device:TPU:0, one launch (start us, length us, event | category | flops | bytes accessed | tf_op | source)
XLA Modules:
  0.0 33.7 jit_solution(16774394574346039685)
XLA Ops:
  0.6 0.0 copy-start.1
  0.6 0.0 copy-start
  0.6 0.0 copy-start.3
  0.7 0.1 shard_map.60.picked
  0.7 0.8 %copy-done.1 = bf16[1,64,1024]{2,1,0:T(8,128)(2,1)S(1)} copy-done((bf16[1,64,1024]{2,1,0:T(8,128)(2,1)S(1)}, bf16[1,64,1024]{2,1,0:T(8,128)(2,1)}, u32[]{:S(2)}) %copy-start.1) | copy-done | bytes 131096
  1.5 0.1 copy-done
  1.6 0.1 shard_map.59._.own
  1.7 0.1 copy-done.3
  1.8 0.0 copy-start.2
  1.8 0.3 shard_map.61
  2.1 3.0 %collective-permute-start = (bf16[64,1024]{1,0:T(8,128)(2,1)S(1)}, bf16[64,1024]{1,0:T(8,128)(2,1)S(1)}, u32[]{:S(2)}, u32[]{:S(2)}) collective-permute-start(bf16[64,1024]{1,0:T(8,128)(2,1)S(1)} %get-tuple-element.25), channel_id=1, source_target_pairs={{0,4},{4,0},{8,12},{12,8},{16,20},{20,16},{24,28},{28,24},{1,5},{5... | collective-permute-start | bytes 393224 | tf_op jit(solution)/shard_map/ppermute | solution.py:207
  5.2 0.7 %collective-permute-start.3 = (bf16[64,1024]{1,0:T(8,128)(2,1)S(1)}, bf16[64,1024]{1,0:T(8,128)(2,1)S(1)}, u32[]{:S(2)}, u32[]{:S(2)}) collective-permute-start(bf16[64,1024]{1,0:T(8,128)(2,1)S(1)} %shard_map.59._.own), channel_id=1, source_target_pairs={{4,8},{12,16},{20,24},{8,4},{16,12},{24,20},{5,9},{13,17},{21,25},... | collective-permute-start | bytes 393224 | tf_op jit(solution)/shard_map/ppermute | solution.py:252
  5.8 1.3 %collective-permute-start.4 = (bf16[64,1024]{1,0:T(8,128)(2,1)S(1)}, bf16[64,1024]{1,0:T(8,128)(2,1)S(1)}, u32[]{:S(2)}, u32[]{:S(2)}) collective-permute-start(bf16[64,1024]{1,0:T(8,128)(2,1)S(1)} %shard_map.59._.own), channel_id=1, source_target_pairs={{8,0},{16,8},{24,16},{4,12},{12,20},{20,28},{9,1},{17,9},{25,17},{... | collective-permute-start | bytes 393224 | tf_op jit(solution)/shard_map/ppermute | solution.py:256
  7.1 6.5 %collective-permute-start.2 = (bf16[64,1024]{1,0:T(8,128)(2,1)S(1)}, bf16[64,1024]{1,0:T(8,128)(2,1)S(1)}, u32[]{:S(2)}, u32[]{:S(2)}) collective-permute-start(bf16[64,1024]{1,0:T(8,128)(2,1)S(1)} %shard_map.59._.own), channel_id=1, source_target_pairs={{0,4},{4,0},{8,12},{12,8},{16,20},{20,16},{24,28},{28,24},{1,5},{5... | collective-permute-start | bytes 393224 | tf_op jit(solution)/shard_map/ppermute | solution.py:207
  13.7 0.0 collective-permute-done.came
  13.7 0.0 collective-permute-start.1
  13.7 0.0 copy-done.2
  13.7 0.1 shard_map.62
  13.8 1.3 %collective-permute-done.1.other = bf16[64,1024]{1,0:T(8,128)(2,1)S(1)} collective-permute-done((bf16[64,1024]{1,0:T(8,128)(2,1)S(1)}, bf16[64,1024]{1,0:T(8,128)(2,1)S(1)}, u32[]{:S(2)}, u32[]{:S(2)}) %collective-permute-start.1) | collective-permute-done | bytes 131104 | tf_op jit(solution)/shard_map/ppermute | solution.py:207
  15.0 2.0 %shard_map.63 = (bf16[256,1024]{1,0:T(8,128)(2,1)S(1)}, f32[256,1152]{1,0:T(8,128)S(1)}, f32[1024,256]{1,0:T(8,128)S(1)}) custom-call(bf16[64,1024]{1,0:T(8,128)(2,1)S(1)} %shard_map.59._.own, bf16[128,1024]{1,0:T(8,128)(2,1)S(1)} %get-tuple-element.24.mine, bf16[64,1024]{1,0:T(8,128)(2,1)S(1)} %collective-permute-done.came, ...), custom_call_target="tpu_custom_call" | custom-call | flops 2717908992 | bytes 4194304 | tf_op jit(solution)/shard_map/pallas_call | solution.py:263
  17.0 0.0 collective-permute-done.4.two_off
  17.0 0.7 %shard_map.64.two = f32[128,1152]{1,0:T(8,128)S(1)} custom-call(bf16[256,1024]{1,0:T(8,128)(2,1)S(1)} %get-tuple-element.28.turned, bf16[64,1024]{1,0:T(8,128)(2,1)S(1)} %collective-permute-done.4.two_off), custom_call_target="tpu_custom_call" | custom-call | flops 2717908992 | tf_op jit(solution)/shard_map/pallas_call | solution.py:270
  17.7 0.0 collective-permute-done.3.one_off
  17.7 0.0 collective-permute-done.2.near
  17.8 1.2 %shard_map.65 = (bf16[1088,384]{1,0:T(8,128)(2,1)S(1)}, f32[512,256]{1,0:T(8,128)S(1)}, bf16[512,256]{1,0:T(8,128)(2,1)S(1)}) custom-call(bf16[64,1024]{1,0:T(8,128)(2,1)S(1)} %collective-permute-done.2.near, bf16[64,1024]{1,0:T(8,128)(2,1)S(1)} %collective-permute-done.3.one_off, bf16[3,384,256]{2,1,0:T(8,128)(2,1)S(1)} %get-tuple-element.30.weight, ...), custom_call_target="tpu_custom_call" | custom-call | flops 2717908992 | bytes 4194304 | tf_op jit(solution)/shard_map/pallas_call | solution.py:276
  19.0 0.2 collective-permute-start.8
  19.2 1.0 %shard_map.66 = (f32[32,1728]{1,0:T(8,128)S(1)}, bf16[32,1728]{1,0:T(8,128)(2,1)S(1)}, bf16[32,1728]{1,0:T(8,128)(2,1)S(1)}, bf16[32,1728]{1,0:T(8,128)(2,1)S(1)}) custom-call(bf16[256,1024]{1,0:T(8,128)(2,1)S(1)} %get-tuple-element.28.turned, bf16[1088,384]{1,0:T(8,128)(2,1)S(1)} %get-tuple-element.33.windows, f32[128,1152]{1,0:T(8,128)S(1)} %shard_map.64.two, ...), custom_call_target="tpu_custom_call" | custom-call | flops 2717908992 | bytes 4194304 | tf_op jit(solution)/shard_map/pallas_call | solution.py:286
  20.2 1.1 %collective-permute-start.5 = (bf16[32,1728]{1,0:T(8,128)(2,1)S(1)}, bf16[32,1728]{1,0:T(8,128)(2,1)S(1)}, u32[]{:S(2)}, u32[]{:S(2)}) collective-permute-start(bf16[32,1728]{1,0:T(8,128)(2,1)S(1)} %get-tuple-element.36), channel_id=1, source_target_pairs={{0,16},{4,20},{8,24},{12,28},{16,0},{20,4},{24,8},{28,12},{1,17},{... | collective-permute-start | bytes 331784 | tf_op jit(solution)/shard_map/ppermute | solution.py:207
  21.3 0.9 %collective-permute-start.6 = (bf16[32,1728]{1,0:T(8,128)(2,1)S(1)}, bf16[32,1728]{1,0:T(8,128)(2,1)S(1)}, u32[]{:S(2)}, u32[]{:S(2)}) collective-permute-start(bf16[32,1728]{1,0:T(8,128)(2,1)S(1)} %get-tuple-element.37), channel_id=1, source_target_pairs={{0,8},{4,12},{8,0},{12,4},{16,24},{20,28},{24,16},{28,20},{1,9},{5... | collective-permute-start | bytes 331784 | tf_op jit(solution)/shard_map/ppermute | solution.py:207
  22.3 2.4 %collective-permute-start.7 = (bf16[32,1728]{1,0:T(8,128)(2,1)S(1)}, bf16[32,1728]{1,0:T(8,128)(2,1)S(1)}, u32[]{:S(2)}, u32[]{:S(2)}) collective-permute-start(bf16[32,1728]{1,0:T(8,128)(2,1)S(1)} %get-tuple-element.38), channel_id=1, source_target_pairs={{0,24},{4,28},{8,16},{12,20},{16,8},{20,12},{24,0},{28,4},{1,25},{... | collective-permute-start | bytes 331784 | tf_op jit(solution)/shard_map/ppermute | solution.py:207
  24.7 0.0 collective-permute-done.8.came
  24.8 1.6 %collective-permute-start.9 = (bf16[256,256]{1,0:T(8,128)(2,1)S(1)}, bf16[256,256]{1,0:T(8,128)(2,1)S(1)}, u32[]{:S(2)}, u32[]{:S(2)}) collective-permute-start(bf16[256,256]{1,0:T(8,128)(2,1)S(1)} %get-tuple-element.43), channel_id=1, source_target_pairs={{0,2},{1,3},{2,0},{3,1},{4,6},{5,7},{6,4},{7,5},{8,10},{9,11},{10,... | collective-permute-start | bytes 393224 | tf_op jit(solution)/shard_map/ppermute | solution.py:207
  26.4 3.4 %collective-permute-done.5.rest_0_ = bf16[32,1728]{1,0:T(8,128)(2,1)S(1)} collective-permute-done((bf16[32,1728]{1,0:T(8,128)(2,1)S(1)}, bf16[32,1728]{1,0:T(8,128)(2,1)S(1)}, u32[]{:S(2)}, u32[]{:S(2)}) %collective-permute-start.5) | collective-permute-done | bytes 110624 | tf_op jit(solution)/shard_map/ppermute | solution.py:207
  29.8 0.0 collective-permute-done.6.rest_1_
  29.8 2.9 %collective-permute-done.7.rest_2_ = bf16[32,1728]{1,0:T(8,128)(2,1)S(1)} collective-permute-done((bf16[32,1728]{1,0:T(8,128)(2,1)S(1)}, bf16[32,1728]{1,0:T(8,128)(2,1)S(1)}, u32[]{:S(2)}, u32[]{:S(2)}) %collective-permute-start.7) | collective-permute-done | bytes 110624 | tf_op jit(solution)/shard_map/ppermute | solution.py:207
  32.7 0.1 shard_map.67.summed
  32.7 0.0 collective-permute-done.9.came
  32.8 0.9 %shard_map.69 = (f32[27,32,64]{2,1,0:T(8,128)}, bf16[256,256]{1,0:T(8,128)(2,1)}) custom-call(f32[32,1728]{1,0:T(8,128)S(1)} %shard_map.67.summed, f32[256,256]{1,0:T(8,128)S(1)} %get-tuple-element.42.kept, bf16[256,256]{1,0:T(8,128)(2,1)S(1)} %collective-permute-done.9.came), custom_call_target="tpu_custom_call" | custom-call | tf_op jit(solution)/shard_map/pallas_call | solution.py:320
  (1 shorter events, 0.0 us)
Async XLA Ops:
  0.6 0.9 %copy-start.1 = (bf16[1,64,1024]{2,1,0:T(8,128)(2,1)S(1)}, bf16[1,64,1024]{2,1,0:T(8,128)(2,1)}, u32[]{:S(2)}) copy-start(bf16[1,64,1024]{2,1,0:T(8,128)(2,1)} %param.6) | copy-start | bytes 393220
  0.6 1.0 %copy-start = (bf16[1,64,1024]{2,1,0:T(8,128)(2,1)S(1)}, bf16[1,64,1024]{2,1,0:T(8,128)(2,1)}, u32[]{:S(2)}) copy-start(bf16[1,64,1024]{2,1,0:T(8,128)(2,1)} %param.5) | copy-start | bytes 393220
  0.6 1.2 %copy-start.3 = (bf16[1,32,32,256]{3,2,1,0:T(8,128)(2,1)S(1)}, bf16[1,32,32,256]{3,2,1,0:T(8,128)(2,1)}, u32[]{:S(2)}) copy-start(bf16[1,32,32,256]{3,2,1,0:T(8,128)(2,1)} %param.4) | copy-start | bytes 1572868
  1.8 11.9 %copy-start.2 = (bf16[27,64,256]{2,1,0:T(8,128)(2,1)S(1)}, bf16[27,64,256]{2,1,0:T(8,128)(2,1)}, u32[]{:S(2)}) copy-start(bf16[27,64,256]{2,1,0:T(8,128)(2,1)} %weight) | copy-start | bytes 2654212
  2.1 11.5 %collective-permute-start = (bf16[64,1024]{1,0:T(8,128)(2,1)S(1)}, bf16[64,1024]{1,0:T(8,128)(2,1)S(1)}, u32[]{:S(2)}, u32[]{:S(2)}) collective-permute-start(bf16[64,1024]{1,0:T(8,128)(2,1)S(1)} %get-tuple-element.25), channel_id=1, source_target_pairs={{0,4},{4,0},{8,12},{12,8},{16,20},{20,16},{24,28},{28,24},{1,5},{5... | collective-permute-start | bytes 393224 | tf_op jit(solution)/shard_map/ppermute | solution.py:207
  5.2 12.6 %collective-permute-start.3 = (bf16[64,1024]{1,0:T(8,128)(2,1)S(1)}, bf16[64,1024]{1,0:T(8,128)(2,1)S(1)}, u32[]{:S(2)}, u32[]{:S(2)}) collective-permute-start(bf16[64,1024]{1,0:T(8,128)(2,1)S(1)} %shard_map.59._.own), channel_id=1, source_target_pairs={{4,8},{12,16},{20,24},{8,4},{16,12},{24,20},{5,9},{13,17},{21,25},... | collective-permute-start | bytes 393224 | tf_op jit(solution)/shard_map/ppermute | solution.py:252
  5.8 11.2 %collective-permute-start.4 = (bf16[64,1024]{1,0:T(8,128)(2,1)S(1)}, bf16[64,1024]{1,0:T(8,128)(2,1)S(1)}, u32[]{:S(2)}, u32[]{:S(2)}) collective-permute-start(bf16[64,1024]{1,0:T(8,128)(2,1)S(1)} %shard_map.59._.own), channel_id=1, source_target_pairs={{8,0},{16,8},{24,16},{4,12},{12,20},{20,28},{9,1},{17,9},{25,17},{... | collective-permute-start | bytes 393224 | tf_op jit(solution)/shard_map/ppermute | solution.py:256
  7.1 10.6 %collective-permute-start.2 = (bf16[64,1024]{1,0:T(8,128)(2,1)S(1)}, bf16[64,1024]{1,0:T(8,128)(2,1)S(1)}, u32[]{:S(2)}, u32[]{:S(2)}) collective-permute-start(bf16[64,1024]{1,0:T(8,128)(2,1)S(1)} %shard_map.59._.own), channel_id=1, source_target_pairs={{0,4},{4,0},{8,12},{12,8},{16,20},{20,16},{24,28},{28,24},{1,5},{5... | collective-permute-start | bytes 393224 | tf_op jit(solution)/shard_map/ppermute | solution.py:207
  13.7 1.3 %collective-permute-start.1 = (bf16[64,1024]{1,0:T(8,128)(2,1)S(1)}, bf16[64,1024]{1,0:T(8,128)(2,1)S(1)}, u32[]{:S(2)}, u32[]{:S(2)}) collective-permute-start(bf16[64,1024]{1,0:T(8,128)(2,1)S(1)} %collective-permute-done.came), channel_id=1, source_target_pairs={{0,1},{1,0},{2,3},{3,2},{4,5},{5,4},{6,7},{7,6},{8,9},{9,8},{10,11... | collective-permute-start | bytes 393224 | tf_op jit(solution)/shard_map/ppermute | solution.py:207
  19.0 5.7 %collective-permute-start.8 = (bf16[512,256]{1,0:T(8,128)(2,1)S(1)}, bf16[512,256]{1,0:T(8,128)(2,1)S(1)}, u32[]{:S(2)}, u32[]{:S(2)}) collective-permute-start(bf16[512,256]{1,0:T(8,128)(2,1)S(1)} %get-tuple-element.40), channel_id=1, source_target_pairs={{0,1},{1,0},{2,3},{3,2},{4,5},{5,4},{6,7},{7,6},{8,9},{9,8},{10,11... | collective-permute-start | bytes 786440 | tf_op jit(solution)/shard_map/ppermute | solution.py:207
  20.2 9.6 %collective-permute-start.5 = (bf16[32,1728]{1,0:T(8,128)(2,1)S(1)}, bf16[32,1728]{1,0:T(8,128)(2,1)S(1)}, u32[]{:S(2)}, u32[]{:S(2)}) collective-permute-start(bf16[32,1728]{1,0:T(8,128)(2,1)S(1)} %get-tuple-element.36), channel_id=1, source_target_pairs={{0,16},{4,20},{8,24},{12,28},{16,0},{20,4},{24,8},{28,12},{1,17},{... | collective-permute-start | bytes 331784 | tf_op jit(solution)/shard_map/ppermute | solution.py:207
  21.3 8.5 %collective-permute-start.6 = (bf16[32,1728]{1,0:T(8,128)(2,1)S(1)}, bf16[32,1728]{1,0:T(8,128)(2,1)S(1)}, u32[]{:S(2)}, u32[]{:S(2)}) collective-permute-start(bf16[32,1728]{1,0:T(8,128)(2,1)S(1)} %get-tuple-element.37), channel_id=1, source_target_pairs={{0,8},{4,12},{8,0},{12,4},{16,24},{20,28},{24,16},{28,20},{1,9},{5... | collective-permute-start | bytes 331784 | tf_op jit(solution)/shard_map/ppermute | solution.py:207
  22.3 10.4 %collective-permute-start.7 = (bf16[32,1728]{1,0:T(8,128)(2,1)S(1)}, bf16[32,1728]{1,0:T(8,128)(2,1)S(1)}, u32[]{:S(2)}, u32[]{:S(2)}) collective-permute-start(bf16[32,1728]{1,0:T(8,128)(2,1)S(1)} %get-tuple-element.38), channel_id=1, source_target_pairs={{0,24},{4,28},{8,16},{12,20},{16,8},{20,12},{24,0},{28,4},{1,25},{... | collective-permute-start | bytes 331784 | tf_op jit(solution)/shard_map/ppermute | solution.py:207
  24.8 8.0 %collective-permute-start.9 = (bf16[256,256]{1,0:T(8,128)(2,1)S(1)}, bf16[256,256]{1,0:T(8,128)(2,1)S(1)}, u32[]{:S(2)}, u32[]{:S(2)}) collective-permute-start(bf16[256,256]{1,0:T(8,128)(2,1)S(1)} %get-tuple-element.43), channel_id=1, source_target_pairs={{0,2},{1,3},{2,0},{3,1},{4,6},{5,7},{6,4},{7,5},{8,10},{9,11},{10,... | collective-permute-start | bytes 393224 | tf_op jit(solution)/shard_map/ppermute | solution.py:207

commit v10 on v9

--- a/solution.py
+++ b/solution.py
@@ -8,7 +8,7 @@
 from jax.sharding import PartitionSpec as P
 
 MIB = 1 << 20
-PICK, TURN, EARLY, TWO, SPREAD, LATE, FINAL, ORDER = 3, 1, 3, 3, 3, 3, 3, 3
+PICK, TURN, NEAR, THEIRS, ONE, FINAL, ORDER = 3, 1, 3, 3, 3, 3, 3
 VMEM = pl.BlockSpec(memory_space=pltpu.VMEM)
 
 
@@ -75,39 +75,61 @@
     own[...] = (out_grad[...].astype(jnp.float32) * silu_grad(pre_act[...].astype(jnp.float32))).astype(own.dtype)
 
 
-def order_kernel(weight, early, late):
+def order_kernel(weight, paired, single):
     filt = weight.shape[1]
     odd = lax.axis_index("space") & 1
     for tap in range(9):
         b, c = divmod(tap, 3)
         low, high = pl.ds(2 * c * filt, filt), pl.ds((2 * c + 1) * filt, filt)
-        early[b, low, :] = weight[9 + tap]
-        early[b, high, :] = jnp.zeros(weight.shape[1:], jnp.bfloat16)
-        late[b, low, :] = weight[18 * odd + tap]
-        late[b, high, :] = weight[18 - 18 * odd + tap]
-
-
-def early_kernel(width, own, mine, came, other, weight, turned, terms, spread, windows, tall):
+        paired[b, low, :] = weight[9 + tap]
+        paired[b, high, :] = weight[18 * odd + tap]
+        single[b, low, :] = weight[18 - 18 * odd + tap]
+        single[b, high, :] = jnp.zeros(weight.shape[1:], jnp.bfloat16)
+
+
+def near_kernel(width, own, near, mine, weight, windows, terms, spread, tall):
     cells = own.shape[1]
-    half = mine.shape[0]
     wide = windows.shape[1]
-    first_core = lax.axis_index("filt") & 1 == 0
-    turned[0:half, :] = mine[...]
-    turned[half : half + half // 2, :] = jnp.where(first_core, came[...], other[...])
-    turned[half + half // 2 :, :] = jnp.where(first_core, other[...], came[...])
-    lay_windows(width, own[...], own[...], windows, tall)
+    lay_windows(width, own[...], near[...], windows, tall)
     total = 0.0
     for b in range(3):
         window = windows[pl.ds((2 - b) * width, cells), :]
-        terms[:, b * wide : (b + 1) * wide] = jnp.dot(turned[...], window, preferred_element_type=jnp.float32)
+        terms[:, b * wide : (b + 1) * wide] = jnp.dot(mine[...], window, preferred_element_type=jnp.float32)
         total = total + jnp.dot(window, weight[b], preferred_element_type=jnp.float32)
     spread[...] = total
 
 
-def spread_kernel(width, groups, near, one_off, weight, spread, windows, keep, send, tall):
-    cells = spread.shape[0]
-    lay_windows(width, near[...], one_off[...], windows, tall)
-    part = cells // groups
+def theirs_kernel(width, came, other, two_off, windows, terms, inner, outer, theirs, twos, tall):
+    part, cells = came.shape
+    wide = windows.shape[1]
+    lanes = wide // 3
+    filt = lanes // 2
+    first_core = lax.axis_index("filt") & 1 == 0
+    theirs[0:part, :] = jnp.where(first_core, came[...], other[...])
+    theirs[part:, :] = jnp.where(first_core, other[...], came[...])
+    lay_windows(width, two_off[...], two_off[...], twos, tall)
+    left = lax.broadcasted_iota(jnp.int32, (2 * part, lanes), 1) < filt
+    for b in range(3):
+        rows = pl.ds((2 - b) * width, cells)
+        near_terms = jnp.dot(theirs[...], windows[rows, :], preferred_element_type=jnp.float32)
+        two_terms = jnp.dot(theirs[...], twos[rows, :], preferred_element_type=jnp.float32)
+        outer[:, b * wide : (b + 1) * wide] = near_terms
+        for c in range(3):
+            cut = slice(c * lanes, (c + 1) * lanes)
+            lo = b * wide + c * lanes
+            crossed = jnp.where(left, pltpu.roll(near_terms[:, cut], filt, 1), two_terms[:, cut])
+            inner[:, lo : lo + lanes] = terms[:, lo : lo + lanes] + crossed
+
+
+def one_kernel(width, groups, one_off, mine, weight, spread, inner, outer, kept_in, sent_in, keep, *rest):
+    *sends, windows, tall = rest
+    half, cells = mine.shape
+    wide = windows.shape[1]
+    lanes = wide // 3
+    filt = lanes // 2
+    lay_windows(width, one_off[...], one_off[...], windows, tall)
+
+    size = cells // groups
     index = lax.axis_index("filt")
     count = bits_of(groups)
     for target in reversed(range(groups)):
@@ -115,35 +137,16 @@
         for bit in range(count):
             differs = (target >> (count - 1 - bit)) & 1
             block = block + (((index >> bit) & 1) ^ differs) * (1 << bit)
-        start = pl.multiple_of(block * part, part)
-        total = spread[pl.ds(start, part), :]
+        start = pl.multiple_of(block * size, size)
+        total = spread[pl.ds(start, size), :]
         for b in range(3):
-            rows = pl.ds(pl.multiple_of(start + (2 - b) * width, width), part)
+            rows = pl.ds(pl.multiple_of(start + (2 - b) * width, width), size)
             total = total + jnp.dot(windows[rows, :], weight[b], preferred_element_type=jnp.float32)
         if target < groups // 2:
-            keep[pl.ds(target * part, part), :] = total
+            kept_in[pl.ds(target * size, size), :] = total
         else:
-            send[pl.ds((target - groups // 2) * part, part), :] = total.astype(jnp.bfloat16)
-
-
-def two_kernel(width, turned, two_off, terms, windows, tall):
-    half = turned.shape[0] // 2
-    cells = turned.shape[1]
-    wide = windows.shape[1]
-    lay_windows(width, two_off[...], two_off[...], windows, tall)
-    for b in range(3):
-        window = windows[pl.ds((2 - b) * width, cells), :]
-        terms[:, b * wide : (b + 1) * wide] = jnp.dot(
-            turned[pl.ds(half, half), :], window, preferred_element_type=jnp.float32
-        )
-
-
-def late_kernel(width, turned, windows, two, early, keep, *sends):
-    half = turned.shape[0] // 2
-    cells = turned.shape[1]
-    wide = windows.shape[1]
-    lanes = wide // 3
-    filt = lanes // 2
+            sent_in[pl.ds((target - groups // 2) * size, size), :] = total.astype(jnp.bfloat16)
+
     left = lax.broadcasted_iota(jnp.int32, (half, lanes), 1) < filt
     part = half // (len(sends) + 1)
 
@@ -153,22 +156,20 @@
             send[:, lo:hi] = value[number * part : (number + 1) * part, :].astype(jnp.bfloat16)
 
     for b in range(3):
+        store(b * wide, (b + 1) * wide, inner[:, b * wide : (b + 1) * wide])
         window = windows[pl.ds((2 - b) * width, cells), :]
-        terms = jnp.dot(turned[...], window, preferred_element_type=jnp.float32)
+        terms = jnp.dot(mine[...], window, preferred_element_type=jnp.float32)
         for c in range(3):
             tap = 3 * b + c
-            cut = slice(c * lanes, (c + 1) * lanes)
             lo = b * wide + c * lanes
-            crossed = jnp.where(left, two[:, lo : lo + lanes], early[half:, lo : lo + lanes])
-            store(lo, lo + lanes, terms[0:half, cut] + crossed)
-            middle = terms[half:, cut] + early[0:half, lo : lo + lanes]
+            total = terms[:, c * lanes : (c + 1) * lanes] + outer[:, lo : lo + lanes]
             lo = 3 * wide + tap // 2 * lanes
             if tap == 8:
-                store(lo, lo + filt, middle[:, 0:filt])
+                store(lo, lo + filt, total[:, 0:filt])
             elif tap % 2 == 0:
-                before = middle
+                before = total
             else:
-                store(lo, lo + lanes, jnp.where(left, before, pltpu.roll(middle, filt, 1)))
+                store(lo, lo + lanes, jnp.where(left, before, pltpu.roll(total, filt, 1)))
 
 
 def halve_kernel(kept, came, keep, send):
@@ -191,7 +192,7 @@
     copies = [pltpu.make_async_copy(rows, grad_input, done.at[3])]
     copies[0].start()
     total = summed[...]
-    for group, (first, step, target) in enumerate(((18, 1, 1), (0, 2, 2 * odd), (1, 2, 2 - 2 * odd))):
+    for group, (first, step, target) in enumerate(((0, 2, 1), (1, 2, 2 * odd), (18, 1, 2 - 2 * odd))):
         for tap in range(9):
             slot = first + step * tap
             taps[group, tap] = total[:, slot * filt : (slot + 1) * filt]
@@ -247,49 +248,48 @@
         (shape((half, cells), bf16), shape((quarter, cells), bf16)),
         flops=TURN * flops,
     )(in_specs=[VMEM] * 3, out_specs=[VMEM] * 2)(picked, inputs.reshape(cells, chans), own)
+    near = swapped(own, "space", 1)
     came = swapped(part, "space", 1)
-    one_pairs = [(i, i + 1) for i in range(1, blocks - 1, 2)]
-    one_off = lax.ppermute(own, "space", one_pairs + [(target, source) for source, target in one_pairs])
-    later = after(own, mine)
-    near = swapped(later, "space", 1)
-    two_pairs = [(i, i - 2) for i in range(2, blocks, 2)] + [(i, i + 2) for i in range(1, blocks - 2, 2)]
-    two_off = lax.ppermute(later, "space", two_pairs)
+    up = [(i, i + 2) for i in range(blocks - 2)]
+    down = [(target, source) for source, target in up]
+    even, odd = slice(0, None, 2), slice(1, None, 2)
+    two_off = lax.ppermute(after(own, mine), "space", down[even] + up[odd])
+    one_off = lax.ppermute(near, "space", up[even] + down[odd])
     other = swapped(came, "filt", 1)
 
     weight_shape = shape((3, lanes, chans), bf16)
-    early_weight, late_weight = call(order_kernel, (weight_shape, weight_shape), flops=ORDER * flops, bytes_accessed=MIB)(
+    paired_weight, single_weight = call(order_kernel, (weight_shape, weight_shape), flops=ORDER * flops, bytes_accessed=MIB)(
         in_specs=[VMEM], out_specs=[VMEM] * 2
     )(after(weight, mine))
-    turned, early, spread = call(
-        functools.partial(early_kernel, width),
-        (shape((chans, cells), bf16), shape((chans, 3 * lanes), f32), shape((cells, chans), f32)),
-        (pltpu.VMEM(windows_shape.shape, bf16), tall),
-        flops=EARLY * flops,
+    windows, terms, spread = call(
+        functools.partial(near_kernel, width),
+        (windows_shape, shape((half, 3 * lanes), f32), shape((cells, chans), f32)),
+        (tall,),
+        flops=NEAR * flops,
         bytes_accessed=4 * MIB,
-    )(in_specs=[VMEM] * 5, out_specs=[VMEM] * 3)(own, mine, came, other, early_weight)
-    two = call(
-        functools.partial(two_kernel, width),
-        shape((half, 3 * lanes), f32),
-        (pltpu.VMEM(windows_shape.shape, bf16), tall),
-        flops=TWO * flops,
-    )(in_specs=[VMEM] * 2, out_specs=VMEM)(turned, two_off)
-    windows, kept_in, sent_in = call(
-        functools.partial(spread_kernel, width, groups),
-        (windows_shape, shape((cells // 2, chans), f32), shape((cells // 2, chans), bf16)),
-        (tall,),
-        flops=SPREAD * flops,
+    )(in_specs=[VMEM] * 4, out_specs=[VMEM] * 3)(own, near, mine, paired_weight)
+    inner, outer = call(
+        functools.partial(theirs_kernel, width),
+        (shape((half, 3 * lanes), f32), shape((half, 3 * lanes), f32)),
+        (pltpu.VMEM((half, cells), bf16), pltpu.VMEM(windows_shape.shape, bf16), tall),
+        flops=THEIRS * flops,
         bytes_accessed=4 * MIB,
-    )(in_specs=[VMEM] * 4, out_specs=[VMEM] * 3)(near, one_off, late_weight, after(spread, two))
-    came_in = swapped(sent_in, "filt", 1)
+    )(in_specs=[VMEM] * 5, out_specs=[VMEM] * 2)(came, other, two_off, windows, terms)
     radix = min(4, blocks // 2)
     piece = half // radix
-    kept, *sends = call(
-        functools.partial(late_kernel, width),
-        (shape((piece, taps * filt), f32),) + (shape((piece, taps * filt), bf16),) * (radix - 1),
-        flops=LATE * flops,
+    kept_in, sent_in, kept, *sends = call(
+        functools.partial(one_kernel, width, groups),
+        (
+            shape((cells // 2, chans), f32),
+            shape((cells // 2, chans), bf16),
+            shape((piece, taps * filt), f32),
+        )
+        + (shape((piece, taps * filt), bf16),) * (radix - 1),
+        (pltpu.VMEM(windows_shape.shape, bf16), tall),
+        flops=ONE * flops,
         bytes_accessed=4 * MIB,
-    )(in_specs=[VMEM] * 4, out_specs=[VMEM] * radix)(turned, windows, two, early)
-    came_in = after(came_in, kept)
+    )(in_specs=[VMEM] * 6, out_specs=[VMEM] * (radix + 2))(one_off, mine, single_weight, spread, inner, outer)
+    came_in = swapped(sent_in, "filt", 1)
 
     distance = 2
     while True:

time: 33.8 us -> 32.9 us (0.973)
  waiting for transfers between devices: 7.6 us -> 6.66 us
  local copies, waits for them, and re-layouts: 0.99 us -> 1.81 us
  Pallas kernels: 6.53 us -> 5.89 us
    ppermute x8, starting transfers between devices: 15.8 us -> 12.7 us  [swapped(): return lax.ppermute(value, axis, [(i, i ^ distance) for i in range(count)])]
    ppermute x2, starting transfers between devices: 1.95 us -> 4.78 us  [the longest x1 3.49 us: on_device(): one_off = lax.ppermute(near, 'space', up[even] + down[odd])]
    ppermute x8, waiting for transfers between devices: 7.6 us -> 6.65 us  [swapped(): return lax.ppermute(value, axis, [(i, i ^ distance) for i in range(count)])]
    unnamed x8, local copies, waits for them, and re-layouts: 0.99 us -> 1.81 us
    pallas_call x4 -> x3, Pallas kernels: 4.97 us -> 4.32 us  [the longest x1 1.7 us: on_device(): call(functools.partial(one_kernel, width, groups), (shape((cells // 2, ch...]
  transfers between devices with their start and end apart: 10 -> 10, of which waited for: 3 -> 2; matrix products, arithmetic and copies ran while one was open for 0% -> 0% of each run, Pallas kernels for 12% -> 10%
where the time goes in v10:
time: 32.9 us; the launch traced here: 32.7 us
  starting transfers between devices  17.5 us (53%)
  waiting for transfers between devices  6.66 us (20%)
  Pallas kernels  5.89 us (18%)
  local copies, waits for them, and re-layouts  1.81 us (6%)
  between operations  0.78 us (2%)
    ppermute x8, starting transfers between devices, swapped(): return lax.ppermute(value, axis, [(i, i ^ distance) for i in range(count)])  12.7 us
    ppermute x8, waiting for transfers between devices, swapped(): return lax.ppermute(value, axis, [(i, i ^ distance) for i in range(count)])  6.65 us
    ppermute x1, starting transfers between devices, on_device(): one_off = lax.ppermute(near, 'space', up[even] + down[odd])  3.49 us
    unnamed x8, local copies, waits for them, and re-layouts  1.81 us
    pallas_call x1, Pallas kernels, on_device(): call(functools.partial(one_kernel, width, groups), (shape((cells // 2, ch...  1.7 us
    pallas_call x1, Pallas kernels, on_device(): call(functools.partial(near_kernel, width), (windows_shape, shape((half,...  1.56 us
    ppermute x1, starting transfers between devices, on_device(): two_off = lax.ppermute(after(own, mine), 'space', down[even] + up[odd])  1.29 us
    pallas_call x1, Pallas kernels, on_device(): call(functools.partial(theirs_kernel, width), (shape((half, 3 * lanes), f...  1.06 us
  transfers between devices with their start and end apart: 10, of which 2 were waited for; matrix products, arithmetic and copies ran while one was open for 0% of the time, Pallas kernels for 10%

profile of v10, /device:TPU:0, one launch (start us, length us, event | category | flops | bytes accessed | tf_op | source)
XLA Modules:
  0.0 32.7 jit_solution(2927061108815654752)
XLA Ops:
  0.6 0.0 copy-start
  0.6 0.9 %copy-done = bf16[1,64,1024]{2,1,0:T(8,128)(2,1)S(1)} copy-done((bf16[1,64,1024]{2,1,0:T(8,128)(2,1)S(1)}, bf16[1,64,1024]{2,1,0:T(8,128)(2,1)}, u32[]{:S(2)}) %copy-start) | copy-done | bytes 131096
  1.5 0.0 copy-start.1
  1.5 0.9 %copy-done.1 = bf16[1,64,1024]{2,1,0:T(8,128)(2,1)S(1)} copy-done((bf16[1,64,1024]{2,1,0:T(8,128)(2,1)S(1)}, bf16[1,64,1024]{2,1,0:T(8,128)(2,1)}, u32[]{:S(2)}) %copy-start.1) | copy-done | bytes 131096
  2.4 0.1 shard_map.59._.own
  2.5 0.0 copy-start.3
  2.5 3.0 %collective-permute-start = (bf16[64,1024]{1,0:T(8,128)(2,1)S(1)}, bf16[64,1024]{1,0:T(8,128)(2,1)S(1)}, u32[]{:S(2)}, u32[]{:S(2)}) collective-permute-start(bf16[64,1024]{1,0:T(8,128)(2,1)S(1)} %shard_map.59._.own), channel_id=1, source_target_pairs={{0,4},{4,0},{8,12},{12,8},{16,20},{20,16},{24,28},{28,24},{1,5},{5... | collective-permute-start | bytes 393224 | tf_op jit(solution)/shard_map/ppermute | solution.py:208
  5.6 0.1 shard_map.60.picked
  5.6 0.0 copy-done.3
  5.6 0.0 copy-start.2
  5.6 0.3 shard_map.61
  6.0 1.3 %collective-permute-start.4 = (bf16[64,1024]{1,0:T(8,128)(2,1)S(1)}, bf16[64,1024]{1,0:T(8,128)(2,1)S(1)}, u32[]{:S(2)}, u32[]{:S(2)}) collective-permute-start(bf16[64,1024]{1,0:T(8,128)(2,1)S(1)} %shard_map.59._.own), channel_id=1, source_target_pairs={{8,0},{16,8},{24,16},{4,12},{12,20},{20,28},{9,1},{17,9},{25,17},{... | collective-permute-start | bytes 393224 | tf_op jit(solution)/shard_map/ppermute | solution.py:256
  7.3 3.1 %collective-permute-start.2 = (bf16[64,1024]{1,0:T(8,128)(2,1)S(1)}, bf16[64,1024]{1,0:T(8,128)(2,1)S(1)}, u32[]{:S(2)}, u32[]{:S(2)}) collective-permute-start(bf16[64,1024]{1,0:T(8,128)(2,1)S(1)} %get-tuple-element.28), channel_id=1, source_target_pairs={{0,4},{4,0},{8,12},{12,8},{16,20},{20,16},{24,28},{28,24},{1,5},{5... | collective-permute-start | bytes 393224 | tf_op jit(solution)/shard_map/ppermute | solution.py:208
  10.4 0.0 copy-done.2
  10.4 0.1 shard_map.62
  10.5 0.0 collective-permute-done.near
  10.5 3.5 %collective-permute-start.1 = (bf16[64,1024]{1,0:T(8,128)(2,1)S(1)}, bf16[64,1024]{1,0:T(8,128)(2,1)S(1)}, u32[]{:S(2)}, u32[]{:S(2)}) collective-permute-start(bf16[64,1024]{1,0:T(8,128)(2,1)S(1)} %collective-permute-done.near), channel_id=1, source_target_pairs={{0,8},{8,16},{16,24},{12,4},{20,12},{28,20},{1,9},{9,17},{17,25},{... | collective-permute-start | bytes 393224 | tf_op jit(solution)/shard_map/ppermute | solution.py:257
  14.0 0.0 collective-permute-done.2.came
  14.0 0.1 collective-permute-start.3
  14.1 1.6 %shard_map.63 = (bf16[1088,384]{1,0:T(8,128)(2,1)S(1)}, f32[128,1152]{1,0:T(8,128)S(1)}, f32[1024,256]{1,0:T(8,128)S(1)}) custom-call(bf16[64,1024]{1,0:T(8,128)(2,1)S(1)} %shard_map.59._.own, bf16[64,1024]{1,0:T(8,128)(2,1)S(1)} %collective-permute-done.near, bf16[128,1024]{1,0:T(8,128)(2,1)S(1)} %get-tuple-element.23.mine, ...), custom_call_target="tpu_custom_call" | custom-call | flops 2717908992 | bytes 4194304 | tf_op jit(solution)/shard_map/pallas_call | solution.py:264
  15.7 0.0 collective-permute-done.4.two_off
  15.7 0.0 collective-permute-done.3.other
  15.7 1.1 %shard_map.64 = (f32[128,1152]{1,0:T(8,128)S(1)}, f32[128,1152]{1,0:T(8,128)S(1)}) custom-call(bf16[64,1024]{1,0:T(8,128)(2,1)S(1)} %collective-permute-done.2.came, bf16[64,1024]{1,0:T(8,128)(2,1)S(1)} %collective-permute-done.3.other, bf16[64,1024]{1,0:T(8,128)(2,1)S(1)} %collective-permute-done.4.two_off, ...), custom_call_target="tpu_custom_call" | custom-call | flops 2717908992 | bytes 4194304 | tf_op jit(solution)/shard_map/pallas_call | solution.py:271
  16.7 0.0 collective-permute-done.1.one_off
  16.7 1.7 %shard_map.65 = (f32[512,256]{1,0:T(8,128)S(1)}, bf16[512,256]{1,0:T(8,128)(2,1)S(1)}, f32[32,1728]{1,0:T(8,128)S(1)}, bf16[32,1728]{1,0:T(8,128)(2,1)S(1)}, bf1...) custom-call(bf16[64,1024]{1,0:T(8,128)(2,1)S(1)} %collective-permute-done.1.one_off, ...), custom_call_target="tpu_custom_call" | custom-call | flops 2717908992 | bytes 4194304 | tf_op jit(solution)/shard_map/pallas_call | solution.py:280
  18.5 0.6 %collective-permute-start.8 = (bf16[512,256]{1,0:T(8,128)(2,1)S(1)}, bf16[512,256]{1,0:T(8,128)(2,1)S(1)}, u32[]{:S(2)}, u32[]{:S(2)}) collective-permute-start(bf16[512,256]{1,0:T(8,128)(2,1)S(1)} %get-tuple-element.39), channel_id=1, source_target_pairs={{0,1},{1,0},{2,3},{3,2},{4,5},{5,4},{6,7},{7,6},{8,9},{9,8},{10,11... | collective-permute-start | bytes 786440 | tf_op jit(solution)/shard_map/ppermute | solution.py:208
  19.0 2.8 %collective-permute-start.5 = (bf16[32,1728]{1,0:T(8,128)(2,1)S(1)}, bf16[32,1728]{1,0:T(8,128)(2,1)S(1)}, u32[]{:S(2)}, u32[]{:S(2)}) collective-permute-start(bf16[32,1728]{1,0:T(8,128)(2,1)S(1)} %get-tuple-element.35), channel_id=1, source_target_pairs={{0,16},{4,20},{8,24},{12,28},{16,0},{20,4},{24,8},{28,12},{1,17},{... | collective-permute-start | bytes 331784 | tf_op jit(solution)/shard_map/ppermute | solution.py:208
  21.8 0.7 %collective-permute-start.6 = (bf16[32,1728]{1,0:T(8,128)(2,1)S(1)}, bf16[32,1728]{1,0:T(8,128)(2,1)S(1)}, u32[]{:S(2)}, u32[]{:S(2)}) collective-permute-start(bf16[32,1728]{1,0:T(8,128)(2,1)S(1)} %get-tuple-element.36), channel_id=1, source_target_pairs={{0,8},{4,12},{8,0},{12,4},{16,24},{20,28},{24,16},{28,20},{1,9},{5... | collective-permute-start | bytes 331784 | tf_op jit(solution)/shard_map/ppermute | solution.py:208
  22.5 0.9 %collective-permute-start.7 = (bf16[32,1728]{1,0:T(8,128)(2,1)S(1)}, bf16[32,1728]{1,0:T(8,128)(2,1)S(1)}, u32[]{:S(2)}, u32[]{:S(2)}) collective-permute-start(bf16[32,1728]{1,0:T(8,128)(2,1)S(1)} %get-tuple-element.37), channel_id=1, source_target_pairs={{0,24},{4,28},{8,16},{12,20},{16,8},{20,12},{24,0},{28,4},{1,25},{... | collective-permute-start | bytes 331784 | tf_op jit(solution)/shard_map/ppermute | solution.py:208
  23.4 0.0 collective-permute-done.8.came
  23.5 1.6 %collective-permute-start.9 = (bf16[256,256]{1,0:T(8,128)(2,1)S(1)}, bf16[256,256]{1,0:T(8,128)(2,1)S(1)}, u32[]{:S(2)}, u32[]{:S(2)}) collective-permute-start(bf16[256,256]{1,0:T(8,128)(2,1)S(1)} %get-tuple-element.41), channel_id=1, source_target_pairs={{0,2},{1,3},{2,0},{3,1},{4,6},{5,7},{6,4},{7,5},{8,10},{9,11},{10,... | collective-permute-start | bytes 393224 | tf_op jit(solution)/shard_map/ppermute | solution.py:208
  25.0 3.3 %collective-permute-done.5.rest_0_ = bf16[32,1728]{1,0:T(8,128)(2,1)S(1)} collective-permute-done((bf16[32,1728]{1,0:T(8,128)(2,1)S(1)}, bf16[32,1728]{1,0:T(8,128)(2,1)S(1)}, u32[]{:S(2)}, u32[]{:S(2)}) %collective-permute-start.5) | collective-permute-done | bytes 110624 | tf_op jit(solution)/shard_map/ppermute | solution.py:208
  28.3 0.0 collective-permute-done.6.rest_1_
  28.3 3.4 %collective-permute-done.7.rest_2_ = bf16[32,1728]{1,0:T(8,128)(2,1)S(1)} collective-permute-done((bf16[32,1728]{1,0:T(8,128)(2,1)S(1)}, bf16[32,1728]{1,0:T(8,128)(2,1)S(1)}, u32[]{:S(2)}, u32[]{:S(2)}) %collective-permute-start.7) | collective-permute-done | bytes 110624 | tf_op jit(solution)/shard_map/ppermute | solution.py:208
  31.7 0.1 shard_map.66.summed
  31.7 0.0 collective-permute-done.9.came
  31.8 0.9 %shard_map.68 = (f32[27,32,64]{2,1,0:T(8,128)}, bf16[256,256]{1,0:T(8,128)(2,1)}) custom-call(f32[32,1728]{1,0:T(8,128)S(1)} %shard_map.66.summed, f32[256,256]{1,0:T(8,128)S(1)} %get-tuple-element.40.kept, bf16[256,256]{1,0:T(8,128)(2,1)S(1)} %collective-permute-done.9.came), custom_call_target="tpu_custom_call" | custom-call | tf_op jit(solution)/shard_map/pallas_call | solution.py:320
  (1 shorter events, 0.0 us)
Async XLA Ops:
  0.6 0.9 %copy-start = (bf16[1,64,1024]{2,1,0:T(8,128)(2,1)S(1)}, bf16[1,64,1024]{2,1,0:T(8,128)(2,1)}, u32[]{:S(2)}) copy-start(bf16[1,64,1024]{2,1,0:T(8,128)(2,1)} %param.5) | copy-start | bytes 393220
  1.5 0.9 %copy-start.1 = (bf16[1,64,1024]{2,1,0:T(8,128)(2,1)S(1)}, bf16[1,64,1024]{2,1,0:T(8,128)(2,1)}, u32[]{:S(2)}) copy-start(bf16[1,64,1024]{2,1,0:T(8,128)(2,1)} %param.6) | copy-start | bytes 393220
  2.5 3.1 %copy-start.3 = (bf16[1,32,32,256]{3,2,1,0:T(8,128)(2,1)S(1)}, bf16[1,32,32,256]{3,2,1,0:T(8,128)(2,1)}, u32[]{:S(2)}) copy-start(bf16[1,32,32,256]{3,2,1,0:T(8,128)(2,1)} %param.4) | copy-start | bytes 1572868
  2.5 7.9 %collective-permute-start = (bf16[64,1024]{1,0:T(8,128)(2,1)S(1)}, bf16[64,1024]{1,0:T(8,128)(2,1)S(1)}, u32[]{:S(2)}, u32[]{:S(2)}) collective-permute-start(bf16[64,1024]{1,0:T(8,128)(2,1)S(1)} %shard_map.59._.own), channel_id=1, source_target_pairs={{0,4},{4,0},{8,12},{12,8},{16,20},{20,16},{24,28},{28,24},{1,5},{5... | collective-permute-start | bytes 393224 | tf_op jit(solution)/shard_map/ppermute | solution.py:208
  5.6 4.8 %copy-start.2 = (bf16[27,64,256]{2,1,0:T(8,128)(2,1)S(1)}, bf16[27,64,256]{2,1,0:T(8,128)(2,1)}, u32[]{:S(2)}) copy-start(bf16[27,64,256]{2,1,0:T(8,128)(2,1)} %weight) | copy-start | bytes 2654212
  6.0 9.7 %collective-permute-start.4 = (bf16[64,1024]{1,0:T(8,128)(2,1)S(1)}, bf16[64,1024]{1,0:T(8,128)(2,1)S(1)}, u32[]{:S(2)}, u32[]{:S(2)}) collective-permute-start(bf16[64,1024]{1,0:T(8,128)(2,1)S(1)} %shard_map.59._.own), channel_id=1, source_target_pairs={{8,0},{16,8},{24,16},{4,12},{12,20},{20,28},{9,1},{17,9},{25,17},{... | collective-permute-start | bytes 393224 | tf_op jit(solution)/shard_map/ppermute | solution.py:256
  7.3 6.7 %collective-permute-start.2 = (bf16[64,1024]{1,0:T(8,128)(2,1)S(1)}, bf16[64,1024]{1,0:T(8,128)(2,1)S(1)}, u32[]{:S(2)}, u32[]{:S(2)}) collective-permute-start(bf16[64,1024]{1,0:T(8,128)(2,1)S(1)} %get-tuple-element.28), channel_id=1, source_target_pairs={{0,4},{4,0},{8,12},{12,8},{16,20},{20,16},{24,28},{28,24},{1,5},{5... | collective-permute-start | bytes 393224 | tf_op jit(solution)/shard_map/ppermute | solution.py:208
  10.5 6.2 %collective-permute-start.1 = (bf16[64,1024]{1,0:T(8,128)(2,1)S(1)}, bf16[64,1024]{1,0:T(8,128)(2,1)S(1)}, u32[]{:S(2)}, u32[]{:S(2)}) collective-permute-start(bf16[64,1024]{1,0:T(8,128)(2,1)S(1)} %collective-permute-done.near), channel_id=1, source_target_pairs={{0,8},{8,16},{16,24},{12,4},{20,12},{28,20},{1,9},{9,17},{17,25},{... | collective-permute-start | bytes 393224 | tf_op jit(solution)/shard_map/ppermute | solution.py:257
  14.0 1.7 %collective-permute-start.3 = (bf16[64,1024]{1,0:T(8,128)(2,1)S(1)}, bf16[64,1024]{1,0:T(8,128)(2,1)S(1)}, u32[]{:S(2)}, u32[]{:S(2)}) collective-permute-start(bf16[64,1024]{1,0:T(8,128)(2,1)S(1)} %collective-permute-done.2.came), channel_id=1, source_target_pairs={{0,1},{1,0},{2,3},{3,2},{4,5},{5,4},{6,7},{7,6},{8,9},{9,8},{10,11... | collective-permute-start | bytes 393224 | tf_op jit(solution)/shard_map/ppermute | solution.py:208
  18.5 5.0 %collective-permute-start.8 = (bf16[512,256]{1,0:T(8,128)(2,1)S(1)}, bf16[512,256]{1,0:T(8,128)(2,1)S(1)}, u32[]{:S(2)}, u32[]{:S(2)}) collective-permute-start(bf16[512,256]{1,0:T(8,128)(2,1)S(1)} %get-tuple-element.39), channel_id=1, source_target_pairs={{0,1},{1,0},{2,3},{3,2},{4,5},{5,4},{6,7},{7,6},{8,9},{9,8},{10,11... | collective-permute-start | bytes 786440 | tf_op jit(solution)/shard_map/ppermute | solution.py:208
  19.0 9.3 %collective-permute-start.5 = (bf16[32,1728]{1,0:T(8,128)(2,1)S(1)}, bf16[32,1728]{1,0:T(8,128)(2,1)S(1)}, u32[]{:S(2)}, u32[]{:S(2)}) collective-permute-start(bf16[32,1728]{1,0:T(8,128)(2,1)S(1)} %get-tuple-element.35), channel_id=1, source_target_pairs={{0,16},{4,20},{8,24},{12,28},{16,0},{20,4},{24,8},{28,12},{1,17},{... | collective-permute-start | bytes 331784 | tf_op jit(solution)/shard_map/ppermute | solution.py:208
  21.8 6.5 %collective-permute-start.6 = (bf16[32,1728]{1,0:T(8,128)(2,1)S(1)}, bf16[32,1728]{1,0:T(8,128)(2,1)S(1)}, u32[]{:S(2)}, u32[]{:S(2)}) collective-permute-start(bf16[32,1728]{1,0:T(8,128)(2,1)S(1)} %get-tuple-element.36), channel_id=1, source_target_pairs={{0,8},{4,12},{8,0},{12,4},{16,24},{20,28},{24,16},{28,20},{1,9},{5... | collective-permute-start | bytes 331784 | tf_op jit(solution)/shard_map/ppermute | solution.py:208
  22.5 9.2 %collective-permute-start.7 = (bf16[32,1728]{1,0:T(8,128)(2,1)S(1)}, bf16[32,1728]{1,0:T(8,128)(2,1)S(1)}, u32[]{:S(2)}, u32[]{:S(2)}) collective-permute-start(bf16[32,1728]{1,0:T(8,128)(2,1)S(1)} %get-tuple-element.37), channel_id=1, source_target_pairs={{0,24},{4,28},{8,16},{12,20},{16,8},{20,12},{24,0},{28,4},{1,25},{... | collective-permute-start | bytes 331784 | tf_op jit(solution)/shard_map/ppermute | solution.py:208
  23.5 8.3 %collective-permute-start.9 = (bf16[256,256]{1,0:T(8,128)(2,1)S(1)}, bf16[256,256]{1,0:T(8,128)(2,1)S(1)}, u32[]{:S(2)}, u32[]{:S(2)}) collective-permute-start(bf16[256,256]{1,0:T(8,128)(2,1)S(1)} %get-tuple-element.41), channel_id=1, source_target_pairs={{0,2},{1,3},{2,0},{3,1},{4,6},{5,7},{6,4},{7,5},{8,10},{9,11},{10,... | collective-permute-start | bytes 393224 | tf_op jit(solution)/shard_map/ppermute | solution.py:208

commit v11 on v10

--- a/solution.py
+++ b/solution.py
@@ -71,7 +71,7 @@
     part[...] = turned[half:, :]
 
 
-def grads_kernel(out_grad, pre_act, own):
+def grads_kernel(_, out_grad, pre_act, own):
     own[...] = (out_grad[...].astype(jnp.float32) * silu_grad(pre_act[...].astype(jnp.float32))).astype(own.dtype)
 
 
@@ -242,7 +242,9 @@
     picked = call(
         functools.partial(pick_kernel, blocks), shape((half + quarter, chans), bf16), flops=PICK * flops
     )(in_specs=[], out_specs=VMEM)()
-    own = call(grads_kernel, shape((filt, cells), bf16))(in_specs=[VMEM] * 2, out_specs=VMEM)(out_grad[0], pre_act[0])
+    own = call(grads_kernel, shape((filt, cells), bf16))(in_specs=[VMEM] * 3, out_specs=VMEM)(
+        picked, out_grad[0], pre_act[0]
+    )
     mine, part = call(
         turn_kernel,
         (shape((half, cells), bf16), shape((quarter, cells), bf16)),

time: 32.9 us -> 31.6 us (0.960)
  local copies, waits for them, and re-layouts: 1.81 us -> 0.87 us
    unnamed x8, local copies, waits for them, and re-layouts: 1.81 us -> 0.87 us
    ppermute x8, starting transfers between devices: 12.7 us -> 12.4 us  [swapped(): return lax.ppermute(value, axis, [(i, i ^ distance) for i in range(count)])]
where the time goes in v11:
time: 31.6 us; the launch traced here: 31.4 us
  starting transfers between devices  17.2 us (54%)
  waiting for transfers between devices  6.66 us (21%)
  Pallas kernels  5.89 us (19%)
  local copies, waits for them, and re-layouts  0.87 us (3%)
  between operations  0.78 us (2%)
    ppermute x8, starting transfers between devices, swapped(): return lax.ppermute(value, axis, [(i, i ^ distance) for i in range(count)])  12.4 us
    ppermute x8, waiting for transfers between devices, swapped(): return lax.ppermute(value, axis, [(i, i ^ distance) for i in range(count)])  6.65 us
    ppermute x1, starting transfers between devices, on_device(): one_off = lax.ppermute(near, 'space', up[even] + down[odd])  3.49 us
    pallas_call x1, Pallas kernels, on_device(): call(functools.partial(one_kernel, width, groups), (shape((cells // 2, ch...  1.7 us
    pallas_call x1, Pallas kernels, on_device(): call(functools.partial(near_kernel, width), (windows_shape, shape((half,...  1.56 us
    ppermute x1, starting transfers between devices, on_device(): two_off = lax.ppermute(after(own, mine), 'space', down[even] + up[odd])  1.29 us
    pallas_call x1, Pallas kernels, on_device(): call(functools.partial(theirs_kernel, width), (shape((half, 3 * lanes), f...  1.06 us
    pallas_call x1, Pallas kernels, on_device(): call(functools.partial(last_kernel, filt), (shape((taps, chans // blocks,...  0.9 us
  transfers between devices with their start and end apart: 10, of which 2 were waited for; matrix products, arithmetic and copies ran while one was open for 0% of the time, Pallas kernels for 10%

profile of v11, /device:TPU:0, one launch (start us, length us, event | category | flops | bytes accessed | tf_op | source)
XLA Modules:
  0.0 31.4 jit_solution(14292521146189408761)
XLA Ops:
  0.6 0.0 copy-start.1
  0.6 0.0 copy-start
  0.6 0.0 copy-start.3
  0.7 0.1 shard_map.59._.picked
  0.7 0.8 %copy-done.1 = bf16[1,64,1024]{2,1,0:T(8,128)(2,1)S(1)} copy-done((bf16[1,64,1024]{2,1,0:T(8,128)(2,1)S(1)}, bf16[1,64,1024]{2,1,0:T(8,128)(2,1)}, u32[]{:S(2)}) %copy-start.1) | copy-done | bytes 131096
  1.5 0.1 copy-done
  1.6 0.1 shard_map.60._.own
  1.7 3.0 %collective-permute-start = (bf16[64,1024]{1,0:T(8,128)(2,1)S(1)}, bf16[64,1024]{1,0:T(8,128)(2,1)S(1)}, u32[]{:S(2)}, u32[]{:S(2)}) collective-permute-start(bf16[64,1024]{1,0:T(8,128)(2,1)S(1)} %shard_map.60._.own), channel_id=1, source_target_pairs={{0,4},{4,0},{8,12},{12,8},{16,20},{20,16},{24,28},{28,24},{1,5},{5... | collective-permute-start | bytes 393224 | tf_op jit(solution)/shard_map/ppermute | solution.py:208
  4.7 0.0 copy-done.3
  4.7 0.0 copy-start.2
  4.7 0.3 %shard_map.61 = (bf16[128,1024]{1,0:T(8,128)(2,1)S(1)}, bf16[64,1024]{1,0:T(8,128)(2,1)S(1)}) custom-call(bf16[192,256]{1,0:T(8,128)(2,1)S(1)} %shard_map.59._.picked, bf16[1024,256]{1,0:T(8,128)(2,1)S(1)} %bitcast.7, bf16[64,1024]{1,0:T(8,128)(2,1)S(1)} %shard_map.60._.own), custom_call_target="tpu_custom_call" | custom-call | flops 905969664 | tf_op jit(solution)/shard_map/pallas_call | solution.py:248
  5.0 1.3 %collective-permute-start.4 = (bf16[64,1024]{1,0:T(8,128)(2,1)S(1)}, bf16[64,1024]{1,0:T(8,128)(2,1)S(1)}, u32[]{:S(2)}, u32[]{:S(2)}) collective-permute-start(bf16[64,1024]{1,0:T(8,128)(2,1)S(1)} %shard_map.60._.own), channel_id=1, source_target_pairs={{8,0},{16,8},{24,16},{4,12},{12,20},{20,28},{9,1},{17,9},{25,17},{... | collective-permute-start | bytes 393224 | tf_op jit(solution)/shard_map/ppermute | solution.py:258
  6.3 2.8 %collective-permute-start.2 = (bf16[64,1024]{1,0:T(8,128)(2,1)S(1)}, bf16[64,1024]{1,0:T(8,128)(2,1)S(1)}, u32[]{:S(2)}, u32[]{:S(2)}) collective-permute-start(bf16[64,1024]{1,0:T(8,128)(2,1)S(1)} %get-tuple-element.28), channel_id=1, source_target_pairs={{0,4},{4,0},{8,12},{12,8},{16,20},{20,16},{24,28},{28,24},{1,5},{5... | collective-permute-start | bytes 393224 | tf_op jit(solution)/shard_map/ppermute | solution.py:208
  9.1 0.0 copy-done.2
  9.1 0.1 shard_map.62
  9.2 0.0 collective-permute-done.near
  9.2 3.5 %collective-permute-start.1 = (bf16[64,1024]{1,0:T(8,128)(2,1)S(1)}, bf16[64,1024]{1,0:T(8,128)(2,1)S(1)}, u32[]{:S(2)}, u32[]{:S(2)}) collective-permute-start(bf16[64,1024]{1,0:T(8,128)(2,1)S(1)} %collective-permute-done.near), channel_id=1, source_target_pairs={{0,8},{8,16},{16,24},{12,4},{20,12},{28,20},{1,9},{9,17},{17,25},{... | collective-permute-start | bytes 393224 | tf_op jit(solution)/shard_map/ppermute | solution.py:259
  12.7 0.0 collective-permute-done.2.came
  12.7 0.1 collective-permute-start.3
  12.8 1.6 %shard_map.63 = (bf16[1088,384]{1,0:T(8,128)(2,1)S(1)}, f32[128,1152]{1,0:T(8,128)S(1)}, f32[1024,256]{1,0:T(8,128)S(1)}) custom-call(bf16[64,1024]{1,0:T(8,128)(2,1)S(1)} %shard_map.60._.own, bf16[64,1024]{1,0:T(8,128)(2,1)S(1)} %collective-permute-done.near, bf16[128,1024]{1,0:T(8,128)(2,1)S(1)} %get-tuple-element.23.mine, ...), custom_call_target="tpu_custom_call" | custom-call | flops 2717908992 | bytes 4194304 | tf_op jit(solution)/shard_map/pallas_call | solution.py:266
  14.4 0.0 collective-permute-done.4.two_off
  14.4 0.0 collective-permute-done.3.other
  14.4 1.1 %shard_map.64 = (f32[128,1152]{1,0:T(8,128)S(1)}, f32[128,1152]{1,0:T(8,128)S(1)}) custom-call(bf16[64,1024]{1,0:T(8,128)(2,1)S(1)} %collective-permute-done.2.came, bf16[64,1024]{1,0:T(8,128)(2,1)S(1)} %collective-permute-done.3.other, bf16[64,1024]{1,0:T(8,128)(2,1)S(1)} %collective-permute-done.4.two_off, ...), custom_call_target="tpu_custom_call" | custom-call | flops 2717908992 | bytes 4194304 | tf_op jit(solution)/shard_map/pallas_call | solution.py:273
  15.5 0.0 collective-permute-done.1.one_off
  15.5 1.7 %shard_map.65 = (f32[512,256]{1,0:T(8,128)S(1)}, bf16[512,256]{1,0:T(8,128)(2,1)S(1)}, f32[32,1728]{1,0:T(8,128)S(1)}, bf16[32,1728]{1,0:T(8,128)(2,1)S(1)}, bf1...) custom-call(bf16[64,1024]{1,0:T(8,128)(2,1)S(1)} %collective-permute-done.1.one_off, ...), custom_call_target="tpu_custom_call" | custom-call | flops 2717908992 | bytes 4194304 | tf_op jit(solution)/shard_map/pallas_call | solution.py:282
  17.2 0.6 %collective-permute-start.8 = (bf16[512,256]{1,0:T(8,128)(2,1)S(1)}, bf16[512,256]{1,0:T(8,128)(2,1)S(1)}, u32[]{:S(2)}, u32[]{:S(2)}) collective-permute-start(bf16[512,256]{1,0:T(8,128)(2,1)S(1)} %get-tuple-element.39), channel_id=1, source_target_pairs={{0,1},{1,0},{2,3},{3,2},{4,5},{5,4},{6,7},{7,6},{8,9},{9,8},{10,11... | collective-permute-start | bytes 786440 | tf_op jit(solution)/shard_map/ppermute | solution.py:208
  17.7 2.8 %collective-permute-start.5 = (bf16[32,1728]{1,0:T(8,128)(2,1)S(1)}, bf16[32,1728]{1,0:T(8,128)(2,1)S(1)}, u32[]{:S(2)}, u32[]{:S(2)}) collective-permute-start(bf16[32,1728]{1,0:T(8,128)(2,1)S(1)} %get-tuple-element.35), channel_id=1, source_target_pairs={{0,16},{4,20},{8,24},{12,28},{16,0},{20,4},{24,8},{28,12},{1,17},{... | collective-permute-start | bytes 331784 | tf_op jit(solution)/shard_map/ppermute | solution.py:208
  20.5 1.0 %collective-permute-start.6 = (bf16[32,1728]{1,0:T(8,128)(2,1)S(1)}, bf16[32,1728]{1,0:T(8,128)(2,1)S(1)}, u32[]{:S(2)}, u32[]{:S(2)}) collective-permute-start(bf16[32,1728]{1,0:T(8,128)(2,1)S(1)} %get-tuple-element.36), channel_id=1, source_target_pairs={{0,8},{4,12},{8,0},{12,4},{16,24},{20,28},{24,16},{28,20},{1,9},{5... | collective-permute-start | bytes 331784 | tf_op jit(solution)/shard_map/ppermute | solution.py:208
  21.5 0.6 %collective-permute-start.7 = (bf16[32,1728]{1,0:T(8,128)(2,1)S(1)}, bf16[32,1728]{1,0:T(8,128)(2,1)S(1)}, u32[]{:S(2)}, u32[]{:S(2)}) collective-permute-start(bf16[32,1728]{1,0:T(8,128)(2,1)S(1)} %get-tuple-element.37), channel_id=1, source_target_pairs={{0,24},{4,28},{8,16},{12,20},{16,8},{20,12},{24,0},{28,4},{1,25},{... | collective-permute-start | bytes 331784 | tf_op jit(solution)/shard_map/ppermute | solution.py:208
  22.1 0.0 collective-permute-done.8.came
  22.2 1.6 %collective-permute-start.9 = (bf16[256,256]{1,0:T(8,128)(2,1)S(1)}, bf16[256,256]{1,0:T(8,128)(2,1)S(1)}, u32[]{:S(2)}, u32[]{:S(2)}) collective-permute-start(bf16[256,256]{1,0:T(8,128)(2,1)S(1)} %get-tuple-element.41), channel_id=1, source_target_pairs={{0,2},{1,3},{2,0},{3,1},{4,6},{5,7},{6,4},{7,5},{8,10},{9,11},{10,... | collective-permute-start | bytes 393224 | tf_op jit(solution)/shard_map/ppermute | solution.py:208
  23.8 3.3 %collective-permute-done.5.rest_0_ = bf16[32,1728]{1,0:T(8,128)(2,1)S(1)} collective-permute-done((bf16[32,1728]{1,0:T(8,128)(2,1)S(1)}, bf16[32,1728]{1,0:T(8,128)(2,1)S(1)}, u32[]{:S(2)}, u32[]{:S(2)}) %collective-permute-start.5) | collective-permute-done | bytes 110624 | tf_op jit(solution)/shard_map/ppermute | solution.py:208
  27.0 0.0 collective-permute-done.6.rest_1_
  27.0 3.4 %collective-permute-done.7.rest_2_ = bf16[32,1728]{1,0:T(8,128)(2,1)S(1)} collective-permute-done((bf16[32,1728]{1,0:T(8,128)(2,1)S(1)}, bf16[32,1728]{1,0:T(8,128)(2,1)S(1)}, u32[]{:S(2)}, u32[]{:S(2)}) %collective-permute-start.7) | collective-permute-done | bytes 110624 | tf_op jit(solution)/shard_map/ppermute | solution.py:208
  30.4 0.1 shard_map.66.summed
  30.5 0.0 collective-permute-done.9.came
  30.5 0.9 %shard_map.68 = (f32[27,32,64]{2,1,0:T(8,128)}, bf16[256,256]{1,0:T(8,128)(2,1)}) custom-call(f32[32,1728]{1,0:T(8,128)S(1)} %shard_map.66.summed, f32[256,256]{1,0:T(8,128)S(1)} %get-tuple-element.40.kept, bf16[256,256]{1,0:T(8,128)(2,1)S(1)} %collective-permute-done.9.came), custom_call_target="tpu_custom_call" | custom-call | tf_op jit(solution)/shard_map/pallas_call | solution.py:322
  (1 shorter events, 0.0 us)
Async XLA Ops:
  0.6 0.9 %copy-start.1 = (bf16[1,64,1024]{2,1,0:T(8,128)(2,1)S(1)}, bf16[1,64,1024]{2,1,0:T(8,128)(2,1)}, u32[]{:S(2)}) copy-start(bf16[1,64,1024]{2,1,0:T(8,128)(2,1)} %param.6) | copy-start | bytes 393220
  0.6 1.0 %copy-start = (bf16[1,64,1024]{2,1,0:T(8,128)(2,1)S(1)}, bf16[1,64,1024]{2,1,0:T(8,128)(2,1)}, u32[]{:S(2)}) copy-start(bf16[1,64,1024]{2,1,0:T(8,128)(2,1)} %param.5) | copy-start | bytes 393220
  0.6 4.1 %copy-start.3 = (bf16[1,32,32,256]{3,2,1,0:T(8,128)(2,1)S(1)}, bf16[1,32,32,256]{3,2,1,0:T(8,128)(2,1)}, u32[]{:S(2)}) copy-start(bf16[1,32,32,256]{3,2,1,0:T(8,128)(2,1)} %param.4) | copy-start | bytes 1572868
  1.7 7.5 %collective-permute-start = (bf16[64,1024]{1,0:T(8,128)(2,1)S(1)}, bf16[64,1024]{1,0:T(8,128)(2,1)S(1)}, u32[]{:S(2)}, u32[]{:S(2)}) collective-permute-start(bf16[64,1024]{1,0:T(8,128)(2,1)S(1)} %shard_map.60._.own), channel_id=1, source_target_pairs={{0,4},{4,0},{8,12},{12,8},{16,20},{20,16},{24,28},{28,24},{1,5},{5... | collective-permute-start | bytes 393224 | tf_op jit(solution)/shard_map/ppermute | solution.py:208
  4.7 4.4 %copy-start.2 = (bf16[27,64,256]{2,1,0:T(8,128)(2,1)S(1)}, bf16[27,64,256]{2,1,0:T(8,128)(2,1)}, u32[]{:S(2)}) copy-start(bf16[27,64,256]{2,1,0:T(8,128)(2,1)} %weight) | copy-start | bytes 2654212
  5.0 9.3 %collective-permute-start.4 = (bf16[64,1024]{1,0:T(8,128)(2,1)S(1)}, bf16[64,1024]{1,0:T(8,128)(2,1)S(1)}, u32[]{:S(2)}, u32[]{:S(2)}) collective-permute-start(bf16[64,1024]{1,0:T(8,128)(2,1)S(1)} %shard_map.60._.own), channel_id=1, source_target_pairs={{8,0},{16,8},{24,16},{4,12},{12,20},{20,28},{9,1},{17,9},{25,17},{... | collective-permute-start | bytes 393224 | tf_op jit(solution)/shard_map/ppermute | solution.py:258
  6.3 6.4 %collective-permute-start.2 = (bf16[64,1024]{1,0:T(8,128)(2,1)S(1)}, bf16[64,1024]{1,0:T(8,128)(2,1)S(1)}, u32[]{:S(2)}, u32[]{:S(2)}) collective-permute-start(bf16[64,1024]{1,0:T(8,128)(2,1)S(1)} %get-tuple-element.28), channel_id=1, source_target_pairs={{0,4},{4,0},{8,12},{12,8},{16,20},{20,16},{24,28},{28,24},{1,5},{5... | collective-permute-start | bytes 393224 | tf_op jit(solution)/shard_map/ppermute | solution.py:208
  9.2 6.2 %collective-permute-start.1 = (bf16[64,1024]{1,0:T(8,128)(2,1)S(1)}, bf16[64,1024]{1,0:T(8,128)(2,1)S(1)}, u32[]{:S(2)}, u32[]{:S(2)}) collective-permute-start(bf16[64,1024]{1,0:T(8,128)(2,1)S(1)} %collective-permute-done.near), channel_id=1, source_target_pairs={{0,8},{8,16},{16,24},{12,4},{20,12},{28,20},{1,9},{9,17},{17,25},{... | collective-permute-start | bytes 393224 | tf_op jit(solution)/shard_map/ppermute | solution.py:259
  12.7 1.7 %collective-permute-start.3 = (bf16[64,1024]{1,0:T(8,128)(2,1)S(1)}, bf16[64,1024]{1,0:T(8,128)(2,1)S(1)}, u32[]{:S(2)}, u32[]{:S(2)}) collective-permute-start(bf16[64,1024]{1,0:T(8,128)(2,1)S(1)} %collective-permute-done.2.came), channel_id=1, source_target_pairs={{0,1},{1,0},{2,3},{3,2},{4,5},{5,4},{6,7},{7,6},{8,9},{9,8},{10,11... | collective-permute-start | bytes 393224 | tf_op jit(solution)/shard_map/ppermute | solution.py:208
  17.2 5.0 %collective-permute-start.8 = (bf16[512,256]{1,0:T(8,128)(2,1)S(1)}, bf16[512,256]{1,0:T(8,128)(2,1)S(1)}, u32[]{:S(2)}, u32[]{:S(2)}) collective-permute-start(bf16[512,256]{1,0:T(8,128)(2,1)S(1)} %get-tuple-element.39), channel_id=1, source_target_pairs={{0,1},{1,0},{2,3},{3,2},{4,5},{5,4},{6,7},{7,6},{8,9},{9,8},{10,11... | collective-permute-start | bytes 786440 | tf_op jit(solution)/shard_map/ppermute | solution.py:208
  17.7 9.3 %collective-permute-start.5 = (bf16[32,1728]{1,0:T(8,128)(2,1)S(1)}, bf16[32,1728]{1,0:T(8,128)(2,1)S(1)}, u32[]{:S(2)}, u32[]{:S(2)}) collective-permute-start(bf16[32,1728]{1,0:T(8,128)(2,1)S(1)} %get-tuple-element.35), channel_id=1, source_target_pairs={{0,16},{4,20},{8,24},{12,28},{16,0},{20,4},{24,8},{28,12},{1,17},{... | collective-permute-start | bytes 331784 | tf_op jit(solution)/shard_map/ppermute | solution.py:208
  20.5 6.5 %collective-permute-start.6 = (bf16[32,1728]{1,0:T(8,128)(2,1)S(1)}, bf16[32,1728]{1,0:T(8,128)(2,1)S(1)}, u32[]{:S(2)}, u32[]{:S(2)}) collective-permute-start(bf16[32,1728]{1,0:T(8,128)(2,1)S(1)} %get-tuple-element.36), channel_id=1, source_target_pairs={{0,8},{4,12},{8,0},{12,4},{16,24},{20,28},{24,16},{28,20},{1,9},{5... | collective-permute-start | bytes 331784 | tf_op jit(solution)/shard_map/ppermute | solution.py:208
  21.5 8.9 %collective-permute-start.7 = (bf16[32,1728]{1,0:T(8,128)(2,1)S(1)}, bf16[32,1728]{1,0:T(8,128)(2,1)S(1)}, u32[]{:S(2)}, u32[]{:S(2)}) collective-permute-start(bf16[32,1728]{1,0:T(8,128)(2,1)S(1)} %get-tuple-element.37), channel_id=1, source_target_pairs={{0,24},{4,28},{8,16},{12,20},{16,8},{20,12},{24,0},{28,4},{1,25},{... | collective-permute-start | bytes 331784 | tf_op jit(solution)/shard_map/ppermute | solution.py:208
  22.2 8.3 %collective-permute-start.9 = (bf16[256,256]{1,0:T(8,128)(2,1)S(1)}, bf16[256,256]{1,0:T(8,128)(2,1)S(1)}, u32[]{:S(2)}, u32[]{:S(2)}) collective-permute-start(bf16[256,256]{1,0:T(8,128)(2,1)S(1)} %get-tuple-element.41), channel_id=1, source_target_pairs={{0,2},{1,3},{2,0},{3,1},{4,6},{5,7},{6,4},{7,5},{8,10},{9,11},{10,... | collective-permute-start | bytes 393224 | tf_op jit(solution)/shard_map/ppermute | solution.py:208

commit v12 on v11

--- a/solution.py
+++ b/solution.py
@@ -25,12 +25,13 @@
     return sum(((value >> bit) & 1) << (width - 1 - bit) for bit in range(width))
 
 
-def call(kernel, outs, scratch=(), flops=0, bytes_accessed=0, limit=24):
+def call(kernel, outs, scratch=(), flops=0, bytes_accessed=0, limit=24, aliases={}):
     return functools.partial(
         pl.pallas_call,
         kernel,
         out_shape=outs,
         scratch_shapes=scratch,
+        input_output_aliases=aliases,
         compiler_params=pltpu.CompilerParams(vmem_limit_bytes=limit * MIB),
         cost_estimate=pl.CostEstimate(flops=flops, bytes_accessed=bytes_accessed, transcendentals=0),
     )
@@ -51,6 +52,23 @@
     windows[body, 2 * lanes : 3 * lanes] = jnp.where(column != 0, tall[pl.ds(7, cells), :], 0.0).astype(jnp.bfloat16)
 
 
+def lay_single(width, layer, windows, tall):
+    filt, cells = layer.shape
+    lanes = 2 * filt
+    tall[pl.ds(8, cells), :] = jnp.concatenate([layer, layer], axis=0).astype(jnp.float32).T
+    row = lax.broadcasted_iota(jnp.int32, (cells, lanes), 0)
+    column = row & (width - 1) if width & (width - 1) == 0 else lax.rem(row, width)
+    left = lax.broadcasted_iota(jnp.int32, (cells, lanes), 1) < filt
+    zero_rows = jnp.zeros((width, windows.shape[1]), jnp.bfloat16)
+    windows[pl.ds(0, width), :] = zero_rows
+    windows[pl.ds(width + cells, width), :] = zero_rows
+    body = pl.ds(width, cells)
+    low = jnp.where(column != width - 1, tall[pl.ds(9, cells), :], 0.0)
+    high = jnp.where(column != 0, tall[pl.ds(7, cells), :], 0.0)
+    windows[body, 0:lanes] = jnp.where(left, low, high).astype(jnp.bfloat16)
+    windows[body, lanes : lanes + filt] = tall[pl.ds(8, cells), 0:filt].astype(jnp.bfloat16)
+
+
 def pick_kernel(blocks, picked):
     size, chans = picked.shape
     rows = chans // blocks
@@ -83,8 +101,7 @@
         low, high = pl.ds(2 * c * filt, filt), pl.ds((2 * c + 1) * filt, filt)
         paired[b, low, :] = weight[9 + tap]
         paired[b, high, :] = weight[18 * odd + tap]
-        single[b, low, :] = weight[18 - 18 * odd + tap]
-        single[b, high, :] = jnp.zeros(weight.shape[1:], jnp.bfloat16)
+        single[b, pl.ds((0, 2, 1)[c] * filt, filt), :] = weight[18 - 18 * odd + tap]
 
 
 def near_kernel(width, own, near, mine, weight, windows, terms, spread, tall):
@@ -99,7 +116,19 @@
     spread[...] = total
 
 
-def theirs_kernel(width, came, other, two_off, windows, terms, inner, outer, theirs, twos, tall):
+def store_tile(value, tile, keep, sends):
+    lanes = keep.shape[1]
+    part = value.shape[0] // (len(sends) + 1)
+    rows = pl.ds(tile * part, part if value.shape[1] == lanes else part // 2)
+    for number, target in enumerate((keep, *sends)):
+        piece = value[number * part : (number + 1) * part, :]
+        if value.shape[1] < lanes:
+            piece = jnp.concatenate([piece[0 : part // 2, :], piece[part // 2 :, :]], axis=1)
+        target[rows, :] = piece.astype(target.dtype)
+
+
+def theirs_kernel(width, came, other, two_off, windows, terms, outer, keep, *rest):
+    *sends, theirs, twos, tall = rest
     part, cells = came.shape
     wide = windows.shape[1]
     lanes = wide // 3
@@ -109,25 +138,41 @@
     theirs[part:, :] = jnp.where(first_core, other[...], came[...])
     lay_windows(width, two_off[...], two_off[...], twos, tall)
     left = lax.broadcasted_iota(jnp.int32, (2 * part, lanes), 1) < filt
+    middle = []
     for b in range(3):
         rows = pl.ds((2 - b) * width, cells)
         near_terms = jnp.dot(theirs[...], windows[rows, :], preferred_element_type=jnp.float32)
         two_terms = jnp.dot(theirs[...], twos[rows, :], preferred_element_type=jnp.float32)
-        outer[:, b * wide : (b + 1) * wide] = near_terms
-        for c in range(3):
-            cut = slice(c * lanes, (c + 1) * lanes)
+        cuts = [slice(c * lanes, (c + 1) * lanes) for c in range(3)]
+        for c, cut in enumerate(cuts):
             lo = b * wide + c * lanes
             crossed = jnp.where(left, pltpu.roll(near_terms[:, cut], filt, 1), two_terms[:, cut])
-            inner[:, lo : lo + lanes] = terms[:, lo : lo + lanes] + crossed
-
-
-def one_kernel(width, groups, one_off, mine, weight, spread, inner, outer, kept_in, sent_in, keep, *rest):
+            store_tile(terms[:, lo : lo + lanes] + crossed, 3 * b + c, keep, sends)
+        outer[:, b * lanes : (b + 1) * lanes] = jnp.where(
+            left, near_terms[:, cuts[0]], pltpu.roll(near_terms[:, cuts[2]], filt, 1)
+        )
+        middle.append(near_terms[:, cuts[1]])
+    outer[:, wide : wide + lanes] = jnp.where(left, middle[0], pltpu.roll(middle[1], filt, 1))
+    outer[:, wide + lanes : wide + lanes + filt] = middle[2][:, 0:filt]
+
+
+def one_kernel(width, groups, radix, one_off, mine, weight, spread, outer, *rest):
+    kept_in, sent_in, keep, *rest = rest[radix:]
     *sends, windows, tall = rest
-    half, cells = mine.shape
-    wide = windows.shape[1]
-    lanes = wide // 3
+    cells = mine.shape[1]
+    lanes = keep.shape[1]
     filt = lanes // 2
-    lay_windows(width, one_off[...], one_off[...], windows, tall)
+    lay_single(width, one_off[...], windows, tall)
+
+    middle = []
+    for b in range(3):
+        window = windows[pl.ds((2 - b) * width, cells), :]
+        terms = jnp.dot(mine[...], window, preferred_element_type=jnp.float32)
+        store_tile(terms[:, 0:lanes] + outer[:, b * lanes : (b + 1) * lanes], 9 + b, keep, sends)
+        middle.append(terms[:, lanes : lanes + filt])
+    both = jnp.concatenate(middle[0:2], axis=1)
+    store_tile(both + outer[:, 3 * lanes : 4 * lanes], 12, keep, sends)
+    store_tile(middle[2] + outer[:, 4 * lanes : 4 * lanes + filt], 13, keep, sends)
 
     size = cells // groups
     index = lax.axis_index("filt")
@@ -147,29 +192,13 @@
         else:
             sent_in[pl.ds((target - groups // 2) * size, size), :] = total.astype(jnp.bfloat16)
 
-    left = lax.broadcasted_iota(jnp.int32, (half, lanes), 1) < filt
-    part = half // (len(sends) + 1)
-
-    def store(lo, hi, value):
-        keep[:, lo:hi] = value[0:part, :]
-        for number, send in enumerate(sends, 1):
-            send[:, lo:hi] = value[number * part : (number + 1) * part, :].astype(jnp.bfloat16)
-
-    for b in range(3):
-        store(b * wide, (b + 1) * wide, inner[:, b * wide : (b + 1) * wide])
-        window = windows[pl.ds((2 - b) * width, cells), :]
-        terms = jnp.dot(mine[...], window, preferred_element_type=jnp.float32)
-        for c in range(3):
-            tap = 3 * b + c
-            lo = b * wide + c * lanes
-            total = terms[:, c * lanes : (c + 1) * lanes] + outer[:, lo : lo + lanes]
-            lo = 3 * wide + tap // 2 * lanes
-            if tap == 8:
-                store(lo, lo + filt, total[:, 0:filt])
-            elif tap % 2 == 0:
-                before = total
-            else:
-                store(lo, lo + lanes, jnp.where(left, before, pltpu.roll(total, filt, 1)))
+
+def unfolded(tiles, rows):
+    full = tiles.shape[0] // rows
+    whole = [tiles[n * rows : (n + 1) * rows] for n in range(full)]
+    half = tiles[full * rows :]
+    lanes = tiles.shape[1]
+    return jnp.concatenate([*whole, jnp.concatenate([half[:, : lanes // 2], half[:, lanes // 2 :]], axis=0)], axis=1)
 
 
 def halve_kernel(kept, came, keep, send):
@@ -178,12 +207,21 @@
     send[...] = (kept[half:, :] + came[half:, :].astype(jnp.float32)).astype(jnp.bfloat16)
 
 
-def sum_kernel(scale, kept, *rest):
+def sum_kernel(scale, folded, kept, *rest):
     *came, out = rest
     total = kept[...]
     for piece in came:
         total = total + piece[...].astype(jnp.float32)
-    out[...] = total * scale
+    total = total * scale
+    if not folded:
+        out[...] = total
+        return
+    rows, lanes = out.shape[0], total.shape[1]
+    full = total.shape[0] // rows
+    for tile in range(full):
+        out[:, tile * lanes : (tile + 1) * lanes] = total[tile * rows : (tile + 1) * rows, :]
+    out[0 : rows // 2, full * lanes :] = total[full * rows :, 0 : lanes // 2]
+    out[rows // 2 :, full * lanes :] = total[full * rows :, lanes // 2 :]
 
 
 def last_kernel(filt, summed, kept, came, out, grad_input, taps, rows, done):
@@ -192,9 +230,9 @@
     copies = [pltpu.make_async_copy(rows, grad_input, done.at[3])]
     copies[0].start()
     total = summed[...]
-    for group, (first, step, target) in enumerate(((0, 2, 1), (1, 2, 2 * odd), (18, 1, 2 - 2 * odd))):
-        for tap in range(9):
-            slot = first + step * tap
+    outer = [18 + 2 * (tap // 3) + tap % 3 // 2 if tap % 3 != 1 else 24 + tap // 3 for tap in range(9)]
+    for group, (slots, target) in enumerate(((range(0, 18, 2), 1), (range(1, 18, 2), 2 * odd), (outer, 2 - 2 * odd))):
+        for tap, slot in enumerate(slots):
             taps[group, tap] = total[:, slot * filt : (slot + 1) * filt]
         copy = pltpu.make_async_copy(taps.at[group], out.at[pl.ds(target * 9, 9)], done.at[group])
         copy.start()
@@ -260,9 +298,9 @@
     other = swapped(came, "filt", 1)
 
     weight_shape = shape((3, lanes, chans), bf16)
-    paired_weight, single_weight = call(order_kernel, (weight_shape, weight_shape), flops=ORDER * flops, bytes_accessed=MIB)(
-        in_specs=[VMEM], out_specs=[VMEM] * 2
-    )(after(weight, mine))
+    paired_weight, single_weight = call(
+        order_kernel, (weight_shape, shape((3, 3 * filt, chans), bf16)), flops=ORDER * flops, bytes_accessed=MIB
+    )(in_specs=[VMEM], out_specs=[VMEM] * 2)(after(weight, mine))
     windows, terms, spread = call(
         functools.partial(near_kernel, width),
         (windows_shape, shape((half, 3 * lanes), f32), shape((cells, chans), f32)),
@@ -270,27 +308,27 @@
         flops=NEAR * flops,
         bytes_accessed=4 * MIB,
     )(in_specs=[VMEM] * 4, out_specs=[VMEM] * 3)(own, near, mine, paired_weight)
-    inner, outer = call(
+    radix = min(4, blocks // 2)
+    piece = half // radix
+    folded = (piece * taps // 2, 2 * filt)
+    pieces = (shape(folded, f32),) + (shape(folded, bf16),) * (radix - 1)
+    outer, *partial = call(
         functools.partial(theirs_kernel, width),
-        (shape((half, 3 * lanes), f32), shape((half, 3 * lanes), f32)),
+        (shape((half, 9 * filt), f32),) + pieces,
         (pltpu.VMEM((half, cells), bf16), pltpu.VMEM(windows_shape.shape, bf16), tall),
         flops=THEIRS * flops,
         bytes_accessed=4 * MIB,
-    )(in_specs=[VMEM] * 5, out_specs=[VMEM] * 2)(came, other, two_off, windows, terms)
-    radix = min(4, blocks // 2)
-    piece = half // radix
+    )(in_specs=[VMEM] * 5, out_specs=[VMEM] * (radix + 1))(came, other, two_off, windows, terms)
     kept_in, sent_in, kept, *sends = call(
-        functools.partial(one_kernel, width, groups),
-        (
-            shape((cells // 2, chans), f32),
-            shape((cells // 2, chans), bf16),
-            shape((piece, taps * filt), f32),
-        )
-        + (shape((piece, taps * filt), bf16),) * (radix - 1),
-        (pltpu.VMEM(windows_shape.shape, bf16), tall),
+        functools.partial(one_kernel, width, groups, radix),
+        (shape((cells // 2, chans), f32), shape((cells // 2, chans), bf16)) + pieces,
+        (pltpu.VMEM((cells + 2 * width, 3 * filt), bf16), tall),
         flops=ONE * flops,
         bytes_accessed=4 * MIB,
-    )(in_specs=[VMEM] * 6, out_specs=[VMEM] * (radix + 2))(one_off, mine, single_weight, spread, inner, outer)
+        aliases={5 + n: 2 + n for n in range(radix)},
+    )(in_specs=[VMEM] * (5 + radix), out_specs=[VMEM] * (radix + 2))(
+        one_off, mine, single_weight, spread, outer, *partial
+    )
     came_in = swapped(sent_in, "filt", 1)
 
     distance = 2
@@ -303,6 +341,8 @@
         total = kept
         for value in arrived:
             total = total + value.astype(f32)
+        if total.shape == folded:
+            total = unfolded(total, piece)
         radix = min(4, blocks // distance)
         piece //= radix
         kept, *sends = (total[n * piece : (n + 1) * piece] for n in range(radix))
@@ -315,7 +355,7 @@
         distance_in *= 2
     grad_scale = float(cells * blocks) ** (-0.5)
     summed = call(
-        functools.partial(sum_kernel, grad_scale), shape((chans // blocks, taps * filt), f32), flops=FINAL * flops
+        functools.partial(sum_kernel, grad_scale, kept.shape == folded), shape((chans // blocks, taps * filt), f32), flops=FINAL * flops
     )(in_specs=[VMEM] * (len(arrived) + 1), out_specs=VMEM)(kept, *arrived)
     any_space = pl.BlockSpec(memory_space=pl.ANY)
     rows_shape = (cells // groups, chans)

time: 31.6 us -> 30.5 us (0.965)
  Pallas kernels: 5.89 us -> 5.14 us
    pallas_call x4, Pallas kernels: 2.9 us -> 2.13 us  [the longest x1 1.06 us: on_device(): call(functools.partial(theirs_kernel, width), (shape((half, 9 * filt), f3...]
where the time goes in v12:
time: 30.5 us; the launch traced here: 30.3 us
  starting transfers between devices  17.2 us (56%)
  waiting for transfers between devices  6.39 us (21%)
  Pallas kernels  5.14 us (17%)
  local copies, waits for them, and re-layouts  0.87 us (3%)
  between operations  0.78 us (3%)
    ppermute x8, starting transfers between devices, swapped(): return lax.ppermute(value, axis, [(i, i ^ distance) for i in range(count)])  12.4 us
    ppermute x8, waiting for transfers between devices, swapped(): return lax.ppermute(value, axis, [(i, i ^ distance) for i in range(count)])  6.38 us
    ppermute x1, starting transfers between devices, on_device(): one_off = lax.ppermute(near, 'space', up[even] + down[odd])  3.49 us
    pallas_call x1, Pallas kernels, on_device(): call(functools.partial(near_kernel, width), (windows_shape, shape((half,...  1.56 us
    ppermute x1, starting transfers between devices, on_device(): two_off = lax.ppermute(after(own, mine), 'space', down[even] + up[odd])  1.29 us
    pallas_call x1, Pallas kernels, on_device(): call(functools.partial(theirs_kernel, width), (shape((half, 9 * filt), f3...  1.06 us
    pallas_call x1, Pallas kernels, on_device(): call(functools.partial(one_kernel, width, groups, radix), (shape((cells /...  0.94 us
    pallas_call x1, Pallas kernels, on_device(): call(functools.partial(last_kernel, filt), (shape((taps, chans // blocks,...  0.9 us
  transfers between devices with their start and end apart: 10, of which 2 were waited for; matrix products, arithmetic and copies ran while one was open for 0% of the time, Pallas kernels for 10%

profile of v12, /device:TPU:0, one launch (start us, length us, event | category | flops | bytes accessed | tf_op | source)
XLA Modules:
  0.0 30.3 jit_solution(8059315890599602088)
XLA Ops:
  0.6 0.0 copy-start.1
  0.6 0.0 copy-start
  0.6 0.0 copy-start.3
  0.7 0.1 shard_map.59._.picked
  0.7 0.8 %copy-done.1 = bf16[1,64,1024]{2,1,0:T(8,128)(2,1)S(1)} copy-done((bf16[1,64,1024]{2,1,0:T(8,128)(2,1)S(1)}, bf16[1,64,1024]{2,1,0:T(8,128)(2,1)}, u32[]{:S(2)}) %copy-start.1) | copy-done | bytes 131096
  1.5 0.1 copy-done
  1.6 0.1 shard_map.60._.own
  1.7 3.0 %collective-permute-start = (bf16[64,1024]{1,0:T(8,128)(2,1)S(1)}, bf16[64,1024]{1,0:T(8,128)(2,1)S(1)}, u32[]{:S(2)}, u32[]{:S(2)}) collective-permute-start(bf16[64,1024]{1,0:T(8,128)(2,1)S(1)} %shard_map.60._.own), channel_id=1, source_target_pairs={{0,4},{4,0},{8,12},{12,8},{16,20},{20,16},{24,28},{28,24},{1,5},{5... | collective-permute-start | bytes 393224 | tf_op jit(solution)/shard_map/ppermute | solution.py:246
  4.7 0.0 copy-done.3
  4.7 0.0 copy-start.2
  4.7 0.3 %shard_map.61 = (bf16[128,1024]{1,0:T(8,128)(2,1)S(1)}, bf16[64,1024]{1,0:T(8,128)(2,1)S(1)}) custom-call(bf16[192,256]{1,0:T(8,128)(2,1)S(1)} %shard_map.59._.picked, bf16[1024,256]{1,0:T(8,128)(2,1)S(1)} %bitcast.7, bf16[64,1024]{1,0:T(8,128)(2,1)S(1)} %shard_map.60._.own), custom_call_target="tpu_custom_call" | custom-call | flops 905969664 | tf_op jit(solution)/shard_map/pallas_call | solution.py:286
  5.0 1.3 %collective-permute-start.4 = (bf16[64,1024]{1,0:T(8,128)(2,1)S(1)}, bf16[64,1024]{1,0:T(8,128)(2,1)S(1)}, u32[]{:S(2)}, u32[]{:S(2)}) collective-permute-start(bf16[64,1024]{1,0:T(8,128)(2,1)S(1)} %shard_map.60._.own), channel_id=1, source_target_pairs={{8,0},{16,8},{24,16},{4,12},{12,20},{20,28},{9,1},{17,9},{25,17},{... | collective-permute-start | bytes 393224 | tf_op jit(solution)/shard_map/ppermute | solution.py:296
  6.3 2.8 %collective-permute-start.2 = (bf16[64,1024]{1,0:T(8,128)(2,1)S(1)}, bf16[64,1024]{1,0:T(8,128)(2,1)S(1)}, u32[]{:S(2)}, u32[]{:S(2)}) collective-permute-start(bf16[64,1024]{1,0:T(8,128)(2,1)S(1)} %get-tuple-element.31), channel_id=1, source_target_pairs={{0,4},{4,0},{8,12},{12,8},{16,20},{20,16},{24,28},{28,24},{1,5},{5... | collective-permute-start | bytes 393224 | tf_op jit(solution)/shard_map/ppermute | solution.py:246
  9.1 0.0 copy-done.2
  9.1 0.1 shard_map.62
  9.2 0.0 collective-permute-done.near
  9.2 3.5 %collective-permute-start.1 = (bf16[64,1024]{1,0:T(8,128)(2,1)S(1)}, bf16[64,1024]{1,0:T(8,128)(2,1)S(1)}, u32[]{:S(2)}, u32[]{:S(2)}) collective-permute-start(bf16[64,1024]{1,0:T(8,128)(2,1)S(1)} %collective-permute-done.near), channel_id=1, source_target_pairs={{0,8},{8,16},{16,24},{12,4},{20,12},{28,20},{1,9},{9,17},{17,25},{... | collective-permute-start | bytes 393224 | tf_op jit(solution)/shard_map/ppermute | solution.py:297
  12.7 0.0 collective-permute-done.2.came
  12.7 0.1 collective-permute-start.3
  12.8 1.6 %shard_map.63 = (bf16[1088,384]{1,0:T(8,128)(2,1)S(1)}, f32[128,1152]{1,0:T(8,128)S(1)}, f32[1024,256]{1,0:T(8,128)S(1)}) custom-call(bf16[64,1024]{1,0:T(8,128)(2,1)S(1)} %shard_map.60._.own, bf16[64,1024]{1,0:T(8,128)(2,1)S(1)} %collective-permute-done.near, bf16[128,1024]{1,0:T(8,128)(2,1)S(1)} %get-tuple-element.26.mine, ...), custom_call_target="tpu_custom_call" | custom-call | flops 2717908992 | bytes 4194304 | tf_op jit(solution)/shard_map/pallas_call | solution.py:304
  14.4 0.0 collective-permute-done.4.two_off
  14.4 0.0 collective-permute-done.3.other
  14.4 1.1 %shard_map.64 = (f32[128,576]{1,0:T(8,128)S(1)}, f32[432,128]{1,0:T(8,128)S(1)}, bf16[432,128]{1,0:T(8,128)(2,1)S(1)}, bf16[432,128]{1,0:T(8,128)(2,1)S(1)}, bf16[432,128]{1,0:T(8,128)(2,1)S(1)}) custom-call(bf16[64,1024]{1,0:T(8,128)(2,1)S(1)} %collective-permute-done.2.came, bf16[64,1024]{1,0:T(8,128)(2,1)S(1)} %collective-permute-done.3.other, ...), custom_call_target="tpu_custom_call" | custom-call | flops 2717908992 | bytes 4194304 | tf_op jit(solution)/shard_map/pallas_call | solution.py:315
  15.4 0.0 collective-permute-done.1.one_off
  15.4 0.9 %shard_map.65 = (f32[512,256]{1,0:T(8,128)S(1)}, bf16[512,256]{1,0:T(8,128)(2,1)S(1)}, f32[432,128]{1,0:T(8,128)S(1)}, bf16[432,128]{1,0:T(8,128)(2,1)S(1)}, bf1...) custom-call(bf16[64,1024]{1,0:T(8,128)(2,1)S(1)} %collective-permute, ...), custom_call_target="tpu_custom_call", output_to_operand_aliasing={{2}: (5, {}), {3}: (6, {}), {4}: (7, {}), {5}: (8, {})} | custom-call | flops 2717908992 | bytes 4194304 | tf_op jit(solution)/shard_map/pallas_call | solution.py:322
  16.4 0.6 %collective-permute-start.8 = (bf16[512,256]{1,0:T(8,128)(2,1)S(1)}, bf16[512,256]{1,0:T(8,128)(2,1)S(1)}, u32[]{:S(2)}, u32[]{:S(2)}) collective-permute-start(bf16[512,256]{1,0:T(8,128)(2,1)S(1)} %get-tuple-element.45), channel_id=1, source_target_pairs={{0,1},{1,0},{2,3},{3,2},{4,5},{5,4},{6,7},{7,6},{8,9},{9,8},{10,11... | collective-permute-start | bytes 786440 | tf_op jit(solution)/shard_map/ppermute | solution.py:246
  17.0 2.8 %collective-permute-start.5 = (bf16[432,128]{1,0:T(8,128)(2,1)S(1)}, bf16[432,128]{1,0:T(8,128)(2,1)S(1)}, u32[]{:S(2)}, u32[]{:S(2)}) collective-permute-start(bf16[432,128]{1,0:T(8,128)(2,1)S(1)} %get-tuple-element.41), channel_id=1, source_target_pairs={{0,16},{4,20},{8,24},{12,28},{16,0},{20,4},{24,8},{28,12},{1,17},{... | collective-permute-start | bytes 331784 | tf_op jit(solution)/shard_map/ppermute | solution.py:246
  19.7 1.0 %collective-permute-start.6 = (bf16[432,128]{1,0:T(8,128)(2,1)S(1)}, bf16[432,128]{1,0:T(8,128)(2,1)S(1)}, u32[]{:S(2)}, u32[]{:S(2)}) collective-permute-start(bf16[432,128]{1,0:T(8,128)(2,1)S(1)} %get-tuple-element.42), channel_id=1, source_target_pairs={{0,8},{4,12},{8,0},{12,4},{16,24},{20,28},{24,16},{28,20},{1,9},{5... | collective-permute-start | bytes 331784 | tf_op jit(solution)/shard_map/ppermute | solution.py:246
  20.8 0.6 %collective-permute-start.7 = (bf16[432,128]{1,0:T(8,128)(2,1)S(1)}, bf16[432,128]{1,0:T(8,128)(2,1)S(1)}, u32[]{:S(2)}, u32[]{:S(2)}) collective-permute-start(bf16[432,128]{1,0:T(8,128)(2,1)S(1)} %get-tuple-element.43), channel_id=1, source_target_pairs={{0,24},{4,28},{8,16},{12,20},{16,8},{20,12},{24,0},{28,4},{1,25},{... | collective-permute-start | bytes 331784 | tf_op jit(solution)/shard_map/ppermute | solution.py:246
  21.3 0.0 collective-permute-done.8.came
  21.3 0.1 shard_map.67
  21.4 1.6 %collective-permute-start.9 = (bf16[256,256]{1,0:T(8,128)(2,1)S(1)}, bf16[256,256]{1,0:T(8,128)(2,1)S(1)}, u32[]{:S(2)}, u32[]{:S(2)}) collective-permute-start(bf16[256,256]{1,0:T(8,128)(2,1)S(1)} %get-tuple-element.47), channel_id=1, source_target_pairs={{0,2},{1,3},{2,0},{3,1},{4,6},{5,7},{6,4},{7,5},{8,10},{9,11},{10,... | collective-permute-start | bytes 393224 | tf_op jit(solution)/shard_map/ppermute | solution.py:246
  23.0 3.1 %collective-permute-done.5.rest_0_ = bf16[432,128]{1,0:T(8,128)(2,1)S(1)} collective-permute-done((bf16[432,128]{1,0:T(8,128)(2,1)S(1)}, bf16[432,128]{1,0:T(8,128)(2,1)S(1)}, u32[]{:S(2)}, u32[]{:S(2)}) %collective-permute-start.5) | collective-permute-done | bytes 110624 | tf_op jit(solution)/shard_map/ppermute | solution.py:246
  26.1 0.0 collective-permute-done.6.rest_1_
  26.1 3.3 %collective-permute-done.7.rest_2_ = bf16[432,128]{1,0:T(8,128)(2,1)S(1)} collective-permute-done((bf16[432,128]{1,0:T(8,128)(2,1)S(1)}, bf16[432,128]{1,0:T(8,128)(2,1)S(1)}, u32[]{:S(2)}, u32[]{:S(2)}) %collective-permute-start.7) | collective-permute-done | bytes 110624 | tf_op jit(solution)/shard_map/ppermute | solution.py:246
  29.4 0.1 shard_map.66.summed
  29.4 0.0 collective-permute-done.9.came
  29.4 0.9 %shard_map.68 = (f32[27,32,64]{2,1,0:T(8,128)}, bf16[256,256]{1,0:T(8,128)(2,1)}) custom-call(f32[32,1728]{1,0:T(8,128)S(1)} %shard_map.66.summed, f32[256,256]{1,0:T(8,128)S(1)} %get-tuple-element.46.kept, bf16[256,256]{1,0:T(8,128)(2,1)S(1)} %collective-permute-done.9.came), custom_call_target="tpu_custom_call" | custom-call | tf_op jit(solution)/shard_map/pallas_call | solution.py:362
Async XLA Ops:
  0.6 0.9 %copy-start.1 = (bf16[1,64,1024]{2,1,0:T(8,128)(2,1)S(1)}, bf16[1,64,1024]{2,1,0:T(8,128)(2,1)}, u32[]{:S(2)}) copy-start(bf16[1,64,1024]{2,1,0:T(8,128)(2,1)} %param.6) | copy-start | bytes 393220
  0.6 1.0 %copy-start = (bf16[1,64,1024]{2,1,0:T(8,128)(2,1)S(1)}, bf16[1,64,1024]{2,1,0:T(8,128)(2,1)}, u32[]{:S(2)}) copy-start(bf16[1,64,1024]{2,1,0:T(8,128)(2,1)} %param.5) | copy-start | bytes 393220
  0.6 4.1 %copy-start.3 = (bf16[1,32,32,256]{3,2,1,0:T(8,128)(2,1)S(1)}, bf16[1,32,32,256]{3,2,1,0:T(8,128)(2,1)}, u32[]{:S(2)}) copy-start(bf16[1,32,32,256]{3,2,1,0:T(8,128)(2,1)} %param.4) | copy-start | bytes 1572868
  1.7 7.5 %collective-permute-start = (bf16[64,1024]{1,0:T(8,128)(2,1)S(1)}, bf16[64,1024]{1,0:T(8,128)(2,1)S(1)}, u32[]{:S(2)}, u32[]{:S(2)}) collective-permute-start(bf16[64,1024]{1,0:T(8,128)(2,1)S(1)} %shard_map.60._.own), channel_id=1, source_target_pairs={{0,4},{4,0},{8,12},{12,8},{16,20},{20,16},{24,28},{28,24},{1,5},{5... | collective-permute-start | bytes 393224 | tf_op jit(solution)/shard_map/ppermute | solution.py:246
  4.7 4.4 %copy-start.2 = (bf16[27,64,256]{2,1,0:T(8,128)(2,1)S(1)}, bf16[27,64,256]{2,1,0:T(8,128)(2,1)}, u32[]{:S(2)}) copy-start(bf16[27,64,256]{2,1,0:T(8,128)(2,1)} %weight) | copy-start | bytes 2654212
  5.0 9.3 %collective-permute-start.4 = (bf16[64,1024]{1,0:T(8,128)(2,1)S(1)}, bf16[64,1024]{1,0:T(8,128)(2,1)S(1)}, u32[]{:S(2)}, u32[]{:S(2)}) collective-permute-start(bf16[64,1024]{1,0:T(8,128)(2,1)S(1)} %shard_map.60._.own), channel_id=1, source_target_pairs={{8,0},{16,8},{24,16},{4,12},{12,20},{20,28},{9,1},{17,9},{25,17},{... | collective-permute-start | bytes 393224 | tf_op jit(solution)/shard_map/ppermute | solution.py:296
  6.3 6.4 %collective-permute-start.2 = (bf16[64,1024]{1,0:T(8,128)(2,1)S(1)}, bf16[64,1024]{1,0:T(8,128)(2,1)S(1)}, u32[]{:S(2)}, u32[]{:S(2)}) collective-permute-start(bf16[64,1024]{1,0:T(8,128)(2,1)S(1)} %get-tuple-element.31), channel_id=1, source_target_pairs={{0,4},{4,0},{8,12},{12,8},{16,20},{20,16},{24,28},{28,24},{1,5},{5... | collective-permute-start | bytes 393224 | tf_op jit(solution)/shard_map/ppermute | solution.py:246
  9.2 6.2 %collective-permute-start.1 = (bf16[64,1024]{1,0:T(8,128)(2,1)S(1)}, bf16[64,1024]{1,0:T(8,128)(2,1)S(1)}, u32[]{:S(2)}, u32[]{:S(2)}) collective-permute-start(bf16[64,1024]{1,0:T(8,128)(2,1)S(1)} %collective-permute-done.near), channel_id=1, source_target_pairs={{0,8},{8,16},{16,24},{12,4},{20,12},{28,20},{1,9},{9,17},{17,25},{... | collective-permute-start | bytes 393224 | tf_op jit(solution)/shard_map/ppermute | solution.py:297
  12.7 1.7 %collective-permute-start.3 = (bf16[64,1024]{1,0:T(8,128)(2,1)S(1)}, bf16[64,1024]{1,0:T(8,128)(2,1)S(1)}, u32[]{:S(2)}, u32[]{:S(2)}) collective-permute-start(bf16[64,1024]{1,0:T(8,128)(2,1)S(1)} %collective-permute-done.2.came), channel_id=1, source_target_pairs={{0,1},{1,0},{2,3},{3,2},{4,5},{5,4},{6,7},{7,6},{8,9},{9,8},{10,11... | collective-permute-start | bytes 393224 | tf_op jit(solution)/shard_map/ppermute | solution.py:246
  16.4 5.0 %collective-permute-start.8 = (bf16[512,256]{1,0:T(8,128)(2,1)S(1)}, bf16[512,256]{1,0:T(8,128)(2,1)S(1)}, u32[]{:S(2)}, u32[]{:S(2)}) collective-permute-start(bf16[512,256]{1,0:T(8,128)(2,1)S(1)} %get-tuple-element.45), channel_id=1, source_target_pairs={{0,1},{1,0},{2,3},{3,2},{4,5},{5,4},{6,7},{7,6},{8,9},{9,8},{10,11... | collective-permute-start | bytes 786440 | tf_op jit(solution)/shard_map/ppermute | solution.py:246
  17.0 9.1 %collective-permute-start.5 = (bf16[432,128]{1,0:T(8,128)(2,1)S(1)}, bf16[432,128]{1,0:T(8,128)(2,1)S(1)}, u32[]{:S(2)}, u32[]{:S(2)}) collective-permute-start(bf16[432,128]{1,0:T(8,128)(2,1)S(1)} %get-tuple-element.41), channel_id=1, source_target_pairs={{0,16},{4,20},{8,24},{12,28},{16,0},{20,4},{24,8},{28,12},{1,17},{... | collective-permute-start | bytes 331784 | tf_op jit(solution)/shard_map/ppermute | solution.py:246
  19.7 6.3 %collective-permute-start.6 = (bf16[432,128]{1,0:T(8,128)(2,1)S(1)}, bf16[432,128]{1,0:T(8,128)(2,1)S(1)}, u32[]{:S(2)}, u32[]{:S(2)}) collective-permute-start(bf16[432,128]{1,0:T(8,128)(2,1)S(1)} %get-tuple-element.42), channel_id=1, source_target_pairs={{0,8},{4,12},{8,0},{12,4},{16,24},{20,28},{24,16},{28,20},{1,9},{5... | collective-permute-start | bytes 331784 | tf_op jit(solution)/shard_map/ppermute | solution.py:246
  20.8 8.6 %collective-permute-start.7 = (bf16[432,128]{1,0:T(8,128)(2,1)S(1)}, bf16[432,128]{1,0:T(8,128)(2,1)S(1)}, u32[]{:S(2)}, u32[]{:S(2)}) collective-permute-start(bf16[432,128]{1,0:T(8,128)(2,1)S(1)} %get-tuple-element.43), channel_id=1, source_target_pairs={{0,24},{4,28},{8,16},{12,20},{16,8},{20,12},{24,0},{28,4},{1,25},{... | collective-permute-start | bytes 331784 | tf_op jit(solution)/shard_map/ppermute | solution.py:246
  21.4 8.0 %collective-permute-start.9 = (bf16[256,256]{1,0:T(8,128)(2,1)S(1)}, bf16[256,256]{1,0:T(8,128)(2,1)S(1)}, u32[]{:S(2)}, u32[]{:S(2)}) collective-permute-start(bf16[256,256]{1,0:T(8,128)(2,1)S(1)} %get-tuple-element.47), channel_id=1, source_target_pairs={{0,2},{1,3},{2,0},{3,1},{4,6},{5,7},{6,4},{7,5},{8,10},{9,11},{10,... | collective-permute-start | bytes 393224 | tf_op jit(solution)/shard_map/ppermute | solution.py:246

commit v13 on v12

--- a/solution.py
+++ b/solution.py
@@ -8,7 +8,7 @@
 from jax.sharding import PartitionSpec as P
 
 MIB = 1 << 20
-PICK, TURN, NEAR, THEIRS, ONE, FINAL, ORDER = 3, 1, 3, 3, 3, 3, 3
+AGAIN, PICK, TURN, NEAR, THEIRS, ONE, FINAL, ORDER = 0, 3, 1, 3, 3, 3, 3, 3
 VMEM = pl.BlockSpec(memory_space=pltpu.VMEM)
 
 
@@ -91,6 +91,10 @@
 
 def grads_kernel(_, out_grad, pre_act, own):
     own[...] = (out_grad[...].astype(jnp.float32) * silu_grad(pre_act[...].astype(jnp.float32))).astype(own.dtype)
+
+
+def again_kernel(own, out):
+    out[...] = own[...]
 
 
 def order_kernel(weight, paired, single):
@@ -283,17 +287,18 @@
     own = call(grads_kernel, shape((filt, cells), bf16))(in_specs=[VMEM] * 3, out_specs=VMEM)(
         picked, out_grad[0], pre_act[0]
     )
+    own_again = call(again_kernel, shape((filt, cells), bf16), flops=AGAIN * flops)(in_specs=[VMEM], out_specs=VMEM)(own)
     mine, part = call(
         turn_kernel,
         (shape((half, cells), bf16), shape((quarter, cells), bf16)),
         flops=TURN * flops,
-    )(in_specs=[VMEM] * 3, out_specs=[VMEM] * 2)(picked, inputs.reshape(cells, chans), own)
+    )(in_specs=[VMEM] * 3, out_specs=[VMEM] * 2)(picked, inputs.reshape(cells, chans), own_again)
     near = swapped(own, "space", 1)
     came = swapped(part, "space", 1)
     up = [(i, i + 2) for i in range(blocks - 2)]
     down = [(target, source) for source, target in up]
     even, odd = slice(0, None, 2), slice(1, None, 2)
-    two_off = lax.ppermute(after(own, mine), "space", down[even] + up[odd])
+    two_off = lax.ppermute(own_again, "space", down[even] + up[odd])
     one_off = lax.ppermute(near, "space", up[even] + down[odd])
     other = swapped(came, "filt", 1)
 

time: 30.5 us -> 30.6 us (level)
  no operation moved by 1% of the time
where the time goes in v13:
time: 30.6 us; the launch traced here: 30.4 us
  starting transfers between devices  17.2 us (56%)
  waiting for transfers between devices  6.39 us (21%)
  Pallas kernels  5.15 us (17%)
  local copies, waits for them, and re-layouts  0.87 us (3%)
  between operations  0.8 us (3%)
    ppermute x8, starting transfers between devices, swapped(): return lax.ppermute(value, axis, [(i, i ^ distance) for i in range(count)])  12.4 us
    ppermute x8, waiting for transfers between devices, swapped(): return lax.ppermute(value, axis, [(i, i ^ distance) for i in range(count)])  6.39 us
    ppermute x1, starting transfers between devices, on_device(): one_off = lax.ppermute(near, 'space', up[even] + down[odd])  3.49 us
    pallas_call x1, Pallas kernels, on_device(): call(functools.partial(near_kernel, width), (windows_shape, shape((half,...  1.56 us
    ppermute x1, starting transfers between devices, on_device(): two_off = lax.ppermute(own_again, 'space', down[even] + up[odd])  1.29 us
    pallas_call x1, Pallas kernels, on_device(): call(functools.partial(theirs_kernel, width), (shape((half, 9 * filt), f3...  1.06 us
    pallas_call x1, Pallas kernels, on_device(): call(functools.partial(one_kernel, width, groups, radix), (shape((cells /...  0.94 us
    pallas_call x1, Pallas kernels, on_device(): call(functools.partial(last_kernel, filt), (shape((taps, chans // blocks,...  0.9 us
  transfers between devices with their start and end apart: 10, of which 2 were waited for; matrix products, arithmetic and copies ran while one was open for 0% of the time, Pallas kernels for 10%

profile of v13, /device:TPU:0, one launch (start us, length us, event | category | flops | bytes accessed | tf_op | source)
XLA Modules:
  0.0 30.4 jit_solution(8186233562258238788)
XLA Ops:
  0.6 0.0 copy-start.1
  0.6 0.0 copy-start
  0.6 0.1 shard_map.59._.picked
  0.7 0.0 copy-start.3
  0.7 0.8 %copy-done.1 = bf16[1,64,1024]{2,1,0:T(8,128)(2,1)S(1)} copy-done((bf16[1,64,1024]{2,1,0:T(8,128)(2,1)S(1)}, bf16[1,64,1024]{2,1,0:T(8,128)(2,1)}, u32[]{:S(2)}) %copy-start.1) | copy-done | bytes 131096
  1.5 0.1 copy-done
  1.6 0.1 shard_map.60.own
  1.7 3.0 %collective-permute-start = (bf16[64,1024]{1,0:T(8,128)(2,1)S(1)}, bf16[64,1024]{1,0:T(8,128)(2,1)S(1)}, u32[]{:S(2)}, u32[]{:S(2)}) collective-permute-start(bf16[64,1024]{1,0:T(8,128)(2,1)S(1)} %shard_map.60.own), channel_id=1, source_target_pairs={{0,4},{4,0},{8,12},{12,8},{16,20},{20,16},{24,28},{28,24},{1,5},{5... | collective-permute-start | bytes 393224 | tf_op jit(solution)/shard_map/ppermute | solution.py:250
  4.7 1.3 %collective-permute-start.4 = (bf16[64,1024]{1,0:T(8,128)(2,1)S(1)}, bf16[64,1024]{1,0:T(8,128)(2,1)S(1)}, u32[]{:S(2)}, u32[]{:S(2)}) collective-permute-start(bf16[64,1024]{1,0:T(8,128)(2,1)S(1)} %shard_map.61._), channel_id=1, source_target_pairs={{8,0},{16,8},{24,16},{4,12},{12,20},{20,28},{9,1},{17,9},{25,17},{... | collective-permute-start | bytes 393224 | tf_op jit(solution)/shard_map/ppermute | solution.py:301
  6.0 0.0 copy-done.3
  6.0 0.0 copy-start.2
  6.0 0.3 %shard_map.62 = (bf16[128,1024]{1,0:T(8,128)(2,1)S(1)}, bf16[64,1024]{1,0:T(8,128)(2,1)S(1)}) custom-call(bf16[192,256]{1,0:T(8,128)(2,1)S(1)} %shard_map.59._.picked, bf16[1024,256]{1,0:T(8,128)(2,1)S(1)} %bitcast.7, bf16[64,1024]{1,0:T(8,128)(2,1)S(1)} %shard_map.61._), custom_call_target="tpu_custom_call" | custom-call | flops 905969664 | tf_op jit(solution)/shard_map/pallas_call | solution.py:291
  6.4 2.8 %collective-permute-start.2 = (bf16[64,1024]{1,0:T(8,128)(2,1)S(1)}, bf16[64,1024]{1,0:T(8,128)(2,1)S(1)}, u32[]{:S(2)}, u32[]{:S(2)}) collective-permute-start(bf16[64,1024]{1,0:T(8,128)(2,1)S(1)} %get-tuple-element.30), channel_id=1, source_target_pairs={{0,4},{4,0},{8,12},{12,8},{16,20},{20,16},{24,28},{28,24},{1,5},{5... | collective-permute-start | bytes 393224 | tf_op jit(solution)/shard_map/ppermute | solution.py:250
  9.2 0.0 copy-done.2
  9.2 0.1 shard_map.63
  9.2 0.0 collective-permute-done.near
  9.2 3.5 %collective-permute-start.1 = (bf16[64,1024]{1,0:T(8,128)(2,1)S(1)}, bf16[64,1024]{1,0:T(8,128)(2,1)S(1)}, u32[]{:S(2)}, u32[]{:S(2)}) collective-permute-start(bf16[64,1024]{1,0:T(8,128)(2,1)S(1)} %collective-permute-done.near), channel_id=1, source_target_pairs={{0,8},{8,16},{16,24},{12,4},{20,12},{28,20},{1,9},{9,17},{17,25},{... | collective-permute-start | bytes 393224 | tf_op jit(solution)/shard_map/ppermute | solution.py:302
  12.7 0.0 collective-permute-done.2.came
  12.7 0.1 collective-permute-start.3
  12.8 1.6 %shard_map.64 = (bf16[1088,384]{1,0:T(8,128)(2,1)S(1)}, f32[128,1152]{1,0:T(8,128)S(1)}, f32[1024,256]{1,0:T(8,128)S(1)}) custom-call(bf16[64,1024]{1,0:T(8,128)(2,1)S(1)} %shard_map.60.own, bf16[64,1024]{1,0:T(8,128)(2,1)S(1)} %collective-permute-done.near, bf16[128,1024]{1,0:T(8,128)(2,1)S(1)} %get-tuple-element.25.mine, ...), custom_call_target="tpu_custom_call" | custom-call | flops 2717908992 | bytes 4194304 | tf_op jit(solution)/shard_map/pallas_call | solution.py:309
  14.4 0.0 collective-permute-done.4.two_off
  14.4 0.0 collective-permute-done.3.other
  14.4 1.1 %shard_map.65 = (f32[128,576]{1,0:T(8,128)S(1)}, f32[432,128]{1,0:T(8,128)S(1)}, bf16[432,128]{1,0:T(8,128)(2,1)S(1)}, bf16[432,128]{1,0:T(8,128)(2,1)S(1)}, bf16[432,128]{1,0:T(8,128)(2,1)S(1)}) custom-call(bf16[64,1024]{1,0:T(8,128)(2,1)S(1)} %collective-permute-done.2.came, bf16[64,1024]{1,0:T(8,128)(2,1)S(1)} %collective-permute-done.3.other, ...), custom_call_target="tpu_custom_call" | custom-call | flops 2717908992 | bytes 4194304 | tf_op jit(solution)/shard_map/pallas_call | solution.py:320
  15.5 0.0 collective-permute-done.1.one_off
  15.5 0.9 %shard_map.66 = (f32[512,256]{1,0:T(8,128)S(1)}, bf16[512,256]{1,0:T(8,128)(2,1)S(1)}, f32[432,128]{1,0:T(8,128)S(1)}, bf16[432,128]{1,0:T(8,128)(2,1)S(1)}, bf1...) custom-call(bf16[64,1024]{1,0:T(8,128)(2,1)S(1)} %collective-permute, ...), custom_call_target="tpu_custom_call", output_to_operand_aliasing={{2}: (5, {}), {3}: (6, {}), {4}: (7, {}), {5}: (8, {})} | custom-call | flops 2717908992 | bytes 4194304 | tf_op jit(solution)/shard_map/pallas_call | solution.py:327
  16.4 0.6 %collective-permute-start.8 = (bf16[512,256]{1,0:T(8,128)(2,1)S(1)}, bf16[512,256]{1,0:T(8,128)(2,1)S(1)}, u32[]{:S(2)}, u32[]{:S(2)}) collective-permute-start(bf16[512,256]{1,0:T(8,128)(2,1)S(1)} %get-tuple-element.43), channel_id=1, source_target_pairs={{0,1},{1,0},{2,3},{3,2},{4,5},{5,4},{6,7},{7,6},{8,9},{9,8},{10,11... | collective-permute-start | bytes 786440 | tf_op jit(solution)/shard_map/ppermute | solution.py:250
  17.0 2.8 %collective-permute-start.5 = (bf16[432,128]{1,0:T(8,128)(2,1)S(1)}, bf16[432,128]{1,0:T(8,128)(2,1)S(1)}, u32[]{:S(2)}, u32[]{:S(2)}) collective-permute-start(bf16[432,128]{1,0:T(8,128)(2,1)S(1)} %get-tuple-element.39), channel_id=1, source_target_pairs={{0,16},{4,20},{8,24},{12,28},{16,0},{20,4},{24,8},{28,12},{1,17},{... | collective-permute-start | bytes 331784 | tf_op jit(solution)/shard_map/ppermute | solution.py:250
  19.8 1.0 %collective-permute-start.6 = (bf16[432,128]{1,0:T(8,128)(2,1)S(1)}, bf16[432,128]{1,0:T(8,128)(2,1)S(1)}, u32[]{:S(2)}, u32[]{:S(2)}) collective-permute-start(bf16[432,128]{1,0:T(8,128)(2,1)S(1)} %get-tuple-element.40), channel_id=1, source_target_pairs={{0,8},{4,12},{8,0},{12,4},{16,24},{20,28},{24,16},{28,20},{1,9},{5... | collective-permute-start | bytes 331784 | tf_op jit(solution)/shard_map/ppermute | solution.py:250
  20.8 0.6 %collective-permute-start.7 = (bf16[432,128]{1,0:T(8,128)(2,1)S(1)}, bf16[432,128]{1,0:T(8,128)(2,1)S(1)}, u32[]{:S(2)}, u32[]{:S(2)}) collective-permute-start(bf16[432,128]{1,0:T(8,128)(2,1)S(1)} %get-tuple-element.41), channel_id=1, source_target_pairs={{0,24},{4,28},{8,16},{12,20},{16,8},{20,12},{24,0},{28,4},{1,25},{... | collective-permute-start | bytes 331784 | tf_op jit(solution)/shard_map/ppermute | solution.py:250
  21.4 0.0 collective-permute-done.8.came
  21.4 0.1 shard_map.68
  21.4 1.6 %collective-permute-start.9 = (bf16[256,256]{1,0:T(8,128)(2,1)S(1)}, bf16[256,256]{1,0:T(8,128)(2,1)S(1)}, u32[]{:S(2)}, u32[]{:S(2)}) collective-permute-start(bf16[256,256]{1,0:T(8,128)(2,1)S(1)} %get-tuple-element.45), channel_id=1, source_target_pairs={{0,2},{1,3},{2,0},{3,1},{4,6},{5,7},{6,4},{7,5},{8,10},{9,11},{10,... | collective-permute-start | bytes 393224 | tf_op jit(solution)/shard_map/ppermute | solution.py:250
  23.0 3.1 %collective-permute-done.5.rest_0_ = bf16[432,128]{1,0:T(8,128)(2,1)S(1)} collective-permute-done((bf16[432,128]{1,0:T(8,128)(2,1)S(1)}, bf16[432,128]{1,0:T(8,128)(2,1)S(1)}, u32[]{:S(2)}, u32[]{:S(2)}) %collective-permute-start.5) | collective-permute-done | bytes 110624 | tf_op jit(solution)/shard_map/ppermute | solution.py:250
  26.1 0.0 collective-permute-done.6.rest_1_
  26.1 3.3 %collective-permute-done.7.rest_2_ = bf16[432,128]{1,0:T(8,128)(2,1)S(1)} collective-permute-done((bf16[432,128]{1,0:T(8,128)(2,1)S(1)}, bf16[432,128]{1,0:T(8,128)(2,1)S(1)}, u32[]{:S(2)}, u32[]{:S(2)}) %collective-permute-start.7) | collective-permute-done | bytes 110624 | tf_op jit(solution)/shard_map/ppermute | solution.py:250
  29.4 0.1 shard_map.67.summed
  29.5 0.0 collective-permute-done.9.came
  29.5 0.9 %shard_map.69 = (f32[27,32,64]{2,1,0:T(8,128)}, bf16[256,256]{1,0:T(8,128)(2,1)}) custom-call(f32[32,1728]{1,0:T(8,128)S(1)} %shard_map.67.summed, f32[256,256]{1,0:T(8,128)S(1)} %get-tuple-element.44.kept, bf16[256,256]{1,0:T(8,128)(2,1)S(1)} %collective-permute-done.9.came), custom_call_target="tpu_custom_call" | custom-call | tf_op jit(solution)/shard_map/pallas_call | solution.py:367
  (1 shorter events, 0.0 us)
Async XLA Ops:
  0.6 0.9 %copy-start.1 = (bf16[1,64,1024]{2,1,0:T(8,128)(2,1)S(1)}, bf16[1,64,1024]{2,1,0:T(8,128)(2,1)}, u32[]{:S(2)}) copy-start(bf16[1,64,1024]{2,1,0:T(8,128)(2,1)} %param.6) | copy-start | bytes 393220
  0.6 1.0 %copy-start = (bf16[1,64,1024]{2,1,0:T(8,128)(2,1)S(1)}, bf16[1,64,1024]{2,1,0:T(8,128)(2,1)}, u32[]{:S(2)}) copy-start(bf16[1,64,1024]{2,1,0:T(8,128)(2,1)} %param.5) | copy-start | bytes 393220
  0.7 5.3 %copy-start.3 = (bf16[1,32,32,256]{3,2,1,0:T(8,128)(2,1)S(1)}, bf16[1,32,32,256]{3,2,1,0:T(8,128)(2,1)}, u32[]{:S(2)}) copy-start(bf16[1,32,32,256]{3,2,1,0:T(8,128)(2,1)} %param.4) | copy-start | bytes 1572868
  1.7 7.5 %collective-permute-start = (bf16[64,1024]{1,0:T(8,128)(2,1)S(1)}, bf16[64,1024]{1,0:T(8,128)(2,1)S(1)}, u32[]{:S(2)}, u32[]{:S(2)}) collective-permute-start(bf16[64,1024]{1,0:T(8,128)(2,1)S(1)} %shard_map.60.own), channel_id=1, source_target_pairs={{0,4},{4,0},{8,12},{12,8},{16,20},{20,16},{24,28},{28,24},{1,5},{5... | collective-permute-start | bytes 393224 | tf_op jit(solution)/shard_map/ppermute | solution.py:250
  4.7 9.7 %collective-permute-start.4 = (bf16[64,1024]{1,0:T(8,128)(2,1)S(1)}, bf16[64,1024]{1,0:T(8,128)(2,1)S(1)}, u32[]{:S(2)}, u32[]{:S(2)}) collective-permute-start(bf16[64,1024]{1,0:T(8,128)(2,1)S(1)} %shard_map.61._), channel_id=1, source_target_pairs={{8,0},{16,8},{24,16},{4,12},{12,20},{20,28},{9,1},{17,9},{25,17},{... | collective-permute-start | bytes 393224 | tf_op jit(solution)/shard_map/ppermute | solution.py:301
  6.0 3.1 %copy-start.2 = (bf16[27,64,256]{2,1,0:T(8,128)(2,1)S(1)}, bf16[27,64,256]{2,1,0:T(8,128)(2,1)}, u32[]{:S(2)}) copy-start(bf16[27,64,256]{2,1,0:T(8,128)(2,1)} %weight) | copy-start | bytes 2654212
  6.4 6.4 %collective-permute-start.2 = (bf16[64,1024]{1,0:T(8,128)(2,1)S(1)}, bf16[64,1024]{1,0:T(8,128)(2,1)S(1)}, u32[]{:S(2)}, u32[]{:S(2)}) collective-permute-start(bf16[64,1024]{1,0:T(8,128)(2,1)S(1)} %get-tuple-element.30), channel_id=1, source_target_pairs={{0,4},{4,0},{8,12},{12,8},{16,20},{20,16},{24,28},{28,24},{1,5},{5... | collective-permute-start | bytes 393224 | tf_op jit(solution)/shard_map/ppermute | solution.py:250
  9.2 6.2 %collective-permute-start.1 = (bf16[64,1024]{1,0:T(8,128)(2,1)S(1)}, bf16[64,1024]{1,0:T(8,128)(2,1)S(1)}, u32[]{:S(2)}, u32[]{:S(2)}) collective-permute-start(bf16[64,1024]{1,0:T(8,128)(2,1)S(1)} %collective-permute-done.near), channel_id=1, source_target_pairs={{0,8},{8,16},{16,24},{12,4},{20,12},{28,20},{1,9},{9,17},{17,25},{... | collective-permute-start | bytes 393224 | tf_op jit(solution)/shard_map/ppermute | solution.py:302
  12.7 1.7 %collective-permute-start.3 = (bf16[64,1024]{1,0:T(8,128)(2,1)S(1)}, bf16[64,1024]{1,0:T(8,128)(2,1)S(1)}, u32[]{:S(2)}, u32[]{:S(2)}) collective-permute-start(bf16[64,1024]{1,0:T(8,128)(2,1)S(1)} %collective-permute-done.2.came), channel_id=1, source_target_pairs={{0,1},{1,0},{2,3},{3,2},{4,5},{5,4},{6,7},{7,6},{8,9},{9,8},{10,11... | collective-permute-start | bytes 393224 | tf_op jit(solution)/shard_map/ppermute | solution.py:250
  16.4 4.9 %collective-permute-start.8 = (bf16[512,256]{1,0:T(8,128)(2,1)S(1)}, bf16[512,256]{1,0:T(8,128)(2,1)S(1)}, u32[]{:S(2)}, u32[]{:S(2)}) collective-permute-start(bf16[512,256]{1,0:T(8,128)(2,1)S(1)} %get-tuple-element.43), channel_id=1, source_target_pairs={{0,1},{1,0},{2,3},{3,2},{4,5},{5,4},{6,7},{7,6},{8,9},{9,8},{10,11... | collective-permute-start | bytes 786440 | tf_op jit(solution)/shard_map/ppermute | solution.py:250
  17.0 9.1 %collective-permute-start.5 = (bf16[432,128]{1,0:T(8,128)(2,1)S(1)}, bf16[432,128]{1,0:T(8,128)(2,1)S(1)}, u32[]{:S(2)}, u32[]{:S(2)}) collective-permute-start(bf16[432,128]{1,0:T(8,128)(2,1)S(1)} %get-tuple-element.39), channel_id=1, source_target_pairs={{0,16},{4,20},{8,24},{12,28},{16,0},{20,4},{24,8},{28,12},{1,17},{... | collective-permute-start | bytes 331784 | tf_op jit(solution)/shard_map/ppermute | solution.py:250
  19.8 6.3 %collective-permute-start.6 = (bf16[432,128]{1,0:T(8,128)(2,1)S(1)}, bf16[432,128]{1,0:T(8,128)(2,1)S(1)}, u32[]{:S(2)}, u32[]{:S(2)}) collective-permute-start(bf16[432,128]{1,0:T(8,128)(2,1)S(1)} %get-tuple-element.40), channel_id=1, source_target_pairs={{0,8},{4,12},{8,0},{12,4},{16,24},{20,28},{24,16},{28,20},{1,9},{5... | collective-permute-start | bytes 331784 | tf_op jit(solution)/shard_map/ppermute | solution.py:250
  20.8 8.6 %collective-permute-start.7 = (bf16[432,128]{1,0:T(8,128)(2,1)S(1)}, bf16[432,128]{1,0:T(8,128)(2,1)S(1)}, u32[]{:S(2)}, u32[]{:S(2)}) collective-permute-start(bf16[432,128]{1,0:T(8,128)(2,1)S(1)} %get-tuple-element.41), channel_id=1, source_target_pairs={{0,24},{4,28},{8,16},{12,20},{16,8},{20,12},{24,0},{28,4},{1,25},{... | collective-permute-start | bytes 331784 | tf_op jit(solution)/shard_map/ppermute | solution.py:250
  21.4 8.0 %collective-permute-start.9 = (bf16[256,256]{1,0:T(8,128)(2,1)S(1)}, bf16[256,256]{1,0:T(8,128)(2,1)S(1)}, u32[]{:S(2)}, u32[]{:S(2)}) collective-permute-start(bf16[256,256]{1,0:T(8,128)(2,1)S(1)} %get-tuple-element.45), channel_id=1, source_target_pairs={{0,2},{1,3},{2,0},{3,1},{4,6},{5,7},{6,4},{7,5},{8,10},{9,11},{10,... | collective-permute-start | bytes 393224 | tf_op jit(solution)/shard_map/ppermute | solution.py:250

commit v14 on v12

--- a/solution.py
+++ b/solution.py
@@ -8,7 +8,7 @@
 from jax.sharding import PartitionSpec as P
 
 MIB = 1 << 20
-PICK, TURN, NEAR, THEIRS, ONE, FINAL, ORDER = 3, 1, 3, 3, 3, 3, 3
+PICK, TURN, NEAR, THEIRS, ONE, FINAL, ORDER = 3, 1, 3, 3, 3, 3, 1
 VMEM = pl.BlockSpec(memory_space=pltpu.VMEM)
 
 

time: 30.5 us -> 30.9 us (1.013)
  waiting for transfers between devices: 6.39 us -> 8.89 us
  starting transfers between devices: 17.2 us -> 15 us
    ppermute x8, starting transfers between devices: 12.4 us -> 9.72 us  [swapped(): return lax.ppermute(value, axis, [(i, i ^ distance) for i in range(count)])]
    ppermute x8, waiting for transfers between devices: 6.38 us -> 8.89 us  [swapped(): return lax.ppermute(value, axis, [(i, i ^ distance) for i in range(count)])]
    ppermute x1, starting transfers between devices: 3.49 us -> 4.04 us  [on_device(): one_off = lax.ppermute(near, 'space', up[even] + down[odd])]
  transfers between devices with their start and end apart: 10 -> 10, of which waited for: 2 -> 3; matrix products, arithmetic and copies ran while one was open for 0% -> 0% of each run, Pallas kernels for 10% -> 10%
where the time goes in v14:
time: 30.9 us; the launch traced here: 30.7 us
  starting transfers between devices  15 us (49%)
  waiting for transfers between devices  8.89 us (29%)
  Pallas kernels  5.14 us (17%)
  local copies, waits for them, and re-layouts  0.87 us (3%)
  between operations  0.78 us (3%)
    ppermute x8, starting transfers between devices, swapped(): return lax.ppermute(value, axis, [(i, i ^ distance) for i in range(count)])  9.72 us
    ppermute x8, waiting for transfers between devices, swapped(): return lax.ppermute(value, axis, [(i, i ^ distance) for i in range(count)])  8.89 us
    ppermute x1, starting transfers between devices, on_device(): one_off = lax.ppermute(near, 'space', up[even] + down[odd])  4.04 us
    pallas_call x1, Pallas kernels, on_device(): call(functools.partial(near_kernel, width), (windows_shape, shape((half,...  1.56 us
    ppermute x1, starting transfers between devices, on_device(): two_off = lax.ppermute(after(own, mine), 'space', down[even] + up[odd])  1.28 us
    pallas_call x1, Pallas kernels, on_device(): call(functools.partial(theirs_kernel, width), (shape((half, 9 * filt), f3...  1.06 us
    pallas_call x1, Pallas kernels, on_device(): call(functools.partial(one_kernel, width, groups, radix), (shape((cells /...  0.94 us
    pallas_call x1, Pallas kernels, on_device(): call(functools.partial(last_kernel, filt), (shape((taps, chans // blocks,...  0.9 us
  transfers between devices with their start and end apart: 10, of which 3 were waited for; matrix products, arithmetic and copies ran while one was open for 0% of the time, Pallas kernels for 10%

profile of v14, /device:TPU:0, one launch (start us, length us, event | category | flops | bytes accessed | tf_op | source)
XLA Modules:
  0.0 30.7 jit_solution(16010658254778828531)
XLA Ops:
  0.6 0.0 copy-start.1
  0.6 0.0 copy-start
  0.6 0.0 copy-start.3
  0.7 0.1 shard_map.59._.picked
  0.7 0.8 %copy-done.1 = bf16[1,64,1024]{2,1,0:T(8,128)(2,1)S(1)} copy-done((bf16[1,64,1024]{2,1,0:T(8,128)(2,1)S(1)}, bf16[1,64,1024]{2,1,0:T(8,128)(2,1)}, u32[]{:S(2)}) %copy-start.1) | copy-done | bytes 131096
  1.5 0.1 copy-done
  1.6 0.1 shard_map.60._.own
  1.7 3.0 %collective-permute-start = (bf16[64,1024]{1,0:T(8,128)(2,1)S(1)}, bf16[64,1024]{1,0:T(8,128)(2,1)S(1)}, u32[]{:S(2)}, u32[]{:S(2)}) collective-permute-start(bf16[64,1024]{1,0:T(8,128)(2,1)S(1)} %shard_map.60._.own), channel_id=1, source_target_pairs={{0,4},{4,0},{8,12},{12,8},{16,20},{20,16},{24,28},{28,24},{1,5},{5... | collective-permute-start | bytes 393224 | tf_op jit(solution)/shard_map/ppermute | solution.py:246
  4.7 0.0 copy-done.3
  4.7 0.0 copy-start.2
  4.7 0.3 %shard_map.61 = (bf16[128,1024]{1,0:T(8,128)(2,1)S(1)}, bf16[64,1024]{1,0:T(8,128)(2,1)S(1)}) custom-call(bf16[192,256]{1,0:T(8,128)(2,1)S(1)} %shard_map.59._.picked, bf16[1024,256]{1,0:T(8,128)(2,1)S(1)} %bitcast.7, bf16[64,1024]{1,0:T(8,128)(2,1)S(1)} %shard_map.60._.own), custom_call_target="tpu_custom_call" | custom-call | flops 905969664 | tf_op jit(solution)/shard_map/pallas_call | solution.py:286
  5.0 0.1 collective-permute-start.2
  5.2 1.3 %collective-permute-start.4 = (bf16[64,1024]{1,0:T(8,128)(2,1)S(1)}, bf16[64,1024]{1,0:T(8,128)(2,1)S(1)}, u32[]{:S(2)}, u32[]{:S(2)}) collective-permute-start(bf16[64,1024]{1,0:T(8,128)(2,1)S(1)} %shard_map.60._.own), channel_id=1, source_target_pairs={{8,0},{16,8},{24,16},{4,12},{12,20},{20,28},{9,1},{17,9},{25,17},{... | collective-permute-start | bytes 393224 | tf_op jit(solution)/shard_map/ppermute | solution.py:296
  6.4 0.0 copy-done.2
  6.5 0.1 shard_map.62
  6.5 2.5 %collective-permute-done.near = bf16[64,1024]{1,0:T(8,128)(2,1)S(1)} collective-permute-done((bf16[64,1024]{1,0:T(8,128)(2,1)S(1)}, bf16[64,1024]{1,0:T(8,128)(2,1)S(1)}, u32[]{:S(2)}, u32[]{:S(2)}) %collective-permute-start) | collective-permute-done | bytes 131104 | tf_op jit(solution)/shard_map/ppermute | solution.py:246
  9.0 4.0 %collective-permute-start.1 = (bf16[64,1024]{1,0:T(8,128)(2,1)S(1)}, bf16[64,1024]{1,0:T(8,128)(2,1)S(1)}, u32[]{:S(2)}, u32[]{:S(2)}) collective-permute-start(bf16[64,1024]{1,0:T(8,128)(2,1)S(1)} %collective-permute-done.near), channel_id=1, source_target_pairs={{0,8},{8,16},{16,24},{12,4},{20,12},{28,20},{1,9},{9,17},{17,25},{... | collective-permute-start | bytes 393224 | tf_op jit(solution)/shard_map/ppermute | solution.py:297
  13.1 0.0 collective-permute-done.2.came
  13.1 0.1 collective-permute-start.3
  13.2 1.6 %shard_map.63 = (bf16[1088,384]{1,0:T(8,128)(2,1)S(1)}, f32[128,1152]{1,0:T(8,128)S(1)}, f32[1024,256]{1,0:T(8,128)S(1)}) custom-call(bf16[64,1024]{1,0:T(8,128)(2,1)S(1)} %shard_map.60._.own, bf16[64,1024]{1,0:T(8,128)(2,1)S(1)} %collective-permute-done.near, bf16[128,1024]{1,0:T(8,128)(2,1)S(1)} %get-tuple-element.26.mine, ...), custom_call_target="tpu_custom_call" | custom-call | flops 2717908992 | bytes 4194304 | tf_op jit(solution)/shard_map/pallas_call | solution.py:304
  14.7 0.0 collective-permute-done.4.two_off
  14.7 0.0 collective-permute-done.3.other
  14.8 1.1 %shard_map.64 = (f32[128,576]{1,0:T(8,128)S(1)}, f32[432,128]{1,0:T(8,128)S(1)}, bf16[432,128]{1,0:T(8,128)(2,1)S(1)}, bf16[432,128]{1,0:T(8,128)(2,1)S(1)}, bf16[432,128]{1,0:T(8,128)(2,1)S(1)}) custom-call(bf16[64,1024]{1,0:T(8,128)(2,1)S(1)} %collective-permute-done.2.came, bf16[64,1024]{1,0:T(8,128)(2,1)S(1)} %collective-permute-done.3.other, ...), custom_call_target="tpu_custom_call" | custom-call | flops 2717908992 | bytes 4194304 | tf_op jit(solution)/shard_map/pallas_call | solution.py:315
  15.8 0.0 collective-permute-done.1.one_off
  15.8 0.9 %shard_map.65 = (f32[512,256]{1,0:T(8,128)S(1)}, bf16[512,256]{1,0:T(8,128)(2,1)S(1)}, f32[432,128]{1,0:T(8,128)S(1)}, bf16[432,128]{1,0:T(8,128)(2,1)S(1)}, bf1...) custom-call(bf16[64,1024]{1,0:T(8,128)(2,1)S(1)} %collective-permute, ...), custom_call_target="tpu_custom_call", output_to_operand_aliasing={{2}: (5, {}), {3}: (6, {}), {4}: (7, {}), {5}: (8, {})} | custom-call | flops 2717908992 | bytes 4194304 | tf_op jit(solution)/shard_map/pallas_call | solution.py:322
  16.8 0.6 %collective-permute-start.8 = (bf16[512,256]{1,0:T(8,128)(2,1)S(1)}, bf16[512,256]{1,0:T(8,128)(2,1)S(1)}, u32[]{:S(2)}, u32[]{:S(2)}) collective-permute-start(bf16[512,256]{1,0:T(8,128)(2,1)S(1)} %get-tuple-element.45), channel_id=1, source_target_pairs={{0,1},{1,0},{2,3},{3,2},{4,5},{5,4},{6,7},{7,6},{8,9},{9,8},{10,11... | collective-permute-start | bytes 786440 | tf_op jit(solution)/shard_map/ppermute | solution.py:246
  17.3 2.8 %collective-permute-start.5 = (bf16[432,128]{1,0:T(8,128)(2,1)S(1)}, bf16[432,128]{1,0:T(8,128)(2,1)S(1)}, u32[]{:S(2)}, u32[]{:S(2)}) collective-permute-start(bf16[432,128]{1,0:T(8,128)(2,1)S(1)} %get-tuple-element.41), channel_id=1, source_target_pairs={{0,16},{4,20},{8,24},{12,28},{16,0},{20,4},{24,8},{28,12},{1,17},{... | collective-permute-start | bytes 331784 | tf_op jit(solution)/shard_map/ppermute | solution.py:246
  20.1 1.6 %collective-permute-start.6 = (bf16[432,128]{1,0:T(8,128)(2,1)S(1)}, bf16[432,128]{1,0:T(8,128)(2,1)S(1)}, u32[]{:S(2)}, u32[]{:S(2)}) collective-permute-start(bf16[432,128]{1,0:T(8,128)(2,1)S(1)} %get-tuple-element.42), channel_id=1, source_target_pairs={{0,8},{4,12},{8,0},{12,4},{16,24},{20,28},{24,16},{28,20},{1,9},{5... | collective-permute-start | bytes 331784 | tf_op jit(solution)/shard_map/ppermute | solution.py:246
  21.7 0.0 collective-permute-start.7
  21.7 0.0 collective-permute-done.8.came
  21.7 0.1 shard_map.67
  21.8 1.6 %collective-permute-start.9 = (bf16[256,256]{1,0:T(8,128)(2,1)S(1)}, bf16[256,256]{1,0:T(8,128)(2,1)S(1)}, u32[]{:S(2)}, u32[]{:S(2)}) collective-permute-start(bf16[256,256]{1,0:T(8,128)(2,1)S(1)} %get-tuple-element.47), channel_id=1, source_target_pairs={{0,2},{1,3},{2,0},{3,1},{4,6},{5,7},{6,4},{7,5},{8,10},{9,11},{10,... | collective-permute-start | bytes 393224 | tf_op jit(solution)/shard_map/ppermute | solution.py:246
  23.4 3.1 %collective-permute-done.5.rest_0_ = bf16[432,128]{1,0:T(8,128)(2,1)S(1)} collective-permute-done((bf16[432,128]{1,0:T(8,128)(2,1)S(1)}, bf16[432,128]{1,0:T(8,128)(2,1)S(1)}, u32[]{:S(2)}, u32[]{:S(2)}) %collective-permute-start.5) | collective-permute-done | bytes 110624 | tf_op jit(solution)/shard_map/ppermute | solution.py:246
  26.4 0.0 collective-permute-done.6.rest_1_
  26.4 3.3 %collective-permute-done.7.rest_2_ = bf16[432,128]{1,0:T(8,128)(2,1)S(1)} collective-permute-done((bf16[432,128]{1,0:T(8,128)(2,1)S(1)}, bf16[432,128]{1,0:T(8,128)(2,1)S(1)}, u32[]{:S(2)}, u32[]{:S(2)}) %collective-permute-start.7) | collective-permute-done | bytes 110624 | tf_op jit(solution)/shard_map/ppermute | solution.py:246
  29.7 0.1 shard_map.66.summed
  29.8 0.0 collective-permute-done.9.came
  29.8 0.9 %shard_map.68 = (f32[27,32,64]{2,1,0:T(8,128)}, bf16[256,256]{1,0:T(8,128)(2,1)}) custom-call(f32[32,1728]{1,0:T(8,128)S(1)} %shard_map.66.summed, f32[256,256]{1,0:T(8,128)S(1)} %get-tuple-element.46.kept, bf16[256,256]{1,0:T(8,128)(2,1)S(1)} %collective-permute-done.9.came), custom_call_target="tpu_custom_call" | custom-call | tf_op jit(solution)/shard_map/pallas_call | solution.py:362
Async XLA Ops:
  0.6 0.9 %copy-start.1 = (bf16[1,64,1024]{2,1,0:T(8,128)(2,1)S(1)}, bf16[1,64,1024]{2,1,0:T(8,128)(2,1)}, u32[]{:S(2)}) copy-start(bf16[1,64,1024]{2,1,0:T(8,128)(2,1)} %param.6) | copy-start | bytes 393220
  0.6 1.0 %copy-start = (bf16[1,64,1024]{2,1,0:T(8,128)(2,1)S(1)}, bf16[1,64,1024]{2,1,0:T(8,128)(2,1)}, u32[]{:S(2)}) copy-start(bf16[1,64,1024]{2,1,0:T(8,128)(2,1)} %param.5) | copy-start | bytes 393220
  0.6 4.1 %copy-start.3 = (bf16[1,32,32,256]{3,2,1,0:T(8,128)(2,1)S(1)}, bf16[1,32,32,256]{3,2,1,0:T(8,128)(2,1)}, u32[]{:S(2)}) copy-start(bf16[1,32,32,256]{3,2,1,0:T(8,128)(2,1)} %param.4) | copy-start | bytes 1572868
  1.7 7.3 %collective-permute-start = (bf16[64,1024]{1,0:T(8,128)(2,1)S(1)}, bf16[64,1024]{1,0:T(8,128)(2,1)S(1)}, u32[]{:S(2)}, u32[]{:S(2)}) collective-permute-start(bf16[64,1024]{1,0:T(8,128)(2,1)S(1)} %shard_map.60._.own), channel_id=1, source_target_pairs={{0,4},{4,0},{8,12},{12,8},{16,20},{20,16},{24,28},{28,24},{1,5},{5... | collective-permute-start | bytes 393224 | tf_op jit(solution)/shard_map/ppermute | solution.py:246
  4.7 1.7 %copy-start.2 = (bf16[27,64,256]{2,1,0:T(8,128)(2,1)S(1)}, bf16[27,64,256]{2,1,0:T(8,128)(2,1)}, u32[]{:S(2)}) copy-start(bf16[27,64,256]{2,1,0:T(8,128)(2,1)} %weight) | copy-start | bytes 2654212
  5.0 8.0 %collective-permute-start.2 = (bf16[64,1024]{1,0:T(8,128)(2,1)S(1)}, bf16[64,1024]{1,0:T(8,128)(2,1)S(1)}, u32[]{:S(2)}, u32[]{:S(2)}) collective-permute-start(bf16[64,1024]{1,0:T(8,128)(2,1)S(1)} %get-tuple-element.31), channel_id=1, source_target_pairs={{0,4},{4,0},{8,12},{12,8},{16,20},{20,16},{24,28},{28,24},{1,5},{5... | collective-permute-start | bytes 393224 | tf_op jit(solution)/shard_map/ppermute | solution.py:246
  5.2 9.6 %collective-permute-start.4 = (bf16[64,1024]{1,0:T(8,128)(2,1)S(1)}, bf16[64,1024]{1,0:T(8,128)(2,1)S(1)}, u32[]{:S(2)}, u32[]{:S(2)}) collective-permute-start(bf16[64,1024]{1,0:T(8,128)(2,1)S(1)} %shard_map.60._.own), channel_id=1, source_target_pairs={{8,0},{16,8},{24,16},{4,12},{12,20},{20,28},{9,1},{17,9},{25,17},{... | collective-permute-start | bytes 393224 | tf_op jit(solution)/shard_map/ppermute | solution.py:296
  9.0 6.8 %collective-permute-start.1 = (bf16[64,1024]{1,0:T(8,128)(2,1)S(1)}, bf16[64,1024]{1,0:T(8,128)(2,1)S(1)}, u32[]{:S(2)}, u32[]{:S(2)}) collective-permute-start(bf16[64,1024]{1,0:T(8,128)(2,1)S(1)} %collective-permute-done.near), channel_id=1, source_target_pairs={{0,8},{8,16},{16,24},{12,4},{20,12},{28,20},{1,9},{9,17},{17,25},{... | collective-permute-start | bytes 393224 | tf_op jit(solution)/shard_map/ppermute | solution.py:297
  13.1 1.7 %collective-permute-start.3 = (bf16[64,1024]{1,0:T(8,128)(2,1)S(1)}, bf16[64,1024]{1,0:T(8,128)(2,1)S(1)}, u32[]{:S(2)}, u32[]{:S(2)}) collective-permute-start(bf16[64,1024]{1,0:T(8,128)(2,1)S(1)} %collective-permute-done.2.came), channel_id=1, source_target_pairs={{0,1},{1,0},{2,3},{3,2},{4,5},{5,4},{6,7},{7,6},{8,9},{9,8},{10,11... | collective-permute-start | bytes 393224 | tf_op jit(solution)/shard_map/ppermute | solution.py:246
  16.8 5.0 %collective-permute-start.8 = (bf16[512,256]{1,0:T(8,128)(2,1)S(1)}, bf16[512,256]{1,0:T(8,128)(2,1)S(1)}, u32[]{:S(2)}, u32[]{:S(2)}) collective-permute-start(bf16[512,256]{1,0:T(8,128)(2,1)S(1)} %get-tuple-element.45), channel_id=1, source_target_pairs={{0,1},{1,0},{2,3},{3,2},{4,5},{5,4},{6,7},{7,6},{8,9},{9,8},{10,11... | collective-permute-start | bytes 786440 | tf_op jit(solution)/shard_map/ppermute | solution.py:246
  17.3 9.1 %collective-permute-start.5 = (bf16[432,128]{1,0:T(8,128)(2,1)S(1)}, bf16[432,128]{1,0:T(8,128)(2,1)S(1)}, u32[]{:S(2)}, u32[]{:S(2)}) collective-permute-start(bf16[432,128]{1,0:T(8,128)(2,1)S(1)} %get-tuple-element.41), channel_id=1, source_target_pairs={{0,16},{4,20},{8,24},{12,28},{16,0},{20,4},{24,8},{28,12},{1,17},{... | collective-permute-start | bytes 331784 | tf_op jit(solution)/shard_map/ppermute | solution.py:246
  20.1 6.3 %collective-permute-start.6 = (bf16[432,128]{1,0:T(8,128)(2,1)S(1)}, bf16[432,128]{1,0:T(8,128)(2,1)S(1)}, u32[]{:S(2)}, u32[]{:S(2)}) collective-permute-start(bf16[432,128]{1,0:T(8,128)(2,1)S(1)} %get-tuple-element.42), channel_id=1, source_target_pairs={{0,8},{4,12},{8,0},{12,4},{16,24},{20,28},{24,16},{28,20},{1,9},{5... | collective-permute-start | bytes 331784 | tf_op jit(solution)/shard_map/ppermute | solution.py:246
  21.7 8.0 %collective-permute-start.7 = (bf16[432,128]{1,0:T(8,128)(2,1)S(1)}, bf16[432,128]{1,0:T(8,128)(2,1)S(1)}, u32[]{:S(2)}, u32[]{:S(2)}) collective-permute-start(bf16[432,128]{1,0:T(8,128)(2,1)S(1)} %get-tuple-element.43), channel_id=1, source_target_pairs={{0,24},{4,28},{8,16},{12,20},{16,8},{20,12},{24,0},{28,4},{1,25},{... | collective-permute-start | bytes 331784 | tf_op jit(solution)/shard_map/ppermute | solution.py:246
  21.8 8.0 %collective-permute-start.9 = (bf16[256,256]{1,0:T(8,128)(2,1)S(1)}, bf16[256,256]{1,0:T(8,128)(2,1)S(1)}, u32[]{:S(2)}, u32[]{:S(2)}) collective-permute-start(bf16[256,256]{1,0:T(8,128)(2,1)S(1)} %get-tuple-element.47), channel_id=1, source_target_pairs={{0,2},{1,3},{2,0},{3,1},{4,6},{5,7},{6,4},{7,5},{8,10},{9,11},{10,... | collective-permute-start | bytes 393224 | tf_op jit(solution)/shard_map/ppermute | solution.py:246

commit v15 on v13

--- a/solution.py
+++ b/solution.py
@@ -339,7 +339,8 @@
     distance = 2
     while True:
         spans = {2: (1,), 4: (2, 1, 3)}[radix]
-        arrived = [swapped(sends[n - 1], "space", spans[n - 1] * distance) for n in range(1, radix)]
+        far_first = sorted(range(1, radix), key=lambda n: spans[n - 1] == 1)
+        arrived = [swapped(sends[n - 1], "space", spans[n - 1] * distance) for n in far_first]
         distance *= radix
         if distance >= blocks:
             break

time: 30.6 us -> 30.7 us (level)
  waiting for transfers between devices: 6.39 us -> 6.78 us
    ppermute x8, waiting for transfers between devices: 6.39 us -> 6.78 us  [swapped(): return lax.ppermute(value, axis, [(i, i ^ distance) for i in range(count)])]
where the time goes in v15:
time: 30.7 us; the launch traced here: 30.5 us
  starting transfers between devices  16.9 us (55%)
  waiting for transfers between devices  6.78 us (22%)
  Pallas kernels  5.15 us (17%)
  local copies, waits for them, and re-layouts  0.87 us (3%)
  between operations  0.8 us (3%)
    ppermute x8, starting transfers between devices, swapped(): return lax.ppermute(value, axis, [(i, i ^ distance) for i in range(count)])  12.1 us
    ppermute x8, waiting for transfers between devices, swapped(): return lax.ppermute(value, axis, [(i, i ^ distance) for i in range(count)])  6.78 us
    ppermute x1, starting transfers between devices, on_device(): one_off = lax.ppermute(near, 'space', up[even] + down[odd])  3.49 us
    pallas_call x1, Pallas kernels, on_device(): call(functools.partial(near_kernel, width), (windows_shape, shape((half,...  1.56 us
    ppermute x1, starting transfers between devices, on_device(): two_off = lax.ppermute(own_again, 'space', down[even] + up[odd])  1.29 us
    pallas_call x1, Pallas kernels, on_device(): call(functools.partial(theirs_kernel, width), (shape((half, 9 * filt), f3...  1.06 us
    pallas_call x1, Pallas kernels, on_device(): call(functools.partial(one_kernel, width, groups, radix), (shape((cells /...  0.94 us
    pallas_call x1, Pallas kernels, on_device(): call(functools.partial(last_kernel, filt), (shape((taps, chans // blocks,...  0.9 us
  transfers between devices with their start and end apart: 10, of which 2 were waited for; matrix products, arithmetic and copies ran while one was open for 0% of the time, Pallas kernels for 10%

profile of v15, /device:TPU:0, one launch (start us, length us, event | category | flops | bytes accessed | tf_op | source)
XLA Modules:
  0.0 30.5 jit_solution(11232340249453687235)
XLA Ops:
  0.6 0.0 copy-start.1
  0.6 0.0 copy-start
  0.6 0.1 shard_map.59._.picked
  0.7 0.0 copy-start.3
  0.7 0.8 %copy-done.1 = bf16[1,64,1024]{2,1,0:T(8,128)(2,1)S(1)} copy-done((bf16[1,64,1024]{2,1,0:T(8,128)(2,1)S(1)}, bf16[1,64,1024]{2,1,0:T(8,128)(2,1)}, u32[]{:S(2)}) %copy-start.1) | copy-done | bytes 131096
  1.5 0.1 copy-done
  1.6 0.1 shard_map.60.own
  1.7 3.0 %collective-permute-start = (bf16[64,1024]{1,0:T(8,128)(2,1)S(1)}, bf16[64,1024]{1,0:T(8,128)(2,1)S(1)}, u32[]{:S(2)}, u32[]{:S(2)}) collective-permute-start(bf16[64,1024]{1,0:T(8,128)(2,1)S(1)} %shard_map.60.own), channel_id=1, source_target_pairs={{0,4},{4,0},{8,12},{12,8},{16,20},{20,16},{24,28},{28,24},{1,5},{5... | collective-permute-start | bytes 393224 | tf_op jit(solution)/shard_map/ppermute | solution.py:250
  4.7 1.3 %collective-permute-start.4 = (bf16[64,1024]{1,0:T(8,128)(2,1)S(1)}, bf16[64,1024]{1,0:T(8,128)(2,1)S(1)}, u32[]{:S(2)}, u32[]{:S(2)}) collective-permute-start(bf16[64,1024]{1,0:T(8,128)(2,1)S(1)} %shard_map.61._), channel_id=1, source_target_pairs={{8,0},{16,8},{24,16},{4,12},{12,20},{20,28},{9,1},{17,9},{25,17},{... | collective-permute-start | bytes 393224 | tf_op jit(solution)/shard_map/ppermute | solution.py:301
  6.0 0.0 copy-done.3
  6.0 0.0 copy-start.2
  6.0 0.3 %shard_map.62 = (bf16[128,1024]{1,0:T(8,128)(2,1)S(1)}, bf16[64,1024]{1,0:T(8,128)(2,1)S(1)}) custom-call(bf16[192,256]{1,0:T(8,128)(2,1)S(1)} %shard_map.59._.picked, bf16[1024,256]{1,0:T(8,128)(2,1)S(1)} %bitcast.7, bf16[64,1024]{1,0:T(8,128)(2,1)S(1)} %shard_map.61._), custom_call_target="tpu_custom_call" | custom-call | flops 905969664 | tf_op jit(solution)/shard_map/pallas_call | solution.py:291
  6.4 2.8 %collective-permute-start.2 = (bf16[64,1024]{1,0:T(8,128)(2,1)S(1)}, bf16[64,1024]{1,0:T(8,128)(2,1)S(1)}, u32[]{:S(2)}, u32[]{:S(2)}) collective-permute-start(bf16[64,1024]{1,0:T(8,128)(2,1)S(1)} %get-tuple-element.30), channel_id=1, source_target_pairs={{0,4},{4,0},{8,12},{12,8},{16,20},{20,16},{24,28},{28,24},{1,5},{5... | collective-permute-start | bytes 393224 | tf_op jit(solution)/shard_map/ppermute | solution.py:250
  9.2 0.0 copy-done.2
  9.2 0.1 shard_map.63
  9.2 0.0 collective-permute-done.near
  9.2 3.5 %collective-permute-start.1 = (bf16[64,1024]{1,0:T(8,128)(2,1)S(1)}, bf16[64,1024]{1,0:T(8,128)(2,1)S(1)}, u32[]{:S(2)}, u32[]{:S(2)}) collective-permute-start(bf16[64,1024]{1,0:T(8,128)(2,1)S(1)} %collective-permute-done.near), channel_id=1, source_target_pairs={{0,8},{8,16},{16,24},{12,4},{20,12},{28,20},{1,9},{9,17},{17,25},{... | collective-permute-start | bytes 393224 | tf_op jit(solution)/shard_map/ppermute | solution.py:302
  12.7 0.0 collective-permute-done.2.came
  12.7 0.1 collective-permute-start.3
  12.8 1.6 %shard_map.64 = (bf16[1088,384]{1,0:T(8,128)(2,1)S(1)}, f32[128,1152]{1,0:T(8,128)S(1)}, f32[1024,256]{1,0:T(8,128)S(1)}) custom-call(bf16[64,1024]{1,0:T(8,128)(2,1)S(1)} %shard_map.60.own, bf16[64,1024]{1,0:T(8,128)(2,1)S(1)} %collective-permute-done.near, bf16[128,1024]{1,0:T(8,128)(2,1)S(1)} %get-tuple-element.25.mine, ...), custom_call_target="tpu_custom_call" | custom-call | flops 2717908992 | bytes 4194304 | tf_op jit(solution)/shard_map/pallas_call | solution.py:309
  14.4 0.0 collective-permute-done.4.two_off
  14.4 0.0 collective-permute-done.3.other
  14.4 1.1 %shard_map.65 = (f32[128,576]{1,0:T(8,128)S(1)}, f32[432,128]{1,0:T(8,128)S(1)}, bf16[432,128]{1,0:T(8,128)(2,1)S(1)}, bf16[432,128]{1,0:T(8,128)(2,1)S(1)}, bf16[432,128]{1,0:T(8,128)(2,1)S(1)}) custom-call(bf16[64,1024]{1,0:T(8,128)(2,1)S(1)} %collective-permute-done.2.came, bf16[64,1024]{1,0:T(8,128)(2,1)S(1)} %collective-permute-done.3.other, ...), custom_call_target="tpu_custom_call" | custom-call | flops 2717908992 | bytes 4194304 | tf_op jit(solution)/shard_map/pallas_call | solution.py:320
  15.5 0.0 collective-permute-done.1.one_off
  15.5 0.9 %shard_map.66 = (f32[512,256]{1,0:T(8,128)S(1)}, bf16[512,256]{1,0:T(8,128)(2,1)S(1)}, f32[432,128]{1,0:T(8,128)S(1)}, bf16[432,128]{1,0:T(8,128)(2,1)S(1)}, bf1...) custom-call(bf16[64,1024]{1,0:T(8,128)(2,1)S(1)} %collective-permute, ...), custom_call_target="tpu_custom_call", output_to_operand_aliasing={{2}: (5, {}), {3}: (6, {}), {4}: (7, {}), {5}: (8, {})} | custom-call | flops 2717908992 | bytes 4194304 | tf_op jit(solution)/shard_map/pallas_call | solution.py:327
  16.4 0.6 %collective-permute-start.8 = (bf16[512,256]{1,0:T(8,128)(2,1)S(1)}, bf16[512,256]{1,0:T(8,128)(2,1)S(1)}, u32[]{:S(2)}, u32[]{:S(2)}) collective-permute-start(bf16[512,256]{1,0:T(8,128)(2,1)S(1)} %get-tuple-element.43), channel_id=1, source_target_pairs={{0,1},{1,0},{2,3},{3,2},{4,5},{5,4},{6,7},{7,6},{8,9},{9,8},{10,11... | collective-permute-start | bytes 786440 | tf_op jit(solution)/shard_map/ppermute | solution.py:250
  17.0 2.8 %collective-permute-start.5 = (bf16[432,128]{1,0:T(8,128)(2,1)S(1)}, bf16[432,128]{1,0:T(8,128)(2,1)S(1)}, u32[]{:S(2)}, u32[]{:S(2)}) collective-permute-start(bf16[432,128]{1,0:T(8,128)(2,1)S(1)} %get-tuple-element.39), channel_id=1, source_target_pairs={{0,16},{4,20},{8,24},{12,28},{16,0},{20,4},{24,8},{28,12},{1,17},{... | collective-permute-start | bytes 331784 | tf_op jit(solution)/shard_map/ppermute | solution.py:250
  19.8 1.3 %collective-permute-start.6 = (bf16[432,128]{1,0:T(8,128)(2,1)S(1)}, bf16[432,128]{1,0:T(8,128)(2,1)S(1)}, u32[]{:S(2)}, u32[]{:S(2)}) collective-permute-start(bf16[432,128]{1,0:T(8,128)(2,1)S(1)} %get-tuple-element.40), channel_id=1, source_target_pairs={{0,24},{4,28},{8,16},{12,20},{16,8},{20,12},{24,0},{28,4},{1,25},{... | collective-permute-start | bytes 331784 | tf_op jit(solution)/shard_map/ppermute | solution.py:250
  21.1 0.0 collective-permute-start.7
  21.1 0.0 collective-permute-done.8.came
  21.1 0.1 shard_map.68
  21.2 1.6 %collective-permute-start.9 = (bf16[256,256]{1,0:T(8,128)(2,1)S(1)}, bf16[256,256]{1,0:T(8,128)(2,1)S(1)}, u32[]{:S(2)}, u32[]{:S(2)}) collective-permute-start(bf16[256,256]{1,0:T(8,128)(2,1)S(1)} %get-tuple-element.45), channel_id=1, source_target_pairs={{0,2},{1,3},{2,0},{3,1},{4,6},{5,7},{6,4},{7,5},{8,10},{9,11},{10,... | collective-permute-start | bytes 393224 | tf_op jit(solution)/shard_map/ppermute | solution.py:250
  22.8 5.8 %collective-permute-done.5.rest_0_ = bf16[432,128]{1,0:T(8,128)(2,1)S(1)} collective-permute-done((bf16[432,128]{1,0:T(8,128)(2,1)S(1)}, bf16[432,128]{1,0:T(8,128)(2,1)S(1)}, u32[]{:S(2)}, u32[]{:S(2)}) %collective-permute-start.5) | collective-permute-done | bytes 110624 | tf_op jit(solution)/shard_map/ppermute | solution.py:250
  28.5 0.0 collective-permute-done.6.rest_1_
  28.5 1.0 %collective-permute-done.7.rest_2_ = bf16[432,128]{1,0:T(8,128)(2,1)S(1)} collective-permute-done((bf16[432,128]{1,0:T(8,128)(2,1)S(1)}, bf16[432,128]{1,0:T(8,128)(2,1)S(1)}, u32[]{:S(2)}, u32[]{:S(2)}) %collective-permute-start.7) | collective-permute-done | bytes 110624 | tf_op jit(solution)/shard_map/ppermute | solution.py:250
  29.5 0.1 shard_map.67.summed
  29.6 0.0 collective-permute-done.9.came
  29.6 0.9 %shard_map.69 = (f32[27,32,64]{2,1,0:T(8,128)}, bf16[256,256]{1,0:T(8,128)(2,1)}) custom-call(f32[32,1728]{1,0:T(8,128)S(1)} %shard_map.67.summed, f32[256,256]{1,0:T(8,128)S(1)} %get-tuple-element.44.kept, bf16[256,256]{1,0:T(8,128)(2,1)S(1)} %collective-permute-done.9.came), custom_call_target="tpu_custom_call" | custom-call | tf_op jit(solution)/shard_map/pallas_call | solution.py:368
  (1 shorter events, 0.0 us)
Async XLA Ops:
  0.6 0.9 %copy-start.1 = (bf16[1,64,1024]{2,1,0:T(8,128)(2,1)S(1)}, bf16[1,64,1024]{2,1,0:T(8,128)(2,1)}, u32[]{:S(2)}) copy-start(bf16[1,64,1024]{2,1,0:T(8,128)(2,1)} %param.6) | copy-start | bytes 393220
  0.6 1.0 %copy-start = (bf16[1,64,1024]{2,1,0:T(8,128)(2,1)S(1)}, bf16[1,64,1024]{2,1,0:T(8,128)(2,1)}, u32[]{:S(2)}) copy-start(bf16[1,64,1024]{2,1,0:T(8,128)(2,1)} %param.5) | copy-start | bytes 393220
  0.7 5.3 %copy-start.3 = (bf16[1,32,32,256]{3,2,1,0:T(8,128)(2,1)S(1)}, bf16[1,32,32,256]{3,2,1,0:T(8,128)(2,1)}, u32[]{:S(2)}) copy-start(bf16[1,32,32,256]{3,2,1,0:T(8,128)(2,1)} %param.4) | copy-start | bytes 1572868
  1.7 7.5 %collective-permute-start = (bf16[64,1024]{1,0:T(8,128)(2,1)S(1)}, bf16[64,1024]{1,0:T(8,128)(2,1)S(1)}, u32[]{:S(2)}, u32[]{:S(2)}) collective-permute-start(bf16[64,1024]{1,0:T(8,128)(2,1)S(1)} %shard_map.60.own), channel_id=1, source_target_pairs={{0,4},{4,0},{8,12},{12,8},{16,20},{20,16},{24,28},{28,24},{1,5},{5... | collective-permute-start | bytes 393224 | tf_op jit(solution)/shard_map/ppermute | solution.py:250
  4.7 9.7 %collective-permute-start.4 = (bf16[64,1024]{1,0:T(8,128)(2,1)S(1)}, bf16[64,1024]{1,0:T(8,128)(2,1)S(1)}, u32[]{:S(2)}, u32[]{:S(2)}) collective-permute-start(bf16[64,1024]{1,0:T(8,128)(2,1)S(1)} %shard_map.61._), channel_id=1, source_target_pairs={{8,0},{16,8},{24,16},{4,12},{12,20},{20,28},{9,1},{17,9},{25,17},{... | collective-permute-start | bytes 393224 | tf_op jit(solution)/shard_map/ppermute | solution.py:301
  6.0 3.1 %copy-start.2 = (bf16[27,64,256]{2,1,0:T(8,128)(2,1)S(1)}, bf16[27,64,256]{2,1,0:T(8,128)(2,1)}, u32[]{:S(2)}) copy-start(bf16[27,64,256]{2,1,0:T(8,128)(2,1)} %weight) | copy-start | bytes 2654212
  6.4 6.4 %collective-permute-start.2 = (bf16[64,1024]{1,0:T(8,128)(2,1)S(1)}, bf16[64,1024]{1,0:T(8,128)(2,1)S(1)}, u32[]{:S(2)}, u32[]{:S(2)}) collective-permute-start(bf16[64,1024]{1,0:T(8,128)(2,1)S(1)} %get-tuple-element.30), channel_id=1, source_target_pairs={{0,4},{4,0},{8,12},{12,8},{16,20},{20,16},{24,28},{28,24},{1,5},{5... | collective-permute-start | bytes 393224 | tf_op jit(solution)/shard_map/ppermute | solution.py:250
  9.2 6.2 %collective-permute-start.1 = (bf16[64,1024]{1,0:T(8,128)(2,1)S(1)}, bf16[64,1024]{1,0:T(8,128)(2,1)S(1)}, u32[]{:S(2)}, u32[]{:S(2)}) collective-permute-start(bf16[64,1024]{1,0:T(8,128)(2,1)S(1)} %collective-permute-done.near), channel_id=1, source_target_pairs={{0,8},{8,16},{16,24},{12,4},{20,12},{28,20},{1,9},{9,17},{17,25},{... | collective-permute-start | bytes 393224 | tf_op jit(solution)/shard_map/ppermute | solution.py:302
  12.7 1.7 %collective-permute-start.3 = (bf16[64,1024]{1,0:T(8,128)(2,1)S(1)}, bf16[64,1024]{1,0:T(8,128)(2,1)S(1)}, u32[]{:S(2)}, u32[]{:S(2)}) collective-permute-start(bf16[64,1024]{1,0:T(8,128)(2,1)S(1)} %collective-permute-done.2.came), channel_id=1, source_target_pairs={{0,1},{1,0},{2,3},{3,2},{4,5},{5,4},{6,7},{7,6},{8,9},{9,8},{10,11... | collective-permute-start | bytes 393224 | tf_op jit(solution)/shard_map/ppermute | solution.py:250
  16.4 4.7 %collective-permute-start.8 = (bf16[512,256]{1,0:T(8,128)(2,1)S(1)}, bf16[512,256]{1,0:T(8,128)(2,1)S(1)}, u32[]{:S(2)}, u32[]{:S(2)}) collective-permute-start(bf16[512,256]{1,0:T(8,128)(2,1)S(1)} %get-tuple-element.43), channel_id=1, source_target_pairs={{0,1},{1,0},{2,3},{3,2},{4,5},{5,4},{6,7},{7,6},{8,9},{9,8},{10,11... | collective-permute-start | bytes 786440 | tf_op jit(solution)/shard_map/ppermute | solution.py:250
  17.0 11.5 %collective-permute-start.5 = (bf16[432,128]{1,0:T(8,128)(2,1)S(1)}, bf16[432,128]{1,0:T(8,128)(2,1)S(1)}, u32[]{:S(2)}, u32[]{:S(2)}) collective-permute-start(bf16[432,128]{1,0:T(8,128)(2,1)S(1)} %get-tuple-element.39), channel_id=1, source_target_pairs={{0,16},{4,20},{8,24},{12,28},{16,0},{20,4},{24,8},{28,12},{1,17},{... | collective-permute-start | bytes 331784 | tf_op jit(solution)/shard_map/ppermute | solution.py:250
  19.8 8.7 %collective-permute-start.6 = (bf16[432,128]{1,0:T(8,128)(2,1)S(1)}, bf16[432,128]{1,0:T(8,128)(2,1)S(1)}, u32[]{:S(2)}, u32[]{:S(2)}) collective-permute-start(bf16[432,128]{1,0:T(8,128)(2,1)S(1)} %get-tuple-element.40), channel_id=1, source_target_pairs={{0,24},{4,28},{8,16},{12,20},{16,8},{20,12},{24,0},{28,4},{1,25},{... | collective-permute-start | bytes 331784 | tf_op jit(solution)/shard_map/ppermute | solution.py:250
  21.1 8.4 %collective-permute-start.7 = (bf16[432,128]{1,0:T(8,128)(2,1)S(1)}, bf16[432,128]{1,0:T(8,128)(2,1)S(1)}, u32[]{:S(2)}, u32[]{:S(2)}) collective-permute-start(bf16[432,128]{1,0:T(8,128)(2,1)S(1)} %get-tuple-element.41), channel_id=1, source_target_pairs={{0,8},{4,12},{8,0},{12,4},{16,24},{20,28},{24,16},{28,20},{1,9},{5... | collective-permute-start | bytes 331784 | tf_op jit(solution)/shard_map/ppermute | solution.py:250
  21.2 8.4 %collective-permute-start.9 = (bf16[256,256]{1,0:T(8,128)(2,1)S(1)}, bf16[256,256]{1,0:T(8,128)(2,1)S(1)}, u32[]{:S(2)}, u32[]{:S(2)}) collective-permute-start(bf16[256,256]{1,0:T(8,128)(2,1)S(1)} %get-tuple-element.45), channel_id=1, source_target_pairs={{0,2},{1,3},{2,0},{3,1},{4,6},{5,7},{6,4},{7,5},{8,10},{9,11},{10,... | collective-permute-start | bytes 393224 | tf_op jit(solution)/shard_map/ppermute | solution.py:250

commit v16 on v13

--- a/solution.py
+++ b/solution.py
@@ -160,9 +160,37 @@
     outer[:, wide + lanes : wide + lanes + filt] = middle[2][:, 0:filt]
 
 
+def rows_total(width, groups, target, windows, weight, spread):
+    size = spread.shape[0] // groups
+    index = lax.axis_index("filt")
+    count = bits_of(groups)
+    block = 0
+    for bit in range(count):
+        differs = (target >> (count - 1 - bit)) & 1
+        block = block + (((index >> bit) & 1) ^ differs) * (1 << bit)
+    start = pl.multiple_of(block * size, size)
+    total = spread[pl.ds(start, size), :]
+    for b in range(3):
+        rows = pl.ds(pl.multiple_of(start + (2 - b) * width, width), size)
+        total = total + jnp.dot(windows[rows, :], weight[b], preferred_element_type=jnp.float32)
+    return total
+
+
+def first_half_kernel(width, groups, windows, weight, spread, came, keep, send):
+    size = spread.shape[0] // groups
+    for target in range(groups // 2):
+        total = rows_total(width, groups, target, windows, weight, spread)
+        total = total + came[target * size : (target + 1) * size, :].astype(jnp.float32)
+        if target < groups // 4:
+            keep[target * size : (target + 1) * size, :] = total
+        else:
+            lo = (target - groups // 4) * size
+            send[lo : lo + size, :] = total.astype(jnp.bfloat16)
+
+
 def one_kernel(width, groups, radix, one_off, mine, weight, spread, outer, *rest):
-    kept_in, sent_in, keep, *rest = rest[radix:]
-    *sends, windows, tall = rest
+    windows, sent_in, keep, *rest = rest[radix:]
+    *sends, tall = rest
     cells = mine.shape[1]
     lanes = keep.shape[1]
     filt = lanes // 2
@@ -179,22 +207,10 @@
     store_tile(middle[2] + outer[:, 4 * lanes : 4 * lanes + filt], 13, keep, sends)
 
     size = cells // groups
-    index = lax.axis_index("filt")
-    count = bits_of(groups)
-    for target in reversed(range(groups)):
-        block = 0
-        for bit in range(count):
-            differs = (target >> (count - 1 - bit)) & 1
-            block = block + (((index >> bit) & 1) ^ differs) * (1 << bit)
-        start = pl.multiple_of(block * size, size)
-        total = spread[pl.ds(start, size), :]
-        for b in range(3):
-            rows = pl.ds(pl.multiple_of(start + (2 - b) * width, width), size)
-            total = total + jnp.dot(windows[rows, :], weight[b], preferred_element_type=jnp.float32)
-        if target < groups // 2:
-            kept_in[pl.ds(target * size, size), :] = total
-        else:
-            sent_in[pl.ds((target - groups // 2) * size, size), :] = total.astype(jnp.bfloat16)
+    for target in range(groups // 2, groups):
+        lo = (target - groups // 2) * size
+        total = rows_total(width, groups, target, windows, weight, spread)
+        sent_in[lo : lo + size, :] = total.astype(jnp.bfloat16)
 
 
 def unfolded(tiles, rows):
@@ -324,10 +340,10 @@
         flops=THEIRS * flops,
         bytes_accessed=4 * MIB,
     )(in_specs=[VMEM] * 5, out_specs=[VMEM] * (radix + 1))(came, other, two_off, windows, terms)
-    kept_in, sent_in, kept, *sends = call(
+    ones, sent_in, kept, *sends = call(
         functools.partial(one_kernel, width, groups, radix),
-        (shape((cells // 2, chans), f32), shape((cells // 2, chans), bf16)) + pieces,
-        (pltpu.VMEM((cells + 2 * width, 3 * filt), bf16), tall),
+        (shape((cells + 2 * width, 3 * filt), bf16), shape((cells // 2, chans), bf16)) + pieces,
+        (tall,),
         flops=ONE * flops,
         bytes_accessed=4 * MIB,
         aliases={5 + n: 2 + n for n in range(radix)},
@@ -353,7 +369,15 @@
         kept, *sends = (total[n * piece : (n + 1) * piece] for n in range(radix))
         sends = [value.astype(bf16) for value in sends]
 
-    distance_in = 2
+    block = (cells // 4, chans)
+    kept_in, sent_in = call(
+        functools.partial(first_half_kernel, width, groups),
+        (shape(block, f32), shape(block, bf16)),
+        flops=flops // 6,
+        bytes_accessed=MIB,
+    )(in_specs=[VMEM] * 4, out_specs=[VMEM] * 2)(ones, single_weight, spread, came_in)
+    came_in = swapped(sent_in, "filt", 2)
+    distance_in = 4
     while distance_in < groups:
         kept_in, sent_in = halved(kept_in, came_in)
         came_in = swapped(sent_in, "filt", distance_in)

time: 30.6 us -> 30.4 us (level)
  waiting for transfers between devices: 6.39 us -> 6.04 us
    ppermute x8, waiting for transfers between devices: 6.39 us -> 6.04 us  [swapped(): return lax.ppermute(value, axis, [(i, i ^ distance) for i in range(count)])]
  transfers between devices with their start and end apart: 10 -> 10, of which waited for: 2 -> 2; matrix products, arithmetic and copies ran while one was open for 0% -> 0% of each run, Pallas kernels for 10% -> 12%
where the time goes in v16:
time: 30.4 us; the launch traced here: 30.2 us
  starting transfers between devices  17.2 us (57%)
  waiting for transfers between devices  6.04 us (20%)
  Pallas kernels  5.33 us (18%)
  local copies, waits for them, and re-layouts  0.87 us (3%)
  between operations  0.8 us (3%)
    ppermute x8, starting transfers between devices, swapped(): return lax.ppermute(value, axis, [(i, i ^ distance) for i in range(count)])  12.4 us
    ppermute x8, waiting for transfers between devices, swapped(): return lax.ppermute(value, axis, [(i, i ^ distance) for i in range(count)])  6.04 us
    ppermute x1, starting transfers between devices, on_device(): one_off = lax.ppermute(near, 'space', up[even] + down[odd])  3.49 us
    pallas_call x1, Pallas kernels, on_device(): call(functools.partial(near_kernel, width), (windows_shape, shape((half,...  1.58 us
    ppermute x1, starting transfers between devices, on_device(): two_off = lax.ppermute(own_again, 'space', down[even] + up[odd])  1.29 us
    pallas_call x1, Pallas kernels, on_device(): call(functools.partial(theirs_kernel, width), (shape((half, 9 * filt), f3...  1.08 us
    pallas_call x1, Pallas kernels, on_device(): call(functools.partial(last_kernel, filt), (shape((taps, chans // blocks,...  0.9 us
    unnamed x8, local copies, waits for them, and re-layouts  0.87 us
  transfers between devices with their start and end apart: 10, of which 2 were waited for; matrix products, arithmetic and copies ran while one was open for 0% of the time, Pallas kernels for 12%

profile of v16, /device:TPU:0, one launch (start us, length us, event | category | flops | bytes accessed | tf_op | source)
XLA Modules:
  0.0 30.2 jit_solution(2112894926614032635)
XLA Ops:
  0.6 0.0 copy-start.1
  0.6 0.0 copy-start
  0.6 0.1 shard_map.59._.picked
  0.7 0.0 copy-start.3
  0.7 0.8 %copy-done.1 = bf16[1,64,1024]{2,1,0:T(8,128)(2,1)S(1)} copy-done((bf16[1,64,1024]{2,1,0:T(8,128)(2,1)S(1)}, bf16[1,64,1024]{2,1,0:T(8,128)(2,1)}, u32[]{:S(2)}) %copy-start.1) | copy-done | bytes 131096
  1.5 0.1 copy-done
  1.6 0.1 shard_map.60.own
  1.7 3.0 %collective-permute-start = (bf16[64,1024]{1,0:T(8,128)(2,1)S(1)}, bf16[64,1024]{1,0:T(8,128)(2,1)S(1)}, u32[]{:S(2)}, u32[]{:S(2)}) collective-permute-start(bf16[64,1024]{1,0:T(8,128)(2,1)S(1)} %shard_map.60.own), channel_id=1, source_target_pairs={{0,4},{4,0},{8,12},{12,8},{16,20},{20,16},{24,28},{28,24},{1,5},{5... | collective-permute-start | bytes 393224 | tf_op jit(solution)/shard_map/ppermute | solution.py:266
  4.7 1.3 %collective-permute-start.4 = (bf16[64,1024]{1,0:T(8,128)(2,1)S(1)}, bf16[64,1024]{1,0:T(8,128)(2,1)S(1)}, u32[]{:S(2)}, u32[]{:S(2)}) collective-permute-start(bf16[64,1024]{1,0:T(8,128)(2,1)S(1)} %shard_map.61._), channel_id=1, source_target_pairs={{8,0},{16,8},{24,16},{4,12},{12,20},{20,28},{9,1},{17,9},{25,17},{... | collective-permute-start | bytes 393224 | tf_op jit(solution)/shard_map/ppermute | solution.py:317
  6.0 0.0 copy-done.3
  6.0 0.0 copy-start.2
  6.0 0.3 %shard_map.62 = (bf16[128,1024]{1,0:T(8,128)(2,1)S(1)}, bf16[64,1024]{1,0:T(8,128)(2,1)S(1)}) custom-call(bf16[192,256]{1,0:T(8,128)(2,1)S(1)} %shard_map.59._.picked, bf16[1024,256]{1,0:T(8,128)(2,1)S(1)} %bitcast.7, bf16[64,1024]{1,0:T(8,128)(2,1)S(1)} %shard_map.61._), custom_call_target="tpu_custom_call" | custom-call | flops 905969664 | tf_op jit(solution)/shard_map/pallas_call | solution.py:307
  6.4 2.8 %collective-permute-start.2 = (bf16[64,1024]{1,0:T(8,128)(2,1)S(1)}, bf16[64,1024]{1,0:T(8,128)(2,1)S(1)}, u32[]{:S(2)}, u32[]{:S(2)}) collective-permute-start(bf16[64,1024]{1,0:T(8,128)(2,1)S(1)} %get-tuple-element.30), channel_id=1, source_target_pairs={{0,4},{4,0},{8,12},{12,8},{16,20},{20,16},{24,28},{28,24},{1,5},{5... | collective-permute-start | bytes 393224 | tf_op jit(solution)/shard_map/ppermute | solution.py:266
  9.2 0.0 copy-done.2
  9.2 0.1 shard_map.63
  9.2 0.0 collective-permute-done.near
  9.2 3.5 %collective-permute-start.1 = (bf16[64,1024]{1,0:T(8,128)(2,1)S(1)}, bf16[64,1024]{1,0:T(8,128)(2,1)S(1)}, u32[]{:S(2)}, u32[]{:S(2)}) collective-permute-start(bf16[64,1024]{1,0:T(8,128)(2,1)S(1)} %collective-permute-done.near), channel_id=1, source_target_pairs={{0,8},{8,16},{16,24},{12,4},{20,12},{28,20},{1,9},{9,17},{17,25},{... | collective-permute-start | bytes 393224 | tf_op jit(solution)/shard_map/ppermute | solution.py:318
  12.7 0.0 collective-permute-done.2.came
  12.7 0.1 collective-permute-start.3
  12.8 1.6 %shard_map.64 = (bf16[1088,384]{1,0:T(8,128)(2,1)S(1)}, f32[128,1152]{1,0:T(8,128)S(1)}, f32[1024,256]{1,0:T(8,128)S(1)}) custom-call(bf16[64,1024]{1,0:T(8,128)(2,1)S(1)} %shard_map.60.own, bf16[64,1024]{1,0:T(8,128)(2,1)S(1)} %collective-permute-done.near, bf16[128,1024]{1,0:T(8,128)(2,1)S(1)} %get-tuple-element.25.mine, ...), custom_call_target="tpu_custom_call" | custom-call | flops 2717908992 | bytes 4194304 | tf_op jit(solution)/shard_map/pallas_call | solution.py:325
  14.4 0.0 collective-permute-done.4.two_off
  14.4 0.0 collective-permute-done.3.other
  14.4 1.1 %shard_map.65 = (f32[128,576]{1,0:T(8,128)S(1)}, f32[432,128]{1,0:T(8,128)S(1)}, bf16[432,128]{1,0:T(8,128)(2,1)S(1)}, bf16[432,128]{1,0:T(8,128)(2,1)S(1)}, bf16[432,128]{1,0:T(8,128)(2,1)S(1)}) custom-call(bf16[64,1024]{1,0:T(8,128)(2,1)S(1)} %collective-permute-done.2.came, bf16[64,1024]{1,0:T(8,128)(2,1)S(1)} %collective-permute-done.3.other, ...), custom_call_target="tpu_custom_call" | custom-call | flops 2717908992 | bytes 4194304 | tf_op jit(solution)/shard_map/pallas_call | solution.py:336
  15.5 0.0 collective-permute-done.1.one_off
  15.5 0.8 %shard_map.66 = (bf16[1088,192]{1,0:T(8,128)(2,1)S(1)}, bf16[512,256]{1,0:T(8,128)(2,1)S(1)}, f32[432,128]{1,0:T(8,128)S(1)}, bf16[432,128]{1,0:T(8,128)(2,1)S(1...) custom-call(bf16[64,1024]{1,0:T(8,128)(2,1)S(1)} %collective-permute, ...), custom_call_target="tpu_custom_call", output_to_operand_aliasing={{2}: (5, {}), {3}: (6, {}), {4}: (7, {}), {5}: (8, {})} | custom-call | flops 2717908992 | bytes 4194304 | tf_op jit(solution)/shard_map/pallas_call | solution.py:343
  16.3 0.6 %collective-permute-start.8 = (bf16[512,256]{1,0:T(8,128)(2,1)S(1)}, bf16[512,256]{1,0:T(8,128)(2,1)S(1)}, u32[]{:S(2)}, u32[]{:S(2)}) collective-permute-start(bf16[512,256]{1,0:T(8,128)(2,1)S(1)} %get-tuple-element.43), channel_id=1, source_target_pairs={{0,1},{1,0},{2,3},{3,2},{4,5},{5,4},{6,7},{7,6},{8,9},{9,8},{10,11... | collective-permute-start | bytes 786440 | tf_op jit(solution)/shard_map/ppermute | solution.py:266
  16.9 2.7 %collective-permute-start.5 = (bf16[432,128]{1,0:T(8,128)(2,1)S(1)}, bf16[432,128]{1,0:T(8,128)(2,1)S(1)}, u32[]{:S(2)}, u32[]{:S(2)}) collective-permute-start(bf16[432,128]{1,0:T(8,128)(2,1)S(1)} %get-tuple-element.39), channel_id=1, source_target_pairs={{0,16},{4,20},{8,24},{12,28},{16,0},{20,4},{24,8},{28,12},{1,17},{... | collective-permute-start | bytes 331784 | tf_op jit(solution)/shard_map/ppermute | solution.py:266
  19.6 1.1 %collective-permute-start.6 = (bf16[432,128]{1,0:T(8,128)(2,1)S(1)}, bf16[432,128]{1,0:T(8,128)(2,1)S(1)}, u32[]{:S(2)}, u32[]{:S(2)}) collective-permute-start(bf16[432,128]{1,0:T(8,128)(2,1)S(1)} %get-tuple-element.40), channel_id=1, source_target_pairs={{0,8},{4,12},{8,0},{12,4},{16,24},{20,28},{24,16},{28,20},{1,9},{5... | collective-permute-start | bytes 331784 | tf_op jit(solution)/shard_map/ppermute | solution.py:266
  20.7 0.6 %collective-permute-start.7 = (bf16[432,128]{1,0:T(8,128)(2,1)S(1)}, bf16[432,128]{1,0:T(8,128)(2,1)S(1)}, u32[]{:S(2)}, u32[]{:S(2)}) collective-permute-start(bf16[432,128]{1,0:T(8,128)(2,1)S(1)} %get-tuple-element.41), channel_id=1, source_target_pairs={{0,24},{4,28},{8,16},{12,20},{16,8},{20,12},{24,0},{28,4},{1,25},{... | collective-permute-start | bytes 331784 | tf_op jit(solution)/shard_map/ppermute | solution.py:266
  21.3 0.0 collective-permute-done.8.came
  21.3 0.4 %shard_map.68 = (f32[256,256]{1,0:T(8,128)S(1)}, bf16[256,256]{1,0:T(8,128)(2,1)S(1)}) custom-call(bf16[1088,192]{1,0:T(8,128)(2,1)S(1)} %get-tuple-element.42.windows, bf16[3,192,256]{2,1,0:T(8,128)(2,1)S(1)} %get-tuple-element.27.weight, f32[1024,256]{1,0:T(8,128)S(1)} %get-tuple-element.29.spread, bf16[512,256]{1,0:T(8,128)(2,1)S(1)} %collective-permute-done.8.came), custom_call_target="tpu_custom_call" | custom-call | flops 150994944 | bytes 1048576 | tf_op jit(solution)/shard_map/pallas_call | solution.py:373
  21.6 1.6 %collective-permute-start.9 = (bf16[256,256]{1,0:T(8,128)(2,1)S(1)}, bf16[256,256]{1,0:T(8,128)(2,1)S(1)}, u32[]{:S(2)}, u32[]{:S(2)}) collective-permute-start(bf16[256,256]{1,0:T(8,128)(2,1)S(1)} %get-tuple-element.45), channel_id=1, source_target_pairs={{0,2},{1,3},{2,0},{3,1},{4,6},{5,7},{6,4},{7,5},{8,10},{9,11},{10,... | collective-permute-start | bytes 393224 | tf_op jit(solution)/shard_map/ppermute | solution.py:266
  23.2 2.8 %collective-permute-done.5.rest_0_ = bf16[432,128]{1,0:T(8,128)(2,1)S(1)} collective-permute-done((bf16[432,128]{1,0:T(8,128)(2,1)S(1)}, bf16[432,128]{1,0:T(8,128)(2,1)S(1)}, u32[]{:S(2)}, u32[]{:S(2)}) %collective-permute-start.5) | collective-permute-done | bytes 110624 | tf_op jit(solution)/shard_map/ppermute | solution.py:266
  26.0 0.0 collective-permute-done.6.rest_1_
  26.0 3.2 %collective-permute-done.7.rest_2_ = bf16[432,128]{1,0:T(8,128)(2,1)S(1)} collective-permute-done((bf16[432,128]{1,0:T(8,128)(2,1)S(1)}, bf16[432,128]{1,0:T(8,128)(2,1)S(1)}, u32[]{:S(2)}, u32[]{:S(2)}) %collective-permute-start.7) | collective-permute-done | bytes 110624 | tf_op jit(solution)/shard_map/ppermute | solution.py:266
  29.2 0.1 shard_map.67.summed
  29.3 0.0 collective-permute-done.9.came
  29.3 0.9 %shard_map.69 = (f32[27,32,64]{2,1,0:T(8,128)}, bf16[256,256]{1,0:T(8,128)(2,1)}) custom-call(f32[32,1728]{1,0:T(8,128)S(1)} %shard_map.67.summed, f32[256,256]{1,0:T(8,128)S(1)} %get-tuple-element.44.kept, bf16[256,256]{1,0:T(8,128)(2,1)S(1)} %collective-permute-done.9.came), custom_call_target="tpu_custom_call" | custom-call | tf_op jit(solution)/shard_map/pallas_call | solution.py:391
  (1 shorter events, 0.0 us)
Async XLA Ops:
  0.6 0.9 %copy-start.1 = (bf16[1,64,1024]{2,1,0:T(8,128)(2,1)S(1)}, bf16[1,64,1024]{2,1,0:T(8,128)(2,1)}, u32[]{:S(2)}) copy-start(bf16[1,64,1024]{2,1,0:T(8,128)(2,1)} %param.6) | copy-start | bytes 393220
  0.6 1.0 %copy-start = (bf16[1,64,1024]{2,1,0:T(8,128)(2,1)S(1)}, bf16[1,64,1024]{2,1,0:T(8,128)(2,1)}, u32[]{:S(2)}) copy-start(bf16[1,64,1024]{2,1,0:T(8,128)(2,1)} %param.5) | copy-start | bytes 393220
  0.7 5.3 %copy-start.3 = (bf16[1,32,32,256]{3,2,1,0:T(8,128)(2,1)S(1)}, bf16[1,32,32,256]{3,2,1,0:T(8,128)(2,1)}, u32[]{:S(2)}) copy-start(bf16[1,32,32,256]{3,2,1,0:T(8,128)(2,1)} %param.4) | copy-start | bytes 1572868
  1.7 7.5 %collective-permute-start = (bf16[64,1024]{1,0:T(8,128)(2,1)S(1)}, bf16[64,1024]{1,0:T(8,128)(2,1)S(1)}, u32[]{:S(2)}, u32[]{:S(2)}) collective-permute-start(bf16[64,1024]{1,0:T(8,128)(2,1)S(1)} %shard_map.60.own), channel_id=1, source_target_pairs={{0,4},{4,0},{8,12},{12,8},{16,20},{20,16},{24,28},{28,24},{1,5},{5... | collective-permute-start | bytes 393224 | tf_op jit(solution)/shard_map/ppermute | solution.py:266
  4.7 9.7 %collective-permute-start.4 = (bf16[64,1024]{1,0:T(8,128)(2,1)S(1)}, bf16[64,1024]{1,0:T(8,128)(2,1)S(1)}, u32[]{:S(2)}, u32[]{:S(2)}) collective-permute-start(bf16[64,1024]{1,0:T(8,128)(2,1)S(1)} %shard_map.61._), channel_id=1, source_target_pairs={{8,0},{16,8},{24,16},{4,12},{12,20},{20,28},{9,1},{17,9},{25,17},{... | collective-permute-start | bytes 393224 | tf_op jit(solution)/shard_map/ppermute | solution.py:317
  6.0 3.1 %copy-start.2 = (bf16[27,64,256]{2,1,0:T(8,128)(2,1)S(1)}, bf16[27,64,256]{2,1,0:T(8,128)(2,1)}, u32[]{:S(2)}) copy-start(bf16[27,64,256]{2,1,0:T(8,128)(2,1)} %weight) | copy-start | bytes 2654212
  6.4 6.4 %collective-permute-start.2 = (bf16[64,1024]{1,0:T(8,128)(2,1)S(1)}, bf16[64,1024]{1,0:T(8,128)(2,1)S(1)}, u32[]{:S(2)}, u32[]{:S(2)}) collective-permute-start(bf16[64,1024]{1,0:T(8,128)(2,1)S(1)} %get-tuple-element.30), channel_id=1, source_target_pairs={{0,4},{4,0},{8,12},{12,8},{16,20},{20,16},{24,28},{28,24},{1,5},{5... | collective-permute-start | bytes 393224 | tf_op jit(solution)/shard_map/ppermute | solution.py:266
  9.2 6.3 %collective-permute-start.1 = (bf16[64,1024]{1,0:T(8,128)(2,1)S(1)}, bf16[64,1024]{1,0:T(8,128)(2,1)S(1)}, u32[]{:S(2)}, u32[]{:S(2)}) collective-permute-start(bf16[64,1024]{1,0:T(8,128)(2,1)S(1)} %collective-permute-done.near), channel_id=1, source_target_pairs={{0,8},{8,16},{16,24},{12,4},{20,12},{28,20},{1,9},{9,17},{17,25},{... | collective-permute-start | bytes 393224 | tf_op jit(solution)/shard_map/ppermute | solution.py:318
  12.7 1.7 %collective-permute-start.3 = (bf16[64,1024]{1,0:T(8,128)(2,1)S(1)}, bf16[64,1024]{1,0:T(8,128)(2,1)S(1)}, u32[]{:S(2)}, u32[]{:S(2)}) collective-permute-start(bf16[64,1024]{1,0:T(8,128)(2,1)S(1)} %collective-permute-done.2.came), channel_id=1, source_target_pairs={{0,1},{1,0},{2,3},{3,2},{4,5},{5,4},{6,7},{7,6},{8,9},{9,8},{10,11... | collective-permute-start | bytes 393224 | tf_op jit(solution)/shard_map/ppermute | solution.py:266
  16.3 5.0 %collective-permute-start.8 = (bf16[512,256]{1,0:T(8,128)(2,1)S(1)}, bf16[512,256]{1,0:T(8,128)(2,1)S(1)}, u32[]{:S(2)}, u32[]{:S(2)}) collective-permute-start(bf16[512,256]{1,0:T(8,128)(2,1)S(1)} %get-tuple-element.43), channel_id=1, source_target_pairs={{0,1},{1,0},{2,3},{3,2},{4,5},{5,4},{6,7},{7,6},{8,9},{9,8},{10,11... | collective-permute-start | bytes 786440 | tf_op jit(solution)/shard_map/ppermute | solution.py:266
  16.9 9.1 %collective-permute-start.5 = (bf16[432,128]{1,0:T(8,128)(2,1)S(1)}, bf16[432,128]{1,0:T(8,128)(2,1)S(1)}, u32[]{:S(2)}, u32[]{:S(2)}) collective-permute-start(bf16[432,128]{1,0:T(8,128)(2,1)S(1)} %get-tuple-element.39), channel_id=1, source_target_pairs={{0,16},{4,20},{8,24},{12,28},{16,0},{20,4},{24,8},{28,12},{1,17},{... | collective-permute-start | bytes 331784 | tf_op jit(solution)/shard_map/ppermute | solution.py:266
  19.6 6.4 %collective-permute-start.6 = (bf16[432,128]{1,0:T(8,128)(2,1)S(1)}, bf16[432,128]{1,0:T(8,128)(2,1)S(1)}, u32[]{:S(2)}, u32[]{:S(2)}) collective-permute-start(bf16[432,128]{1,0:T(8,128)(2,1)S(1)} %get-tuple-element.40), channel_id=1, source_target_pairs={{0,8},{4,12},{8,0},{12,4},{16,24},{20,28},{24,16},{28,20},{1,9},{5... | collective-permute-start | bytes 331784 | tf_op jit(solution)/shard_map/ppermute | solution.py:266
  20.7 8.5 %collective-permute-start.7 = (bf16[432,128]{1,0:T(8,128)(2,1)S(1)}, bf16[432,128]{1,0:T(8,128)(2,1)S(1)}, u32[]{:S(2)}, u32[]{:S(2)}) collective-permute-start(bf16[432,128]{1,0:T(8,128)(2,1)S(1)} %get-tuple-element.41), channel_id=1, source_target_pairs={{0,24},{4,28},{8,16},{12,20},{16,8},{20,12},{24,0},{28,4},{1,25},{... | collective-permute-start | bytes 331784 | tf_op jit(solution)/shard_map/ppermute | solution.py:266
  21.6 7.7 %collective-permute-start.9 = (bf16[256,256]{1,0:T(8,128)(2,1)S(1)}, bf16[256,256]{1,0:T(8,128)(2,1)S(1)}, u32[]{:S(2)}, u32[]{:S(2)}) collective-permute-start(bf16[256,256]{1,0:T(8,128)(2,1)S(1)} %get-tuple-element.45), channel_id=1, source_target_pairs={{0,2},{1,3},{2,0},{3,1},{4,6},{5,7},{6,4},{7,5},{8,10},{9,11},{10,... | collective-permute-start | bytes 393224 | tf_op jit(solution)/shard_map/ppermute | solution.py:266

commit v17 on v16

--- a/solution.py
+++ b/solution.py
@@ -140,17 +140,19 @@
     first_core = lax.axis_index("filt") & 1 == 0
     theirs[0:part, :] = jnp.where(first_core, came[...], other[...])
     theirs[part:, :] = jnp.where(first_core, other[...], came[...])
-    lay_windows(width, two_off[...], two_off[...], twos, tall)
+    lay_single(width, two_off[...], twos, tall)
     left = lax.broadcasted_iota(jnp.int32, (2 * part, lanes), 1) < filt
     middle = []
     for b in range(3):
         rows = pl.ds((2 - b) * width, cells)
         near_terms = jnp.dot(theirs[...], windows[rows, :], preferred_element_type=jnp.float32)
         two_terms = jnp.dot(theirs[...], twos[rows, :], preferred_element_type=jnp.float32)
+        outside, centre = two_terms[:, 0:lanes], two_terms[:, lanes : lanes + filt]
+        far_side = (pltpu.roll(outside, filt, 1), jnp.concatenate([centre, centre], axis=1), outside)
         cuts = [slice(c * lanes, (c + 1) * lanes) for c in range(3)]
         for c, cut in enumerate(cuts):
             lo = b * wide + c * lanes
-            crossed = jnp.where(left, pltpu.roll(near_terms[:, cut], filt, 1), two_terms[:, cut])
+            crossed = jnp.where(left, pltpu.roll(near_terms[:, cut], filt, 1), far_side[c])
             store_tile(terms[:, lo : lo + lanes] + crossed, 3 * b + c, keep, sends)
         outer[:, b * lanes : (b + 1) * lanes] = jnp.where(
             left, near_terms[:, cuts[0]], pltpu.roll(near_terms[:, cuts[2]], filt, 1)
@@ -336,7 +338,7 @@
     outer, *partial = call(
         functools.partial(theirs_kernel, width),
         (shape((half, 9 * filt), f32),) + pieces,
-        (pltpu.VMEM((half, cells), bf16), pltpu.VMEM(windows_shape.shape, bf16), tall),
+        (pltpu.VMEM((half, cells), bf16), pltpu.VMEM((cells + 2 * width, 3 * filt), bf16), tall),
         flops=THEIRS * flops,
         bytes_accessed=4 * MIB,
     )(in_specs=[VMEM] * 5, out_specs=[VMEM] * (radix + 1))(came, other, two_off, windows, terms)

time: 30.4 us -> 30.4 us (level)
  transfers between devices with their start and end apart: 10 -> 10, of which waited for: 2 -> 2; matrix products, arithmetic and copies ran while one was open for 0% -> 0% of each run, Pallas kernels for 12% -> 11%
where the time goes in v17:
time: 30.4 us; the launch traced here: 30.2 us
  starting transfers between devices  17.2 us (57%)
  waiting for transfers between devices  6.14 us (20%)
  Pallas kernels  5.21 us (17%)
  local copies, waits for them, and re-layouts  0.87 us (3%)
  between operations  0.8 us (3%)
    ppermute x8, starting transfers between devices, swapped(): return lax.ppermute(value, axis, [(i, i ^ distance) for i in range(count)])  12.4 us
    ppermute x8, waiting for transfers between devices, swapped(): return lax.ppermute(value, axis, [(i, i ^ distance) for i in range(count)])  6.14 us
    ppermute x1, starting transfers between devices, on_device(): one_off = lax.ppermute(near, 'space', up[even] + down[odd])  3.49 us
    pallas_call x1, Pallas kernels, on_device(): call(functools.partial(near_kernel, width), (windows_shape, shape((half,...  1.58 us
    ppermute x1, starting transfers between devices, on_device(): two_off = lax.ppermute(own_again, 'space', down[even] + up[odd])  1.29 us
    pallas_call x1, Pallas kernels, on_device(): call(functools.partial(theirs_kernel, width), (shape((half, 9 * filt), f3...  0.97 us
    pallas_call x1, Pallas kernels, on_device(): call(functools.partial(last_kernel, filt), (shape((taps, chans // blocks,...  0.9 us
    unnamed x8, local copies, waits for them, and re-layouts  0.87 us
  transfers between devices with their start and end apart: 10, of which 2 were waited for; matrix products, arithmetic and copies ran while one was open for 0% of the time, Pallas kernels for 11%

profile of v17, /device:TPU:0, one launch (start us, length us, event | category | flops | bytes accessed | tf_op | source)
XLA Modules:
  0.0 30.2 jit_solution(700032298273114299)
XLA Ops:
  0.6 0.0 copy-start.1
  0.6 0.0 copy-start
  0.6 0.1 shard_map.59._.picked
  0.7 0.0 copy-start.3
  0.7 0.8 %copy-done.1 = bf16[1,64,1024]{2,1,0:T(8,128)(2,1)S(1)} copy-done((bf16[1,64,1024]{2,1,0:T(8,128)(2,1)S(1)}, bf16[1,64,1024]{2,1,0:T(8,128)(2,1)}, u32[]{:S(2)}) %copy-start.1) | copy-done | bytes 131096
  1.5 0.1 copy-done
  1.6 0.1 shard_map.60.own
  1.7 3.0 %collective-permute-start = (bf16[64,1024]{1,0:T(8,128)(2,1)S(1)}, bf16[64,1024]{1,0:T(8,128)(2,1)S(1)}, u32[]{:S(2)}, u32[]{:S(2)}) collective-permute-start(bf16[64,1024]{1,0:T(8,128)(2,1)S(1)} %shard_map.60.own), channel_id=1, source_target_pairs={{0,4},{4,0},{8,12},{12,8},{16,20},{20,16},{24,28},{28,24},{1,5},{5... | collective-permute-start | bytes 393224 | tf_op jit(solution)/shard_map/ppermute | solution.py:268
  4.7 1.3 %collective-permute-start.4 = (bf16[64,1024]{1,0:T(8,128)(2,1)S(1)}, bf16[64,1024]{1,0:T(8,128)(2,1)S(1)}, u32[]{:S(2)}, u32[]{:S(2)}) collective-permute-start(bf16[64,1024]{1,0:T(8,128)(2,1)S(1)} %shard_map.61._), channel_id=1, source_target_pairs={{8,0},{16,8},{24,16},{4,12},{12,20},{20,28},{9,1},{17,9},{25,17},{... | collective-permute-start | bytes 393224 | tf_op jit(solution)/shard_map/ppermute | solution.py:319
  6.0 0.0 copy-done.3
  6.0 0.0 copy-start.2
  6.0 0.3 %shard_map.62 = (bf16[128,1024]{1,0:T(8,128)(2,1)S(1)}, bf16[64,1024]{1,0:T(8,128)(2,1)S(1)}) custom-call(bf16[192,256]{1,0:T(8,128)(2,1)S(1)} %shard_map.59._.picked, bf16[1024,256]{1,0:T(8,128)(2,1)S(1)} %bitcast.7, bf16[64,1024]{1,0:T(8,128)(2,1)S(1)} %shard_map.61._), custom_call_target="tpu_custom_call" | custom-call | flops 905969664 | tf_op jit(solution)/shard_map/pallas_call | solution.py:309
  6.4 2.8 %collective-permute-start.2 = (bf16[64,1024]{1,0:T(8,128)(2,1)S(1)}, bf16[64,1024]{1,0:T(8,128)(2,1)S(1)}, u32[]{:S(2)}, u32[]{:S(2)}) collective-permute-start(bf16[64,1024]{1,0:T(8,128)(2,1)S(1)} %get-tuple-element.30), channel_id=1, source_target_pairs={{0,4},{4,0},{8,12},{12,8},{16,20},{20,16},{24,28},{28,24},{1,5},{5... | collective-permute-start | bytes 393224 | tf_op jit(solution)/shard_map/ppermute | solution.py:268
  9.2 0.0 copy-done.2
  9.2 0.1 shard_map.63
  9.2 0.0 collective-permute-done.near
  9.2 3.5 %collective-permute-start.1 = (bf16[64,1024]{1,0:T(8,128)(2,1)S(1)}, bf16[64,1024]{1,0:T(8,128)(2,1)S(1)}, u32[]{:S(2)}, u32[]{:S(2)}) collective-permute-start(bf16[64,1024]{1,0:T(8,128)(2,1)S(1)} %collective-permute-done.near), channel_id=1, source_target_pairs={{0,8},{8,16},{16,24},{12,4},{20,12},{28,20},{1,9},{9,17},{17,25},{... | collective-permute-start | bytes 393224 | tf_op jit(solution)/shard_map/ppermute | solution.py:320
  12.7 0.0 collective-permute-done.2.came
  12.7 0.1 collective-permute-start.3
  12.8 1.6 %shard_map.64 = (bf16[1088,384]{1,0:T(8,128)(2,1)S(1)}, f32[128,1152]{1,0:T(8,128)S(1)}, f32[1024,256]{1,0:T(8,128)S(1)}) custom-call(bf16[64,1024]{1,0:T(8,128)(2,1)S(1)} %shard_map.60.own, bf16[64,1024]{1,0:T(8,128)(2,1)S(1)} %collective-permute-done.near, bf16[128,1024]{1,0:T(8,128)(2,1)S(1)} %get-tuple-element.25.mine, ...), custom_call_target="tpu_custom_call" | custom-call | flops 2717908992 | bytes 4194304 | tf_op jit(solution)/shard_map/pallas_call | solution.py:327
  14.4 0.0 collective-permute-done.4.two_off
  14.4 0.0 collective-permute-done.3.other
  14.4 1.0 %shard_map.65 = (f32[128,576]{1,0:T(8,128)S(1)}, f32[432,128]{1,0:T(8,128)S(1)}, bf16[432,128]{1,0:T(8,128)(2,1)S(1)}, bf16[432,128]{1,0:T(8,128)(2,1)S(1)}, bf16[432,128]{1,0:T(8,128)(2,1)S(1)}) custom-call(bf16[64,1024]{1,0:T(8,128)(2,1)S(1)} %collective-permute-done.2.came, bf16[64,1024]{1,0:T(8,128)(2,1)S(1)} %collective-permute-done.3.other, ...), custom_call_target="tpu_custom_call" | custom-call | flops 2717908992 | bytes 4194304 | tf_op jit(solution)/shard_map/pallas_call | solution.py:338
  15.4 0.0 collective-permute-done.1.one_off
  15.4 0.8 %shard_map.66 = (bf16[1088,192]{1,0:T(8,128)(2,1)S(1)}, bf16[512,256]{1,0:T(8,128)(2,1)S(1)}, f32[432,128]{1,0:T(8,128)S(1)}, bf16[432,128]{1,0:T(8,128)(2,1)S(1...) custom-call(bf16[64,1024]{1,0:T(8,128)(2,1)S(1)} %collective-permute, ...), custom_call_target="tpu_custom_call", output_to_operand_aliasing={{2}: (5, {}), {3}: (6, {}), {4}: (7, {}), {5}: (8, {})} | custom-call | flops 2717908992 | bytes 4194304 | tf_op jit(solution)/shard_map/pallas_call | solution.py:345
  16.2 0.6 %collective-permute-start.8 = (bf16[512,256]{1,0:T(8,128)(2,1)S(1)}, bf16[512,256]{1,0:T(8,128)(2,1)S(1)}, u32[]{:S(2)}, u32[]{:S(2)}) collective-permute-start(bf16[512,256]{1,0:T(8,128)(2,1)S(1)} %get-tuple-element.43), channel_id=1, source_target_pairs={{0,1},{1,0},{2,3},{3,2},{4,5},{5,4},{6,7},{7,6},{8,9},{9,8},{10,11... | collective-permute-start | bytes 786440 | tf_op jit(solution)/shard_map/ppermute | solution.py:268
  16.7 2.9 %collective-permute-start.5 = (bf16[432,128]{1,0:T(8,128)(2,1)S(1)}, bf16[432,128]{1,0:T(8,128)(2,1)S(1)}, u32[]{:S(2)}, u32[]{:S(2)}) collective-permute-start(bf16[432,128]{1,0:T(8,128)(2,1)S(1)} %get-tuple-element.39), channel_id=1, source_target_pairs={{0,16},{4,20},{8,24},{12,28},{16,0},{20,4},{24,8},{28,12},{1,17},{... | collective-permute-start | bytes 331784 | tf_op jit(solution)/shard_map/ppermute | solution.py:268
  19.6 1.0 %collective-permute-start.6 = (bf16[432,128]{1,0:T(8,128)(2,1)S(1)}, bf16[432,128]{1,0:T(8,128)(2,1)S(1)}, u32[]{:S(2)}, u32[]{:S(2)}) collective-permute-start(bf16[432,128]{1,0:T(8,128)(2,1)S(1)} %get-tuple-element.40), channel_id=1, source_target_pairs={{0,8},{4,12},{8,0},{12,4},{16,24},{20,28},{24,16},{28,20},{1,9},{5... | collective-permute-start | bytes 331784 | tf_op jit(solution)/shard_map/ppermute | solution.py:268
  20.6 0.6 %collective-permute-start.7 = (bf16[432,128]{1,0:T(8,128)(2,1)S(1)}, bf16[432,128]{1,0:T(8,128)(2,1)S(1)}, u32[]{:S(2)}, u32[]{:S(2)}) collective-permute-start(bf16[432,128]{1,0:T(8,128)(2,1)S(1)} %get-tuple-element.41), channel_id=1, source_target_pairs={{0,24},{4,28},{8,16},{12,20},{16,8},{20,12},{24,0},{28,4},{1,25},{... | collective-permute-start | bytes 331784 | tf_op jit(solution)/shard_map/ppermute | solution.py:268
  21.1 0.0 collective-permute-done.8.came
  21.1 0.4 %shard_map.68 = (f32[256,256]{1,0:T(8,128)S(1)}, bf16[256,256]{1,0:T(8,128)(2,1)S(1)}) custom-call(bf16[1088,192]{1,0:T(8,128)(2,1)S(1)} %get-tuple-element.42.windows, bf16[3,192,256]{2,1,0:T(8,128)(2,1)S(1)} %get-tuple-element.27.weight, f32[1024,256]{1,0:T(8,128)S(1)} %get-tuple-element.29.spread, bf16[512,256]{1,0:T(8,128)(2,1)S(1)} %collective-permute-done.8.came), custom_call_target="tpu_custom_call" | custom-call | flops 150994944 | bytes 1048576 | tf_op jit(solution)/shard_map/pallas_call | solution.py:375
  21.5 1.6 %collective-permute-start.9 = (bf16[256,256]{1,0:T(8,128)(2,1)S(1)}, bf16[256,256]{1,0:T(8,128)(2,1)S(1)}, u32[]{:S(2)}, u32[]{:S(2)}) collective-permute-start(bf16[256,256]{1,0:T(8,128)(2,1)S(1)} %get-tuple-element.45), channel_id=1, source_target_pairs={{0,2},{1,3},{2,0},{3,1},{4,6},{5,7},{6,4},{7,5},{8,10},{9,11},{10,... | collective-permute-start | bytes 393224 | tf_op jit(solution)/shard_map/ppermute | solution.py:268
  23.1 2.9 %collective-permute-done.5.rest_0_ = bf16[432,128]{1,0:T(8,128)(2,1)S(1)} collective-permute-done((bf16[432,128]{1,0:T(8,128)(2,1)S(1)}, bf16[432,128]{1,0:T(8,128)(2,1)S(1)}, u32[]{:S(2)}, u32[]{:S(2)}) %collective-permute-start.5) | collective-permute-done | bytes 110624 | tf_op jit(solution)/shard_map/ppermute | solution.py:268
  25.9 0.0 collective-permute-done.6.rest_1_
  25.9 3.3 %collective-permute-done.7.rest_2_ = bf16[432,128]{1,0:T(8,128)(2,1)S(1)} collective-permute-done((bf16[432,128]{1,0:T(8,128)(2,1)S(1)}, bf16[432,128]{1,0:T(8,128)(2,1)S(1)}, u32[]{:S(2)}, u32[]{:S(2)}) %collective-permute-start.7) | collective-permute-done | bytes 110624 | tf_op jit(solution)/shard_map/ppermute | solution.py:268
  29.2 0.1 shard_map.67.summed
  29.3 0.0 collective-permute-done.9.came
  29.3 0.9 %shard_map.69 = (f32[27,32,64]{2,1,0:T(8,128)}, bf16[256,256]{1,0:T(8,128)(2,1)}) custom-call(f32[32,1728]{1,0:T(8,128)S(1)} %shard_map.67.summed, f32[256,256]{1,0:T(8,128)S(1)} %get-tuple-element.44.kept, bf16[256,256]{1,0:T(8,128)(2,1)S(1)} %collective-permute-done.9.came), custom_call_target="tpu_custom_call" | custom-call | tf_op jit(solution)/shard_map/pallas_call | solution.py:393
  (1 shorter events, 0.0 us)
Async XLA Ops:
  0.6 0.9 %copy-start.1 = (bf16[1,64,1024]{2,1,0:T(8,128)(2,1)S(1)}, bf16[1,64,1024]{2,1,0:T(8,128)(2,1)}, u32[]{:S(2)}) copy-start(bf16[1,64,1024]{2,1,0:T(8,128)(2,1)} %param.6) | copy-start | bytes 393220
  0.6 1.0 %copy-start = (bf16[1,64,1024]{2,1,0:T(8,128)(2,1)S(1)}, bf16[1,64,1024]{2,1,0:T(8,128)(2,1)}, u32[]{:S(2)}) copy-start(bf16[1,64,1024]{2,1,0:T(8,128)(2,1)} %param.5) | copy-start | bytes 393220
  0.7 5.3 %copy-start.3 = (bf16[1,32,32,256]{3,2,1,0:T(8,128)(2,1)S(1)}, bf16[1,32,32,256]{3,2,1,0:T(8,128)(2,1)}, u32[]{:S(2)}) copy-start(bf16[1,32,32,256]{3,2,1,0:T(8,128)(2,1)} %param.4) | copy-start | bytes 1572868
  1.7 7.5 %collective-permute-start = (bf16[64,1024]{1,0:T(8,128)(2,1)S(1)}, bf16[64,1024]{1,0:T(8,128)(2,1)S(1)}, u32[]{:S(2)}, u32[]{:S(2)}) collective-permute-start(bf16[64,1024]{1,0:T(8,128)(2,1)S(1)} %shard_map.60.own), channel_id=1, source_target_pairs={{0,4},{4,0},{8,12},{12,8},{16,20},{20,16},{24,28},{28,24},{1,5},{5... | collective-permute-start | bytes 393224 | tf_op jit(solution)/shard_map/ppermute | solution.py:268
  4.7 9.7 %collective-permute-start.4 = (bf16[64,1024]{1,0:T(8,128)(2,1)S(1)}, bf16[64,1024]{1,0:T(8,128)(2,1)S(1)}, u32[]{:S(2)}, u32[]{:S(2)}) collective-permute-start(bf16[64,1024]{1,0:T(8,128)(2,1)S(1)} %shard_map.61._), channel_id=1, source_target_pairs={{8,0},{16,8},{24,16},{4,12},{12,20},{20,28},{9,1},{17,9},{25,17},{... | collective-permute-start | bytes 393224 | tf_op jit(solution)/shard_map/ppermute | solution.py:319
  6.0 3.1 %copy-start.2 = (bf16[27,64,256]{2,1,0:T(8,128)(2,1)S(1)}, bf16[27,64,256]{2,1,0:T(8,128)(2,1)}, u32[]{:S(2)}) copy-start(bf16[27,64,256]{2,1,0:T(8,128)(2,1)} %weight) | copy-start | bytes 2654212
  6.4 6.4 %collective-permute-start.2 = (bf16[64,1024]{1,0:T(8,128)(2,1)S(1)}, bf16[64,1024]{1,0:T(8,128)(2,1)S(1)}, u32[]{:S(2)}, u32[]{:S(2)}) collective-permute-start(bf16[64,1024]{1,0:T(8,128)(2,1)S(1)} %get-tuple-element.30), channel_id=1, source_target_pairs={{0,4},{4,0},{8,12},{12,8},{16,20},{20,16},{24,28},{28,24},{1,5},{5... | collective-permute-start | bytes 393224 | tf_op jit(solution)/shard_map/ppermute | solution.py:268
  9.2 6.2 %collective-permute-start.1 = (bf16[64,1024]{1,0:T(8,128)(2,1)S(1)}, bf16[64,1024]{1,0:T(8,128)(2,1)S(1)}, u32[]{:S(2)}, u32[]{:S(2)}) collective-permute-start(bf16[64,1024]{1,0:T(8,128)(2,1)S(1)} %collective-permute-done.near), channel_id=1, source_target_pairs={{0,8},{8,16},{16,24},{12,4},{20,12},{28,20},{1,9},{9,17},{17,25},{... | collective-permute-start | bytes 393224 | tf_op jit(solution)/shard_map/ppermute | solution.py:320
  12.7 1.7 %collective-permute-start.3 = (bf16[64,1024]{1,0:T(8,128)(2,1)S(1)}, bf16[64,1024]{1,0:T(8,128)(2,1)S(1)}, u32[]{:S(2)}, u32[]{:S(2)}) collective-permute-start(bf16[64,1024]{1,0:T(8,128)(2,1)S(1)} %collective-permute-done.2.came), channel_id=1, source_target_pairs={{0,1},{1,0},{2,3},{3,2},{4,5},{5,4},{6,7},{7,6},{8,9},{9,8},{10,11... | collective-permute-start | bytes 393224 | tf_op jit(solution)/shard_map/ppermute | solution.py:268
  16.2 5.0 %collective-permute-start.8 = (bf16[512,256]{1,0:T(8,128)(2,1)S(1)}, bf16[512,256]{1,0:T(8,128)(2,1)S(1)}, u32[]{:S(2)}, u32[]{:S(2)}) collective-permute-start(bf16[512,256]{1,0:T(8,128)(2,1)S(1)} %get-tuple-element.43), channel_id=1, source_target_pairs={{0,1},{1,0},{2,3},{3,2},{4,5},{5,4},{6,7},{7,6},{8,9},{9,8},{10,11... | collective-permute-start | bytes 786440 | tf_op jit(solution)/shard_map/ppermute | solution.py:268
  16.7 9.2 %collective-permute-start.5 = (bf16[432,128]{1,0:T(8,128)(2,1)S(1)}, bf16[432,128]{1,0:T(8,128)(2,1)S(1)}, u32[]{:S(2)}, u32[]{:S(2)}) collective-permute-start(bf16[432,128]{1,0:T(8,128)(2,1)S(1)} %get-tuple-element.39), channel_id=1, source_target_pairs={{0,16},{4,20},{8,24},{12,28},{16,0},{20,4},{24,8},{28,12},{1,17},{... | collective-permute-start | bytes 331784 | tf_op jit(solution)/shard_map/ppermute | solution.py:268
  19.6 6.3 %collective-permute-start.6 = (bf16[432,128]{1,0:T(8,128)(2,1)S(1)}, bf16[432,128]{1,0:T(8,128)(2,1)S(1)}, u32[]{:S(2)}, u32[]{:S(2)}) collective-permute-start(bf16[432,128]{1,0:T(8,128)(2,1)S(1)} %get-tuple-element.40), channel_id=1, source_target_pairs={{0,8},{4,12},{8,0},{12,4},{16,24},{20,28},{24,16},{28,20},{1,9},{5... | collective-permute-start | bytes 331784 | tf_op jit(solution)/shard_map/ppermute | solution.py:268
  20.6 8.7 %collective-permute-start.7 = (bf16[432,128]{1,0:T(8,128)(2,1)S(1)}, bf16[432,128]{1,0:T(8,128)(2,1)S(1)}, u32[]{:S(2)}, u32[]{:S(2)}) collective-permute-start(bf16[432,128]{1,0:T(8,128)(2,1)S(1)} %get-tuple-element.41), channel_id=1, source_target_pairs={{0,24},{4,28},{8,16},{12,20},{16,8},{20,12},{24,0},{28,4},{1,25},{... | collective-permute-start | bytes 331784 | tf_op jit(solution)/shard_map/ppermute | solution.py:268
  21.5 7.8 %collective-permute-start.9 = (bf16[256,256]{1,0:T(8,128)(2,1)S(1)}, bf16[256,256]{1,0:T(8,128)(2,1)S(1)}, u32[]{:S(2)}, u32[]{:S(2)}) collective-permute-start(bf16[256,256]{1,0:T(8,128)(2,1)S(1)} %get-tuple-element.45), channel_id=1, source_target_pairs={{0,2},{1,3},{2,0},{3,1},{4,6},{5,7},{6,4},{7,5},{8,10},{9,11},{10,... | collective-permute-start | bytes 393224 | tf_op jit(solution)/shard_map/ppermute | solution.py:268
